TPU v7x, 32 devices: a whole 2x2x4 slice. The times are simulated.
32 devices in a mesh: layer: 2 (over y), pos: 16 (over z, x, core).
Axes of the slice: x: 2, y: 2, z: 4, core: 2. Of those that a mesh axis runs over, the one named last changes fastest.
Arguments:
- layer_inputs: bfloat16 [2, 32, 16, 16, 128], P('layer', 'pos'), may hold values from -6 to 6
- output_grads: bfloat16 [2, 32, 16, 16, 128], P('layer', 'pos'), may hold values from -2 to 2
- input_inverse: float32 [2, 1152, 1152], P('layer', 'pos'), may hold values from -0.06 to 2.1
- grad_inverse: float32 [2, 128, 128], P('layer'), may hold values from -4 to 54
Outputs:
- update: float32 [2, 1152, 128], P('layer', 'pos')
- grad_grams: float32 [2, 2, 128, 128], P('layer')
All inputs are finite; a program needn't handle non-finite values.
Results may differ from a plain program's by a relative error of at most 0.0023.
Values may be sent and summed in bfloat16 or wider, within the bound.
No kernel may reach another device: no remote copies, remote signals or barrier semaphores. Data moves between devices by JAX's collectives and lax.ppermute only.
A program may use at most 64 MiB of HBM per device.

v0:
```python
import jax
import jax.numpy as jnp
from jax import lax
from jax.sharding import PartitionSpec as P


def shifted(block, axis, distance):
    devices = range(lax.axis_size(axis))
    route = [(i - distance, i) for i in devices if i - distance in devices]
    return lax.ppermute(block, axis, route)


def pad_maps(layer_maps):
    return jnp.pad(layer_maps, ((0, 0), (1, 1), (1, 1), (0, 0)))


def unfold_piece(padded, kernel_tap, width):
    offset_row = kernel_tap // 3
    offset_col = kernel_tap % 3
    side = padded.shape[1] - 2
    return padded[:, offset_row : offset_row + side, offset_col : offset_col + side, :].reshape(
        -1, width
    )


def apply_patches(padded_maps, precond_all, row_count, width):
    mapped = jnp.zeros((row_count, width), jnp.float32)
    for kernel_tap in range(9):
        mapped = mapped + jnp.dot(
            unfold_piece(padded_maps, kernel_tap, width),
            precond_all[kernel_tap * width : (kernel_tap + 1) * width],
            preferred_element_type=jnp.float32,
        )
    return mapped.astype(jnp.bfloat16)


def per_device(layer_inputs, output_grads, input_inverse, grad_inverse):
    high = lax.Precision.HIGHEST
    layer_maps = layer_inputs[0]
    grad_maps = output_grads[0]
    width = layer_maps.shape[3]
    row_count = layer_maps.shape[0] * layer_maps.shape[1] * layer_maps.shape[2]
    scale_all = 1.0 / (row_count * lax.axis_size("pos"))
    maps_after, grads_after = shifted((layer_maps, grad_maps), "layer", -1)
    padded = pad_maps(layer_maps)
    grad_rows = grad_maps.reshape(-1, width)
    blocks = [
        jnp.dot(
            unfold_piece(padded, kernel_tap, width).T, grad_rows, preferred_element_type=jnp.float32
        )
        for kernel_tap in range(9)
    ]
    grad_part = jnp.concatenate(blocks, axis=0)
    own_part = jnp.dot(grad_rows.T, grad_rows, preferred_element_type=jnp.float32)
    cross_part = jnp.dot(
        grad_rows.T, grads_after.reshape(-1, width), preferred_element_type=jnp.float32
    )
    grad_sum, own_sum, cross_sum = lax.psum((grad_part, own_part, cross_part), "pos")
    grad_w = grad_sum * scale_all
    g_own = own_sum * scale_all
    g_cross = cross_sum * scale_all
    inverse_rows = input_inverse[0]
    grad_inv = grad_inverse[0]
    shard_rows = inverse_rows.shape[0]
    precond_mine = jnp.dot(
        jnp.dot(inverse_rows, grad_w, precision=high), grad_inv, precision=high
    ).astype(jnp.bfloat16)
    padded_after = pad_maps(maps_after)
    precond_layer = lax.all_gather(precond_mine, "pos", axis=0, tiled=True)
    precond_all = shifted(precond_layer, "layer", -1)
    mapped = apply_patches(padded_after, precond_all, row_count, width)
    blocks = [
        jnp.dot(
            unfold_piece(padded, kernel_tap, width).T, mapped, preferred_element_type=jnp.float32
        )
        for kernel_tap in range(9)
    ]
    cross_local = jnp.concatenate(blocks, axis=0)
    cross_share = lax.psum_scatter(cross_local, "pos", scatter_dimension=0, tiled=True) * scale_all
    row_start = lax.axis_index("pos") * shard_rows
    grad_share = lax.dynamic_slice_in_dim(grad_w, row_start, shard_rows, 0)
    corrected_share = grad_share - jnp.dot(cross_share, g_cross.T, precision=high)
    corrected = lax.all_gather(corrected_share, "pos", axis=0, tiled=True)
    update = jnp.dot(jnp.dot(inverse_rows, corrected, precision=high), grad_inv, precision=high)
    grad_grams = jnp.stack([g_own, g_cross], axis=0)
    return (update[None], grad_grams[None])


def solution(mesh):
    return jax.shard_map(
        per_device,
        mesh=mesh,
        in_specs=(
            P("layer", "pos", None, None, None),
            P("layer", "pos", None, None, None),
            P("layer", "pos", None),
            P("layer", None, None),
        ),
        out_specs=(P("layer", "pos", None), P("layer", None, None, None)),
        check_vma=False,
    )
```

profile of v0, /device:TPU:0, one launch (start us, length us, event | category | flops | bytes accessed | tf_op | source)
XLA Modules:
  0.0 235.1 jit_solution(1695000215966046205)
XLA Ops:
  7.2 1.4 collective-permute-start.2
  8.7 1.8 pad_slice_fusion.8
  11.4 0.7 copy-done.5
  13.2 0.8 convolution_bitcast_fusion.1
  14.1 1.2 collective-permute-done.2
  15.3 0.9 fusion.40
  16.2 94.5 %all-reduce.6.cloned.1.call-done = (f32[128,128]{1,0:T(8,128)}, f32[1152,128]{1,0:T(8,128)}, f32[128,128]{1,0:T(8,128)}) async-done(((f32[128,128]{1,0:T(8,128)}, f32[1152,128]{1,0:T(8,128)}, f32[128,128]{1,0:T(8,128)}), (f32[128,128]{1,0:T(8,128)}, f32[1152,128]{1,0:T(8,128)}, f32[128,128]{1,0:T(8,128)})) %all-reduce.6.cloned.1.call-update) | async-done | bytes 720912 | tf_op jit(solution)/shard_map/psum | solution.py:58
  110.7 2.2 fusion.12
  113.0 0.3 convolution_convert_fusion
  113.2 21.4 %all_gather.6 = bf16[1152,128]{1,0:T(8,128)(2,1)S(1)} all-gather(bf16[72,128]{1,0:T(8,128)(2,1)S(1)} %convolution_convert_fusion), channel_id=1, replica_groups=mesh['layer'=2,'pos'=16] {'pos'}, dimensions={0}, use_global_device_ids=true | all-gather | bytes 313344 | tf_op jit(solution)/shard_map/all_gather | solution.py:69
  134.6 1.3 collective-permute-start.1
  135.9 1.3 collective-permute-start
  137.2 11.4 %collective-permute-done = bf16[2,16,16,128]{3,2,1,0:T(8,128)(2,1)S(1)} collective-permute-done((bf16[2,16,16,128]{3,2,1,0:T(8,128)(2,1)S(1)}, bf16[2,16,16,128]{3,2,1,0:T(8,128)(2,1)S(1)}, u32[]{:S(2)}, u32[]{:S(2)}) %collective-permute-start) | collective-permute-done | bytes 131104 | tf_op jit(solution)/shard_map/ppermute | solution.py:10
  150.4 0.2 convolution_dynamic-update-slice_fusion.7
  151.1 0.2 convolution_dynamic-update-slice_fusion.4
  151.3 0.2 fusion.8
  152.0 0.2 convolution_dynamic-update-slice_fusion.1
  152.5 0.8 copy-done.3
  153.4 0.7 maximum_bitcast_fusion
  154.1 50.0 %reduce-scatter.4.cloned.1.call-done = f32[72,128]{1,0:T(8,128)} async-done(((f32[1152,128]{1,0:T(8,128)}), f32[72,128]{1,0:T(8,128)}) %reduce-scatter.4.cloned.1.call-update) | async-done | bytes 36880
  204.1 1.0 convolution_subtract_fusion
  205.2 21.1 %all_gather.7 = f32[1152,128]{1,0:T(8,128)S(1)} all-gather(f32[72,128]{1,0:T(8,128)S(1)} %convolution_subtract_fusion), channel_id=1, replica_groups=mesh['layer'=2,'pos'=16] {'pos'}, dimensions={0}, use_global_device_ids=true | all-gather | bytes 626688 | tf_op jit(solution)/shard_map/all_gather | solution.py:83
  226.3 1.1 fusion.10
  227.4 0.9 convolution_bitcast_fusion.4
  (47 shorter events, 5.1 us)
Async XLA Ops:
  7.2 103.6 %copy-start = (f32[1,72,1152]{2,1,0:T(8,128)S(1)}, f32[1,72,1152]{2,1,0:T(8,128)}, u32[]{:S(2)}) copy-start(f32[1,72,1152]{2,1,0:T(8,128)} %param.6) | copy-start | bytes 995332
  7.2 103.6 %all-reduce.6.cloned.1.call-start = ((), (), s32[]{:S(2)}) async-start(), calls=%async_computation.2 | async-start | bytes 1441792 | tf_op jit(solution)/shard_map/psum | solution.py:58
  7.2 8.1 %collective-permute-start.2 = (bf16[2,16,16,128]{3,2,1,0:T(8,128)(2,1)}, bf16[2,16,16,128]{3,2,1,0:T(8,128)(2,1)S(1)}, u32[]{:S(2)}, u32[]{:S(2)}) collective-permute-start(bf16[2,16,16,128]{3,2,1,0:T(8,128)(2,1)} %bitcast.111), channel_id=1, source_target_pairs={{16,0},{17,1},{18,2},{19,3},{20,4},{21,5},{22,6},{23,7},{24,8},{25... | collective-permute-start | bytes 393224 | tf_op jit(solution)/shard_map/ppermute | solution.py:10
  8.7 1.8 copy-start.1
  11.2 0.9 copy-start.5
  13.2 2.9 %copy-start.4 = (f32[1152,128]{1,0:T(8,128)}, f32[1152,128]{1,0:T(8,128)S(1)}, u32[]{:S(2)}) copy-start(f32[1152,128]{1,0:T(8,128)S(1)} %convolution_dynamic-update-slice_fusion.8) | copy-start | bytes 1769476
  16.2 187.9 %reduce-scatter.4.cloned.1.call-start = ((), (), s32[]{:S(2)}) async-start(), calls=%async_computation.1 | async-start | bytes 626688
  110.7 2.2 copy-start.6
  134.6 14.1 %collective-permute-start.1 = (bf16[1152,128]{1,0:T(8,128)(2,1)S(1)}, bf16[1152,128]{1,0:T(8,128)(2,1)S(1)}, u32[]{:S(2)}, u32[]{:S(2)}) collective-permute-start(bf16[1152,128]{1,0:T(8,128)(2,1)S(1)} %all_gather.6), channel_id=1, source_target_pairs={{16,0},{17,1},{18,2},{19,3},{20,4},{21,5},{22,6},{23,7},{24,8},{25... | collective-permute-start | bytes 884744 | tf_op jit(solution)/shard_map/ppermute | solution.py:10
  135.9 12.7 %collective-permute-start = (bf16[2,16,16,128]{3,2,1,0:T(8,128)(2,1)S(1)}, bf16[2,16,16,128]{3,2,1,0:T(8,128)(2,1)S(1)}, u32[]{:S(2)}, u32[]{:S(2)}) collective-permute-start(bf16[2,16,16,128]{3,2,1,0:T(8,128)(2,1)S(1)} %bitcast.139), channel_id=1, source_target_pairs={{16,0},{17,1},{18,2},{19,3},{20,4},{21,5},{22,6},{23,7},{24,8},{25... | collective-permute-start | bytes 393224 | tf_op jit(solution)/shard_map/ppermute | solution.py:10
  152.3 1.1 copy-start.7
  152.3 1.1 copy-start.8
  152.5 0.8 copy-start.3
  152.5 1.5 copy-start.2
Sparse Core Ops, SparseCore 0:
  16.3 94.3 all-reduce.5
  153.5 50.6 reduce-scatter.3
where the time goes:
time: 235 us
  waiting for transfers between devices  157 us (67%)
  blocking collectives  42.5 us (18%)
  between operations  14.4 us (6%)
  matrix products  12.9 us (5%)
  starting transfers between devices  4.07 us (2%)
  local copies, waits for them, and re-layouts  3.44 us (1%)
    psum x1, waiting for transfers between devices, per_device(): lax.psum((grad_part, own_part, cross_part), 'pos')  94.5 us
    unnamed x3, waiting for transfers between devices  50.1 us
    all_gather x1, blocking collectives, per_device(): precond_layer = lax.all_gather(precond_mine, 'pos', axis=0, tiled=True)  21.4 us
    all_gather x1, blocking collectives, per_device(): corrected = lax.all_gather(corrected_share, 'pos', axis=0, tiled=True)  21.1 us
    ppermute x3, waiting for transfers between devices, shifted(): return lax.ppermute(block, axis, route)  12.6 us
  transfers between devices with their start and end apart: 5, of which 4 were waited for; matrix products, arithmetic and copies ran while one was open for 2% of the time, Pallas kernels for 0%

commit v1 on v0

v1 whole, which is shorter than its diff:
```python
import jax
import jax.numpy as jnp
from jax import lax
from jax.sharding import PartitionSpec as P

F32 = jnp.float32
BF16 = jnp.bfloat16
HIGH = lax.Precision.HIGHEST


def after(block):
    devices = range(lax.axis_size("layer"))
    route = [(i + 1, i) for i in devices if i + 1 in devices]
    return lax.ppermute(block, "layer", route)


def swap(block, bit):
    return lax.ppermute(block, "pos", [(i, i ^ bit) for i in range(lax.axis_size("pos"))])


def pad_maps(layer_maps):
    return jnp.pad(layer_maps, ((0, 0), (1, 1), (1, 1), (0, 0)))


def patches(layer_maps):
    side = layer_maps.shape[1]
    width = layer_maps.shape[3]
    padded = pad_maps(layer_maps)
    return jnp.concatenate(
        [
            padded[:, r : r + side, s : s + side, :].reshape(-1, width)
            for r in range(3)
            for s in range(3)
        ],
        axis=1,
    )


def dot_t(a, b, **kw):
    return lax.dot_general(a, b, (((0,), (0,)), ((), ())), preferred_element_type=F32, **kw)


def dot_nt(a, b, **kw):
    return lax.dot_general(a, b, (((1,), (1,)), ((), ())), preferred_element_type=F32, **kw)


def blocks_from(own, block, count):
    parts = own.reshape((count, own.shape[0] // count) + own.shape[1:])
    return jnp.stack([lax.dynamic_index_in_dim(parts, block ^ j, 0, False) for j in range(count)])


def per_device(layer_inputs, output_grads, input_inverse, grad_inverse):
    maps = layer_inputs[0]
    grads = output_grads[0]
    k_rows = input_inverse[0]
    g_inv = grad_inverse[0]
    width = maps.shape[3]
    group = lax.axis_size("pos")
    rows = k_rows.shape[0]
    full = k_rows.shape[1]
    scale = 1.0 / (maps.shape[0] * maps.shape[1] * maps.shape[2] * group)
    me = lax.axis_index("pos")
    core = me & 1
    xbit = (me >> 1) & 1
    cols = 2 * core + xbit
    zbits = [b for b in (1 << i for i in range(2, 32)) if b < group]
    quarter = width // 4

    maps_next = after(maps)
    grads_next = after(grads)
    k_two = [k_rows, swap(k_rows, 2)]

    grad_rows = grads.reshape(-1, width)
    cuts = patches(maps)
    part_t = dot_t(grad_rows, cuts)
    e_t = dot_t(g_inv, part_t, precision=HIGH)
    e_blocks = blocks_from(e_t, cols, 4)

    h = e_blocks[:2] + swap(e_blocks[2:], 1)
    h = h[0] + swap(h[1], 2)
    for b in zbits:
        h = h + swap(h, b)
    e_mine = h * scale

    own_part = dot_t(grad_rows, grad_rows)
    cross_part = dot_t(grad_rows, grads_next.reshape(-1, width))
    gram = blocks_from(jnp.concatenate([own_part, cross_part], axis=1), cols, 4)
    gram = gram[:2] + swap(gram[2:], 1)
    gram = gram[0] + swap(gram[1], 2)
    for b in zbits:
        gram = gram + swap(gram, b)
    gram = gram * scale
    other = swap(gram, 2)
    gram = jnp.where(xbit == 0, jnp.concatenate([gram, other]), jnp.concatenate([other, gram]))
    other = swap(gram, 1)
    gram = jnp.where(core == 0, jnp.concatenate([gram, other]), jnp.concatenate([other, gram]))
    g_own, g_cross = gram[:, :width], gram[:, width:]
    big_h = dot_t(g_cross, g_inv, precision=HIGH)
    h_mine = lax.dynamic_slice_in_dim(big_h, cols * quarter, quarter, 0)

    k_x = jnp.where(xbit == 0, jnp.stack(k_two), jnp.stack(k_two[::-1]))
    k_c = swap(k_x, 1)
    k_z = jnp.where(core == 0, jnp.stack([k_x, k_c], 1), jnp.stack([k_c, k_x], 1)).reshape(4 * rows, full)

    p_t = dot_nt(e_mine, k_z, precision=HIGH).astype(BF16)
    for b in zbits:
        other = swap(p_t, b)
        p_t = jnp.where((me & b) == 0, jnp.concatenate([p_t, other], 1), jnp.concatenate([other, p_t], 1))
    p_t = after(p_t)

    def gathered(m):
        m = jnp.concatenate([m, swap(m, 2)], 0)
        return jnp.concatenate([m, swap(m, 1)], 0)

    maps_z = gathered(maps)
    next_z = gathered(maps_next)
    taps = p_t.T.reshape(3, 3, width, quarter)
    mapped = lax.conv_general_dilated(
        next_z, taps, (1, 1), "SAME", dimension_numbers=("NHWC", "HWIO", "NHWC"), preferred_element_type=F32
    ).astype(BF16)
    cross_t = dot_t(mapped.reshape(-1, quarter), patches(maps_z))
    for b in zbits:
        cross_t = cross_t + swap(cross_t.astype(BF16), b).astype(F32)
    cross_t = cross_t * scale

    main = dot_nt(k_z, e_mine, precision=HIGH)
    fix = jnp.dot(dot_nt(k_z, cross_t, precision=HIGH), h_mine, precision=HIGH)
    out = lax.dynamic_update_slice(jnp.zeros((4 * rows, width), F32), main, (0, cols * quarter)) - fix
    out = out.reshape(2, 2, rows, width)
    keep = lax.dynamic_index_in_dim(out, xbit, 0, False)
    send = lax.dynamic_index_in_dim(out, 1 - xbit, 0, False)
    out = keep + swap(send, 2)
    keep = lax.dynamic_index_in_dim(out, core, 0, False)
    send = lax.dynamic_index_in_dim(out, 1 - core, 0, False)
    update = keep + swap(send, 1)
    return (update[None], jnp.stack([g_own, g_cross])[None])


def solution(mesh):
    return jax.shard_map(
        per_device,
        mesh=mesh,
        in_specs=(
            P("layer", "pos", None, None, None),
            P("layer", "pos", None, None, None),
            P("layer", "pos", None),
            P("layer", None, None),
        ),
        out_specs=(P("layer", "pos", None), P("layer", None, None, None)),
        check_vma=False,
    )
```

time: 235 us -> 94.4 us (0.40)
  waiting for transfers between devices: 157 us -> 37.1 us
  blocking collectives: 42.5 us -> 0 us
  starting transfers between devices: 4.07 us -> 29.3 us
  between operations: 14.4 us -> 1.31 us
  local copies, waits for them, and re-layouts: 3.44 us -> 13.2 us
  matrix products: 12.9 us -> 10.4 us
    psum x1 -> x0, waiting for transfers between devices: 94.5 us -> none  [per_device(): lax.psum((grad_part, own_part, cross_part), 'pos')]
    unnamed x3 -> x0, waiting for transfers between devices: 50.1 us -> none
    all_gather x2 -> x0, blocking collectives: 42.5 us -> none  [the longest x1 21.4 us: per_device(): precond_layer = lax.all_gather(precond_mine, 'pos', axis=0, tiled=True)]
    ppermute x3 -> x25, starting transfers between devices: 4 us -> 29.3 us  [the longest x22 25.3 us: swap(): lax.ppermute(block, 'pos', [(i, i ^ bit) for i in range(lax.axis_size('po...]
    ppermute x3 -> x25, waiting for transfers between devices: 12.6 us -> 37.1 us  [the longest x22 30.8 us: swap(): lax.ppermute(block, 'pos', [(i, i ^ bit) for i in range(lax.axis_size('po...]
    unnamed x18 -> x25, local copies, waits for them, and re-layouts: 1.5 us -> 9.1 us
    dot_general x34 -> x10, matrix products: 12.9 us -> 9 us  [the longest x6 5.15 us: dot_t(): lax.dot_general(a, b, (((0,), (0,)), ((), ())), preferred_element_type=F3...]
  transfers between devices with their start and end apart: 5 -> 25, of which waited for: 4 -> 16; matrix products, arithmetic and copies ran while one was open for 2% -> 19% of each run, Pallas kernels for 0% -> 0%
where the time goes in v1:
time: 94.4 us; the launch traced here: 94.2 us
  waiting for transfers between devices  37.1 us (39%)
  starting transfers between devices  29.3 us (31%)
  local copies, waits for them, and re-layouts  13.2 us (14%)
  matrix products  10.4 us (11%)
  other arithmetic  2.83 us (3%)
  between operations  1.31 us (1%)
    ppermute x22, waiting for transfers between devices, swap(): lax.ppermute(block, 'pos', [(i, i ^ bit) for i in range(lax.axis_size('po...  30.8 us
    ppermute x22, starting transfers between devices, swap(): lax.ppermute(block, 'pos', [(i, i ^ bit) for i in range(lax.axis_size('po...  25.3 us
    unnamed x25, local copies, waits for them, and re-layouts  9.1 us
    ppermute x3, waiting for transfers between devices, after(): return lax.ppermute(block, 'layer', route)  6.33 us
    dot_general x6, matrix products, dot_t(): lax.dot_general(a, b, (((0,), (0,)), ((), ())), preferred_element_type=F3...  5.15 us
    ppermute x3, starting transfers between devices, after(): return lax.ppermute(block, 'layer', route)  4.04 us
    dot_general x3, matrix products, dot_nt(): lax.dot_general(a, b, (((1,), (1,)), ((), ())), preferred_element_type=F3...  3.58 us
    slice x18, local copies, waits for them, and re-layouts, patches(): padded[:, r:r + side, s:s + side, :].reshape(-1, width)  2.09 us
  transfers between devices with their start and end apart: 25, of which 16 were waited for; matrix products, arithmetic and copies ran while one was open for 19% of the time, Pallas kernels for 0%

profile of v1, /device:TPU:0, one launch (start us, length us, event | category | flops | bytes accessed | tf_op | source)
XLA Modules:
  0.0 94.2 jit_solution(4920615117337532317)
XLA Ops:
  3.0 3.0 %collective-permute-start.12 = (bf16[2,16,16,128]{3,0,2,1:T(2,128)(2,1)S(1)}, bf16[2,16,16,128]{3,0,2,1:T(2,128)(2,1)S(1)}, u32[]{:S(2)}, u32[]{:S(2)}) collective-permute-start(bf16[2,16,16,128]{3,0,2,1:T(2,128)(2,1)S(1)} %bitcast.105), channel_id=1, source_target_pairs={{0,2},{1,3},{2,0},{3,1},{4,6},{5,7},{6,4},{7,5},{8,10},{9,11},{10,... | collective-permute-start | bytes 393224 | tf_op jit(solution)/shard_map/ppermute | solution.py:18
  10.7 2.4 %collective-permute-done.16 = bf16[2,16,16,128]{3,2,1,0:T(8,128)(2,1)S(1)} collective-permute-done((bf16[2,16,16,128]{3,2,1,0:T(8,128)(2,1)}, bf16[2,16,16,128]{3,2,1,0:T(8,128)(2,1)S(1)}, u32[]{:S(2)}, u32[]{:S(2)}) %collective-permute-start.16) | collective-permute-done | bytes 131104 | tf_op jit(solution)/shard_map/ppermute | solution.py:14
  14.9 2.0 %collective-permute-start.18 = (f32[32,256]{1,0:T(8,128)S(1)}, f32[32,256]{1,0:T(8,128)S(1)}, u32[]{:S(2)}, u32[]{:S(2)}) collective-permute-start(f32[32,256]{1,0:T(8,128)S(1)} %slice_bitcast_fusion.4), channel_id=1, source_target_pairs={{0,2},{1,3},{2,0},{3,1},{4,6},{5,7},{6,4},{7,5},{8,10},{9,11},{10,... | collective-permute-start | bytes 98312 | tf_op jit(solution)/shard_map/ppermute | solution.py:18
  17.2 1.7 %collective-permute-done.18 = f32[32,256]{1,0:T(8,128)S(1)} collective-permute-done((f32[32,256]{1,0:T(8,128)S(1)}, f32[32,256]{1,0:T(8,128)S(1)}, u32[]{:S(2)}, u32[]{:S(2)}) %collective-permute-start.18) | collective-permute-done | bytes 32800 | tf_op jit(solution)/shard_map/ppermute | solution.py:18
  18.9 2.0 %collective-permute-start.19 = (f32[32,256]{1,0:T(8,128)S(1)}, f32[32,256]{1,0:T(8,128)S(1)}, u32[]{:S(2)}, u32[]{:S(2)}) collective-permute-start(f32[32,256]{1,0:T(8,128)S(1)} %fusion.20), channel_id=1, source_target_pairs={{0,4},{1,5},{2,6},{3,7},{4,0},{5,1},{6,2},{7,3},{8,12},{9,13},{10,... | collective-permute-start | bytes 98312 | tf_op jit(solution)/shard_map/ppermute | solution.py:18
  21.3 1.5 %collective-permute-done.19 = f32[32,256]{1,0:T(8,128)S(1)} collective-permute-done((f32[32,256]{1,0:T(8,128)S(1)}, f32[32,256]{1,0:T(8,128)S(1)}, u32[]{:S(2)}, u32[]{:S(2)}) %collective-permute-start.19) | collective-permute-done | bytes 32800 | tf_op jit(solution)/shard_map/ppermute | solution.py:18
  22.8 3.0 %collective-permute-start.20 = (f32[32,256]{1,0:T(8,128)S(1)}, f32[32,256]{1,0:T(8,128)S(1)}, u32[]{:S(2)}, u32[]{:S(2)}) collective-permute-start(f32[32,256]{1,0:T(8,128)S(1)} %add.95), channel_id=1, source_target_pairs={{0,8},{1,9},{2,10},{3,11},{4,12},{5,13},{6,14},{7,15},{8,0},{9,1},... | collective-permute-start | bytes 98312 | tf_op jit(solution)/shard_map/ppermute | solution.py:18
  26.2 1.5 %collective-permute-done.20 = f32[32,256]{1,0:T(8,128)S(1)} collective-permute-done((f32[32,256]{1,0:T(8,128)S(1)}, f32[32,256]{1,0:T(8,128)S(1)}, u32[]{:S(2)}, u32[]{:S(2)}) %collective-permute-start.20) | collective-permute-done | bytes 32800 | tf_op jit(solution)/shard_map/ppermute | solution.py:18
  27.8 2.2 %collective-permute-start.21 = (f32[32,256]{1,0:T(8,128)S(1)}, f32[32,256]{1,0:T(8,128)S(1)}, u32[]{:S(2)}, u32[]{:S(2)}) collective-permute-start(f32[32,256]{1,0:T(8,128)S(1)} %add_multiply_fusion.3), channel_id=1, source_target_pairs={{0,2},{1,3},{2,0},{3,1},{4,6},{5,7},{6,4},{7,5},{8,10},{9,11},{10,... | collective-permute-start | bytes 98312 | tf_op jit(solution)/shard_map/ppermute | solution.py:18
  30.1 2.0 %collective-permute-done.21 = f32[32,256]{1,0:T(8,128)S(1)} collective-permute-done((f32[32,256]{1,0:T(8,128)S(1)}, f32[32,256]{1,0:T(8,128)S(1)}, u32[]{:S(2)}, u32[]{:S(2)}) %collective-permute-start.21) | collective-permute-done | bytes 32800 | tf_op jit(solution)/shard_map/ppermute | solution.py:18
  39.7 1.9 %collective-permute-start.4 = (f32[32,1152]{1,0:T(8,128)S(1)}, f32[32,1152]{1,0:T(8,128)S(1)}, u32[]{:S(2)}, u32[]{:S(2)}) collective-permute-start(f32[32,1152]{1,0:T(8,128)S(1)} %fusion.5), channel_id=1, source_target_pairs={{0,4},{1,5},{2,6},{3,7},{4,0},{5,1},{6,2},{7,3},{8,12},{9,13},{10,... | collective-permute-start | bytes 442376 | tf_op jit(solution)/shard_map/ppermute | solution.py:18
  42.5 3.3 %collective-permute-done.4 = f32[32,1152]{1,0:T(8,128)S(1)} collective-permute-done((f32[32,1152]{1,0:T(8,128)S(1)}, f32[32,1152]{1,0:T(8,128)S(1)}, u32[]{:S(2)}, u32[]{:S(2)}) %collective-permute-start.4) | collective-permute-done | bytes 147488 | tf_op jit(solution)/shard_map/ppermute | solution.py:18
  45.8 2.6 %collective-permute-start.5 = (f32[32,1152]{1,0:T(8,128)S(1)}, f32[32,1152]{1,0:T(8,128)S(1)}, u32[]{:S(2)}, u32[]{:S(2)}) collective-permute-start(f32[32,1152]{1,0:T(8,128)S(1)} %add.88), channel_id=1, source_target_pairs={{0,8},{1,9},{2,10},{3,11},{4,12},{5,13},{6,14},{7,15},{8,0},{9,1},... | collective-permute-start | bytes 442376 | tf_op jit(solution)/shard_map/ppermute | solution.py:18
  48.4 6.6 %collective-permute-done.5 = f32[32,1152]{1,0:T(8,128)S(1)} collective-permute-done((f32[32,1152]{1,0:T(8,128)S(1)}, f32[32,1152]{1,0:T(8,128)S(1)}, u32[]{:S(2)}, u32[]{:S(2)}) %collective-permute-start.5) | collective-permute-done | bytes 147488 | tf_op jit(solution)/shard_map/ppermute | solution.py:18
  57.9 2.3 %collective-permute-done.9 = bf16[32,288]{1,0:T(8,128)(2,1)S(1)} collective-permute-done((bf16[32,288]{1,0:T(8,128)(2,1)S(1)}, bf16[32,288]{1,0:T(8,128)(2,1)S(1)}, u32[]{:S(2)}, u32[]{:S(2)}) %collective-permute-start.9) | collective-permute-done | bytes 18464 | tf_op jit(solution)/shard_map/ppermute | solution.py:18
  60.2 2.0 %collective-permute-start.10 = (bf16[32,576]{1,0:T(8,128)(2,1)S(1)}, bf16[32,576]{1,0:T(8,128)(2,1)S(1)}, u32[]{:S(2)}, u32[]{:S(2)}) collective-permute-start(bf16[32,576]{1,0:T(8,128)(2,1)S(1)} %maximum_select_fusion.6), channel_id=1, source_target_pairs={{0,8},{1,9},{2,10},{3,11},{4,12},{5,13},{6,14},{7,15},{8,0},{9,1},... | collective-permute-start | bytes 110600 | tf_op jit(solution)/shard_map/ppermute | solution.py:18
  63.2 2.0 %collective-permute-done.10 = bf16[32,576]{1,0:T(8,128)(2,1)S(1)} collective-permute-done((bf16[32,576]{1,0:T(8,128)(2,1)S(1)}, bf16[32,576]{1,0:T(8,128)(2,1)S(1)}, u32[]{:S(2)}, u32[]{:S(2)}) %collective-permute-start.10) | collective-permute-done | bytes 36896 | tf_op jit(solution)/shard_map/ppermute | solution.py:18
  67.7 3.9 %collective-permute-done.11 = bf16[32,1152]{1,0:T(8,128)(2,1)S(1)} collective-permute-done((bf16[32,1152]{1,0:T(8,128)(2,1)S(1)}, bf16[32,1152]{1,0:T(8,128)(2,1)S(1)}, u32[]{:S(2)}, u32[]{:S(2)}) %collective-permute-start.11) | collective-permute-done | bytes 73760 | tf_op jit(solution)/shard_map/ppermute | solution.py:14
  73.0 3.2 %fusion.28 = (bf16[32,1152]{1,0:T(8,128)(2,1)S(1)}, f32[32,1152]{1,0:T(8,128)S(1)}) fusion(bf16[2048,32]{1,0:T(8,128)(2,1)S(1)} %bitcast.109, bf16[2048,1152]{1,0:T(8,128)(2,1)} %constant_dynamic-update-slice_fusion.9), kind=kOutput, calls=%fused_computation.104 | convolution fusion | flops 151031808 | bytes 5070848 | tf_op jit(solution)/shard_map/dot_general | solution.py:40
  77.7 3.3 %collective-permute-done.14 = bf16[32,1152]{1,0:T(8,128)(2,1)S(1)} collective-permute-done((bf16[32,1152]{1,0:T(8,128)(2,1)S(1)}, bf16[32,1152]{1,0:T(8,128)(2,1)S(1)}, u32[]{:S(2)}, u32[]{:S(2)}) %collective-permute-start.14) | collective-permute-done | bytes 73760 | tf_op jit(solution)/shard_map/ppermute | solution.py:18
  81.0 1.8 %collective-permute-start.15 = (bf16[32,1152]{1,0:T(8,128)(2,1)S(1)}, bf16[32,1152]{1,0:T(8,128)(2,1)S(1)}, u32[]{:S(2)}, u32[]{:S(2)}) collective-permute-start(bf16[32,1152]{1,0:T(8,128)(2,1)S(1)} %fusion.10), channel_id=1, source_target_pairs={{0,8},{1,9},{2,10},{3,11},{4,12},{5,13},{6,14},{7,15},{8,0},{9,1},... | collective-permute-start | bytes 221192 | tf_op jit(solution)/shard_map/ppermute | solution.py:18
  84.7 1.6 %collective-permute-done.15 = bf16[32,1152]{1,0:T(8,128)(2,1)S(1)} collective-permute-done((bf16[32,1152]{1,0:T(8,128)(2,1)S(1)}, bf16[32,1152]{1,0:T(8,128)(2,1)S(1)}, u32[]{:S(2)}, u32[]{:S(2)}) %collective-permute-start.15) | collective-permute-done | bytes 73760 | tf_op jit(solution)/shard_map/ppermute | solution.py:18
  87.8 1.7 %collective-permute-start.23 = (f32[2,72,128]{2,1,0:T(8,128)S(1)}, f32[2,72,128]{2,1,0:T(8,128)S(1)}, u32[]{:S(2)}, u32[]{:S(2)}) collective-permute-start(f32[2,72,128]{2,1,0:T(8,128)S(1)} %dynamic-slice_bitcast_fusion), channel_id=1, source_target_pairs={{0,2},{1,3},{2,0},{3,1},{4,6},{5,7},{6,4},{7,5},{8,10},{9,11},{10,... | collective-permute-start | bytes 221192 | tf_op jit(solution)/shard_map/ppermute | solution.py:18
  89.5 2.7 %collective-permute-done.23 = f32[2,72,128]{2,1,0:T(8,128)S(1)} collective-permute-done((f32[2,72,128]{2,1,0:T(8,128)S(1)}, f32[2,72,128]{2,1,0:T(8,128)S(1)}, u32[]{:S(2)}, u32[]{:S(2)}) %collective-permute-start.23) | collective-permute-done | bytes 73760 | tf_op jit(solution)/shard_map/ppermute | solution.py:18
  (119 shorter events, 32.7 us)
Async XLA Ops:
  1.7 15.3 %collective-permute-start.6 = (bf16[2,16,16,128]{3,0,2,1:T(2,128)(2,1)S(1)}, bf16[2,16,16,128]{3,0,2,1:T(2,128)(2,1)S(1)}, u32[]{:S(2)}, u32[]{:S(2)}) collective-permute-start(bf16[2,16,16,128]{3,0,2,1:T(2,128)(2,1)S(1)} %bitcast.104), channel_id=1, source_target_pairs={{16,0},{17,1},{18,2},{19,3},{20,4},{21,5},{22,6},{23,7},{24,8},{25... | collective-permute-start | bytes 393224 | tf_op jit(solution)/shard_map/ppermute | solution.py:14
  3.0 17.9 %collective-permute-start.12 = (bf16[2,16,16,128]{3,0,2,1:T(2,128)(2,1)S(1)}, bf16[2,16,16,128]{3,0,2,1:T(2,128)(2,1)S(1)}, u32[]{:S(2)}, u32[]{:S(2)}) collective-permute-start(bf16[2,16,16,128]{3,0,2,1:T(2,128)(2,1)S(1)} %bitcast.105), channel_id=1, source_target_pairs={{0,2},{1,3},{2,0},{3,1},{4,6},{5,7},{6,4},{7,5},{8,10},{9,11},{10,... | collective-permute-start | bytes 393224 | tf_op jit(solution)/shard_map/ppermute | solution.py:18
  6.0 26.2 %collective-permute-start = (f32[72,1152]{1,0:T(8,128)}, f32[72,1152]{1,0:T(8,128)S(1)}, u32[]{:S(2)}, u32[]{:S(2)}) collective-permute-start(f32[72,1152]{1,0:T(8,128)} %bitcast.110), channel_id=1, source_target_pairs={{0,2},{1,3},{2,0},{3,1},{4,6},{5,7},{6,4},{7,5},{8,10},{9,11},{10,... | collective-permute-start | bytes 995336 | tf_op jit(solution)/shard_map/ppermute | solution.py:18
  6.1 7.1 %collective-permute-start.16 = (bf16[2,16,16,128]{3,2,1,0:T(8,128)(2,1)}, bf16[2,16,16,128]{3,2,1,0:T(8,128)(2,1)S(1)}, u32[]{:S(2)}, u32[]{:S(2)}) collective-permute-start(bf16[2,16,16,128]{3,2,1,0:T(8,128)(2,1)} %bitcast.114), channel_id=1, source_target_pairs={{16,0},{17,1},{18,2},{19,3},{20,4},{21,5},{22,6},{23,7},{24,8},{25... | collective-permute-start | bytes 393224 | tf_op jit(solution)/shard_map/ppermute | solution.py:14
  13.6 1.3 %collective-permute-start.17 = (f32[2,32,256]{2,1,0:T(8,128)S(1)}, f32[2,32,256]{2,1,0:T(8,128)S(1)}, u32[]{:S(2)}, u32[]{:S(2)}) collective-permute-start(f32[2,32,256]{2,1,0:T(8,128)S(1)} %pad_maximum_fusion.5), channel_id=1, source_target_pairs={{0,1},{1,0},{2,3},{3,2},{4,5},{5,4},{6,7},{7,6},{8,9},{9,8},{10,11... | collective-permute-start | bytes 196616 | tf_op jit(solution)/shard_map/ppermute | solution.py:18
  14.9 4.0 %collective-permute-start.18 = (f32[32,256]{1,0:T(8,128)S(1)}, f32[32,256]{1,0:T(8,128)S(1)}, u32[]{:S(2)}, u32[]{:S(2)}) collective-permute-start(f32[32,256]{1,0:T(8,128)S(1)} %slice_bitcast_fusion.4), channel_id=1, source_target_pairs={{0,2},{1,3},{2,0},{3,1},{4,6},{5,7},{6,4},{7,5},{8,10},{9,11},{10,... | collective-permute-start | bytes 98312 | tf_op jit(solution)/shard_map/ppermute | solution.py:18
  17.0 13.0 %collective-permute-start.2 = (f32[2,32,1152]{2,1,0:T(8,128)S(1)}, f32[2,32,1152]{2,1,0:T(8,128)S(1)}, u32[]{:S(2)}, u32[]{:S(2)}) collective-permute-start(f32[2,32,1152]{2,1,0:T(8,128)S(1)} %pad_maximum_fusion.1), channel_id=1, source_target_pairs={{0,1},{1,0},{2,3},{3,2},{4,5},{5,4},{6,7},{7,6},{8,9},{9,8},{10,11... | collective-permute-start | bytes 884744 | tf_op jit(solution)/shard_map/ppermute | solution.py:18
  17.1 8.8 %collective-permute-start.7 = (bf16[2,16,16,128]{3,0,2,1:T(2,128)(2,1)S(1)}, bf16[2,16,16,128]{3,0,2,1:T(2,128)(2,1)S(1)}, u32[]{:S(2)}, u32[]{:S(2)}) collective-permute-start(bf16[2,16,16,128]{3,0,2,1:T(2,128)(2,1)S(1)} %collective-permute-done.6), channel_id=1, source_target_pairs={{0,2},{1,3},{2,0},{3,1},{4,6},{5,7},{6,4},{7,5},{8,10},{9,11},{10,... | collective-permute-start | bytes 393224 | tf_op jit(solution)/shard_map/ppermute | solution.py:18
  18.9 3.9 %collective-permute-start.19 = (f32[32,256]{1,0:T(8,128)S(1)}, f32[32,256]{1,0:T(8,128)S(1)}, u32[]{:S(2)}, u32[]{:S(2)}) collective-permute-start(f32[32,256]{1,0:T(8,128)S(1)} %fusion.20), channel_id=1, source_target_pairs={{0,4},{1,5},{2,6},{3,7},{4,0},{5,1},{6,2},{7,3},{8,12},{9,13},{10,... | collective-permute-start | bytes 98312 | tf_op jit(solution)/shard_map/ppermute | solution.py:18
  21.2 12.2 %collective-permute-start.13 = (bf16[4,16,16,128]{3,0,2,1:T(4,128)(2,1)S(1)}, bf16[4,16,16,128]{3,0,2,1:T(4,128)(2,1)S(1)}, u32[]{:S(2)}, u32[]{:S(2)}) collective-permute-start(bf16[4,16,16,128]{3,0,2,1:T(4,128)(2,1)S(1)} %pad_maximum_fusion.3), channel_id=1, source_target_pairs={{0,1},{1,0},{2,3},{3,2},{4,5},{5,4},{6,7},{7,6},{8,9},{9,8},{10,11... | collective-permute-start | bytes 786440 | tf_op jit(solution)/shard_map/ppermute | solution.py:18
  22.8 4.9 %collective-permute-start.20 = (f32[32,256]{1,0:T(8,128)S(1)}, f32[32,256]{1,0:T(8,128)S(1)}, u32[]{:S(2)}, u32[]{:S(2)}) collective-permute-start(f32[32,256]{1,0:T(8,128)S(1)} %add.95), channel_id=1, source_target_pairs={{0,8},{1,9},{2,10},{3,11},{4,12},{5,13},{6,14},{7,15},{8,0},{9,1},... | collective-permute-start | bytes 98312 | tf_op jit(solution)/shard_map/ppermute | solution.py:18
  26.2 45.4 %collective-permute-start.8 = (bf16[4,16,16,128]{3,0,2,1:T(4,128)(2,1)S(1)}, bf16[4,16,16,128]{3,0,2,1:T(4,128)(2,1)S(1)}, u32[]{:S(2)}, u32[]{:S(2)}) collective-permute-start(bf16[4,16,16,128]{3,0,2,1:T(4,128)(2,1)S(1)} %pad_maximum_fusion.2), channel_id=1, source_target_pairs={{0,1},{1,0},{2,3},{3,2},{4,5},{5,4},{6,7},{7,6},{8,9},{9,8},{10,11... | collective-permute-start | bytes 786440 | tf_op jit(solution)/shard_map/ppermute | solution.py:18
  27.8 4.3 %collective-permute-start.21 = (f32[32,256]{1,0:T(8,128)S(1)}, f32[32,256]{1,0:T(8,128)S(1)}, u32[]{:S(2)}, u32[]{:S(2)}) collective-permute-start(f32[32,256]{1,0:T(8,128)S(1)} %add_multiply_fusion.3), channel_id=1, source_target_pairs={{0,2},{1,3},{2,0},{3,1},{4,6},{5,7},{6,4},{7,5},{8,10},{9,11},{10,... | collective-permute-start | bytes 98312 | tf_op jit(solution)/shard_map/ppermute | solution.py:18
  30.0 9.7 %collective-permute-start.3 = (f32[32,1152]{1,0:T(8,128)S(1)}, f32[32,1152]{1,0:T(8,128)S(1)}, u32[]{:S(2)}, u32[]{:S(2)}) collective-permute-start(f32[32,1152]{1,0:T(8,128)S(1)} %slice_bitcast_fusion), channel_id=1, source_target_pairs={{0,2},{1,3},{2,0},{3,1},{4,6},{5,7},{6,4},{7,5},{8,10},{9,11},{10,... | collective-permute-start | bytes 442376 | tf_op jit(solution)/shard_map/ppermute | solution.py:18
  32.1 1.3 %collective-permute-start.22 = (f32[64,256]{1,0:T(8,128)S(1)}, f32[64,256]{1,0:T(8,128)S(1)}, u32[]{:S(2)}, u32[]{:S(2)}) collective-permute-start(f32[64,256]{1,0:T(8,128)S(1)} %maximum_select_fusion.5), channel_id=1, source_target_pairs={{0,1},{1,0},{2,3},{3,2},{4,5},{5,4},{6,7},{7,6},{8,9},{9,8},{10,11... | collective-permute-start | bytes 196616 | tf_op jit(solution)/shard_map/ppermute | solution.py:18
  32.3 16.1 %collective-permute-start.1 = (f32[2,72,1152]{2,1,0:T(8,128)S(1)}, f32[2,72,1152]{2,1,0:T(8,128)S(1)}, u32[]{:S(2)}, u32[]{:S(2)}) collective-permute-start(f32[2,72,1152]{2,1,0:T(8,128)S(1)} %maximum_select_fusion.2), channel_id=1, source_target_pairs={{0,1},{1,0},{2,3},{3,2},{4,5},{5,4},{6,7},{7,6},{8,9},{9,8},{10,11... | collective-permute-start | bytes 1990664 | tf_op jit(solution)/shard_map/ppermute | solution.py:18
  39.7 6.0 %collective-permute-start.4 = (f32[32,1152]{1,0:T(8,128)S(1)}, f32[32,1152]{1,0:T(8,128)S(1)}, u32[]{:S(2)}, u32[]{:S(2)}) collective-permute-start(f32[32,1152]{1,0:T(8,128)S(1)} %fusion.5), channel_id=1, source_target_pairs={{0,4},{1,5},{2,6},{3,7},{4,0},{5,1},{6,2},{7,3},{8,12},{9,13},{10,... | collective-permute-start | bytes 442376 | tf_op jit(solution)/shard_map/ppermute | solution.py:18
  45.8 9.3 %collective-permute-start.5 = (f32[32,1152]{1,0:T(8,128)S(1)}, f32[32,1152]{1,0:T(8,128)S(1)}, u32[]{:S(2)}, u32[]{:S(2)}) collective-permute-start(f32[32,1152]{1,0:T(8,128)S(1)} %add.88), channel_id=1, source_target_pairs={{0,8},{1,9},{2,10},{3,11},{4,12},{5,13},{6,14},{7,15},{8,0},{9,1},... | collective-permute-start | bytes 442376 | tf_op jit(solution)/shard_map/ppermute | solution.py:18
  56.2 3.9 %collective-permute-start.9 = (bf16[32,288]{1,0:T(8,128)(2,1)S(1)}, bf16[32,288]{1,0:T(8,128)(2,1)S(1)}, u32[]{:S(2)}, u32[]{:S(2)}) collective-permute-start(bf16[32,288]{1,0:T(8,128)(2,1)S(1)} %convolution_convert_fusion.1), channel_id=1, source_target_pairs={{0,4},{1,5},{2,6},{3,7},{4,0},{5,1},{6,2},{7,3},{8,12},{9,13},{10,... | collective-permute-start | bytes 55304 | tf_op jit(solution)/shard_map/ppermute | solution.py:18
  60.2 5.0 %collective-permute-start.10 = (bf16[32,576]{1,0:T(8,128)(2,1)S(1)}, bf16[32,576]{1,0:T(8,128)(2,1)S(1)}, u32[]{:S(2)}, u32[]{:S(2)}) collective-permute-start(bf16[32,576]{1,0:T(8,128)(2,1)S(1)} %maximum_select_fusion.6), channel_id=1, source_target_pairs={{0,8},{1,9},{2,10},{3,11},{4,12},{5,13},{6,14},{7,15},{8,0},{9,1},... | collective-permute-start | bytes 110600 | tf_op jit(solution)/shard_map/ppermute | solution.py:18
  65.3 6.2 %collective-permute-start.11 = (bf16[32,1152]{1,0:T(8,128)(2,1)S(1)}, bf16[32,1152]{1,0:T(8,128)(2,1)S(1)}, u32[]{:S(2)}, u32[]{:S(2)}) collective-permute-start(bf16[32,1152]{1,0:T(8,128)(2,1)S(1)} %maximum_select_fusion.4), channel_id=1, source_target_pairs={{16,0},{17,1},{18,2},{19,3},{20,4},{21,5},{22,6},{23,7},{24,8},{25... | collective-permute-start | bytes 221192 | tf_op jit(solution)/shard_map/ppermute | solution.py:14
  76.2 4.8 %collective-permute-start.14 = (bf16[32,1152]{1,0:T(8,128)(2,1)S(1)}, bf16[32,1152]{1,0:T(8,128)(2,1)S(1)}, u32[]{:S(2)}, u32[]{:S(2)}) collective-permute-start(bf16[32,1152]{1,0:T(8,128)(2,1)S(1)} %get-tuple-element.28), channel_id=1, source_target_pairs={{0,4},{1,5},{2,6},{3,7},{4,0},{5,1},{6,2},{7,3},{8,12},{9,13},{10,... | collective-permute-start | bytes 221192 | tf_op jit(solution)/shard_map/ppermute | solution.py:18
  81.0 5.3 %collective-permute-start.15 = (bf16[32,1152]{1,0:T(8,128)(2,1)S(1)}, bf16[32,1152]{1,0:T(8,128)(2,1)S(1)}, u32[]{:S(2)}, u32[]{:S(2)}) collective-permute-start(bf16[32,1152]{1,0:T(8,128)(2,1)S(1)} %fusion.10), channel_id=1, source_target_pairs={{0,8},{1,9},{2,10},{3,11},{4,12},{5,13},{6,14},{7,15},{8,0},{9,1},... | collective-permute-start | bytes 221192 | tf_op jit(solution)/shard_map/ppermute | solution.py:18
  87.8 4.4 %collective-permute-start.23 = (f32[2,72,128]{2,1,0:T(8,128)S(1)}, f32[2,72,128]{2,1,0:T(8,128)S(1)}, u32[]{:S(2)}, u32[]{:S(2)}) collective-permute-start(f32[2,72,128]{2,1,0:T(8,128)S(1)} %dynamic-slice_bitcast_fusion), channel_id=1, source_target_pairs={{0,2},{1,3},{2,0},{3,1},{4,6},{5,7},{6,4},{7,5},{8,10},{9,11},{10,... | collective-permute-start | bytes 221192 | tf_op jit(solution)/shard_map/ppermute | solution.py:18
  (5 other events, 27.4 us)

commit v2 on v1

v2 whole, which is shorter than its diff:
```python
import functools

import jax
import jax.numpy as jnp
from jax import lax
from jax.experimental import pallas as pl
from jax.experimental.pallas import tpu as pltpu
from jax.sharding import PartitionSpec as P

F32 = jnp.float32
BF16 = jnp.bfloat16
HIGH = lax.Precision.HIGHEST
hold = lax.optimization_barrier


def after(block):
    devices = range(lax.axis_size("layer"))
    route = [(i + 1, i) for i in devices if i + 1 in devices]
    return lax.ppermute(block, "layer", route)


def swap(block, bit):
    return lax.ppermute(block, "pos", [(i, i ^ bit) for i in range(lax.axis_size("pos"))])


def dot_t(a, b, **kw):
    return lax.dot_general(a, b, (((0,), (0,)), ((), ())), preferred_element_type=F32, **kw)


def dot_nt(a, b, **kw):
    return lax.dot_general(a, b, (((1,), (1,)), ((), ())), preferred_element_type=F32, **kw)


def shifted(block, dy, dx, side):
    lanes = block.shape[1]
    place = lax.broadcasted_iota(jnp.int32, (1, lanes), 1)
    x = place % side
    y = (place // side) % side
    if dx:
        block = jnp.where((x + dx >= 0) & (x + dx < side), pltpu.roll(block, (-dx) % lanes, 1), 0.0)
    if dy:
        block = jnp.where((y + dy >= 0) & (y + dy < side), pltpu.roll(block, (-dy * side) % lanes, 1), 0.0)
    return block


def taps_to_rows(block, side):
    moved = []
    for r in range(3):
        for s in range(3):
            moved.append(shifted(shifted(block, 0, 1 - s, side), 1 - r, 0, side).astype(BF16))
    return jnp.concatenate(moved, axis=0)


def grad_kernel(side, maps, grads, g_two, out):
    quarter = out.shape[0]
    width = maps.shape[1]
    first = g_two[...].astype(BF16)
    rest = g_two[...] - first.astype(F32)
    second = rest.astype(BF16)
    third = (rest - second.astype(F32)).astype(BF16)
    g = grads[...]
    mixed = dot_nt(first, g) + (dot_nt(second, g) + dot_nt(third, g))
    high = mixed.astype(BF16).astype(F32)
    row = lax.broadcasted_iota(jnp.int32, mixed.shape, 0)
    mixed = jnp.where(row < quarter, high, mixed - high)
    both = jnp.dot(taps_to_rows(mixed, side), maps[...], preferred_element_type=F32)
    for tap in range(9):
        low = 2 * quarter * tap
        out[:, tap * width : (tap + 1) * width] = (
            both[low : low + quarter] + both[low + quarter : low + 2 * quarter]
        )


def cross_kernel(side, maps, maps_next, precond_t, out, out_half):
    quarter = precond_t.shape[0]
    width = maps.shape[1]
    taps = jnp.concatenate([precond_t[:, t * width : (t + 1) * width] for t in range(9)], axis=0)
    spread = dot_nt(taps, maps_next[...])
    mapped = None
    for s in range(3):
        column = None
        for r in range(3):
            low = quarter * (3 * r + s)
            part = shifted(spread[low : low + quarter], r - 1, 0, side)
            column = part if column is None else column + part
        column = shifted(column, 0, s - 1, side)
        mapped = column if mapped is None else mapped + column
    mapped = mapped.astype(BF16).astype(F32)
    both = jnp.dot(taps_to_rows(mapped, side), maps[...], preferred_element_type=F32)
    for tap in range(9):
        part = both[quarter * tap : quarter * (tap + 1)]
        out[:, tap * width : (tap + 1) * width] = part
        out_half[:, tap * width : (tap + 1) * width] = part.astype(BF16)


VMEM = pl.BlockSpec(memory_space=pltpu.VMEM)
PARAMS = pltpu.CompilerParams(vmem_limit_bytes=32 * 1024 * 1024)


def per_device(layer_inputs, output_grads, input_inverse, grad_inverse):
    maps = layer_inputs[0]
    grads = output_grads[0]
    k_rows = input_inverse[0]
    g_inv = grad_inverse[0]
    side = maps.shape[1]
    width = maps.shape[3]
    group = lax.axis_size("pos")
    rows, full = k_rows.shape
    scale = 1.0 / (maps.shape[0] * maps.shape[1] * maps.shape[2] * group)
    me = lax.axis_index("pos")
    core = me & 1
    xbit = (me >> 1) & 1
    cols = 2 * core + xbit
    zbits = [b for b in (1 << i for i in range(2, 32)) if b < group]
    quarter = width // 4
    flat_maps = maps.reshape(-1, width)
    flat_grads = grads.reshape(-1, width)

    own = jnp.concatenate([flat_grads, flat_maps], axis=0)
    pair = jnp.concatenate([own[None], swap(own, 2)[None]], axis=0)
    four = jnp.concatenate([pair, swap(pair, 1)], axis=0)
    count = flat_maps.shape[0]
    grads_z = four[:, :count].reshape(-1, width)
    maps_z = four[:, count:].reshape(-1, width)

    next_both = after(own)
    k_x = swap(k_rows, 2)

    g_cols = lax.dynamic_slice_in_dim(g_inv, cols * quarter, quarter, 1).T
    h = pl.pallas_call(
        functools.partial(grad_kernel, side),
        out_shape=jax.ShapeDtypeStruct((quarter, full), F32),
        in_specs=[VMEM] * 3,
        out_specs=VMEM,
        compiler_params=PARAMS,
    )(maps_z, grads_z, jnp.concatenate([g_cols, g_cols], axis=0))

    h, k_x, k_rows, next_both = hold((h, k_x, k_rows, next_both))
    k_two = jnp.where(xbit == 0, jnp.stack([k_rows, k_x]), jnp.stack([k_x, k_rows]))
    k_c = swap(k_two, 1)
    next_pair = jnp.concatenate([next_both[None], swap(next_both, 2)[None]], axis=0)
    h = h + swap(h, zbits[0])

    h, k_c, k_two, next_pair = hold((h, k_c, k_two, next_pair))
    k_z = jnp.where(core == 0, jnp.stack([k_two, k_c], 1), jnp.stack([k_c, k_two], 1)).reshape(4 * rows, full)
    next_four = jnp.concatenate([next_pair, swap(next_pair, 1)], axis=0)
    next_maps_z = next_four[:, :, :].reshape(4, 2, count, width)[:, 1].reshape(-1, width)
    next_grads_z = next_four.reshape(4, 2, count, width)[:, 0].reshape(-1, width)
    for b in zbits[1:]:
        h = h + swap(h, b)
    e_mine = h * scale

    p_t = dot_nt(e_mine, k_z, precision=HIGH).astype(BF16)
    p_t, next_grads_z, next_maps_z = hold((p_t, next_grads_z, next_maps_z))
    p_t = after(p_t)

    g_mine = lax.dynamic_slice_in_dim(grads_z, cols * quarter, quarter, 1)
    gram = dot_t(g_mine, jnp.concatenate([grads_z, next_grads_z], axis=1))
    p_t, gram = hold((p_t, gram))
    for b in zbits:
        gram_other = swap(gram, b)
        other = swap(p_t, b)
        p_t = jnp.where((me & b) == 0, jnp.concatenate([p_t, other], 1), jnp.concatenate([other, p_t], 1))
        gram = gram + gram_other
        p_t, gram = hold((p_t, gram))
    gram = gram * scale

    cross_t, cross_half = pl.pallas_call(
        functools.partial(cross_kernel, side),
        out_shape=[jax.ShapeDtypeStruct((quarter, full), F32), jax.ShapeDtypeStruct((quarter, full), BF16)],
        in_specs=[VMEM] * 3,
        out_specs=[VMEM] * 2,
        compiler_params=PARAMS,
    )(maps_z, next_maps_z, p_t)

    cross_t, cross_half, gram = hold((cross_t, cross_half, gram))
    other = swap(gram, 2)
    cross_t = cross_t + swap(cross_half, zbits[0]).astype(F32)
    cross_t, other, gram = hold((cross_t, other, gram))
    gram = jnp.where(xbit == 0, jnp.concatenate([gram, other]), jnp.concatenate([other, gram]))
    other = swap(gram, 1)
    for b in zbits[1:]:
        cross_t = cross_t + swap(cross_t.astype(BF16), b).astype(F32)
    gram = jnp.where(core == 0, jnp.concatenate([gram, other]), jnp.concatenate([other, gram]))
    g_own, g_cross = gram[:, :width], gram[:, width:]
    big_h = dot_t(g_cross, g_inv, precision=HIGH)
    h_mine = lax.dynamic_slice_in_dim(big_h, cols * quarter, quarter, 0) * scale

    main = dot_nt(k_z, e_mine, precision=HIGH)
    main = lax.dynamic_update_slice(jnp.zeros((4 * rows, width), F32), main, (0, cols * quarter))
    fix = jnp.dot(dot_nt(k_z, cross_t, precision=HIGH), h_mine, precision=HIGH)
    out = (main - fix).reshape(2, 2, rows, width)
    keep = lax.dynamic_index_in_dim(out, xbit, 0, False)
    send = lax.dynamic_index_in_dim(out, 1 - xbit, 0, False)
    out = keep + swap(send, 2)
    keep = lax.dynamic_index_in_dim(out, core, 0, False)
    send = lax.dynamic_index_in_dim(out, 1 - core, 0, False)
    update = keep + swap(send, 1)
    return (update[None], jnp.stack([g_own, g_cross])[None])


def solution(mesh):
    return jax.shard_map(
        per_device,
        mesh=mesh,
        in_specs=(
            P("layer", "pos", None, None, None),
            P("layer", "pos", None, None, None),
            P("layer", "pos", None),
            P("layer", None, None),
        ),
        out_specs=(P("layer", "pos", None), P("layer", None, None, None)),
        check_vma=False,
    )
```

time: 94.4 us -> 89.1 us (0.944)
  local copies, waits for them, and re-layouts: 13.2 us -> 1.78 us
  waiting for transfers between devices: 37.1 us -> 48 us
  starting transfers between devices: 29.3 us -> 23.2 us
  matrix products: 10.4 us -> 4.65 us
  Pallas kernels: 0 us -> 3.72 us
  other arithmetic: 2.83 us -> 6.47 us
    unnamed x25 -> x10, local copies, waits for them, and re-layouts: 9.1 us -> 0.74 us
    ppermute x22 -> x18, waiting for transfers between devices: 30.8 us -> 38.2 us  [swap(): lax.ppermute(block, 'pos', [(i, i ^ bit) for i in range(lax.axis_size('po...]
    ppermute x22 -> x18, starting transfers between devices: 25.3 us -> 20.6 us  [swap(): lax.ppermute(block, 'pos', [(i, i ^ bit) for i in range(lax.axis_size('po...]
    dot_general x6 -> x2, matrix products: 5.15 us -> 0.79 us  [dot_t(): lax.dot_general(a, b, (((0,), (0,)), ((), ())), preferred_element_type=F3...]
    pallas_call x0 -> x2, Pallas kernels: none -> 3.72 us  [the longest x1 2.08 us: per_device(): pl.pallas_call(functools.partial(cross_kernel, side), out_shape=[jax.Shap...]
    ppermute x3 -> x2, waiting for transfers between devices: 6.33 us -> 9.81 us  [after(): return lax.ppermute(block, 'layer', route)]
    select_n x3 -> x2, other arithmetic: 0.18 us -> 2.56 us  [the longest x1 1.4 us: per_device(): jnp.where(core == 0, jnp.stack([k_two, k_c], 1), jnp.stack([k_c, k_two], 1))]
    slice x18 -> x2, local copies, waits for them, and re-layouts: 2.09 us -> 0.15 us  [the longest x1 0.07 us: per_device(): grads_z = four[:, :count].reshape(-1, width)]
  transfers between devices with their start and end apart: 25 -> 20, of which waited for: 16 -> 14; matrix products, arithmetic and copies ran while one was open for 19% -> 8% of each run, Pallas kernels for 0% -> 2%
where the time goes in v2:
time: 89.1 us; the launch traced here: 88.8 us
  waiting for transfers between devices  48 us (54%)
  starting transfers between devices  23.2 us (26%)
  other arithmetic  6.47 us (7%)
  matrix products  4.65 us (5%)
  Pallas kernels  3.72 us (4%)
  local copies, waits for them, and re-layouts  1.78 us (2%)
  between operations  0.96 us (1%)
    ppermute x18, waiting for transfers between devices, swap(): lax.ppermute(block, 'pos', [(i, i ^ bit) for i in range(lax.axis_size('po...  38.2 us
    ppermute x18, starting transfers between devices, swap(): lax.ppermute(block, 'pos', [(i, i ^ bit) for i in range(lax.axis_size('po...  20.6 us
    ppermute x2, waiting for transfers between devices, after(): return lax.ppermute(block, 'layer', route)  9.81 us
    dot_general x3, matrix products, dot_nt(): lax.dot_general(a, b, (((1,), (1,)), ((), ())), preferred_element_type=F3...  3.59 us
    ppermute x2, starting transfers between devices, after(): return lax.ppermute(block, 'layer', route)  2.58 us
    pallas_call x1, Pallas kernels, per_device(): pl.pallas_call(functools.partial(cross_kernel, side), out_shape=[jax.Shap...  2.08 us
  transfers between devices with their start and end apart: 20, of which 14 were waited for; matrix products, arithmetic and copies ran while one was open for 8% of the time, Pallas kernels for 2%

profile of v2, /device:TPU:0, one launch (start us, length us, event | category | flops | bytes accessed | tf_op | source)
XLA Modules:
  0.0 88.8 jit_solution(10930089022347191793)
XLA Ops:
  1.7 3.0 %collective-permute-start = (bf16[1024,128]{1,0:T(8,128)(2,1)S(1)}, bf16[1024,128]{1,0:T(8,128)(2,1)S(1)}, u32[]{:S(2)}, u32[]{:S(2)}) collective-permute-start(bf16[1024,128]{1,0:T(8,128)(2,1)S(1)} %get-tuple-element.57), channel_id=1, source_target_pairs={{0,2},{1,3},{2,0},{3,1},{4,6},{5,7},{6,4},{7,5},{8,10},{9,11},{10,... | collective-permute-start | bytes 786440 | tf_op jit(solution)/shard_map/ppermute | solution.py:23
  4.8 6.3 %collective-permute-done = bf16[1024,128]{1,0:T(8,128)(2,1)S(1)} collective-permute-done((bf16[1024,128]{1,0:T(8,128)(2,1)S(1)}, bf16[1024,128]{1,0:T(8,128)(2,1)S(1)}, u32[]{:S(2)}, u32[]{:S(2)}) %collective-permute-start) | collective-permute-done | bytes 262176 | tf_op jit(solution)/shard_map/ppermute | solution.py:23
  11.2 1.3 %collective-permute-start.3 = (bf16[1024,128]{1,0:T(8,128)(2,1)S(1)}, bf16[1024,128]{1,0:T(8,128)(2,1)}, u32[]{:S(2)}, u32[]{:S(2)}) collective-permute-start(bf16[1024,128]{1,0:T(8,128)(2,1)S(1)} %get-tuple-element.57), channel_id=1, source_target_pairs={{16,0},{17,1},{18,2},{19,3},{20,4},{21,5},{22,6},{23,7},{24,8},{25... | collective-permute-start | bytes 786440 | tf_op jit(solution)/shard_map/ppermute | solution.py:19
  12.5 1.8 %collective-permute-start.2 = (f32[72,1152]{1,0:T(8,128)S(1)}, f32[72,1152]{1,0:T(8,128)S(1)}, u32[]{:S(2)}, u32[]{:S(2)}) collective-permute-start(f32[72,1152]{1,0:T(8,128)S(1)} %bitcast.63), channel_id=1, source_target_pairs={{0,2},{1,3},{2,0},{3,1},{4,6},{5,7},{6,4},{7,5},{8,10},{9,11},{10,... | collective-permute-start | bytes 995336 | tf_op jit(solution)/shard_map/ppermute | solution.py:23
  14.7 1.6 %shard_map.59 = f32[32,1152]{1,0:T(8,128)S(1)} custom-call(bf16[2048,128]{1,0:T(8,128)(2,1)S(1)} %bitcast.47, bf16[2048,128]{1,0:T(8,128)(2,1)S(1)} %bitcast.49, f32[64,128]{1,0:T(8,128)S(1)} %pad_maximum_fusion.5.g_two), custom_call_target="tpu_custom_call" | custom-call | tf_op jit(solution)/shard_map/pallas_call | solution.py:130
  16.3 5.6 %collective-permute-done.3 = bf16[1024,128]{1,0:T(8,128)(2,1)} collective-permute-done((bf16[1024,128]{1,0:T(8,128)(2,1)S(1)}, bf16[1024,128]{1,0:T(8,128)(2,1)}, u32[]{:S(2)}, u32[]{:S(2)}) %collective-permute-start.3) | collective-permute-done | bytes 262176 | tf_op jit(solution)/shard_map/ppermute | solution.py:19
  24.7 1.8 %collective-permute-start.6 = (bf16[1024,128]{1,0:T(8,128)(2,1)}, bf16[1024,128]{1,0:T(8,128)(2,1)S(1)}, u32[]{:S(2)}, u32[]{:S(2)}) collective-permute-start(bf16[1024,128]{1,0:T(8,128)(2,1)} %collective-permute-done.3), channel_id=1, source_target_pairs={{0,2},{1,3},{2,0},{3,1},{4,6},{5,7},{6,4},{7,5},{8,10},{9,11},{10,... | collective-permute-start | bytes 786440 | tf_op jit(solution)/shard_map/ppermute | solution.py:23
  26.5 1.6 %collective-permute-start.4 = (f32[32,1152]{1,0:T(8,128)S(1)}, f32[32,1152]{1,0:T(8,128)S(1)}, u32[]{:S(2)}, u32[]{:S(2)}) collective-permute-start(f32[32,1152]{1,0:T(8,128)S(1)} %shard_map.59), channel_id=1, source_target_pairs={{0,4},{1,5},{2,6},{3,7},{4,0},{5,1},{6,2},{7,3},{8,12},{9,13},{10,... | collective-permute-start | bytes 442376 | tf_op jit(solution)/shard_map/ppermute | solution.py:23
  28.1 4.3 %collective-permute-done.4 = f32[32,1152]{1,0:T(8,128)S(1)} collective-permute-done((f32[32,1152]{1,0:T(8,128)S(1)}, f32[32,1152]{1,0:T(8,128)S(1)}, u32[]{:S(2)}, u32[]{:S(2)}) %collective-permute-start.4) | collective-permute-done | bytes 147488 | tf_op jit(solution)/shard_map/ppermute | solution.py:23
  34.7 2.9 %collective-permute-start.7 = (f32[32,1152]{1,0:T(8,128)S(1)}, f32[32,1152]{1,0:T(8,128)S(1)}, u32[]{:S(2)}, u32[]{:S(2)}) collective-permute-start(f32[32,1152]{1,0:T(8,128)S(1)} %add.51), channel_id=1, source_target_pairs={{0,8},{1,9},{2,10},{3,11},{4,12},{5,13},{6,14},{7,15},{8,0},{9,1},... | collective-permute-start | bytes 442376 | tf_op jit(solution)/shard_map/ppermute | solution.py:23
  37.6 1.4 %maximum_select_fusion = f32[2,2,72,1152]{3,2,1,0:T(8,128)S(1)} fusion(f32[2,1,72,1152]{3,2,1,0:T(8,128)} %bitcast.59, f32[2,1,72,1152]{3,2,1,0:T(8,128)S(1)} %bitcast.56, pred[]{:T(512)S(6)} %eq.14), kind=kLoop, calls=%fused_computation | loop fusion | flops 995328 | bytes 2654209 | tf_op jit(solution)/shard_map/jit(_where)/select_n | solution.py:145
  39.0 5.4 %collective-permute-done.7 = f32[32,1152]{1,0:T(8,128)S(1)} collective-permute-done((f32[32,1152]{1,0:T(8,128)S(1)}, f32[32,1152]{1,0:T(8,128)S(1)}, u32[]{:S(2)}, u32[]{:S(2)}) %collective-permute-start.7) | collective-permute-done | bytes 147488 | tf_op jit(solution)/shard_map/ppermute | solution.py:23
  45.8 1.3 %collective-permute-start.9 = (bf16[32,288]{1,0:T(8,128)(2,1)S(1)}, bf16[32,288]{1,0:T(8,128)(2,1)S(1)}, u32[]{:S(2)}, u32[]{:S(2)}) collective-permute-start(bf16[32,288]{1,0:T(8,128)(2,1)S(1)} %convolution_convert_fusion), channel_id=1, source_target_pairs={{16,0},{17,1},{18,2},{19,3},{20,4},{21,5},{22,6},{23,7},{24,8},{25... | collective-permute-start | bytes 55304 | tf_op jit(solution)/shard_map/ppermute | solution.py:19
  47.6 4.3 %collective-permute-done.9 = bf16[32,288]{1,0:T(8,128)(2,1)S(1)} collective-permute-done((bf16[32,288]{1,0:T(8,128)(2,1)S(1)}, bf16[32,288]{1,0:T(8,128)(2,1)S(1)}, u32[]{:S(2)}, u32[]{:S(2)}) %collective-permute-start.9) | collective-permute-done | bytes 18464 | tf_op jit(solution)/shard_map/ppermute | solution.py:19
  52.6 1.3 %collective-permute-start.11 = (f32[32,256]{1,0:T(8,128)S(1)}, f32[32,256]{1,0:T(8,128)S(1)}, u32[]{:S(2)}, u32[]{:S(2)}) collective-permute-start(f32[32,256]{1,0:T(8,128)S(1)} %fusion), channel_id=1, source_target_pairs={{0,4},{1,5},{2,6},{3,7},{4,0},{5,1},{6,2},{7,3},{8,12},{9,13},{10,... | collective-permute-start | bytes 98312 | tf_op jit(solution)/shard_map/ppermute | solution.py:23
  53.9 1.8 %collective-permute-done.10 = bf16[32,288]{1,0:T(8,128)(2,1)S(1)} collective-permute-done((bf16[32,288]{1,0:T(8,128)(2,1)S(1)}, bf16[32,288]{1,0:T(8,128)(2,1)S(1)}, u32[]{:S(2)}, u32[]{:S(2)}) %collective-permute-start.10) | collective-permute-done | bytes 18464 | tf_op jit(solution)/shard_map/ppermute | solution.py:23
  56.5 3.4 %collective-permute-start.12 = (bf16[32,576]{1,0:T(8,128)(2,1)S(1)}, bf16[32,576]{1,0:T(8,128)(2,1)S(1)}, u32[]{:S(2)}, u32[]{:S(2)}) collective-permute-start(bf16[32,576]{1,0:T(8,128)(2,1)S(1)} %maximum_select_fusion.5), channel_id=1, source_target_pairs={{0,8},{1,9},{2,10},{3,11},{4,12},{5,13},{6,14},{7,15},{8,0},{9,1},... | collective-permute-start | bytes 110600 | tf_op jit(solution)/shard_map/ppermute | solution.py:23
  60.0 4.8 %collective-permute-done.13 = f32[32,256]{1,0:T(8,128)S(1)} collective-permute-done((f32[32,256]{1,0:T(8,128)S(1)}, f32[32,256]{1,0:T(8,128)S(1)}, u32[]{:S(2)}, u32[]{:S(2)}) %collective-permute-start.13) | collective-permute-done | bytes 32800 | tf_op jit(solution)/shard_map/ppermute | solution.py:23
  64.9 2.1 %shard_map.60 = (f32[32,1152]{1,0:T(8,128)S(1)}, bf16[32,1152]{1,0:T(8,128)(2,1)S(1)}) custom-call(bf16[2048,128]{1,0:T(8,128)(2,1)S(1)} %bitcast.48, bf16[2048,128]{1,0:T(8,128)(2,1)S(1)} %bitcast.51, bf16[32,1152]{1,0:T(8,128)(2,1)S(1)} %maximum_select_fusion.3.precond_t), custom_call_target="tpu_custom_call" | custom-call | tf_op jit(solution)/shard_map/pallas_call | solution.py:168
  67.3 1.5 %collective-permute-start.15 = (f32[32,256]{1,0:T(8,128)S(1)}, f32[32,256]{1,0:T(8,128)S(1)}, u32[]{:S(2)}, u32[]{:S(2)}) collective-permute-start(f32[32,256]{1,0:T(8,128)S(1)} %broadcast_multiply_fusion), channel_id=1, source_target_pairs={{0,2},{1,3},{2,0},{3,1},{4,6},{5,7},{6,4},{7,5},{8,10},{9,11},{10,... | collective-permute-start | bytes 98312 | tf_op jit(solution)/shard_map/ppermute | solution.py:23
  68.8 2.6 %collective-permute-done.14 = bf16[32,1152]{1,0:T(8,128)(2,1)S(1)} collective-permute-done((bf16[32,1152]{1,0:T(8,128)(2,1)S(1)}, bf16[32,1152]{1,0:T(8,128)(2,1)S(1)}, u32[]{:S(2)}, u32[]{:S(2)}) %collective-permute-start.14) | collective-permute-done | bytes 73760 | tf_op jit(solution)/shard_map/ppermute | solution.py:23
  74.2 6.7 %collective-permute-done.16 = bf16[32,1152]{1,0:T(8,128)(2,1)S(1)} collective-permute-done((bf16[32,1152]{1,0:T(8,128)(2,1)S(1)}, bf16[32,1152]{1,0:T(8,128)(2,1)S(1)}, u32[]{:S(2)}, u32[]{:S(2)}) %collective-permute-start.16) | collective-permute-done | bytes 73760 | tf_op jit(solution)/shard_map/ppermute | solution.py:23
  82.5 1.6 %collective-permute-start.18 = (f32[2,72,128]{2,1,0:T(8,128)S(1)}, f32[2,72,128]{2,1,0:T(8,128)S(1)}, u32[]{:S(2)}, u32[]{:S(2)}) collective-permute-start(f32[2,72,128]{2,1,0:T(8,128)S(1)} %dynamic-slice_bitcast_fusion), channel_id=1, source_target_pairs={{0,2},{1,3},{2,0},{3,1},{4,6},{5,7},{6,4},{7,5},{8,10},{9,11},{10,... | collective-permute-start | bytes 221192 | tf_op jit(solution)/shard_map/ppermute | solution.py:23
  84.0 2.8 %collective-permute-done.18 = f32[2,72,128]{2,1,0:T(8,128)S(1)} collective-permute-done((f32[2,72,128]{2,1,0:T(8,128)S(1)}, f32[2,72,128]{2,1,0:T(8,128)S(1)}, u32[]{:S(2)}, u32[]{:S(2)}) %collective-permute-start.18) | collective-permute-done | bytes 73760 | tf_op jit(solution)/shard_map/ppermute | solution.py:23
  (64 shorter events, 16.6 us)
Async XLA Ops:
  0.6 13.7 %copy-start = (f32[1,128,128]{2,1,0:T(8,128)S(1)}, f32[1,128,128]{2,1,0:T(8,128)}, u32[]{:S(2)}) copy-start(f32[1,128,128]{2,1,0:T(8,128)} %param.7) | copy-start | bytes 196612
  0.6 11.8 %copy-start.2 = (f32[1,72,1152]{2,1,0:T(8,128)S(1)}, f32[1,72,1152]{2,1,0:T(8,128)}, u32[]{:S(2)}) copy-start(f32[1,72,1152]{2,1,0:T(8,128)} %param.6) | copy-start | bytes 995332
  1.7 9.3 %collective-permute-start = (bf16[1024,128]{1,0:T(8,128)(2,1)S(1)}, bf16[1024,128]{1,0:T(8,128)(2,1)S(1)}, u32[]{:S(2)}, u32[]{:S(2)}) collective-permute-start(bf16[1024,128]{1,0:T(8,128)(2,1)S(1)} %get-tuple-element.57), channel_id=1, source_target_pairs={{0,2},{1,3},{2,0},{3,1},{4,6},{5,7},{6,4},{7,5},{8,10},{9,11},{10,... | collective-permute-start | bytes 786440 | tf_op jit(solution)/shard_map/ppermute | solution.py:23
  11.1 3.4 %collective-permute-start.1 = (bf16[2,1024,128]{2,1,0:T(8,128)(2,1)S(1)}, bf16[2,1024,128]{2,1,0:T(8,128)(2,1)S(1)}, u32[]{:S(2)}, u32[]{:S(2)}) collective-permute-start(bf16[2,1024,128]{2,1,0:T(8,128)(2,1)S(1)} %pad_maximum_fusion.2), channel_id=1, source_target_pairs={{0,1},{1,0},{2,3},{3,2},{4,5},{5,4},{6,7},{7,6},{8,9},{9,8},{10,11... | collective-permute-start | bytes 1572872 | tf_op jit(solution)/shard_map/ppermute | solution.py:23
  11.2 10.7 %collective-permute-start.3 = (bf16[1024,128]{1,0:T(8,128)(2,1)S(1)}, bf16[1024,128]{1,0:T(8,128)(2,1)}, u32[]{:S(2)}, u32[]{:S(2)}) collective-permute-start(bf16[1024,128]{1,0:T(8,128)(2,1)S(1)} %get-tuple-element.57), channel_id=1, source_target_pairs={{16,0},{17,1},{18,2},{19,3},{20,4},{21,5},{22,6},{23,7},{24,8},{25... | collective-permute-start | bytes 786440 | tf_op jit(solution)/shard_map/ppermute | solution.py:19
  12.5 10.3 %collective-permute-start.2 = (f32[72,1152]{1,0:T(8,128)S(1)}, f32[72,1152]{1,0:T(8,128)S(1)}, u32[]{:S(2)}, u32[]{:S(2)}) collective-permute-start(f32[72,1152]{1,0:T(8,128)S(1)} %bitcast.63), channel_id=1, source_target_pairs={{0,2},{1,3},{2,0},{3,1},{4,6},{5,7},{6,4},{7,5},{8,10},{9,11},{10,... | collective-permute-start | bytes 995336 | tf_op jit(solution)/shard_map/ppermute | solution.py:23
  14.6 8.9 %copy-start.3 = (f32[1,72,1152]{2,1,0:T(8,128)S(1)}, f32[1,72,1152]{2,1,0:T(8,128)}, u32[]{:S(2)}) copy-start(f32[1,72,1152]{2,1,0:T(8,128)} %param.6) | copy-start | bytes 995332
  24.6 10.0 %collective-permute-start.5 = (f32[2,72,1152]{2,1,0:T(8,128)S(1)}, f32[2,72,1152]{2,1,0:T(8,128)S(1)}, u32[]{:S(2)}, u32[]{:S(2)}) collective-permute-start(f32[2,72,1152]{2,1,0:T(8,128)S(1)} %maximum_select_fusion.1), channel_id=1, source_target_pairs={{0,1},{1,0},{2,3},{3,2},{4,5},{5,4},{6,7},{7,6},{8,9},{9,8},{10,11... | collective-permute-start | bytes 1990664 | tf_op jit(solution)/shard_map/ppermute | solution.py:23
  24.7 8.9 %collective-permute-start.6 = (bf16[1024,128]{1,0:T(8,128)(2,1)}, bf16[1024,128]{1,0:T(8,128)(2,1)S(1)}, u32[]{:S(2)}, u32[]{:S(2)}) collective-permute-start(bf16[1024,128]{1,0:T(8,128)(2,1)} %collective-permute-done.3), channel_id=1, source_target_pairs={{0,2},{1,3},{2,0},{3,1},{4,6},{5,7},{6,4},{7,5},{8,10},{9,11},{10,... | collective-permute-start | bytes 786440 | tf_op jit(solution)/shard_map/ppermute | solution.py:23
  26.5 5.9 %collective-permute-start.4 = (f32[32,1152]{1,0:T(8,128)S(1)}, f32[32,1152]{1,0:T(8,128)S(1)}, u32[]{:S(2)}, u32[]{:S(2)}) collective-permute-start(f32[32,1152]{1,0:T(8,128)S(1)} %shard_map.59), channel_id=1, source_target_pairs={{0,4},{1,5},{2,6},{3,7},{4,0},{5,1},{6,2},{7,3},{8,12},{9,13},{10,... | collective-permute-start | bytes 442376 | tf_op jit(solution)/shard_map/ppermute | solution.py:23
  34.7 2.9 %copy-start.1 = (f32[2,72,1152]{2,1,0:T(8,128)}, f32[2,72,1152]{2,1,0:T(8,128)S(1)}, u32[]{:S(2)}) copy-start(f32[2,72,1152]{2,1,0:T(8,128)S(1)} %collective-permute-done.5) | copy-start | bytes 1990660
  34.7 9.7 %collective-permute-start.7 = (f32[32,1152]{1,0:T(8,128)S(1)}, f32[32,1152]{1,0:T(8,128)S(1)}, u32[]{:S(2)}, u32[]{:S(2)}) collective-permute-start(f32[32,1152]{1,0:T(8,128)S(1)} %add.51), channel_id=1, source_target_pairs={{0,8},{1,9},{2,10},{3,11},{4,12},{5,13},{6,14},{7,15},{8,0},{9,1},... | collective-permute-start | bytes 442376 | tf_op jit(solution)/shard_map/ppermute | solution.py:23
  37.6 8.1 %collective-permute-start.8 = (bf16[2,1024,128]{2,1,0:T(8,128)(2,1)S(1)}, bf16[2,1024,128]{2,1,0:T(8,128)(2,1)S(1)}, u32[]{:S(2)}, u32[]{:S(2)}) collective-permute-start(bf16[2,1024,128]{2,1,0:T(8,128)(2,1)S(1)} %pad_maximum_fusion.3), channel_id=1, source_target_pairs={{0,1},{1,0},{2,3},{3,2},{4,5},{5,4},{6,7},{7,6},{8,9},{9,8},{10,11... | collective-permute-start | bytes 1572872 | tf_op jit(solution)/shard_map/ppermute | solution.py:23
  45.8 6.1 %collective-permute-start.9 = (bf16[32,288]{1,0:T(8,128)(2,1)S(1)}, bf16[32,288]{1,0:T(8,128)(2,1)S(1)}, u32[]{:S(2)}, u32[]{:S(2)}) collective-permute-start(bf16[32,288]{1,0:T(8,128)(2,1)S(1)} %convolution_convert_fusion), channel_id=1, source_target_pairs={{16,0},{17,1},{18,2},{19,3},{20,4},{21,5},{22,6},{23,7},{24,8},{25... | collective-permute-start | bytes 55304 | tf_op jit(solution)/shard_map/ppermute | solution.py:19
  51.9 3.8 %collective-permute-start.10 = (bf16[32,288]{1,0:T(8,128)(2,1)S(1)}, bf16[32,288]{1,0:T(8,128)(2,1)S(1)}, u32[]{:S(2)}, u32[]{:S(2)}) collective-permute-start(bf16[32,288]{1,0:T(8,128)(2,1)S(1)} %collective-permute-done.9), channel_id=1, source_target_pairs={{0,4},{1,5},{2,6},{3,7},{4,0},{5,1},{6,2},{7,3},{8,12},{9,13},{10,... | collective-permute-start | bytes 55304 | tf_op jit(solution)/shard_map/ppermute | solution.py:23
  52.6 3.9 %collective-permute-start.11 = (f32[32,256]{1,0:T(8,128)S(1)}, f32[32,256]{1,0:T(8,128)S(1)}, u32[]{:S(2)}, u32[]{:S(2)}) collective-permute-start(f32[32,256]{1,0:T(8,128)S(1)} %fusion), channel_id=1, source_target_pairs={{0,4},{1,5},{2,6},{3,7},{4,0},{5,1},{6,2},{7,3},{8,12},{9,13},{10,... | collective-permute-start | bytes 98312 | tf_op jit(solution)/shard_map/ppermute | solution.py:23
  56.5 8.3 %collective-permute-start.12 = (bf16[32,576]{1,0:T(8,128)(2,1)S(1)}, bf16[32,576]{1,0:T(8,128)(2,1)S(1)}, u32[]{:S(2)}, u32[]{:S(2)}) collective-permute-start(bf16[32,576]{1,0:T(8,128)(2,1)S(1)} %maximum_select_fusion.5), channel_id=1, source_target_pairs={{0,8},{1,9},{2,10},{3,11},{4,12},{5,13},{6,14},{7,15},{8,0},{9,1},... | collective-permute-start | bytes 110600 | tf_op jit(solution)/shard_map/ppermute | solution.py:23
  59.9 4.9 %collective-permute-start.13 = (f32[32,256]{1,0:T(8,128)S(1)}, f32[32,256]{1,0:T(8,128)S(1)}, u32[]{:S(2)}, u32[]{:S(2)}) collective-permute-start(f32[32,256]{1,0:T(8,128)S(1)} %add.53), channel_id=1, source_target_pairs={{0,8},{1,9},{2,10},{3,11},{4,12},{5,13},{6,14},{7,15},{8,0},{9,1},... | collective-permute-start | bytes 98312 | tf_op jit(solution)/shard_map/ppermute | solution.py:23
  67.0 4.4 %collective-permute-start.14 = (bf16[32,1152]{1,0:T(8,128)(2,1)S(1)}, bf16[32,1152]{1,0:T(8,128)(2,1)S(1)}, u32[]{:S(2)}, u32[]{:S(2)}) collective-permute-start(bf16[32,1152]{1,0:T(8,128)(2,1)S(1)} %get-tuple-element.47), channel_id=1, source_target_pairs={{0,4},{1,5},{2,6},{3,7},{4,0},{5,1},{6,2},{7,3},{8,12},{9,13},{10,... | collective-permute-start | bytes 221192 | tf_op jit(solution)/shard_map/ppermute | solution.py:23
  67.3 4.2 %collective-permute-start.15 = (f32[32,256]{1,0:T(8,128)S(1)}, f32[32,256]{1,0:T(8,128)S(1)}, u32[]{:S(2)}, u32[]{:S(2)}) collective-permute-start(f32[32,256]{1,0:T(8,128)S(1)} %broadcast_multiply_fusion), channel_id=1, source_target_pairs={{0,2},{1,3},{2,0},{3,1},{4,6},{5,7},{6,4},{7,5},{8,10},{9,11},{10,... | collective-permute-start | bytes 98312 | tf_op jit(solution)/shard_map/ppermute | solution.py:23
  71.5 2.5 %collective-permute-start.17 = (f32[64,256]{1,0:T(8,128)S(1)}, f32[64,256]{1,0:T(8,128)S(1)}, u32[]{:S(2)}, u32[]{:S(2)}) collective-permute-start(f32[64,256]{1,0:T(8,128)S(1)} %maximum_select_fusion.4), channel_id=1, source_target_pairs={{0,1},{1,0},{2,3},{3,2},{4,5},{5,4},{6,7},{7,6},{8,9},{9,8},{10,11... | collective-permute-start | bytes 196616 | tf_op jit(solution)/shard_map/ppermute | solution.py:23
  73.5 7.5 %collective-permute-start.16 = (bf16[32,1152]{1,0:T(8,128)(2,1)S(1)}, bf16[32,1152]{1,0:T(8,128)(2,1)S(1)}, u32[]{:S(2)}, u32[]{:S(2)}) collective-permute-start(bf16[32,1152]{1,0:T(8,128)(2,1)S(1)} %convert_element_type.14), channel_id=1, source_target_pairs={{0,8},{1,9},{2,10},{3,11},{4,12},{5,13},{6,14},{7,15},{8,0},{9,1},... | collective-permute-start | bytes 221192 | tf_op jit(solution)/shard_map/ppermute | solution.py:23
  82.5 4.4 %collective-permute-start.18 = (f32[2,72,128]{2,1,0:T(8,128)S(1)}, f32[2,72,128]{2,1,0:T(8,128)S(1)}, u32[]{:S(2)}, u32[]{:S(2)}) collective-permute-start(f32[2,72,128]{2,1,0:T(8,128)S(1)} %dynamic-slice_bitcast_fusion), channel_id=1, source_target_pairs={{0,2},{1,3},{2,0},{3,1},{4,6},{5,7},{6,4},{7,5},{8,10},{9,11},{10,... | collective-permute-start | bytes 221192 | tf_op jit(solution)/shard_map/ppermute | solution.py:23
  86.9 1.3 %collective-permute-start.19 = (f32[72,128]{1,0:T(8,128)S(1)}, f32[72,128]{1,0:T(8,128)S(1)}, u32[]{:S(2)}, u32[]{:S(2)}) collective-permute-start(f32[72,128]{1,0:T(8,128)S(1)} %dynamic-slice_bitcast_fusion.1), channel_id=1, source_target_pairs={{0,1},{1,0},{2,3},{3,2},{4,5},{5,4},{6,7},{7,6},{8,9},{9,8},{10,11... | collective-permute-start | bytes 110600 | tf_op jit(solution)/shard_map/ppermute | solution.py:23
  (1 other events, 0.7 us)

commit v3 on v2

--- a/solution.py
+++ b/solution.py
@@ -10,7 +10,10 @@
 F32 = jnp.float32
 BF16 = jnp.bfloat16
 HIGH = lax.Precision.HIGHEST
-hold = lax.optimization_barrier
+
+
+def behind(block, point):
+    return lax.optimization_barrier((block, point))[0]
 
 
 def after(block):
@@ -116,15 +119,12 @@
     flat_maps = maps.reshape(-1, width)
     flat_grads = grads.reshape(-1, width)
 
+    count = flat_maps.shape[0]
     own = jnp.concatenate([flat_grads, flat_maps], axis=0)
     pair = jnp.concatenate([own[None], swap(own, 2)[None]], axis=0)
     four = jnp.concatenate([pair, swap(pair, 1)], axis=0)
-    count = flat_maps.shape[0]
     grads_z = four[:, :count].reshape(-1, width)
     maps_z = four[:, count:].reshape(-1, width)
-
-    next_both = after(own)
-    k_x = swap(k_rows, 2)
 
     g_cols = lax.dynamic_slice_in_dim(g_inv, cols * quarter, quarter, 1).T
     h = pl.pallas_call(
@@ -135,34 +135,39 @@
         compiler_params=PARAMS,
     )(maps_z, grads_z, jnp.concatenate([g_cols, g_cols], axis=0))
 
-    h, k_x, k_rows, next_both = hold((h, k_x, k_rows, next_both))
+    k_rows = behind(k_rows, h)
+    k_x = swap(k_rows, 2)
+    next_pair = after(behind(pair, h))
+    h = h + swap(h, zbits[0])
     k_two = jnp.where(xbit == 0, jnp.stack([k_rows, k_x]), jnp.stack([k_x, k_rows]))
+    k_two = behind(k_two, h)
     k_c = swap(k_two, 1)
-    next_pair = jnp.concatenate([next_both[None], swap(next_both, 2)[None]], axis=0)
-    h = h + swap(h, zbits[0])
-
-    h, k_c, k_two, next_pair = hold((h, k_c, k_two, next_pair))
     k_z = jnp.where(core == 0, jnp.stack([k_two, k_c], 1), jnp.stack([k_c, k_two], 1)).reshape(4 * rows, full)
-    next_four = jnp.concatenate([next_pair, swap(next_pair, 1)], axis=0)
-    next_maps_z = next_four[:, :, :].reshape(4, 2, count, width)[:, 1].reshape(-1, width)
-    next_grads_z = next_four.reshape(4, 2, count, width)[:, 0].reshape(-1, width)
     for b in zbits[1:]:
         h = h + swap(h, b)
-    e_mine = h * scale
-
-    p_t = dot_nt(e_mine, k_z, precision=HIGH).astype(BF16)
-    p_t, next_grads_z, next_maps_z = hold((p_t, next_grads_z, next_maps_z))
+
+    main_t = dot_nt(h * scale, k_z, precision=HIGH)
+    p_t = main_t.astype(BF16)
+    next_pair = behind(next_pair, p_t)
+    next_four = jnp.concatenate([next_pair, swap(next_pair, 1)], axis=0)
+    next_grads_z = next_four[:, :count].reshape(-1, width)
+    next_maps_z = next_four[:, count:].reshape(-1, width)
     p_t = after(p_t)
 
-    g_mine = lax.dynamic_slice_in_dim(grads_z, cols * quarter, quarter, 1)
-    gram = dot_t(g_mine, jnp.concatenate([grads_z, next_grads_z], axis=1))
-    p_t, gram = hold((p_t, gram))
+    low = cols * quarter
+    both = jnp.concatenate(
+        [
+            lax.dynamic_slice_in_dim(grads_z, low, quarter, 1),
+            lax.dynamic_slice_in_dim(next_grads_z, low, quarter, 1),
+        ],
+        axis=1,
+    )
+    gram = dot_t(behind(both, p_t), grads_z)
     for b in zbits:
-        gram_other = swap(gram, b)
+        gram = behind(gram, p_t)
         other = swap(p_t, b)
+        gram = gram + swap(gram, b)
         p_t = jnp.where((me & b) == 0, jnp.concatenate([p_t, other], 1), jnp.concatenate([other, p_t], 1))
-        gram = gram + gram_other
-        p_t, gram = hold((p_t, gram))
     gram = gram * scale
 
     cross_t, cross_half = pl.pallas_call(
@@ -173,30 +178,30 @@
         compiler_params=PARAMS,
     )(maps_z, next_maps_z, p_t)
 
-    cross_t, cross_half, gram = hold((cross_t, cross_half, gram))
-    other = swap(gram, 2)
+    gram = behind(gram, cross_half)
+    main_t = behind(main_t, cross_half)
+    h_mine = jnp.dot(gram[quarter:], g_inv, precision=HIGH) * scale
+    place = (jnp.arange(width)[None, :] == low + jnp.arange(quarter)[:, None]).astype(F32)
+    main = dot_t(main_t, place, precision=HIGH)
     cross_t = cross_t + swap(cross_half, zbits[0]).astype(F32)
-    cross_t, other, gram = hold((cross_t, other, gram))
-    gram = jnp.where(xbit == 0, jnp.concatenate([gram, other]), jnp.concatenate([other, gram]))
-    other = swap(gram, 1)
     for b in zbits[1:]:
         cross_t = cross_t + swap(cross_t.astype(BF16), b).astype(F32)
-    gram = jnp.where(core == 0, jnp.concatenate([gram, other]), jnp.concatenate([other, gram]))
-    g_own, g_cross = gram[:, :width], gram[:, width:]
-    big_h = dot_t(g_cross, g_inv, precision=HIGH)
-    h_mine = lax.dynamic_slice_in_dim(big_h, cols * quarter, quarter, 0) * scale
-
-    main = dot_nt(k_z, e_mine, precision=HIGH)
-    main = lax.dynamic_update_slice(jnp.zeros((4 * rows, width), F32), main, (0, cols * quarter))
+
     fix = jnp.dot(dot_nt(k_z, cross_t, precision=HIGH), h_mine, precision=HIGH)
     out = (main - fix).reshape(2, 2, rows, width)
+    gram = behind(gram, fix)
+    gram = jnp.stack([gram, swap(gram, 2)])
     keep = lax.dynamic_index_in_dim(out, xbit, 0, False)
     send = lax.dynamic_index_in_dim(out, 1 - xbit, 0, False)
     out = keep + swap(send, 2)
+    gram = jnp.stack([gram, swap(gram, 1)])
     keep = lax.dynamic_index_in_dim(out, core, 0, False)
     send = lax.dynamic_index_in_dim(out, 1 - core, 0, False)
     update = keep + swap(send, 1)
-    return (update[None], jnp.stack([g_own, g_cross])[None])
+    gram = jnp.where(xbit == 0, gram, gram[:, ::-1])
+    gram = jnp.where(core == 0, gram, gram[::-1])
+    gram = gram.reshape(4, 2, quarter, width).transpose(1, 3, 0, 2).reshape(2, width, width)
+    return (update[None], gram[None])
 
 
 def solution(mesh):

time: 89.1 us -> 83 us (0.932)
  waiting for transfers between devices: 48 us -> 41.3 us
  starting transfers between devices: 23.2 us -> 25.1 us
  other arithmetic: 6.47 us -> 4.72 us
  local copies, waits for them, and re-layouts: 1.78 us -> 3.49 us
  matrix products: 4.65 us -> 3.46 us
    ppermute x18 -> x17, waiting for transfers between devices: 38.2 us -> 33.7 us  [swap(): lax.ppermute(block, 'pos', [(i, i ^ bit) for i in range(lax.axis_size('po...]
    ppermute x2, waiting for transfers between devices: 9.81 us -> 7.63 us  [after(): return lax.ppermute(block, 'layer', route)]
    unnamed x10, local copies, waits for them, and re-layouts: 0.74 us -> 2.69 us
    ppermute x18 -> x17, starting transfers between devices: 20.6 us -> 22.6 us  [swap(): lax.ppermute(block, 'pos', [(i, i ^ bit) for i in range(lax.axis_size('po...]
    dot_general x3 -> x2, matrix products: 3.59 us -> 2.42 us  [dot_nt(): lax.dot_general(a, b, (((1,), (1,)), ((), ())), preferred_element_type=F3...]
    select_n x1, other arithmetic: 1.16 us -> 0.08 us  [per_device(): jnp.where(xbit == 0, jnp.stack([k_rows, k_x]), jnp.stack([k_x, k_rows]))]
  transfers between devices with their start and end apart: 20 -> 19, of which waited for: 14 -> 15; matrix products, arithmetic and copies ran while one was open for 8% -> 8% of each run, Pallas kernels for 2% -> 3%
where the time goes in v3:
time: 83 us; the launch traced here: 82.8 us
  waiting for transfers between devices  41.3 us (50%)
  starting transfers between devices  25.1 us (30%)
  other arithmetic  4.72 us (6%)
  Pallas kernels  3.72 us (4%)
  local copies, waits for them, and re-layouts  3.49 us (4%)
  matrix products  3.46 us (4%)
  between operations  0.91 us (1%)
    ppermute x17, waiting for transfers between devices, swap(): lax.ppermute(block, 'pos', [(i, i ^ bit) for i in range(lax.axis_size('po...  33.7 us
    ppermute x17, starting transfers between devices, swap(): lax.ppermute(block, 'pos', [(i, i ^ bit) for i in range(lax.axis_size('po...  22.6 us
    ppermute x2, waiting for transfers between devices, after(): return lax.ppermute(block, 'layer', route)  7.63 us
    unnamed x10, local copies, waits for them, and re-layouts  2.69 us
    ppermute x2, starting transfers between devices, after(): return lax.ppermute(block, 'layer', route)  2.57 us
    dot_general x2, matrix products, dot_nt(): lax.dot_general(a, b, (((1,), (1,)), ((), ())), preferred_element_type=F3...  2.42 us
    pallas_call x1, Pallas kernels, per_device(): pl.pallas_call(functools.partial(cross_kernel, side), out_shape=[jax.Shap...  2.08 us
  transfers between devices with their start and end apart: 19, of which 15 were waited for; matrix products, arithmetic and copies ran while one was open for 8% of the time, Pallas kernels for 3%

profile of v3, /device:TPU:0, one launch (start us, length us, event | category | flops | bytes accessed | tf_op | source)
XLA Modules:
  0.0 82.8 jit_solution(14766915822163902634)
XLA Ops:
  1.7 3.0 %collective-permute-start = (bf16[1024,128]{1,0:T(8,128)(2,1)S(1)}, bf16[1024,128]{1,0:T(8,128)(2,1)S(1)}, u32[]{:S(2)}, u32[]{:S(2)}) collective-permute-start(bf16[1024,128]{1,0:T(8,128)(2,1)S(1)} %get-tuple-element.33), channel_id=1, source_target_pairs={{0,2},{1,3},{2,0},{3,1},{4,6},{5,7},{6,4},{7,5},{8,10},{9,11},{10,... | collective-permute-start | bytes 786440 | tf_op jit(solution)/shard_map/ppermute | solution.py:26
  4.7 6.3 %collective-permute-done = bf16[1024,128]{1,0:T(8,128)(2,1)S(1)} collective-permute-done((bf16[1024,128]{1,0:T(8,128)(2,1)S(1)}, bf16[1024,128]{1,0:T(8,128)(2,1)S(1)}, u32[]{:S(2)}, u32[]{:S(2)}) %collective-permute-start) | collective-permute-done | bytes 262176 | tf_op jit(solution)/shard_map/ppermute | solution.py:26
  12.0 2.0 %collective-permute-done.1 = bf16[2,1024,128]{2,1,0:T(8,128)(2,1)S(1)} collective-permute-done((bf16[2,1024,128]{2,1,0:T(8,128)(2,1)}, bf16[2,1024,128]{2,1,0:T(8,128)(2,1)S(1)}, u32[]{:S(2)}, u32[]{:S(2)}) %collective-permute-start.1) | collective-permute-done | bytes 524320 | tf_op jit(solution)/shard_map/ppermute | solution.py:26
  14.2 1.6 %shard_map.59 = f32[32,1152]{1,0:T(8,128)S(1)} custom-call(bf16[2048,128]{1,0:T(8,128)(2,1)S(1)} %bitcast.53, bf16[2048,128]{1,0:T(8,128)(2,1)S(1)} %bitcast.50, f32[64,128]{1,0:T(8,128)S(1)} %pad_maximum_fusion.6.g_two), custom_call_target="tpu_custom_call" | custom-call | tf_op jit(solution)/shard_map/pallas_call | solution.py:130
  15.9 1.8 %collective-permute-start.4 = (f32[72,1152]{1,0:T(8,128)S(1)}, f32[72,1152]{1,0:T(8,128)S(1)}, u32[]{:S(2)}, u32[]{:S(2)}) collective-permute-start(f32[72,1152]{1,0:T(8,128)S(1)} %bitcast.67), channel_id=1, source_target_pairs={{0,2},{1,3},{2,0},{3,1},{4,6},{5,7},{6,4},{7,5},{8,10},{9,11},{10,... | collective-permute-start | bytes 995336 | tf_op jit(solution)/shard_map/ppermute | solution.py:26
  17.7 1.6 %collective-permute-start.2 = (f32[32,1152]{1,0:T(8,128)S(1)}, f32[32,1152]{1,0:T(8,128)S(1)}, u32[]{:S(2)}, u32[]{:S(2)}) collective-permute-start(f32[32,1152]{1,0:T(8,128)S(1)} %shard_map.59), channel_id=1, source_target_pairs={{0,4},{1,5},{2,6},{3,7},{4,0},{5,1},{6,2},{7,3},{8,12},{9,13},{10,... | collective-permute-start | bytes 442376 | tf_op jit(solution)/shard_map/ppermute | solution.py:26
  19.3 4.0 %collective-permute-done.2 = f32[32,1152]{1,0:T(8,128)S(1)} collective-permute-done((f32[32,1152]{1,0:T(8,128)S(1)}, f32[32,1152]{1,0:T(8,128)S(1)}, u32[]{:S(2)}, u32[]{:S(2)}) %collective-permute-start.2) | collective-permute-done | bytes 147488 | tf_op jit(solution)/shard_map/ppermute | solution.py:26
  23.3 2.5 %collective-permute-done.4 = f32[72,1152]{1,0:T(8,128)S(1)} collective-permute-done((f32[72,1152]{1,0:T(8,128)S(1)}, f32[72,1152]{1,0:T(8,128)S(1)}, u32[]{:S(2)}, u32[]{:S(2)}) %collective-permute-start.4) | collective-permute-done | bytes 331808 | tf_op jit(solution)/shard_map/ppermute | solution.py:26
  27.2 2.9 %collective-permute-start.3 = (f32[32,1152]{1,0:T(8,128)S(1)}, f32[32,1152]{1,0:T(8,128)S(1)}, u32[]{:S(2)}, u32[]{:S(2)}) collective-permute-start(f32[32,1152]{1,0:T(8,128)S(1)} %add.61), channel_id=1, source_target_pairs={{0,8},{1,9},{2,10},{3,11},{4,12},{5,13},{6,14},{7,15},{8,0},{9,1},... | collective-permute-start | bytes 442376 | tf_op jit(solution)/shard_map/ppermute | solution.py:26
  32.4 5.4 %collective-permute-done.3 = f32[32,1152]{1,0:T(8,128)S(1)} collective-permute-done((f32[32,1152]{1,0:T(8,128)S(1)}, f32[32,1152]{1,0:T(8,128)S(1)}, u32[]{:S(2)}, u32[]{:S(2)}) %collective-permute-start.3) | collective-permute-done | bytes 147488 | tf_op jit(solution)/shard_map/ppermute | solution.py:26
  39.0 3.4 %collective-permute-done.6 = bf16[2,1024,128]{2,1,0:T(8,128)(2,1)} collective-permute-done((bf16[2,1024,128]{2,1,0:T(8,128)(2,1)}, bf16[2,1024,128]{2,1,0:T(8,128)(2,1)}, u32[]{:S(2)}, u32[]{:S(2)}) %collective-permute-start.6) | collective-permute-done | bytes 524320 | tf_op jit(solution)/shard_map/ppermute | solution.py:22
  44.0 4.2 %collective-permute-done.8 = bf16[32,288]{1,0:T(8,128)(2,1)S(1)} collective-permute-done((bf16[32,288]{1,0:T(8,128)(2,1)S(1)}, bf16[32,288]{1,0:T(8,128)(2,1)S(1)}, u32[]{:S(2)}, u32[]{:S(2)}) %collective-permute-start.8) | collective-permute-done | bytes 18464 | tf_op jit(solution)/shard_map/ppermute | solution.py:22
  48.2 1.8 %collective-permute-start.9 = (bf16[32,288]{1,0:T(8,128)(2,1)S(1)}, bf16[32,288]{1,0:T(8,128)(2,1)S(1)}, u32[]{:S(2)}, u32[]{:S(2)}) collective-permute-start(bf16[32,288]{1,0:T(8,128)(2,1)S(1)} %collective-permute-done.8), channel_id=1, source_target_pairs={{0,4},{1,5},{2,6},{3,7},{4,0},{5,1},{6,2},{7,3},{8,12},{9,13},{10,... | collective-permute-start | bytes 55304 | tf_op jit(solution)/shard_map/ppermute | solution.py:26
  52.1 2.9 %collective-permute-start.10 = (bf16[32,576]{1,0:T(8,128)(2,1)S(1)}, bf16[32,576]{1,0:T(8,128)(2,1)S(1)}, u32[]{:S(2)}, u32[]{:S(2)}) collective-permute-start(bf16[32,576]{1,0:T(8,128)(2,1)S(1)} %maximum_select_fusion.3), channel_id=1, source_target_pairs={{0,8},{1,9},{2,10},{3,11},{4,12},{5,13},{6,14},{7,15},{8,0},{9,1},... | collective-permute-start | bytes 110600 | tf_op jit(solution)/shard_map/ppermute | solution.py:26
  56.0 1.6 %collective-permute-start.13 = (f32[64,128]{1,0:T(8,128)S(1)}, f32[64,128]{1,0:T(8,128)S(1)}, u32[]{:S(2)}, u32[]{:S(2)}) collective-permute-start(f32[64,128]{1,0:T(8,128)S(1)} %fusion.18), channel_id=1, source_target_pairs={{0,4},{1,5},{2,6},{3,7},{4,0},{5,1},{6,2},{7,3},{8,12},{9,13},{10,... | collective-permute-start | bytes 98312 | tf_op jit(solution)/shard_map/ppermute | solution.py:26
  57.6 2.3 %collective-permute-done.13 = f32[64,128]{1,0:T(8,128)S(1)} collective-permute-done((f32[64,128]{1,0:T(8,128)S(1)}, f32[64,128]{1,0:T(8,128)S(1)}, u32[]{:S(2)}, u32[]{:S(2)}) %collective-permute-start.13) | collective-permute-done | bytes 32800 | tf_op jit(solution)/shard_map/ppermute | solution.py:26
  60.1 2.1 %shard_map.60 = (f32[32,1152]{1,0:T(8,128)S(1)}, bf16[32,1152]{1,0:T(8,128)(2,1)S(1)}) custom-call(bf16[2048,128]{1,0:T(8,128)(2,1)S(1)} %bitcast.54, bf16[2048,128]{1,0:T(8,128)(2,1)S(1)} %bitcast.55, bf16[32,1152]{1,0:T(8,128)(2,1)S(1)} %maximum_select_fusion.2.precond_t), custom_call_target="tpu_custom_call" | custom-call | tf_op jit(solution)/shard_map/pallas_call | solution.py:173
  62.2 2.2 %collective-permute-start.11 = (bf16[32,1152]{1,0:T(8,128)(2,1)S(1)}, bf16[32,1152]{1,0:T(8,128)(2,1)S(1)}, u32[]{:S(2)}, u32[]{:S(2)}) collective-permute-start(bf16[32,1152]{1,0:T(8,128)(2,1)S(1)} %get-tuple-element.18), channel_id=1, source_target_pairs={{0,4},{1,5},{2,6},{3,7},{4,0},{5,1},{6,2},{7,3},{8,12},{9,13},{10,... | collective-permute-start | bytes 221192 | tf_op jit(solution)/shard_map/ppermute | solution.py:26
  64.8 2.8 %collective-permute-done.11 = bf16[32,1152]{1,0:T(8,128)(2,1)S(1)} collective-permute-done((bf16[32,1152]{1,0:T(8,128)(2,1)S(1)}, bf16[32,1152]{1,0:T(8,128)(2,1)S(1)}, u32[]{:S(2)}, u32[]{:S(2)}) %collective-permute-start.11) | collective-permute-done | bytes 73760 | tf_op jit(solution)/shard_map/ppermute | solution.py:26
  67.6 2.3 %collective-permute-start.12 = (bf16[32,1152]{1,0:T(8,128)(2,1)S(1)}, bf16[32,1152]{1,0:T(8,128)(2,1)S(1)}, u32[]{:S(2)}, u32[]{:S(2)}) collective-permute-start(bf16[32,1152]{1,0:T(8,128)(2,1)S(1)} %fusion.6), channel_id=1, source_target_pairs={{0,8},{1,9},{2,10},{3,11},{4,12},{5,13},{6,14},{7,15},{8,0},{9,1},... | collective-permute-start | bytes 221192 | tf_op jit(solution)/shard_map/ppermute | solution.py:26
  70.0 2.9 %collective-permute-done.12 = bf16[32,1152]{1,0:T(8,128)(2,1)S(1)} collective-permute-done((bf16[32,1152]{1,0:T(8,128)(2,1)S(1)}, bf16[32,1152]{1,0:T(8,128)(2,1)S(1)}, u32[]{:S(2)}, u32[]{:S(2)}) %collective-permute-start.12) | collective-permute-done | bytes 73760 | tf_op jit(solution)/shard_map/ppermute | solution.py:26
  74.3 1.7 %collective-permute-start.17 = (f32[64,128]{1,0:T(8,128)S(1)}, f32[64,128]{1,0:T(8,128)S(1)}, u32[]{:S(2)}, u32[]{:S(2)}) collective-permute-start(f32[64,128]{1,0:T(8,128)S(1)} %add_multiply_fusion), channel_id=1, source_target_pairs={{0,2},{1,3},{2,0},{3,1},{4,6},{5,7},{6,4},{7,5},{8,10},{9,11},{10,... | collective-permute-start | bytes 98312 | tf_op jit(solution)/shard_map/ppermute | solution.py:26
  76.8 1.5 %collective-permute-done.17 = f32[64,128]{1,0:T(8,128)S(1)} collective-permute-done((f32[64,128]{1,0:T(8,128)S(1)}, f32[64,128]{1,0:T(8,128)S(1)}, u32[]{:S(2)}, u32[]{:S(2)}) %collective-permute-start.17) | collective-permute-done | bytes 32800 | tf_op jit(solution)/shard_map/ppermute | solution.py:26
  78.4 2.4 %collective-permute-done.15 = f32[2,72,128]{2,1,0:T(8,128)S(1)} collective-permute-done((f32[2,72,128]{2,1,0:T(8,128)S(1)}, f32[2,72,128]{2,1,0:T(8,128)S(1)}, u32[]{:S(2)}, u32[]{:S(2)}) %collective-permute-start.15) | collective-permute-done | bytes 73760 | tf_op jit(solution)/shard_map/ppermute | solution.py:26
  (62 shorter events, 16.6 us)
Async XLA Ops:
  0.6 11.3 %copy-start = (f32[1,128,128]{2,1,0:T(8,128)S(1)}, f32[1,128,128]{2,1,0:T(8,128)}, u32[]{:S(2)}) copy-start(f32[1,128,128]{2,1,0:T(8,128)} %param.7) | copy-start | bytes 196612
  1.7 9.3 %collective-permute-start = (bf16[1024,128]{1,0:T(8,128)(2,1)S(1)}, bf16[1024,128]{1,0:T(8,128)(2,1)S(1)}, u32[]{:S(2)}, u32[]{:S(2)}) collective-permute-start(bf16[1024,128]{1,0:T(8,128)(2,1)S(1)} %get-tuple-element.33), channel_id=1, source_target_pairs={{0,2},{1,3},{2,0},{3,1},{4,6},{5,7},{6,4},{7,5},{8,10},{9,11},{10,... | collective-permute-start | bytes 786440 | tf_op jit(solution)/shard_map/ppermute | solution.py:26
  11.9 2.1 %collective-permute-start.1 = (bf16[2,1024,128]{2,1,0:T(8,128)(2,1)}, bf16[2,1024,128]{2,1,0:T(8,128)(2,1)S(1)}, u32[]{:S(2)}, u32[]{:S(2)}) collective-permute-start(bf16[2,1024,128]{2,1,0:T(8,128)(2,1)} %pad_maximum_fusion.1), channel_id=1, source_target_pairs={{0,1},{1,0},{2,3},{3,2},{4,5},{5,4},{6,7},{7,6},{8,9},{9,8},{10,11... | collective-permute-start | bytes 1572872 | tf_op jit(solution)/shard_map/ppermute | solution.py:26
  14.1 1.7 %copy-start.2 = (f32[1,72,1152]{2,1,0:T(8,128)S(1)}, f32[1,72,1152]{2,1,0:T(8,128)}, u32[]{:S(2)}) copy-start(f32[1,72,1152]{2,1,0:T(8,128)} %param.6) | copy-start | bytes 995332
  14.2 11.6 %copy-start.3 = (f32[1,72,1152]{2,1,0:T(8,128)S(1)}, f32[1,72,1152]{2,1,0:T(8,128)}, u32[]{:S(2)}) copy-start(f32[1,72,1152]{2,1,0:T(8,128)} %param.6) | copy-start | bytes 995332
  15.9 9.9 %collective-permute-start.4 = (f32[72,1152]{1,0:T(8,128)S(1)}, f32[72,1152]{1,0:T(8,128)S(1)}, u32[]{:S(2)}, u32[]{:S(2)}) collective-permute-start(f32[72,1152]{1,0:T(8,128)S(1)} %bitcast.67), channel_id=1, source_target_pairs={{0,2},{1,3},{2,0},{3,1},{4,6},{5,7},{6,4},{7,5},{8,10},{9,11},{10,... | collective-permute-start | bytes 995336 | tf_op jit(solution)/shard_map/ppermute | solution.py:26
  17.7 5.6 %collective-permute-start.2 = (f32[32,1152]{1,0:T(8,128)S(1)}, f32[32,1152]{1,0:T(8,128)S(1)}, u32[]{:S(2)}, u32[]{:S(2)}) collective-permute-start(f32[32,1152]{1,0:T(8,128)S(1)} %shard_map.59), channel_id=1, source_target_pairs={{0,4},{1,5},{2,6},{3,7},{4,0},{5,1},{6,2},{7,3},{8,12},{9,13},{10,... | collective-permute-start | bytes 442376 | tf_op jit(solution)/shard_map/ppermute | solution.py:26
  25.9 4.3 %collective-permute-start.5 = (f32[2,72,1152]{2,1,0:T(8,128)S(1)}, f32[2,72,1152]{2,1,0:T(8,128)S(1)}, u32[]{:S(2)}, u32[]{:S(2)}) collective-permute-start(f32[2,72,1152]{2,1,0:T(8,128)S(1)} %maximum_select_fusion.1), channel_id=1, source_target_pairs={{0,1},{1,0},{2,3},{3,2},{4,5},{5,4},{6,7},{7,6},{8,9},{9,8},{10,11... | collective-permute-start | bytes 1990664 | tf_op jit(solution)/shard_map/ppermute | solution.py:26
  25.9 16.5 %collective-permute-start.6 = (bf16[2,1024,128]{2,1,0:T(8,128)(2,1)}, bf16[2,1024,128]{2,1,0:T(8,128)(2,1)}, u32[]{:S(2)}, u32[]{:S(2)}) collective-permute-start(bf16[2,1024,128]{2,1,0:T(8,128)(2,1)} %pad_maximum_fusion.1), channel_id=1, source_target_pairs={{16,0},{17,1},{18,2},{19,3},{20,4},{21,5},{22,6},{23,7},{24,8},{25... | collective-permute-start | bytes 1572872 | tf_op jit(solution)/shard_map/ppermute | solution.py:22
  27.2 10.6 %collective-permute-start.3 = (f32[32,1152]{1,0:T(8,128)S(1)}, f32[32,1152]{1,0:T(8,128)S(1)}, u32[]{:S(2)}, u32[]{:S(2)}) collective-permute-start(f32[32,1152]{1,0:T(8,128)S(1)} %add.61), channel_id=1, source_target_pairs={{0,8},{1,9},{2,10},{3,11},{4,12},{5,13},{6,14},{7,15},{8,0},{9,1},... | collective-permute-start | bytes 442376 | tf_op jit(solution)/shard_map/ppermute | solution.py:26
  30.1 0.8 %copy-start.1 = (f32[2,72,1152]{2,1,0:T(8,128)}, f32[2,72,1152]{2,1,0:T(8,128)S(1)}, u32[]{:S(2)}) copy-start(f32[2,72,1152]{2,1,0:T(8,128)S(1)} %collective-permute-done.5) | copy-start | bytes 1990660
  42.5 12.5 %collective-permute-start.7 = (bf16[2,1024,128]{2,1,0:T(8,128)(2,1)}, bf16[2,1024,128]{2,1,0:T(8,128)(2,1)S(1)}, u32[]{:S(2)}, u32[]{:S(2)}) collective-permute-start(bf16[2,1024,128]{2,1,0:T(8,128)(2,1)} %collective-permute-done.6), channel_id=1, source_target_pairs={{0,1},{1,0},{2,3},{3,2},{4,5},{5,4},{6,7},{7,6},{8,9},{9,8},{10,11... | collective-permute-start | bytes 1572872 | tf_op jit(solution)/shard_map/ppermute | solution.py:26
  42.5 5.7 %collective-permute-start.8 = (bf16[32,288]{1,0:T(8,128)(2,1)S(1)}, bf16[32,288]{1,0:T(8,128)(2,1)S(1)}, u32[]{:S(2)}, u32[]{:S(2)}) collective-permute-start(bf16[32,288]{1,0:T(8,128)(2,1)S(1)} %get-tuple-element.36), channel_id=1, source_target_pairs={{16,0},{17,1},{18,2},{19,3},{20,4},{21,5},{22,6},{23,7},{24,8},{25... | collective-permute-start | bytes 55304 | tf_op jit(solution)/shard_map/ppermute | solution.py:22
  48.2 3.8 %collective-permute-start.9 = (bf16[32,288]{1,0:T(8,128)(2,1)S(1)}, bf16[32,288]{1,0:T(8,128)(2,1)S(1)}, u32[]{:S(2)}, u32[]{:S(2)}) collective-permute-start(bf16[32,288]{1,0:T(8,128)(2,1)S(1)} %collective-permute-done.8), channel_id=1, source_target_pairs={{0,4},{1,5},{2,6},{3,7},{4,0},{5,1},{6,2},{7,3},{8,12},{9,13},{10,... | collective-permute-start | bytes 55304 | tf_op jit(solution)/shard_map/ppermute | solution.py:26
  52.1 8.0 %collective-permute-start.10 = (bf16[32,576]{1,0:T(8,128)(2,1)S(1)}, bf16[32,576]{1,0:T(8,128)(2,1)S(1)}, u32[]{:S(2)}, u32[]{:S(2)}) collective-permute-start(bf16[32,576]{1,0:T(8,128)(2,1)S(1)} %maximum_select_fusion.3), channel_id=1, source_target_pairs={{0,8},{1,9},{2,10},{3,11},{4,12},{5,13},{6,14},{7,15},{8,0},{9,1},... | collective-permute-start | bytes 110600 | tf_op jit(solution)/shard_map/ppermute | solution.py:26
  56.0 4.0 %collective-permute-start.13 = (f32[64,128]{1,0:T(8,128)S(1)}, f32[64,128]{1,0:T(8,128)S(1)}, u32[]{:S(2)}, u32[]{:S(2)}) collective-permute-start(f32[64,128]{1,0:T(8,128)S(1)} %fusion.18), channel_id=1, source_target_pairs={{0,4},{1,5},{2,6},{3,7},{4,0},{5,1},{6,2},{7,3},{8,12},{9,13},{10,... | collective-permute-start | bytes 98312 | tf_op jit(solution)/shard_map/ppermute | solution.py:26
  60.0 4.8 %collective-permute-start.14 = (f32[64,128]{1,0:T(8,128)S(1)}, f32[64,128]{1,0:T(8,128)S(1)}, u32[]{:S(2)}, u32[]{:S(2)}) collective-permute-start(f32[64,128]{1,0:T(8,128)S(1)} %add.67), channel_id=1, source_target_pairs={{0,8},{1,9},{2,10},{3,11},{4,12},{5,13},{6,14},{7,15},{8,0},{9,1},... | collective-permute-start | bytes 98312 | tf_op jit(solution)/shard_map/ppermute | solution.py:26
  62.2 5.3 %collective-permute-start.11 = (bf16[32,1152]{1,0:T(8,128)(2,1)S(1)}, bf16[32,1152]{1,0:T(8,128)(2,1)S(1)}, u32[]{:S(2)}, u32[]{:S(2)}) collective-permute-start(bf16[32,1152]{1,0:T(8,128)(2,1)S(1)} %get-tuple-element.18), channel_id=1, source_target_pairs={{0,4},{1,5},{2,6},{3,7},{4,0},{5,1},{6,2},{7,3},{8,12},{9,13},{10,... | collective-permute-start | bytes 221192 | tf_op jit(solution)/shard_map/ppermute | solution.py:26
  67.6 5.3 %collective-permute-start.12 = (bf16[32,1152]{1,0:T(8,128)(2,1)S(1)}, bf16[32,1152]{1,0:T(8,128)(2,1)S(1)}, u32[]{:S(2)}, u32[]{:S(2)}) collective-permute-start(bf16[32,1152]{1,0:T(8,128)(2,1)S(1)} %fusion.6), channel_id=1, source_target_pairs={{0,8},{1,9},{2,10},{3,11},{4,12},{5,13},{6,14},{7,15},{8,0},{9,1},... | collective-permute-start | bytes 221192 | tf_op jit(solution)/shard_map/ppermute | solution.py:26
  74.3 4.0 %collective-permute-start.17 = (f32[64,128]{1,0:T(8,128)S(1)}, f32[64,128]{1,0:T(8,128)S(1)}, u32[]{:S(2)}, u32[]{:S(2)}) collective-permute-start(f32[64,128]{1,0:T(8,128)S(1)} %add_multiply_fusion), channel_id=1, source_target_pairs={{0,2},{1,3},{2,0},{3,1},{4,6},{5,7},{6,4},{7,5},{8,10},{9,11},{10,... | collective-permute-start | bytes 98312 | tf_op jit(solution)/shard_map/ppermute | solution.py:26
  76.4 4.4 %collective-permute-start.15 = (f32[2,72,128]{2,1,0:T(8,128)S(1)}, f32[2,72,128]{2,1,0:T(8,128)S(1)}, u32[]{:S(2)}, u32[]{:S(2)}) collective-permute-start(f32[2,72,128]{2,1,0:T(8,128)S(1)} %dynamic-slice_bitcast_fusion), channel_id=1, source_target_pairs={{0,2},{1,3},{2,0},{3,1},{4,6},{5,7},{6,4},{7,5},{8,10},{9,11},{10,... | collective-permute-start | bytes 221192 | tf_op jit(solution)/shard_map/ppermute | solution.py:26
  78.3 2.6 %collective-permute-start.18 = (f32[2,64,128]{2,1,0:T(8,128)S(1)}, f32[2,64,128]{2,1,0:T(8,128)S(1)}, u32[]{:S(2)}, u32[]{:S(2)}) collective-permute-start(f32[2,64,128]{2,1,0:T(8,128)S(1)} %get-tuple-element.35), channel_id=1, source_target_pairs={{0,1},{1,0},{2,3},{3,2},{4,5},{5,4},{6,7},{7,6},{8,9},{9,8},{10,11... | collective-permute-start | bytes 196616 | tf_op jit(solution)/shard_map/ppermute | solution.py:26
  80.9 1.3 %collective-permute-start.16 = (f32[72,128]{1,0:T(8,128)S(1)}, f32[72,128]{1,0:T(8,128)S(1)}, u32[]{:S(2)}, u32[]{:S(2)}) collective-permute-start(f32[72,128]{1,0:T(8,128)S(1)} %dynamic-slice_bitcast_fusion.1), channel_id=1, source_target_pairs={{0,1},{1,0},{2,3},{3,2},{4,5},{5,4},{6,7},{7,6},{8,9},{9,8},{10,11... | collective-permute-start | bytes 110600 | tf_op jit(solution)/shard_map/ppermute | solution.py:26

commit v4 on v3

--- a/solution.py
+++ b/solution.py
@@ -54,24 +54,33 @@
     return jnp.concatenate(moved, axis=0)
 
 
-def grad_kernel(side, maps, grads, g_two, out):
-    quarter = out.shape[0]
+def grad_kernel(side, maps, grads, g_inv, keep, send, all_rows):
     width = maps.shape[1]
-    first = g_two[...].astype(BF16)
-    rest = g_two[...] - first.astype(F32)
+    g_t = g_inv[...]
+    first = g_t.astype(BF16)
+    rest = g_t - first.astype(F32)
     second = rest.astype(BF16)
     third = (rest - second.astype(F32)).astype(BF16)
     g = grads[...]
-    mixed = dot_nt(first, g) + (dot_nt(second, g) + dot_nt(third, g))
+
+    def mix(part):
+        return lax.dot_general(part, g, (((0,), (1,)), ((), ())), preferred_element_type=F32)
+
+    mixed = mix(first) + (mix(second) + mix(third))
     high = mixed.astype(BF16).astype(F32)
-    row = lax.broadcasted_iota(jnp.int32, mixed.shape, 0)
-    mixed = jnp.where(row < quarter, high, mixed - high)
-    both = jnp.dot(taps_to_rows(mixed, side), maps[...], preferred_element_type=F32)
+    rows = taps_to_rows(jnp.concatenate([high, mixed - high], axis=0), side)
+    both = jnp.dot(rows, maps[...], preferred_element_type=F32)
     for tap in range(9):
-        low = 2 * quarter * tap
-        out[:, tap * width : (tap + 1) * width] = (
-            both[low : low + quarter] + both[low + quarter : low + 2 * quarter]
+        low = 2 * width * tap
+        all_rows[:, tap * width : (tap + 1) * width] = (
+            both[low : low + width] + both[low + width : low + 2 * width]
         )
+    me = lax.axis_index("pos")
+    mine = 2 * (me & 1) + ((me >> 1) & 1)
+    quarter = width // 4
+    for j in range(4):
+        block = all_rows[pl.ds(pl.multiple_of((mine ^ j) * quarter, quarter), quarter), :]
+        (keep if j < 2 else send)[j % 2] = block
 
 
 def cross_kernel(side, maps, maps_next, precond_t, out, out_half):
@@ -119,39 +128,35 @@
     flat_maps = maps.reshape(-1, width)
     flat_grads = grads.reshape(-1, width)
 
-    count = flat_maps.shape[0]
+    keep, send = pl.pallas_call(
+        functools.partial(grad_kernel, side),
+        out_shape=[jax.ShapeDtypeStruct((2, quarter, full), F32)] * 2,
+        in_specs=[VMEM] * 3,
+        out_specs=[VMEM] * 2,
+        scratch_shapes=[pltpu.VMEM((width, full), F32)],
+        compiler_params=PARAMS,
+    )(flat_maps, flat_grads, g_inv)
     own = jnp.concatenate([flat_grads, flat_maps], axis=0)
-    pair = jnp.concatenate([own[None], swap(own, 2)[None]], axis=0)
-    four = jnp.concatenate([pair, swap(pair, 1)], axis=0)
-    grads_z = four[:, :count].reshape(-1, width)
-    maps_z = four[:, count:].reshape(-1, width)
-
-    g_cols = lax.dynamic_slice_in_dim(g_inv, cols * quarter, quarter, 1).T
-    h = pl.pallas_call(
-        functools.partial(grad_kernel, side),
-        out_shape=jax.ShapeDtypeStruct((quarter, full), F32),
-        in_specs=[VMEM] * 3,
-        out_specs=VMEM,
-        compiler_params=PARAMS,
-    )(maps_z, grads_z, jnp.concatenate([g_cols, g_cols], axis=0))
-
-    k_rows = behind(k_rows, h)
+    next_own = after(own)
     k_x = swap(k_rows, 2)
-    next_pair = after(behind(pair, h))
+    h = keep + swap(send, 1)
+    h = h[0] + swap(h[1], 2)
+    h, k_x, next_own = lax.optimization_barrier((h, k_x, next_own))
+
+    k_two = jnp.where(xbit == 0, jnp.stack([k_rows, k_x]), jnp.stack([k_x, k_rows]))
+    k_c = swap(k_two, 1)
+    two_own = jnp.concatenate([own, next_own], axis=0)
+    pair = jnp.stack([two_own, swap(two_own, 2)])
     h = h + swap(h, zbits[0])
-    k_two = jnp.where(xbit == 0, jnp.stack([k_rows, k_x]), jnp.stack([k_x, k_rows]))
-    k_two = behind(k_two, h)
-    k_c = swap(k_two, 1)
     k_z = jnp.where(core == 0, jnp.stack([k_two, k_c], 1), jnp.stack([k_c, k_two], 1)).reshape(4 * rows, full)
     for b in zbits[1:]:
         h = h + swap(h, b)
 
     main_t = dot_nt(h * scale, k_z, precision=HIGH)
     p_t = main_t.astype(BF16)
-    next_pair = behind(next_pair, p_t)
-    next_four = jnp.concatenate([next_pair, swap(next_pair, 1)], axis=0)
-    next_grads_z = next_four[:, :count].reshape(-1, width)
-    next_maps_z = next_four[:, count:].reshape(-1, width)
+    pair = behind(pair, p_t)
+    four = jnp.concatenate([pair, swap(pair, 1)], axis=0).reshape(4, 4, -1, width)
+    grads_z, maps_z, next_grads_z, next_maps_z = (four[:, i].reshape(-1, width) for i in range(4))
     p_t = after(p_t)
 
     low = cols * quarter
@@ -164,11 +169,8 @@
     )
     gram = dot_t(behind(both, p_t), grads_z)
     for b in zbits:
-        gram = behind(gram, p_t)
         other = swap(p_t, b)
-        gram = gram + swap(gram, b)
         p_t = jnp.where((me & b) == 0, jnp.concatenate([p_t, other], 1), jnp.concatenate([other, p_t], 1))
-    gram = gram * scale
 
     cross_t, cross_half = pl.pallas_call(
         functools.partial(cross_kernel, side),
@@ -180,16 +182,19 @@
 
     gram = behind(gram, cross_half)
     main_t = behind(main_t, cross_half)
-    h_mine = jnp.dot(gram[quarter:], g_inv, precision=HIGH) * scale
     place = (jnp.arange(width)[None, :] == low + jnp.arange(quarter)[:, None]).astype(F32)
     main = dot_t(main_t, place, precision=HIGH)
-    cross_t = cross_t + swap(cross_half, zbits[0]).astype(F32)
-    for b in zbits[1:]:
-        cross_t = cross_t + swap(cross_t.astype(BF16), b).astype(F32)
+    for b in zbits:
+        gram = gram + swap(gram, b)
+        cross_t = cross_t + swap(cross_half, b).astype(F32)
+        cross_half = cross_t.astype(BF16)
+        gram = behind(gram, cross_half)
+    gram = gram * scale
+    h_mine = jnp.dot(gram[quarter:], g_inv, precision=HIGH) * scale
 
     fix = jnp.dot(dot_nt(k_z, cross_t, precision=HIGH), h_mine, precision=HIGH)
     out = (main - fix).reshape(2, 2, rows, width)
-    gram = behind(gram, fix)
+    gram = behind(gram, out)
     gram = jnp.stack([gram, swap(gram, 2)])
     keep = lax.dynamic_index_in_dim(out, xbit, 0, False)
     send = lax.dynamic_index_in_dim(out, 1 - xbit, 0, False)

time: 83 us -> 82.9 us (level)
  starting transfers between devices: 25.1 us -> 22.5 us
  waiting for transfers between devices: 41.3 us -> 42.6 us
    ppermute x17 -> x18, starting transfers between devices: 22.6 us -> 20 us  [swap(): lax.ppermute(block, 'pos', [(i, i ^ bit) for i in range(lax.axis_size('po...]
    ppermute x2, waiting for transfers between devices: 7.63 us -> 9.84 us  [after(): return lax.ppermute(block, 'layer', route)]
    another operation x0 -> x2, other arithmetic: none -> 1.21 us  [per_device(): pair = jnp.stack([two_own, swap(two_own, 2)])]
    broadcast_in_dim x1 -> x0, other arithmetic: 1.07 us -> none  [per_device(): pair = jnp.concatenate([own[None], swap(own, 2)[None]], axis=0)]
    ppermute x17 -> x18, waiting for transfers between devices: 33.7 us -> 32.8 us  [swap(): lax.ppermute(block, 'pos', [(i, i ^ bit) for i in range(lax.axis_size('po...]
    unnamed x10 -> x15, local copies, waits for them, and re-layouts: 2.69 us -> 3.41 us
  transfers between devices with their start and end apart: 19 -> 20, of which waited for: 15 -> 17; matrix products, arithmetic and copies ran while one was open for 8% -> 6% of each run, Pallas kernels for 3% -> 0%
where the time goes in v4:
time: 82.9 us; the launch traced here: 82.5 us
  waiting for transfers between devices  42.6 us (51%)
  starting transfers between devices  22.5 us (27%)
  other arithmetic  5.5 us (7%)
  local copies, waits for them, and re-layouts  3.96 us (5%)
  matrix products  3.49 us (4%)
  Pallas kernels  3.45 us (4%)
  between operations  0.93 us (1%)
    ppermute x18, waiting for transfers between devices, swap(): lax.ppermute(block, 'pos', [(i, i ^ bit) for i in range(lax.axis_size('po...  32.8 us
    ppermute x18, starting transfers between devices, swap(): lax.ppermute(block, 'pos', [(i, i ^ bit) for i in range(lax.axis_size('po...  20 us
    ppermute x2, waiting for transfers between devices, after(): return lax.ppermute(block, 'layer', route)  9.84 us
    unnamed x15, local copies, waits for them, and re-layouts  3.41 us
    ppermute x2, starting transfers between devices, after(): return lax.ppermute(block, 'layer', route)  2.58 us
    dot_general x2, matrix products, dot_nt(): lax.dot_general(a, b, (((1,), (1,)), ((), ())), preferred_element_type=F3...  2.43 us
    pallas_call x1, Pallas kernels, per_device(): pl.pallas_call(functools.partial(cross_kernel, side), out_shape=[jax.Shap...  2.08 us
  transfers between devices with their start and end apart: 20, of which 17 were waited for; matrix products, arithmetic and copies ran while one was open for 6% of the time, Pallas kernels for 0%

profile of v4, /device:TPU:0, one launch (start us, length us, event | category | flops | bytes accessed | tf_op | source)
XLA Modules:
  0.0 82.5 jit_solution(8985048024168565435)
XLA Ops:
  3.3 1.4 %shard_map.59 = (f32[2,32,1152]{2,1,0:T(8,128)S(1)}, f32[2,32,1152]{2,1,0:T(8,128)S(1)}) custom-call(bf16[512,128]{1,0:T(8,128)(2,1)S(1)} %bitcast.60, bf16[512,128]{1,0:T(8,128)(2,1)S(1)} %bitcast.63, f32[128,128]{1,0:T(8,128)S(1)} %bitcast.66), custom_call_target="tpu_custom_call" | custom-call | tf_op jit(solution)/shard_map/pallas_call | solution.py:131
  6.4 2.9 %collective-permute-start.1 = (f32[32,1152]{1,0:T(8,128)S(1)}, f32[32,1152]{1,0:T(8,128)S(1)}, u32[]{:S(2)}, u32[]{:S(2)}) collective-permute-start(f32[32,1152]{1,0:T(8,128)S(1)} %slice_bitcast_fusion), channel_id=1, source_target_pairs={{0,2},{1,3},{2,0},{3,1},{4,6},{5,7},{6,4},{7,5},{8,10},{9,11},{10,... | collective-permute-start | bytes 442376 | tf_op jit(solution)/shard_map/ppermute | solution.py:26
  9.5 1.3 %collective-permute-start.3 = (bf16[1024,128]{1,0:T(8,128)(2,1)S(1)}, bf16[1024,128]{1,0:T(8,128)(2,1)S(1)}, u32[]{:S(2)}, u32[]{:S(2)}) collective-permute-start(bf16[1024,128]{1,0:T(8,128)(2,1)S(1)} %pad_maximum_fusion.4), channel_id=1, source_target_pairs={{16,0},{17,1},{18,2},{19,3},{20,4},{21,5},{22,6},{23,7},{24,8},{25... | collective-permute-start | bytes 786440 | tf_op jit(solution)/shard_map/ppermute | solution.py:22
  10.8 3.2 %collective-permute-done.1 = f32[32,1152]{1,0:T(8,128)S(1)} collective-permute-done((f32[32,1152]{1,0:T(8,128)S(1)}, f32[32,1152]{1,0:T(8,128)S(1)}, u32[]{:S(2)}, u32[]{:S(2)}) %collective-permute-start.1) | collective-permute-done | bytes 147488 | tf_op jit(solution)/shard_map/ppermute | solution.py:26
  14.0 5.4 %collective-permute-done.3 = bf16[1024,128]{1,0:T(8,128)(2,1)S(1)} collective-permute-done((bf16[1024,128]{1,0:T(8,128)(2,1)S(1)}, bf16[1024,128]{1,0:T(8,128)(2,1)S(1)}, u32[]{:S(2)}, u32[]{:S(2)}) %collective-permute-start.3) | collective-permute-done | bytes 262176 | tf_op jit(solution)/shard_map/ppermute | solution.py:22
  20.7 1.8 %collective-permute-start.7 = (bf16[2048,128]{1,0:T(8,128)(2,1)S(1)}, bf16[2048,128]{1,0:T(8,128)(2,1)}, u32[]{:S(2)}, u32[]{:S(2)}) collective-permute-start(bf16[2048,128]{1,0:T(8,128)(2,1)S(1)} %get-tuple-element.35), channel_id=1, source_target_pairs={{0,2},{1,3},{2,0},{3,1},{4,6},{5,7},{6,4},{7,5},{8,10},{9,11},{10,... | collective-permute-start | bytes 1572872 | tf_op jit(solution)/shard_map/ppermute | solution.py:26
  22.7 1.6 %collective-permute-start.4 = (f32[32,1152]{1,0:T(8,128)S(1)}, f32[32,1152]{1,0:T(8,128)S(1)}, u32[]{:S(2)}, u32[]{:S(2)}) collective-permute-start(f32[32,1152]{1,0:T(8,128)S(1)} %fusion), channel_id=1, source_target_pairs={{0,4},{1,5},{2,6},{3,7},{4,0},{5,1},{6,2},{7,3},{8,12},{9,13},{10,... | collective-permute-start | bytes 442376 | tf_op jit(solution)/shard_map/ppermute | solution.py:26
  24.4 4.5 %collective-permute-done.4 = f32[32,1152]{1,0:T(8,128)S(1)} collective-permute-done((f32[32,1152]{1,0:T(8,128)S(1)}, f32[32,1152]{1,0:T(8,128)S(1)}, u32[]{:S(2)}, u32[]{:S(2)}) %collective-permute-start.4) | collective-permute-done | bytes 147488 | tf_op jit(solution)/shard_map/ppermute | solution.py:26
  29.0 2.6 %collective-permute-start.5 = (f32[32,1152]{1,0:T(8,128)S(1)}, f32[32,1152]{1,0:T(8,128)S(1)}, u32[]{:S(2)}, u32[]{:S(2)}) collective-permute-start(f32[32,1152]{1,0:T(8,128)S(1)} %add.66), channel_id=1, source_target_pairs={{0,8},{1,9},{2,10},{3,11},{4,12},{5,13},{6,14},{7,15},{8,0},{9,1},... | collective-permute-start | bytes 442376 | tf_op jit(solution)/shard_map/ppermute | solution.py:26
  31.6 2.7 %collective-permute-done.7 = bf16[2048,128]{1,0:T(8,128)(2,1)} collective-permute-done((bf16[2048,128]{1,0:T(8,128)(2,1)S(1)}, bf16[2048,128]{1,0:T(8,128)(2,1)}, u32[]{:S(2)}, u32[]{:S(2)}) %collective-permute-start.7) | collective-permute-done | bytes 524320 | tf_op jit(solution)/shard_map/ppermute | solution.py:26
  35.5 1.4 %maximum_select_fusion = f32[2,2,72,1152]{3,2,1,0:T(8,128)S(1)} fusion(f32[2,1,72,1152]{3,2,1,0:T(8,128)} %bitcast.9, f32[2,1,72,1152]{3,2,1,0:T(8,128)S(1)} %maximum_select_fusion.1, pred[]{:T(512)S(6)} %eq.27), kind=kLoop, calls=%fused_computation.1 | loop fusion | flops 995328 | bytes 2654209 | tf_op jit(solution)/shard_map/jit(_where)/select_n | solution.py:151
  36.9 1.7 %collective-permute-done.5 = f32[32,1152]{1,0:T(8,128)S(1)} collective-permute-done((f32[32,1152]{1,0:T(8,128)S(1)}, f32[32,1152]{1,0:T(8,128)S(1)}, u32[]{:S(2)}, u32[]{:S(2)}) %collective-permute-start.5) | collective-permute-done | bytes 147488 | tf_op jit(solution)/shard_map/ppermute | solution.py:26
  41.2 4.4 %collective-permute-done.9 = bf16[32,288]{1,0:T(8,128)(2,1)S(1)} collective-permute-done((bf16[32,288]{1,0:T(8,128)(2,1)S(1)}, bf16[32,288]{1,0:T(8,128)(2,1)S(1)}, u32[]{:S(2)}, u32[]{:S(2)}) %collective-permute-start.9) | collective-permute-done | bytes 18464 | tf_op jit(solution)/shard_map/ppermute | solution.py:22
  46.3 3.2 %collective-permute-done.10 = bf16[32,288]{1,0:T(8,128)(2,1)S(1)} collective-permute-done((bf16[32,288]{1,0:T(8,128)(2,1)S(1)}, bf16[32,288]{1,0:T(8,128)(2,1)S(1)}, u32[]{:S(2)}, u32[]{:S(2)}) %collective-permute-start.10) | collective-permute-done | bytes 18464 | tf_op jit(solution)/shard_map/ppermute | solution.py:26
  49.6 2.1 %collective-permute-start.11 = (bf16[32,576]{1,0:T(8,128)(2,1)S(1)}, bf16[32,576]{1,0:T(8,128)(2,1)S(1)}, u32[]{:S(2)}, u32[]{:S(2)}) collective-permute-start(bf16[32,576]{1,0:T(8,128)(2,1)S(1)} %maximum_select_fusion.4), channel_id=1, source_target_pairs={{0,8},{1,9},{2,10},{3,11},{4,12},{5,13},{6,14},{7,15},{8,0},{9,1},... | collective-permute-start | bytes 110600 | tf_op jit(solution)/shard_map/ppermute | solution.py:26
  51.7 2.9 %collective-permute-done.11 = bf16[32,576]{1,0:T(8,128)(2,1)S(1)} collective-permute-done((bf16[32,576]{1,0:T(8,128)(2,1)S(1)}, bf16[32,576]{1,0:T(8,128)(2,1)S(1)}, u32[]{:S(2)}, u32[]{:S(2)}) %collective-permute-start.11) | collective-permute-done | bytes 36896 | tf_op jit(solution)/shard_map/ppermute | solution.py:26
  54.6 1.4 %pad_maximum_fusion = bf16[4,2048,128]{2,1,0:T(8,128)(2,1)S(1)} fusion(bf16[2,2048,128]{2,1,0:T(8,128)(2,1)} %collective-permute-done.8, bf16[2,2048,128]{2,1,0:T(8,128)(2,1)S(1)} %pad_maximum_fusion.1), kind=kLoop, calls=%fused_computation | loop fusion | flops 1048576 | bytes 4194304 | tf_op jit(solution)/shard_map/concatenate | solution.py:158
  56.2 2.1 %shard_map.60 = (f32[32,1152]{1,0:T(8,128)S(1)}, bf16[32,1152]{1,0:T(8,128)(2,1)S(1)}) custom-call(bf16[2048,128]{1,0:T(8,128)(2,1)S(1)} %bitcast.58, bf16[2048,128]{1,0:T(8,128)(2,1)S(1)} %bitcast.59, bf16[32,1152]{1,0:T(8,128)(2,1)S(1)} %maximum_select_fusion.3.precond_t), custom_call_target="tpu_custom_call" | custom-call | tf_op jit(solution)/shard_map/pallas_call | solution.py:175
  61.5 3.4 %collective-permute-done.14 = f32[64,128]{1,0:T(8,128)S(1)} collective-permute-done((f32[64,128]{1,0:T(8,128)S(1)}, f32[64,128]{1,0:T(8,128)S(1)}, u32[]{:S(2)}, u32[]{:S(2)}) %collective-permute-start.14) | collective-permute-done | bytes 32800 | tf_op jit(solution)/shard_map/ppermute | solution.py:26
  64.8 2.9 %collective-permute-start.15 = (f32[64,128]{1,0:T(8,128)S(1)}, f32[64,128]{1,0:T(8,128)S(1)}, u32[]{:S(2)}, u32[]{:S(2)}) collective-permute-start(f32[64,128]{1,0:T(8,128)S(1)} %add.74), channel_id=1, source_target_pairs={{0,8},{1,9},{2,10},{3,11},{4,12},{5,13},{6,14},{7,15},{8,0},{9,1},... | collective-permute-start | bytes 98312 | tf_op jit(solution)/shard_map/ppermute | solution.py:26
  68.2 1.8 %collective-permute-done.15 = f32[64,128]{1,0:T(8,128)S(1)} collective-permute-done((f32[64,128]{1,0:T(8,128)S(1)}, f32[64,128]{1,0:T(8,128)S(1)}, u32[]{:S(2)}, u32[]{:S(2)}) %collective-permute-start.15) | collective-permute-done | bytes 32800 | tf_op jit(solution)/shard_map/ppermute | solution.py:26
  70.3 3.9 %collective-permute-done.13 = bf16[32,1152]{1,0:T(8,128)(2,1)S(1)} collective-permute-done((bf16[32,1152]{1,0:T(8,128)(2,1)S(1)}, bf16[32,1152]{1,0:T(8,128)(2,1)S(1)}, u32[]{:S(2)}, u32[]{:S(2)}) %collective-permute-start.13) | collective-permute-done | bytes 73760 | tf_op jit(solution)/shard_map/ppermute | solution.py:26
  76.2 1.5 %collective-permute-start.16 = (f32[2,72,128]{2,1,0:T(8,128)S(1)}, f32[2,72,128]{2,1,0:T(8,128)S(1)}, u32[]{:S(2)}, u32[]{:S(2)}) collective-permute-start(f32[2,72,128]{2,1,0:T(8,128)S(1)} %dynamic-slice_bitcast_fusion), channel_id=1, source_target_pairs={{0,2},{1,3},{2,0},{3,1},{4,6},{5,7},{6,4},{7,5},{8,10},{9,11},{10,... | collective-permute-start | bytes 221192 | tf_op jit(solution)/shard_map/ppermute | solution.py:26
  77.7 1.9 %collective-permute-done.18 = f32[64,128]{1,0:T(8,128)S(1)} collective-permute-done((f32[64,128]{1,0:T(8,128)S(1)}, f32[64,128]{1,0:T(8,128)S(1)}, u32[]{:S(2)}, u32[]{:S(2)}) %collective-permute-start.18) | collective-permute-done | bytes 32800 | tf_op jit(solution)/shard_map/ppermute | solution.py:26
  (69 shorter events, 19.5 us)
Async XLA Ops:
  3.3 6.1 %copy-start.6 = (f32[1,72,1152]{2,1,0:T(8,128)S(1)}, f32[1,72,1152]{2,1,0:T(8,128)}, u32[]{:S(2)}) copy-start(f32[1,72,1152]{2,1,0:T(8,128)} %param.6) | copy-start | bytes 995332
  3.3 17.4 %copy-start.1 = (bf16[1,2,16,16,128]{4,3,2,1,0:T(8,128)(2,1)S(1)}, bf16[1,2,16,16,128]{4,3,2,1,0:T(8,128)(2,1)}, u32[]{:S(2)}) copy-start(bf16[1,2,16,16,128]{4,3,2,1,0:T(8,128)(2,1)} %param.4) | copy-start | bytes 393220
  3.3 17.4 %copy-start.3 = (bf16[1,2,16,16,128]{4,3,2,1,0:T(8,128)(2,1)S(1)}, bf16[1,2,16,16,128]{4,3,2,1,0:T(8,128)(2,1)}, u32[]{:S(2)}) copy-start(bf16[1,2,16,16,128]{4,3,2,1,0:T(8,128)(2,1)} %param.5) | copy-start | bytes 393220
  4.7 1.7 %collective-permute-start = (f32[2,32,1152]{2,1,0:T(8,128)S(1)}, f32[2,32,1152]{2,1,0:T(8,128)S(1)}, u32[]{:S(2)}, u32[]{:S(2)}) collective-permute-start(f32[2,32,1152]{2,1,0:T(8,128)S(1)} %get-tuple-element.16), channel_id=1, source_target_pairs={{0,1},{1,0},{2,3},{3,2},{4,5},{5,4},{6,7},{7,6},{8,9},{9,8},{10,11... | collective-permute-start | bytes 884744 | tf_op jit(solution)/shard_map/ppermute | solution.py:26
  6.4 7.6 %collective-permute-start.1 = (f32[32,1152]{1,0:T(8,128)S(1)}, f32[32,1152]{1,0:T(8,128)S(1)}, u32[]{:S(2)}, u32[]{:S(2)}) collective-permute-start(f32[32,1152]{1,0:T(8,128)S(1)} %slice_bitcast_fusion), channel_id=1, source_target_pairs={{0,2},{1,3},{2,0},{3,1},{4,6},{5,7},{6,4},{7,5},{8,10},{9,11},{10,... | collective-permute-start | bytes 442376 | tf_op jit(solution)/shard_map/ppermute | solution.py:26
  9.4 11.3 %collective-permute-start.2 = (f32[72,1152]{1,0:T(8,128)S(1)}, f32[72,1152]{1,0:T(8,128)S(1)}, u32[]{:S(2)}, u32[]{:S(2)}) collective-permute-start(f32[72,1152]{1,0:T(8,128)S(1)} %bitcast.73), channel_id=1, source_target_pairs={{0,2},{1,3},{2,0},{3,1},{4,6},{5,7},{6,4},{7,5},{8,10},{9,11},{10,... | collective-permute-start | bytes 995336 | tf_op jit(solution)/shard_map/ppermute | solution.py:26
  9.5 10.0 %collective-permute-start.3 = (bf16[1024,128]{1,0:T(8,128)(2,1)S(1)}, bf16[1024,128]{1,0:T(8,128)(2,1)S(1)}, u32[]{:S(2)}, u32[]{:S(2)}) collective-permute-start(bf16[1024,128]{1,0:T(8,128)(2,1)S(1)} %pad_maximum_fusion.4), channel_id=1, source_target_pairs={{16,0},{17,1},{18,2},{19,3},{20,4},{21,5},{22,6},{23,7},{24,8},{25... | collective-permute-start | bytes 786440 | tf_op jit(solution)/shard_map/ppermute | solution.py:22
  20.7 13.6 %collective-permute-start.7 = (bf16[2048,128]{1,0:T(8,128)(2,1)S(1)}, bf16[2048,128]{1,0:T(8,128)(2,1)}, u32[]{:S(2)}, u32[]{:S(2)}) collective-permute-start(bf16[2048,128]{1,0:T(8,128)(2,1)S(1)} %get-tuple-element.35), channel_id=1, source_target_pairs={{0,2},{1,3},{2,0},{3,1},{4,6},{5,7},{6,4},{7,5},{8,10},{9,11},{10,... | collective-permute-start | bytes 1572872 | tf_op jit(solution)/shard_map/ppermute | solution.py:26
  22.6 12.9 %collective-permute-start.6 = (f32[2,72,1152]{2,1,0:T(8,128)S(1)}, f32[2,72,1152]{2,1,0:T(8,128)}, u32[]{:S(2)}, u32[]{:S(2)}) collective-permute-start(f32[2,72,1152]{2,1,0:T(8,128)S(1)} %maximum_select_fusion.2), channel_id=1, source_target_pairs={{0,1},{1,0},{2,3},{3,2},{4,5},{5,4},{6,7},{7,6},{8,9},{9,8},{10,11... | collective-permute-start | bytes 1990664 | tf_op jit(solution)/shard_map/ppermute | solution.py:26
  22.7 6.3 %collective-permute-start.4 = (f32[32,1152]{1,0:T(8,128)S(1)}, f32[32,1152]{1,0:T(8,128)S(1)}, u32[]{:S(2)}, u32[]{:S(2)}) collective-permute-start(f32[32,1152]{1,0:T(8,128)S(1)} %fusion), channel_id=1, source_target_pairs={{0,4},{1,5},{2,6},{3,7},{4,0},{5,1},{6,2},{7,3},{8,12},{9,13},{10,... | collective-permute-start | bytes 442376 | tf_op jit(solution)/shard_map/ppermute | solution.py:26
  29.0 9.6 %collective-permute-start.5 = (f32[32,1152]{1,0:T(8,128)S(1)}, f32[32,1152]{1,0:T(8,128)S(1)}, u32[]{:S(2)}, u32[]{:S(2)}) collective-permute-start(f32[32,1152]{1,0:T(8,128)S(1)} %add.66), channel_id=1, source_target_pairs={{0,8},{1,9},{2,10},{3,11},{4,12},{5,13},{6,14},{7,15},{8,0},{9,1},... | collective-permute-start | bytes 442376 | tf_op jit(solution)/shard_map/ppermute | solution.py:26
  39.9 14.8 %collective-permute-start.8 = (bf16[2,2048,128]{2,1,0:T(8,128)(2,1)S(1)}, bf16[2,2048,128]{2,1,0:T(8,128)(2,1)}, u32[]{:S(2)}, u32[]{:S(2)}) collective-permute-start(bf16[2,2048,128]{2,1,0:T(8,128)(2,1)S(1)} %pad_maximum_fusion.1), channel_id=1, source_target_pairs={{0,1},{1,0},{2,3},{3,2},{4,5},{5,4},{6,7},{7,6},{8,9},{9,8},{10,11... | collective-permute-start | bytes 3145736 | tf_op jit(solution)/shard_map/ppermute | solution.py:26
  39.9 5.7 %collective-permute-start.9 = (bf16[32,288]{1,0:T(8,128)(2,1)S(1)}, bf16[32,288]{1,0:T(8,128)(2,1)S(1)}, u32[]{:S(2)}, u32[]{:S(2)}) collective-permute-start(bf16[32,288]{1,0:T(8,128)(2,1)S(1)} %get-tuple-element.38), channel_id=1, source_target_pairs={{16,0},{17,1},{18,2},{19,3},{20,4},{21,5},{22,6},{23,7},{24,8},{25... | collective-permute-start | bytes 55304 | tf_op jit(solution)/shard_map/ppermute | solution.py:22
  45.7 3.8 %collective-permute-start.10 = (bf16[32,288]{1,0:T(8,128)(2,1)S(1)}, bf16[32,288]{1,0:T(8,128)(2,1)S(1)}, u32[]{:S(2)}, u32[]{:S(2)}) collective-permute-start(bf16[32,288]{1,0:T(8,128)(2,1)S(1)} %collective-permute-done.9), channel_id=1, source_target_pairs={{0,4},{1,5},{2,6},{3,7},{4,0},{5,1},{6,2},{7,3},{8,12},{9,13},{10,... | collective-permute-start | bytes 55304 | tf_op jit(solution)/shard_map/ppermute | solution.py:26
  49.6 5.0 %collective-permute-start.11 = (bf16[32,576]{1,0:T(8,128)(2,1)S(1)}, bf16[32,576]{1,0:T(8,128)(2,1)S(1)}, u32[]{:S(2)}, u32[]{:S(2)}) collective-permute-start(bf16[32,576]{1,0:T(8,128)(2,1)S(1)} %maximum_select_fusion.4), channel_id=1, source_target_pairs={{0,8},{1,9},{2,10},{3,11},{4,12},{5,13},{6,14},{7,15},{8,0},{9,1},... | collective-permute-start | bytes 110600 | tf_op jit(solution)/shard_map/ppermute | solution.py:26
  58.3 6.5 %collective-permute-start.12 = (bf16[32,1152]{1,0:T(8,128)(2,1)S(1)}, bf16[32,1152]{1,0:T(8,128)(2,1)S(1)}, u32[]{:S(2)}, u32[]{:S(2)}) collective-permute-start(bf16[32,1152]{1,0:T(8,128)(2,1)S(1)} %get-tuple-element.21), channel_id=1, source_target_pairs={{0,4},{1,5},{2,6},{3,7},{4,0},{5,1},{6,2},{7,3},{8,12},{9,13},{10,... | collective-permute-start | bytes 221192 | tf_op jit(solution)/shard_map/ppermute | solution.py:26
  60.1 9.9 %copy-start.5 = (f32[1,128,128]{2,1,0:T(8,128)S(1)}, f32[1,128,128]{2,1,0:T(8,128)}, u32[]{:S(2)}) copy-start(f32[1,128,128]{2,1,0:T(8,128)} %param.7) | copy-start | bytes 196612
  60.5 4.3 %collective-permute-start.14 = (f32[64,128]{1,0:T(8,128)S(1)}, f32[64,128]{1,0:T(8,128)S(1)}, u32[]{:S(2)}, u32[]{:S(2)}) collective-permute-start(f32[64,128]{1,0:T(8,128)S(1)} %fusion.19), channel_id=1, source_target_pairs={{0,4},{1,5},{2,6},{3,7},{4,0},{5,1},{6,2},{7,3},{8,12},{9,13},{10,... | collective-permute-start | bytes 98312 | tf_op jit(solution)/shard_map/ppermute | solution.py:26
  64.8 5.2 %collective-permute-start.15 = (f32[64,128]{1,0:T(8,128)S(1)}, f32[64,128]{1,0:T(8,128)S(1)}, u32[]{:S(2)}, u32[]{:S(2)}) collective-permute-start(f32[64,128]{1,0:T(8,128)S(1)} %add.74), channel_id=1, source_target_pairs={{0,8},{1,9},{2,10},{3,11},{4,12},{5,13},{6,14},{7,15},{8,0},{9,1},... | collective-permute-start | bytes 98312 | tf_op jit(solution)/shard_map/ppermute | solution.py:26
  68.0 6.1 %collective-permute-start.13 = (bf16[32,1152]{1,0:T(8,128)(2,1)S(1)}, bf16[32,1152]{1,0:T(8,128)(2,1)S(1)}, u32[]{:S(2)}, u32[]{:S(2)}) collective-permute-start(bf16[32,1152]{1,0:T(8,128)(2,1)S(1)} %fusion.7), channel_id=1, source_target_pairs={{0,8},{1,9},{2,10},{3,11},{4,12},{5,13},{6,14},{7,15},{8,0},{9,1},... | collective-permute-start | bytes 221192 | tf_op jit(solution)/shard_map/ppermute | solution.py:26
  75.6 4.0 %collective-permute-start.18 = (f32[64,128]{1,0:T(8,128)S(1)}, f32[64,128]{1,0:T(8,128)S(1)}, u32[]{:S(2)}, u32[]{:S(2)}) collective-permute-start(f32[64,128]{1,0:T(8,128)S(1)} %broadcast_multiply_fusion), channel_id=1, source_target_pairs={{0,2},{1,3},{2,0},{3,1},{4,6},{5,7},{6,4},{7,5},{8,10},{9,11},{10,... | collective-permute-start | bytes 98312 | tf_op jit(solution)/shard_map/ppermute | solution.py:26
  76.2 4.4 %collective-permute-start.16 = (f32[2,72,128]{2,1,0:T(8,128)S(1)}, f32[2,72,128]{2,1,0:T(8,128)S(1)}, u32[]{:S(2)}, u32[]{:S(2)}) collective-permute-start(f32[2,72,128]{2,1,0:T(8,128)S(1)} %dynamic-slice_bitcast_fusion), channel_id=1, source_target_pairs={{0,2},{1,3},{2,0},{3,1},{4,6},{5,7},{6,4},{7,5},{8,10},{9,11},{10,... | collective-permute-start | bytes 221192 | tf_op jit(solution)/shard_map/ppermute | solution.py:26
  79.6 1.3 %collective-permute-start.19 = (f32[2,64,128]{2,1,0:T(8,128)S(1)}, f32[2,64,128]{2,1,0:T(8,128)S(1)}, u32[]{:S(2)}, u32[]{:S(2)}) collective-permute-start(f32[2,64,128]{2,1,0:T(8,128)S(1)} %get-tuple-element.37), channel_id=1, source_target_pairs={{0,1},{1,0},{2,3},{3,2},{4,5},{5,4},{6,7},{7,6},{8,9},{9,8},{10,11... | collective-permute-start | bytes 196616 | tf_op jit(solution)/shard_map/ppermute | solution.py:26
  80.6 1.3 %collective-permute-start.17 = (f32[72,128]{1,0:T(8,128)S(1)}, f32[72,128]{1,0:T(8,128)S(1)}, u32[]{:S(2)}, u32[]{:S(2)}) collective-permute-start(f32[72,128]{1,0:T(8,128)S(1)} %dynamic-slice_bitcast_fusion.1), channel_id=1, source_target_pairs={{0,1},{1,0},{2,3},{3,2},{4,5},{5,4},{6,7},{7,6},{8,9},{9,8},{10,11... | collective-permute-start | bytes 110600 | tf_op jit(solution)/shard_map/ppermute | solution.py:26
  (3 other events, 2.6 us)

commit v5 on v4

--- a/solution.py
+++ b/solution.py
@@ -16,10 +16,10 @@
     return lax.optimization_barrier((block, point))[0]
 
 
-def after(block):
-    devices = range(lax.axis_size("layer"))
-    route = [(i + 1, i) for i in devices if i + 1 in devices]
-    return lax.ppermute(block, "layer", route)
+def after(block, bit=0):
+    layers, group = lax.axis_size("layer"), lax.axis_size("pos")
+    route = [(((i + 1) % layers) * group + (p ^ bit), i * group + p) for i in range(layers) for p in range(group)]
+    return lax.ppermute(block, ("layer", "pos"), route)
 
 
 def swap(block, bit):
@@ -54,7 +54,15 @@
     return jnp.concatenate(moved, axis=0)
 
 
-def grad_kernel(side, maps, grads, g_inv, keep, send, all_rows):
+def grad_kernel(side, maps_in, grads_in, g_in, keep, send, all_rows, maps, grads, g_inv, sems):
+    copies = [
+        pltpu.make_async_copy(source, target, sems.at[i])
+        for i, (source, target) in enumerate([(g_in, g_inv), (grads_in, grads), (maps_in, maps)])
+    ]
+    for copy in copies:
+        copy.start()
+    for copy in copies:
+        copy.wait()
     width = maps.shape[1]
     g_t = g_inv[...]
     first = g_t.astype(BF16)
@@ -83,29 +91,43 @@
         (keep if j < 2 else send)[j % 2] = block
 
 
-def cross_kernel(side, maps, maps_next, precond_t, out, out_half):
+def cross_kernel(side, half_a, half_b, precond_t, gram, out, out_half):
     quarter = precond_t.shape[0]
-    width = maps.shape[1]
+    width = half_a.shape[3]
+    full = precond_t.shape[1]
     taps = jnp.concatenate([precond_t[:, t * width : (t + 1) * width] for t in range(9)], axis=0)
-    spread = dot_nt(taps, maps_next[...])
-    mapped = None
-    for s in range(3):
-        column = None
-        for r in range(3):
-            low = quarter * (3 * r + s)
-            part = shifted(spread[low : low + quarter], r - 1, 0, side)
-            column = part if column is None else column + part
-        column = shifted(column, 0, s - 1, side)
-        mapped = column if mapped is None else mapped + column
-    mapped = mapped.astype(BF16).astype(F32)
-    both = jnp.dot(taps_to_rows(mapped, side), maps[...], preferred_element_type=F32)
+    both = None
+    for half in (half_a, half_b):
+        for d in range(2):
+            spread = dot_nt(taps, half[d, 1])
+            mapped = None
+            for s in range(3):
+                column = None
+                for r in range(3):
+                    low = quarter * (3 * r + s)
+                    part = shifted(spread[low : low + quarter], r - 1, 0, side)
+                    column = part if column is None else column + part
+                column = shifted(column, 0, s - 1, side)
+                mapped = column if mapped is None else mapped + column
+            mapped = mapped.astype(BF16).astype(F32)
+            part = jnp.dot(taps_to_rows(mapped, side), half[d, 0], preferred_element_type=F32)
+            both = part if both is None else both + part
     for tap in range(9):
         part = both[quarter * tap : quarter * (tap + 1)]
         out[:, tap * width : (tap + 1) * width] = part
         out_half[:, tap * width : (tap + 1) * width] = part.astype(BF16)
+    for i in range(2):
+        part = gram[i * quarter : (i + 1) * quarter]
+        high = part.astype(BF16)
+        rest = (part - high.astype(F32)).astype(BF16)
+        low = full + i * width
+        out[:, low : low + width] = high.astype(F32) + rest.astype(F32)
+        out_half[:, low : low + width] = high
+        out_half[:, low + 2 * width : low + 3 * width] = rest
 
 
 VMEM = pl.BlockSpec(memory_space=pltpu.VMEM)
+ANY = pl.BlockSpec(memory_space=pl.ANY)
 PARAMS = pltpu.CompilerParams(vmem_limit_bytes=32 * 1024 * 1024)
 
 
@@ -131,69 +153,93 @@
     keep, send = pl.pallas_call(
         functools.partial(grad_kernel, side),
         out_shape=[jax.ShapeDtypeStruct((2, quarter, full), F32)] * 2,
-        in_specs=[VMEM] * 3,
+        in_specs=[ANY] * 3,
         out_specs=[VMEM] * 2,
-        scratch_shapes=[pltpu.VMEM((width, full), F32)],
+        scratch_shapes=[
+            pltpu.VMEM((width, full), F32),
+            pltpu.VMEM(flat_maps.shape, BF16),
+            pltpu.VMEM(flat_grads.shape, BF16),
+            pltpu.VMEM(g_inv.shape, F32),
+            pltpu.SemaphoreType.DMA((3,)),
+        ],
         compiler_params=PARAMS,
     )(flat_maps, flat_grads, g_inv)
-    own = jnp.concatenate([flat_grads, flat_maps], axis=0)
-    next_own = after(own)
-    k_x = swap(k_rows, 2)
     h = keep + swap(send, 1)
     h = h[0] + swap(h[1], 2)
-    h, k_x, next_own = lax.optimization_barrier((h, k_x, next_own))
-
+    h = h + swap(h, zbits[0])
+    for b in zbits[1:]:
+        h = h + swap(h, b)
+
+    k_x = swap(k_rows, 2)
     k_two = jnp.where(xbit == 0, jnp.stack([k_rows, k_x]), jnp.stack([k_x, k_rows]))
     k_c = swap(k_two, 1)
-    two_own = jnp.concatenate([own, next_own], axis=0)
-    pair = jnp.stack([two_own, swap(two_own, 2)])
-    h = h + swap(h, zbits[0])
-    k_z = jnp.where(core == 0, jnp.stack([k_two, k_c], 1), jnp.stack([k_c, k_two], 1)).reshape(4 * rows, full)
-    for b in zbits[1:]:
-        h = h + swap(h, b)
-
-    main_t = dot_nt(h * scale, k_z, precision=HIGH)
+
+    own = jnp.stack([flat_maps, flat_grads])
+    next_own = after(own)
+    two_own = jnp.stack([own[0], next_own[0], own[1], next_own[1]])
+    half_a = jnp.stack([two_own, swap(two_own, 2)])
+    half_b = swap(half_a, 1)
+
+    def k_times(k_part, e_t):
+        return dot_nt(e_t, k_part.reshape(2 * rows, full), precision=HIGH).reshape(-1, 2, rows)
+
+    h = h * scale
+    main_a = k_times(k_two, h)
+    main_b = k_times(k_c, h)
+    main_t = jnp.where(core == 0, jnp.stack([main_a, main_b], 2), jnp.stack([main_b, main_a], 2))
+    main_t = main_t.reshape(quarter, 4 * rows)
     p_t = main_t.astype(BF16)
-    pair = behind(pair, p_t)
-    four = jnp.concatenate([pair, swap(pair, 1)], axis=0).reshape(4, 4, -1, width)
-    grads_z, maps_z, next_grads_z, next_maps_z = (four[:, i].reshape(-1, width) for i in range(4))
-    p_t = after(p_t)
+
+    def by_bit(mine, other, b):
+        return jnp.where((me & b) == 0, jnp.concatenate([mine, other], 1), jnp.concatenate([other, mine], 1))
+
+    for b in zbits[:-1]:
+        p_t = by_bit(p_t, swap(p_t, b), b)
+    p_t = by_bit(after(p_t), after(p_t, zbits[-1]), zbits[-1])
+    last = lax.axis_index("layer") == lax.axis_size("layer") - 1
+    p_t = jnp.where(last, jnp.zeros_like(p_t), p_t)
 
     low = cols * quarter
-    both = jnp.concatenate(
-        [
-            lax.dynamic_slice_in_dim(grads_z, low, quarter, 1),
-            lax.dynamic_slice_in_dim(next_grads_z, low, quarter, 1),
-        ],
-        axis=1,
-    )
-    gram = dot_t(behind(both, p_t), grads_z)
-    for b in zbits:
-        other = swap(p_t, b)
-        p_t = jnp.where((me & b) == 0, jnp.concatenate([p_t, other], 1), jnp.concatenate([other, p_t], 1))
-
+    grads_a, grads_b = (half[:, 2].reshape(-1, width) for half in (half_a, half_b))
+    gram = 0.0
+    for half in (half_a, half_b):
+        here, following = (
+            lax.dynamic_slice_in_dim(half[:, i].reshape(-1, width), low, quarter, 1) for i in (2, 3)
+        )
+        following = jnp.where(last, jnp.zeros_like(following), following)
+        gram = gram + dot_t(jnp.concatenate([here, following], axis=1), half[:, 2].reshape(-1, width))
+
+    out_width = full + 2 * width
     cross_t, cross_half = pl.pallas_call(
         functools.partial(cross_kernel, side),
-        out_shape=[jax.ShapeDtypeStruct((quarter, full), F32), jax.ShapeDtypeStruct((quarter, full), BF16)],
-        in_specs=[VMEM] * 3,
+        out_shape=[
+            jax.ShapeDtypeStruct((quarter, out_width), F32),
+            jax.ShapeDtypeStruct((quarter, out_width + 2 * width), BF16),
+        ],
+        in_specs=[VMEM] * 4,
         out_specs=[VMEM] * 2,
         compiler_params=PARAMS,
-    )(maps_z, next_maps_z, p_t)
-
-    gram = behind(gram, cross_half)
-    main_t = behind(main_t, cross_half)
+    )(half_a, half_b, p_t, gram)
+
     place = (jnp.arange(width)[None, :] == low + jnp.arange(quarter)[:, None]).astype(F32)
     main = dot_t(main_t, place, precision=HIGH)
+    cross_t, gram = cross_t[:, :full], cross_t[:, full:]
     for b in zbits:
-        gram = gram + swap(gram, b)
-        cross_t = cross_t + swap(cross_half, b).astype(F32)
-        cross_half = cross_t.astype(BF16)
-        gram = behind(gram, cross_half)
+        other = swap(cross_half, b).astype(F32)
+        cross_t = cross_t + other[:, :full]
+        gram = gram + (other[:, full:out_width] + other[:, out_width:])
+        high = lax.reduce_precision(gram, 8, 7)
+        rest = lax.reduce_precision(gram - high, 8, 7)
+        gram = high + rest
+        cross_half = jnp.concatenate([cross_t, high, rest], axis=1).astype(BF16)
     gram = gram * scale
-    h_mine = jnp.dot(gram[quarter:], g_inv, precision=HIGH) * scale
-
-    fix = jnp.dot(dot_nt(k_z, cross_t, precision=HIGH), h_mine, precision=HIGH)
-    out = (main - fix).reshape(2, 2, rows, width)
+    h_mine = jnp.dot(gram[:, width:], g_inv, precision=HIGH) * scale
+
+    fix_a = dot_nt(k_two.reshape(2 * rows, full), cross_t, precision=HIGH).reshape(2, 1, rows, quarter)
+    fix_b = dot_nt(k_c.reshape(2 * rows, full), cross_t, precision=HIGH).reshape(2, 1, rows, quarter)
+    fix = jnp.where(core == 0, jnp.concatenate([fix_a, fix_b], 1), jnp.concatenate([fix_b, fix_a], 1))
+    out = main - jnp.dot(fix.reshape(4 * rows, quarter), h_mine, precision=HIGH)
+    out = out.reshape(2, 2, rows, width)
     gram = behind(gram, out)
     gram = jnp.stack([gram, swap(gram, 2)])
     keep = lax.dynamic_index_in_dim(out, xbit, 0, False)
@@ -205,7 +251,7 @@
     update = keep + swap(send, 1)
     gram = jnp.where(xbit == 0, gram, gram[:, ::-1])
     gram = jnp.where(core == 0, gram, gram[::-1])
-    gram = gram.reshape(4, 2, quarter, width).transpose(1, 3, 0, 2).reshape(2, width, width)
+    gram = gram.reshape(width, 2, width).transpose(1, 2, 0)
     return (update[None], gram[None])
 
 

time: 82.9 us -> 88.8 us (1.071)
  matrix products: 3.49 us -> 8.83 us
  waiting for transfers between devices: 42.6 us -> 46.1 us
  starting transfers between devices: 22.5 us -> 20.9 us
  local copies, waits for them, and re-layouts: 3.96 us -> 2.48 us
    ppermute x18 -> x15, waiting for transfers between devices: 32.8 us -> 40.6 us  [swap(): lax.ppermute(block, 'pos', [(i, i ^ bit) for i in range(lax.axis_size('po...]
    ppermute x18 -> x15, starting transfers between devices: 20 us -> 14.3 us  [swap(): lax.ppermute(block, 'pos', [(i, i ^ bit) for i in range(lax.axis_size('po...]
    dot_general x2 -> x4, matrix products: 2.43 us -> 7.28 us  [dot_nt(): lax.dot_general(a, b, (((1,), (1,)), ((), ())), preferred_element_type=F3...]
    ppermute x2 -> x3, waiting for transfers between devices: 9.84 us -> 5.53 us  [after(): return lax.ppermute(block, ('layer', 'pos'), route)]
    ppermute x2 -> x3, starting transfers between devices: 2.58 us -> 6.59 us  [after(): return lax.ppermute(block, ('layer', 'pos'), route)]
    unnamed x15 -> x18, local copies, waits for them, and re-layouts: 3.41 us -> 0.96 us
    concatenate x3 -> x1, other arithmetic: 1.72 us -> 0.01 us  [per_device(): cross_half = jnp.concatenate([cross_t, high, rest], axis=1).astype(BF16)]
    select_n x3 -> x6, other arithmetic: 1.61 us -> 0.48 us  [the longest x2 0.28 us: per_device(): following = jnp.where(last, jnp.zeros_like(following), following)]
  transfers between devices with their start and end apart: 20 -> 18, of which waited for: 17 -> 13; matrix products, arithmetic and copies ran while one was open for 6% -> 11% of each run, Pallas kernels for 0% -> 2%
where the time goes in v5:
time: 88.8 us; the launch traced here: 88.5 us
  waiting for transfers between devices  46.1 us (52%)
  starting transfers between devices  20.9 us (24%)
  matrix products  8.83 us (10%)
  other arithmetic  5.6 us (6%)
  Pallas kernels  3.5 us (4%)
  local copies, waits for them, and re-layouts  2.48 us (3%)
  between operations  1.05 us (1%)
    ppermute x15, waiting for transfers between devices, swap(): lax.ppermute(block, 'pos', [(i, i ^ bit) for i in range(lax.axis_size('po...  40.6 us
    ppermute x15, starting transfers between devices, swap(): lax.ppermute(block, 'pos', [(i, i ^ bit) for i in range(lax.axis_size('po...  14.3 us
    dot_general x4, matrix products, dot_nt(): lax.dot_general(a, b, (((1,), (1,)), ((), ())), preferred_element_type=F3...  7.28 us
    ppermute x3, starting transfers between devices, after(): return lax.ppermute(block, ('layer', 'pos'), route)  6.59 us
    ppermute x3, waiting for transfers between devices, after(): return lax.ppermute(block, ('layer', 'pos'), route)  5.53 us
    pallas_call x1, Pallas kernels, per_device(): pl.pallas_call(functools.partial(grad_kernel, side), out_shape=[jax.Shape...  1.81 us
  transfers between devices with their start and end apart: 18, of which 13 were waited for; matrix products, arithmetic and copies ran while one was open for 11% of the time, Pallas kernels for 2%

profile of v5, /device:TPU:0, one launch (start us, length us, event | category | flops | bytes accessed | tf_op | source)
XLA Modules:
  0.0 88.5 jit_solution(6259652345621315222)
XLA Ops:
  1.7 3.0 %collective-permute-start.6 = (bf16[2,512,128]{2,1,0:T(8,128)(2,1)S(1)}, bf16[2,512,128]{2,1,0:T(8,128)(2,1)S(1)}, u32[]{:S(2)}, u32[]{:S(2)}) collective-permute-start(bf16[2,512,128]{2,1,0:T(8,128)(2,1)S(1)} %pad_maximum_fusion.2), channel_id=1, source_target_pairs={{16,0},{17,1},{18,2},{19,3},{20,4},{21,5},{22,6},{23,7},{24,8},{25... | collective-permute-start | bytes 786440 | tf_op jit(solution)/shard_map/ppermute | solution.py:22
  4.8 1.8 %shard_map.59 = (f32[2,32,1152]{2,1,0:T(8,128)S(1)}, f32[2,32,1152]{2,1,0:T(8,128)S(1)}) custom-call(bf16[512,128]{1,0:T(8,128)(2,1)S(1)} %bitcast.74, bf16[512,128]{1,0:T(8,128)(2,1)S(1)} %bitcast.77, f32[128,128]{1,0:T(8,128)S(1)} %bitcast.79), custom_call_target="tpu_custom_call" | custom-call | tf_op jit(solution)/shard_map/pallas_call | solution.py:153
  6.7 1.6 %collective-permute-start.4 = (f32[72,1152]{1,0:T(8,128)S(1)}, f32[72,1152]{1,0:T(8,128)}, u32[]{:S(2)}, u32[]{:S(2)}) collective-permute-start(f32[72,1152]{1,0:T(8,128)S(1)} %bitcast.90), channel_id=1, source_target_pairs={{0,2},{1,3},{2,0},{3,1},{4,6},{5,7},{6,4},{7,5},{8,10},{9,11},{10,... | collective-permute-start | bytes 995336 | tf_op jit(solution)/shard_map/ppermute | solution.py:26
  8.2 2.8 %collective-permute-done.6 = bf16[2,512,128]{2,1,0:T(8,128)(2,1)S(1)} collective-permute-done((bf16[2,512,128]{2,1,0:T(8,128)(2,1)S(1)}, bf16[2,512,128]{2,1,0:T(8,128)(2,1)S(1)}, u32[]{:S(2)}, u32[]{:S(2)}) %collective-permute-start.6) | collective-permute-done | bytes 262176 | tf_op jit(solution)/shard_map/ppermute | solution.py:22
  11.2 1.8 %collective-permute-start.7 = (bf16[4,512,128]{2,1,0:T(8,128)(2,1)S(1)}, bf16[4,512,128]{2,1,0:T(8,128)(2,1)S(1)}, u32[]{:S(2)}, u32[]{:S(2)}) collective-permute-start(bf16[4,512,128]{2,1,0:T(8,128)(2,1)S(1)} %get-tuple-element.19), channel_id=1, source_target_pairs={{0,2},{1,3},{2,0},{3,1},{4,6},{5,7},{6,4},{7,5},{8,10},{9,11},{10,... | collective-permute-start | bytes 1572872 | tf_op jit(solution)/shard_map/ppermute | solution.py:26
  14.4 3.0 %collective-permute-done.4 = f32[72,1152]{1,0:T(8,128)} collective-permute-done((f32[72,1152]{1,0:T(8,128)S(1)}, f32[72,1152]{1,0:T(8,128)}, u32[]{:S(2)}, u32[]{:S(2)}) %collective-permute-start.4) | collective-permute-done | bytes 331808 | tf_op jit(solution)/shard_map/ppermute | solution.py:26
  18.7 12.6 %collective-permute-done.1 = f32[32,1152]{1,0:T(8,128)S(1)} collective-permute-done((f32[32,1152]{1,0:T(8,128)S(1)}, f32[32,1152]{1,0:T(8,128)S(1)}, u32[]{:S(2)}, u32[]{:S(2)}) %collective-permute-start.1) | collective-permute-done | bytes 147488 | tf_op jit(solution)/shard_map/ppermute | solution.py:26
  31.3 1.7 %collective-permute-start.2 = (f32[32,1152]{1,0:T(8,128)S(1)}, f32[32,1152]{1,0:T(8,128)S(1)}, u32[]{:S(2)}, u32[]{:S(2)}) collective-permute-start(f32[32,1152]{1,0:T(8,128)S(1)} %fusion.14), channel_id=1, source_target_pairs={{0,4},{1,5},{2,6},{3,7},{4,0},{5,1},{6,2},{7,3},{8,12},{9,13},{10,... | collective-permute-start | bytes 442376 | tf_op jit(solution)/shard_map/ppermute | solution.py:26
  33.0 3.8 %collective-permute-done.2 = f32[32,1152]{1,0:T(8,128)S(1)} collective-permute-done((f32[32,1152]{1,0:T(8,128)S(1)}, f32[32,1152]{1,0:T(8,128)S(1)}, u32[]{:S(2)}, u32[]{:S(2)}) %collective-permute-start.2) | collective-permute-done | bytes 147488 | tf_op jit(solution)/shard_map/ppermute | solution.py:26
  36.8 2.7 %collective-permute-start.3 = (f32[32,1152]{1,0:T(8,128)S(1)}, f32[32,1152]{1,0:T(8,128)}, u32[]{:S(2)}, u32[]{:S(2)}) collective-permute-start(f32[32,1152]{1,0:T(8,128)S(1)} %add.83), channel_id=1, source_target_pairs={{0,8},{1,9},{2,10},{3,11},{4,12},{5,13},{6,14},{7,15},{8,0},{9,1},... | collective-permute-start | bytes 442376 | tf_op jit(solution)/shard_map/ppermute | solution.py:26
  40.5 5.1 %collective-permute-done.3 = f32[32,1152]{1,0:T(8,128)} collective-permute-done((f32[32,1152]{1,0:T(8,128)S(1)}, f32[32,1152]{1,0:T(8,128)}, u32[]{:S(2)}, u32[]{:S(2)}) %collective-permute-start.3) | collective-permute-done | bytes 147488 | tf_op jit(solution)/shard_map/ppermute | solution.py:26
  45.5 1.9 %convolution_bitcast_fusion.3 = f32[32,2,1,72]{3,0,1,2:T(8,128)S(1)} fusion(f32[2,72,1152]{2,1,0:T(8,128)S(1)} %maximum_select_fusion, f32[32,1152]{1,0:T(8,128)S(1)} %add.83, f32[32,1152]{1,0:T(8,128)} %collective-permute-done.3), kind=kOutput, calls=%fused_computation.9 | convolution fusion | flops 63774720 | bytes 976896 | tf_op jit(solution)/shard_map/dot_general | solution.py:34
  48.3 2.2 %convolution_bitcast_fusion.2 = f32[32,2,1,72]{3,0,1,2:T(8,128)S(1)} fusion(f32[2,72,1152]{2,1,0:T(8,128)} %collective-permute-done.5, f32[32,1152]{1,0:T(8,128)S(1)} %add.83, f32[32,1152]{1,0:T(8,128)} %collective-permute-done.3), kind=kOutput, calls=%fused_computation.8 | convolution fusion | flops 63774720 | bytes 976896 | tf_op jit(solution)/shard_map/dot_general | solution.py:34
  51.6 3.0 %collective-permute-done.9 = bf16[32,288]{1,0:T(8,128)(2,1)S(1)} collective-permute-done((bf16[32,288]{1,0:T(8,128)(2,1)S(1)}, bf16[32,288]{1,0:T(8,128)(2,1)S(1)}, u32[]{:S(2)}, u32[]{:S(2)}) %collective-permute-start.9) | collective-permute-done | bytes 18464 | tf_op jit(solution)/shard_map/ppermute | solution.py:26
  55.3 3.0 %collective-permute-start.11 = (bf16[32,576]{1,0:T(8,128)(2,1)S(1)}, bf16[32,576]{1,0:T(8,128)(2,1)S(1)}, u32[]{:S(2)}, u32[]{:S(2)}) collective-permute-start(bf16[32,576]{1,0:T(8,128)(2,1)S(1)} %maximum_select_fusion.4), channel_id=1, source_target_pairs={{24,0},{25,1},{26,2},{27,3},{28,4},{29,5},{30,6},{31,7},{16,8},{17... | collective-permute-start | bytes 110600 | tf_op jit(solution)/shard_map/ppermute | solution.py:22
  58.8 2.3 %collective-permute-done.11 = bf16[32,576]{1,0:T(8,128)(2,1)S(1)} collective-permute-done((bf16[32,576]{1,0:T(8,128)(2,1)S(1)}, bf16[32,576]{1,0:T(8,128)(2,1)S(1)}, u32[]{:S(2)}, u32[]{:S(2)}) %collective-permute-start.11) | collective-permute-done | bytes 36896 | tf_op jit(solution)/shard_map/ppermute | solution.py:22
  62.3 1.7 %shard_map.60 = (f32[32,1408]{1,0:T(8,128)S(1)}, bf16[32,1664]{1,0:T(8,128)(2,1)S(1)}) custom-call(bf16[2,4,512,128]{3,2,1,0:T(8,128)(2,1)S(1)} %pad_maximum_fusion.half_a, bf16[2,4,512,128]{3,2,1,0:T(8,128)(2,1)S(1)} %collective-permute-done.8.half_b, bf16[32,1152]{1,0:T(8,128)(2,1)S(1)} %fusion.17.precond_t, f32[64,128]{1,0:T(8,128)S(1)} %fusion.4.gram), custom_call_target="tpu_custom_call" | custom-call | tf_op jit(solution)/shard_map/pallas_call | solution.py:213
  65.2 4.7 %collective-permute-done.12 = bf16[32,1664]{1,0:T(8,128)(2,1)S(1)} collective-permute-done((bf16[32,1664]{1,0:T(8,128)(2,1)S(1)}, bf16[32,1664]{1,0:T(8,128)(2,1)S(1)}, u32[]{:S(2)}, u32[]{:S(2)}) %collective-permute-start.12) | collective-permute-done | bytes 106528 | tf_op jit(solution)/shard_map/ppermute | solution.py:26
  70.0 2.0 %collective-permute-start.13 = (bf16[32,1664]{1,0:T(8,128)(2,1)S(1)}, bf16[32,1664]{1,0:T(8,128)(2,1)S(1)}, u32[]{:S(2)}, u32[]{:S(2)}) collective-permute-start(bf16[32,1664]{1,0:T(8,128)(2,1)S(1)} %pad_maximum_fusion.4), channel_id=1, source_target_pairs={{0,8},{1,9},{2,10},{3,11},{4,12},{5,13},{6,14},{7,15},{8,0},{9,1},... | collective-permute-start | bytes 319496 | tf_op jit(solution)/shard_map/ppermute | solution.py:26
  72.3 4.4 %collective-permute-done.13 = bf16[32,1664]{1,0:T(8,128)(2,1)S(1)} collective-permute-done((bf16[32,1664]{1,0:T(8,128)(2,1)S(1)}, bf16[32,1664]{1,0:T(8,128)(2,1)S(1)}, u32[]{:S(2)}, u32[]{:S(2)}) %collective-permute-start.13) | collective-permute-done | bytes 106528 | tf_op jit(solution)/shard_map/ppermute | solution.py:26
  77.9 2.1 %convolution_bitcast_fusion = f32[2,1,72,32]{2,3,0,1:T(8,128)S(1)} fusion(f32[2,72,1152]{2,1,0:T(8,128)} %collective-permute-done.5, f32[32,1664]{1,0:T(8,128)S(1)} %convert_element_type.13, f32[32,1664]{1,0:T(8,128)S(1)} %convert_element_type.12, f32[32,1408]{1,0:T(8,128)S(1)} %get-tuple-element.9), kind=kOutput, calls=%fused_computation.6 | convolution fusion | flops 63774720 | bytes 1124352 | tf_op jit(solution)/shard_map/dot_general | solution.py:34
  80.6 1.6 %collective-permute-start.16 = (f32[32,256]{1,0:T(8,128)S(1)}, f32[32,256]{1,0:T(8,128)S(1)}, u32[]{:S(2)}, u32[]{:S(2)}) collective-permute-start(f32[32,256]{1,0:T(8,128)S(1)} %fusion.24), channel_id=1, source_target_pairs={{0,2},{1,3},{2,0},{3,1},{4,6},{5,7},{6,4},{7,5},{8,10},{9,11},{10,... | collective-permute-start | bytes 98312 | tf_op jit(solution)/shard_map/ppermute | solution.py:26
  82.7 1.9 %collective-permute-done.16 = f32[32,256]{1,0:T(8,128)S(1)} collective-permute-done((f32[32,256]{1,0:T(8,128)S(1)}, f32[32,256]{1,0:T(8,128)S(1)}, u32[]{:S(2)}, u32[]{:S(2)}) %collective-permute-start.16) | collective-permute-done | bytes 32800 | tf_op jit(solution)/shard_map/ppermute | solution.py:26
  84.7 1.8 %collective-permute-done.14 = f32[2,72,128]{2,1,0:T(8,128)S(1)} collective-permute-done((f32[2,72,128]{2,1,0:T(8,128)S(1)}, f32[2,72,128]{2,1,0:T(8,128)S(1)}, u32[]{:S(2)}, u32[]{:S(2)}) %collective-permute-start.14) | collective-permute-done | bytes 73760 | tf_op jit(solution)/shard_map/ppermute | solution.py:26
  (83 shorter events, 15.0 us)
Async XLA Ops:
  0.6 4.1 %copy-start = (bf16[1,2,16,16,128]{4,3,2,1,0:T(8,128)(2,1)S(1)}, bf16[1,2,16,16,128]{4,3,2,1,0:T(8,128)(2,1)}, u32[]{:S(2)}) copy-start(bf16[1,2,16,16,128]{4,3,2,1,0:T(8,128)(2,1)} %param.4) | copy-start | bytes 393220
  0.6 4.1 %copy-start.1 = (bf16[1,2,16,16,128]{4,3,2,1,0:T(8,128)(2,1)S(1)}, bf16[1,2,16,16,128]{4,3,2,1,0:T(8,128)(2,1)}, u32[]{:S(2)}) copy-start(bf16[1,2,16,16,128]{4,3,2,1,0:T(8,128)(2,1)} %param.5) | copy-start | bytes 393220
  0.7 6.0 %copy-start.7 = (f32[1,72,1152]{2,1,0:T(8,128)S(1)}, f32[1,72,1152]{2,1,0:T(8,128)}, u32[]{:S(2)}) copy-start(f32[1,72,1152]{2,1,0:T(8,128)} %param.6) | copy-start | bytes 995332
  1.7 9.3 %collective-permute-start.6 = (bf16[2,512,128]{2,1,0:T(8,128)(2,1)S(1)}, bf16[2,512,128]{2,1,0:T(8,128)(2,1)S(1)}, u32[]{:S(2)}, u32[]{:S(2)}) collective-permute-start(bf16[2,512,128]{2,1,0:T(8,128)(2,1)S(1)} %pad_maximum_fusion.2), channel_id=1, source_target_pairs={{16,0},{17,1},{18,2},{19,3},{20,4},{21,5},{22,6},{23,7},{24,8},{25... | collective-permute-start | bytes 786440 | tf_op jit(solution)/shard_map/ppermute | solution.py:22
  6.6 6.4 %collective-permute-start = (f32[2,32,1152]{2,1,0:T(8,128)S(1)}, f32[2,32,1152]{2,1,0:T(8,128)}, u32[]{:S(2)}, u32[]{:S(2)}) collective-permute-start(f32[2,32,1152]{2,1,0:T(8,128)S(1)} %get-tuple-element.8), channel_id=1, source_target_pairs={{0,1},{1,0},{2,3},{3,2},{4,5},{5,4},{6,7},{7,6},{8,9},{9,8},{10,11... | collective-permute-start | bytes 884744 | tf_op jit(solution)/shard_map/ppermute | solution.py:26
  6.7 10.8 %collective-permute-start.4 = (f32[72,1152]{1,0:T(8,128)S(1)}, f32[72,1152]{1,0:T(8,128)}, u32[]{:S(2)}, u32[]{:S(2)}) collective-permute-start(f32[72,1152]{1,0:T(8,128)S(1)} %bitcast.90), channel_id=1, source_target_pairs={{0,2},{1,3},{2,0},{3,1},{4,6},{5,7},{6,4},{7,5},{8,10},{9,11},{10,... | collective-permute-start | bytes 995336 | tf_op jit(solution)/shard_map/ppermute | solution.py:26
  11.2 28.3 %collective-permute-start.7 = (bf16[4,512,128]{2,1,0:T(8,128)(2,1)S(1)}, bf16[4,512,128]{2,1,0:T(8,128)(2,1)S(1)}, u32[]{:S(2)}, u32[]{:S(2)}) collective-permute-start(bf16[4,512,128]{2,1,0:T(8,128)(2,1)S(1)} %get-tuple-element.19), channel_id=1, source_target_pairs={{0,2},{1,3},{2,0},{3,1},{4,6},{5,7},{6,4},{7,5},{8,10},{9,11},{10,... | collective-permute-start | bytes 1572872 | tf_op jit(solution)/shard_map/ppermute | solution.py:26
  13.0 4.5 %copy-start.8 = (f32[1,72,1152]{2,1,0:T(8,128)S(1)}, f32[1,72,1152]{2,1,0:T(8,128)}, u32[]{:S(2)}) copy-start(f32[1,72,1152]{2,1,0:T(8,128)} %param.6) | copy-start | bytes 995332
  14.0 17.2 %collective-permute-start.1 = (f32[32,1152]{1,0:T(8,128)S(1)}, f32[32,1152]{1,0:T(8,128)S(1)}, u32[]{:S(2)}, u32[]{:S(2)}) collective-permute-start(f32[32,1152]{1,0:T(8,128)S(1)} %slice_bitcast_fusion), channel_id=1, source_target_pairs={{0,2},{1,3},{2,0},{3,1},{4,6},{5,7},{6,4},{7,5},{8,10},{9,11},{10,... | collective-permute-start | bytes 442376 | tf_op jit(solution)/shard_map/ppermute | solution.py:26
  18.6 29.7 %collective-permute-start.5 = (f32[2,72,1152]{2,1,0:T(8,128)S(1)}, f32[2,72,1152]{2,1,0:T(8,128)}, u32[]{:S(2)}, u32[]{:S(2)}) collective-permute-start(f32[2,72,1152]{2,1,0:T(8,128)S(1)} %maximum_select_fusion), channel_id=1, source_target_pairs={{0,1},{1,0},{2,3},{3,2},{4,5},{5,4},{6,7},{7,6},{8,9},{9,8},{10,11... | collective-permute-start | bytes 1990664 | tf_op jit(solution)/shard_map/ppermute | solution.py:26
  31.3 5.5 %collective-permute-start.2 = (f32[32,1152]{1,0:T(8,128)S(1)}, f32[32,1152]{1,0:T(8,128)S(1)}, u32[]{:S(2)}, u32[]{:S(2)}) collective-permute-start(f32[32,1152]{1,0:T(8,128)S(1)} %fusion.14), channel_id=1, source_target_pairs={{0,4},{1,5},{2,6},{3,7},{4,0},{5,1},{6,2},{7,3},{8,12},{9,13},{10,... | collective-permute-start | bytes 442376 | tf_op jit(solution)/shard_map/ppermute | solution.py:26
  36.8 8.7 %collective-permute-start.3 = (f32[32,1152]{1,0:T(8,128)S(1)}, f32[32,1152]{1,0:T(8,128)}, u32[]{:S(2)}, u32[]{:S(2)}) collective-permute-start(f32[32,1152]{1,0:T(8,128)S(1)} %add.83), channel_id=1, source_target_pairs={{0,8},{1,9},{2,10},{3,11},{4,12},{5,13},{6,14},{7,15},{8,0},{9,1},... | collective-permute-start | bytes 442376 | tf_op jit(solution)/shard_map/ppermute | solution.py:26
  40.4 7.1 %copy-start.5 = (bf16[4,512,128]{2,1,0:T(8,128)(2,1)S(1)}, bf16[4,512,128]{2,1,0:T(8,128)(2,1)}, u32[]{:S(2)}) copy-start(bf16[4,512,128]{2,1,0:T(8,128)(2,1)} %copy-done.4) | copy-start | bytes 1572868
  40.4 20.9 %collective-permute-start.8 = (bf16[2,4,512,128]{3,2,1,0:T(8,128)(2,1)S(1)}, bf16[2,4,512,128]{3,2,1,0:T(8,128)(2,1)S(1)}, u32[]{:S(2)}, u32[]{:S(2)}) collective-permute-start(bf16[2,4,512,128]{3,2,1,0:T(8,128)(2,1)S(1)} %pad_maximum_fusion.half_a), channel_id=1, source_target_pairs={{0,1},{1,0},{2,3},{3,2},{4,5},{5,4},{6,7},{7,6},{8,9},{9,8},{10,11... | collective-permute-start | bytes 3145736 | tf_op jit(solution)/shard_map/ppermute | solution.py:26
  50.8 3.9 %collective-permute-start.9 = (bf16[32,288]{1,0:T(8,128)(2,1)S(1)}, bf16[32,288]{1,0:T(8,128)(2,1)S(1)}, u32[]{:S(2)}, u32[]{:S(2)}) collective-permute-start(bf16[32,288]{1,0:T(8,128)(2,1)S(1)} %convert_element_type.11), channel_id=1, source_target_pairs={{0,4},{1,5},{2,6},{3,7},{4,0},{5,1},{6,2},{7,3},{8,12},{9,13},{10,... | collective-permute-start | bytes 55304 | tf_op jit(solution)/shard_map/ppermute | solution.py:26
  51.5 6.8 %copy-start.6 = (bf16[2,1,512,128]{3,2,1,0:T(8,128)(2,1)S(1)}, bf16[2,1,512,128]{3,2,1,0:T(8,128)(2,1)}, u32[]{:S(2)}) copy-start(bf16[2,1,512,128]{3,2,1,0:T(8,128)(2,1)} %get-tuple-element.14) | copy-start | bytes 786436
  54.7 4.1 %collective-permute-start.10 = (bf16[32,576]{1,0:T(8,128)(2,1)S(1)}, bf16[32,576]{1,0:T(8,128)(2,1)S(1)}, u32[]{:S(2)}, u32[]{:S(2)}) collective-permute-start(bf16[32,576]{1,0:T(8,128)(2,1)S(1)} %maximum_select_fusion.4), channel_id=1, source_target_pairs={{16,0},{17,1},{18,2},{19,3},{20,4},{21,5},{22,6},{23,7},{24,8},{25... | collective-permute-start | bytes 110600 | tf_op jit(solution)/shard_map/ppermute | solution.py:22
  55.3 5.8 %collective-permute-start.11 = (bf16[32,576]{1,0:T(8,128)(2,1)S(1)}, bf16[32,576]{1,0:T(8,128)(2,1)S(1)}, u32[]{:S(2)}, u32[]{:S(2)}) collective-permute-start(bf16[32,576]{1,0:T(8,128)(2,1)S(1)} %maximum_select_fusion.4), channel_id=1, source_target_pairs={{24,0},{25,1},{26,2},{27,3},{28,4},{29,5},{30,6},{31,7},{16,8},{17... | collective-permute-start | bytes 110600 | tf_op jit(solution)/shard_map/ppermute | solution.py:22
  63.9 5.9 %collective-permute-start.12 = (bf16[32,1664]{1,0:T(8,128)(2,1)S(1)}, bf16[32,1664]{1,0:T(8,128)(2,1)S(1)}, u32[]{:S(2)}, u32[]{:S(2)}) collective-permute-start(bf16[32,1664]{1,0:T(8,128)(2,1)S(1)} %get-tuple-element.10), channel_id=1, source_target_pairs={{0,4},{1,5},{2,6},{3,7},{4,0},{5,1},{6,2},{7,3},{8,12},{9,13},{10,... | collective-permute-start | bytes 319496 | tf_op jit(solution)/shard_map/ppermute | solution.py:26
  70.0 6.7 %collective-permute-start.13 = (bf16[32,1664]{1,0:T(8,128)(2,1)S(1)}, bf16[32,1664]{1,0:T(8,128)(2,1)S(1)}, u32[]{:S(2)}, u32[]{:S(2)}) collective-permute-start(bf16[32,1664]{1,0:T(8,128)(2,1)S(1)} %pad_maximum_fusion.4), channel_id=1, source_target_pairs={{0,8},{1,9},{2,10},{3,11},{4,12},{5,13},{6,14},{7,15},{8,0},{9,1},... | collective-permute-start | bytes 319496 | tf_op jit(solution)/shard_map/ppermute | solution.py:26
  80.6 4.0 %collective-permute-start.16 = (f32[32,256]{1,0:T(8,128)S(1)}, f32[32,256]{1,0:T(8,128)S(1)}, u32[]{:S(2)}, u32[]{:S(2)}) collective-permute-start(f32[32,256]{1,0:T(8,128)S(1)} %fusion.24), channel_id=1, source_target_pairs={{0,2},{1,3},{2,0},{3,1},{4,6},{5,7},{6,4},{7,5},{8,10},{9,11},{10,... | collective-permute-start | bytes 98312 | tf_op jit(solution)/shard_map/ppermute | solution.py:26
  82.2 4.4 %collective-permute-start.14 = (f32[2,72,128]{2,1,0:T(8,128)S(1)}, f32[2,72,128]{2,1,0:T(8,128)S(1)}, u32[]{:S(2)}, u32[]{:S(2)}) collective-permute-start(f32[2,72,128]{2,1,0:T(8,128)S(1)} %dynamic-slice_bitcast_fusion), channel_id=1, source_target_pairs={{0,2},{1,3},{2,0},{3,1},{4,6},{5,7},{6,4},{7,5},{8,10},{9,11},{10,... | collective-permute-start | bytes 221192 | tf_op jit(solution)/shard_map/ppermute | solution.py:26
  84.6 2.0 %collective-permute-start.17 = (f32[2,32,256]{2,1,0:T(8,128)S(1)}, f32[2,32,256]{2,1,0:T(8,128)S(1)}, u32[]{:S(2)}, u32[]{:S(2)}) collective-permute-start(f32[2,32,256]{2,1,0:T(8,128)S(1)} %get-tuple-element.23), channel_id=1, source_target_pairs={{0,1},{1,0},{2,3},{3,2},{4,5},{5,4},{6,7},{7,6},{8,9},{9,8},{10,11... | collective-permute-start | bytes 196616 | tf_op jit(solution)/shard_map/ppermute | solution.py:26
  86.6 1.3 %collective-permute-start.15 = (f32[72,128]{1,0:T(8,128)S(1)}, f32[72,128]{1,0:T(8,128)S(1)}, u32[]{:S(2)}, u32[]{:S(2)}) collective-permute-start(f32[72,128]{1,0:T(8,128)S(1)} %dynamic-slice_bitcast_fusion.1), channel_id=1, source_target_pairs={{0,1},{1,0},{2,3},{3,2},{4,5},{5,4},{6,7},{7,6},{8,9},{9,8},{10,11... | collective-permute-start | bytes 110600 | tf_op jit(solution)/shard_map/ppermute | solution.py:26
  (3 other events, 5.9 us)

commit v6 on v5

--- a/solution.py
+++ b/solution.py
@@ -165,29 +165,26 @@
         compiler_params=PARAMS,
     )(flat_maps, flat_grads, g_inv)
     h = keep + swap(send, 1)
+    k_rows = behind(k_rows, h)
+    own = behind(jnp.stack([flat_maps, flat_grads]), h)
     h = h[0] + swap(h[1], 2)
     h = h + swap(h, zbits[0])
+    point = h
     for b in zbits[1:]:
         h = h + swap(h, b)
 
-    k_x = swap(k_rows, 2)
-    k_two = jnp.where(xbit == 0, jnp.stack([k_rows, k_x]), jnp.stack([k_x, k_rows]))
-    k_c = swap(k_two, 1)
-
-    own = jnp.stack([flat_maps, flat_grads])
+    k_a = jnp.concatenate([k_rows, swap(k_rows, 2)], axis=0)
+    k_b = swap(k_a, 1)
+
     next_own = after(own)
-    two_own = jnp.stack([own[0], next_own[0], own[1], next_own[1]])
+    two_own = behind(jnp.stack([own[0], next_own[0], own[1], next_own[1]]), point)
     half_a = jnp.stack([two_own, swap(two_own, 2)])
     half_b = swap(half_a, 1)
 
-    def k_times(k_part, e_t):
-        return dot_nt(e_t, k_part.reshape(2 * rows, full), precision=HIGH).reshape(-1, 2, rows)
-
     h = h * scale
-    main_a = k_times(k_two, h)
-    main_b = k_times(k_c, h)
-    main_t = jnp.where(core == 0, jnp.stack([main_a, main_b], 2), jnp.stack([main_b, main_a], 2))
-    main_t = main_t.reshape(quarter, 4 * rows)
+    main_t = jnp.concatenate(
+        [dot_nt(h, k_a, precision=HIGH), dot_nt(h, k_b, precision=HIGH)], axis=1
+    )
     p_t = main_t.astype(BF16)
 
     def by_bit(mine, other, b):
@@ -195,12 +192,18 @@
 
     for b in zbits[:-1]:
         p_t = by_bit(p_t, swap(p_t, b), b)
-    p_t = by_bit(after(p_t), after(p_t, zbits[-1]), zbits[-1])
     last = lax.axis_index("layer") == lax.axis_size("layer") - 1
-    p_t = jnp.where(last, jnp.zeros_like(p_t), p_t)
+    early = p_t
+
+    def in_order(p_t):
+        p_t = by_bit(after(p_t), after(p_t, zbits[-1]), zbits[-1])
+        p_t = jnp.where(last, jnp.zeros_like(p_t), p_t)
+        p_t = p_t.reshape(quarter, -1, 2, 2, rows).transpose(0, 1, 3, 2, 4)
+        p_t = jnp.where(xbit == 0, p_t, p_t[:, :, ::-1])
+        p_t = jnp.where(core == 0, p_t, p_t[:, :, :, ::-1])
+        return p_t.reshape(quarter, full)
 
     low = cols * quarter
-    grads_a, grads_b = (half[:, 2].reshape(-1, width) for half in (half_a, half_b))
     gram = 0.0
     for half in (half_a, half_b):
         here, following = (
@@ -208,6 +211,8 @@
         )
         following = jnp.where(last, jnp.zeros_like(following), following)
         gram = gram + dot_t(jnp.concatenate([here, following], axis=1), half[:, 2].reshape(-1, width))
+
+    p_t = in_order(behind(early, gram))
 
     out_width = full + 2 * width
     cross_t, cross_half = pl.pallas_call(
@@ -235,20 +240,16 @@
     gram = gram * scale
     h_mine = jnp.dot(gram[:, width:], g_inv, precision=HIGH) * scale
 
-    fix_a = dot_nt(k_two.reshape(2 * rows, full), cross_t, precision=HIGH).reshape(2, 1, rows, quarter)
-    fix_b = dot_nt(k_c.reshape(2 * rows, full), cross_t, precision=HIGH).reshape(2, 1, rows, quarter)
-    fix = jnp.where(core == 0, jnp.concatenate([fix_a, fix_b], 1), jnp.concatenate([fix_b, fix_a], 1))
-    out = main - jnp.dot(fix.reshape(4 * rows, quarter), h_mine, precision=HIGH)
+    fix = jnp.concatenate(
+        [dot_nt(k_a, cross_t, precision=HIGH), dot_nt(k_b, cross_t, precision=HIGH)], axis=0
+    )
+    out = main - jnp.dot(fix, h_mine, precision=HIGH)
     out = out.reshape(2, 2, rows, width)
     gram = behind(gram, out)
     gram = jnp.stack([gram, swap(gram, 2)])
-    keep = lax.dynamic_index_in_dim(out, xbit, 0, False)
-    send = lax.dynamic_index_in_dim(out, 1 - xbit, 0, False)
-    out = keep + swap(send, 2)
+    out = out[:, 0] + swap(out[:, 1], 2)
     gram = jnp.stack([gram, swap(gram, 1)])
-    keep = lax.dynamic_index_in_dim(out, core, 0, False)
-    send = lax.dynamic_index_in_dim(out, 1 - core, 0, False)
-    update = keep + swap(send, 1)
+    update = out[0] + swap(out[1], 1)
     gram = jnp.where(xbit == 0, gram, gram[:, ::-1])
     gram = jnp.where(core == 0, gram, gram[::-1])
     gram = gram.reshape(width, 2, width).transpose(1, 2, 0)

time: 88.8 us -> 77.5 us (0.87)
  waiting for transfers between devices: 46.1 us -> 31.4 us
  local copies, waits for them, and re-layouts: 2.48 us -> 6.43 us
  starting transfers between devices: 20.9 us -> 24.5 us
  other arithmetic: 5.6 us -> 2.3 us
    ppermute x15, waiting for transfers between devices: 40.6 us -> 29.4 us  [swap(): lax.ppermute(block, 'pos', [(i, i ^ bit) for i in range(lax.axis_size('po...]
    ppermute x3, waiting for transfers between devices: 5.53 us -> 1.94 us  [after(): return lax.ppermute(block, ('layer', 'pos'), route)]
    unnamed x18 -> x15, local copies, waits for them, and re-layouts: 0.96 us -> 4.3 us
    ppermute x15, starting transfers between devices: 14.3 us -> 17.4 us  [swap(): lax.ppermute(block, 'pos', [(i, i ^ bit) for i in range(lax.axis_size('po...]
    add x1, other arithmetic: 1.04 us -> 0.04 us  [per_device(): h = keep + swap(send, 1)]
    another operation x4 -> x5, other arithmetic: 1.1 us -> 0.14 us  [the longest x1 0.07 us: per_device(): jnp.stack([own[0], next_own[0], own[1], next_own[1]])]
    another operation x3 -> x2, other arithmetic: 1.05 us -> 0.15 us  [per_device(): half_a = jnp.stack([two_own, swap(two_own, 2)])]
    select_n x4 -> x2, other arithmetic: 1.24 us -> 0.35 us  [the longest x1 0.21 us: in_order(): p_t = jnp.where(core == 0, p_t, p_t[:, :, :, ::-1])]
  transfers between devices with their start and end apart: 18 -> 18, of which waited for: 13 -> 12; matrix products, arithmetic and copies ran while one was open for 11% -> 8% of each run, Pallas kernels for 2% -> 0%
where the time goes in v6:
time: 77.5 us; the launch traced here: 77.1 us
  waiting for transfers between devices  31.4 us (41%)
  starting transfers between devices  24.5 us (32%)
  matrix products  8.03 us (10%)
  local copies, waits for them, and re-layouts  6.43 us (8%)
  Pallas kernels  3.47 us (4%)
  other arithmetic  2.3 us (3%)
  between operations  1.05 us (1%)
    ppermute x15, waiting for transfers between devices, swap(): lax.ppermute(block, 'pos', [(i, i ^ bit) for i in range(lax.axis_size('po...  29.4 us
    ppermute x15, starting transfers between devices, swap(): lax.ppermute(block, 'pos', [(i, i ^ bit) for i in range(lax.axis_size('po...  17.4 us
    ppermute x3, starting transfers between devices, after(): return lax.ppermute(block, ('layer', 'pos'), route)  7.07 us
    dot_general x4, matrix products, dot_nt(): lax.dot_general(a, b, (((1,), (1,)), ((), ())), preferred_element_type=F3...  6.41 us
    unnamed x15, local copies, waits for them, and re-layouts  4.3 us
    ppermute x3, waiting for transfers between devices, after(): return lax.ppermute(block, ('layer', 'pos'), route)  1.94 us
    pallas_call x1, Pallas kernels, per_device(): pl.pallas_call(functools.partial(grad_kernel, side), out_shape=[jax.Shape...  1.78 us
    pallas_call x1, Pallas kernels, per_device(): pl.pallas_call(functools.partial(cross_kernel, side), out_shape=[jax.Shap...  1.69 us
  transfers between devices with their start and end apart: 18, of which 12 were waited for; matrix products, arithmetic and copies ran while one was open for 8% of the time, Pallas kernels for 0%

profile of v6, /device:TPU:0, one launch (start us, length us, event | category | flops | bytes accessed | tf_op | source)
XLA Modules:
  0.0 77.1 jit_solution(13849401793730390251)
XLA Ops:
  3.3 1.8 %shard_map.59 = (f32[2,32,1152]{2,1,0:T(8,128)S(1)}, f32[2,32,1152]{2,1,0:T(8,128)S(1)}) custom-call(bf16[512,128]{1,0:T(8,128)(2,1)S(1)} %bitcast.60, bf16[512,128]{1,0:T(8,128)(2,1)S(1)} %bitcast.62, f32[128,128]{1,0:T(8,128)S(1)} %bitcast.64), custom_call_target="tpu_custom_call" | custom-call | tf_op jit(solution)/shard_map/pallas_call | solution.py:153
  6.9 3.0 %collective-permute-start.6 = (bf16[2,512,128]{2,1,0:T(8,128)(2,1)S(1)}, bf16[2,512,128]{2,1,0:T(8,128)(2,1)S(1)}, u32[]{:S(2)}, u32[]{:S(2)}) collective-permute-start(bf16[2,512,128]{2,1,0:T(8,128)(2,1)S(1)} %pad_maximum_fusion.2), channel_id=1, source_target_pairs={{16,0},{17,1},{18,2},{19,3},{20,4},{21,5},{22,6},{23,7},{24,8},{25... | collective-permute-start | bytes 786440 | tf_op jit(solution)/shard_map/ppermute | solution.py:22
  9.8 1.5 %collective-permute-start.1 = (f32[32,1152]{1,0:T(8,128)S(1)}, f32[32,1152]{1,0:T(8,128)S(1)}, u32[]{:S(2)}, u32[]{:S(2)}) collective-permute-start(f32[32,1152]{1,0:T(8,128)S(1)} %slice_bitcast_fusion), channel_id=1, source_target_pairs={{0,2},{1,3},{2,0},{3,1},{4,6},{5,7},{6,4},{7,5},{8,10},{9,11},{10,... | collective-permute-start | bytes 442376 | tf_op jit(solution)/shard_map/ppermute | solution.py:26
  11.9 4.7 %collective-permute-done.1 = f32[32,1152]{1,0:T(8,128)S(1)} collective-permute-done((f32[32,1152]{1,0:T(8,128)S(1)}, f32[32,1152]{1,0:T(8,128)S(1)}, u32[]{:S(2)}, u32[]{:S(2)}) %collective-permute-start.1) | collective-permute-done | bytes 147488 | tf_op jit(solution)/shard_map/ppermute | solution.py:26
  16.6 1.7 %collective-permute-start.2 = (f32[32,1152]{1,0:T(8,128)S(1)}, f32[32,1152]{1,0:T(8,128)S(1)}, u32[]{:S(2)}, u32[]{:S(2)}) collective-permute-start(f32[32,1152]{1,0:T(8,128)S(1)} %fusion.13), channel_id=1, source_target_pairs={{0,4},{1,5},{2,6},{3,7},{4,0},{5,1},{6,2},{7,3},{8,12},{9,13},{10,... | collective-permute-start | bytes 442376 | tf_op jit(solution)/shard_map/ppermute | solution.py:26
  18.3 3.5 %collective-permute-done.2 = f32[32,1152]{1,0:T(8,128)S(1)} collective-permute-done((f32[32,1152]{1,0:T(8,128)S(1)}, f32[32,1152]{1,0:T(8,128)S(1)}, u32[]{:S(2)}, u32[]{:S(2)}) %collective-permute-start.2) | collective-permute-done | bytes 147488 | tf_op jit(solution)/shard_map/ppermute | solution.py:26
  21.8 1.6 %collective-permute-start.7 = (bf16[4,512,128]{2,1,0:T(8,128)(2,1)S(1)}, bf16[4,512,128]{2,1,0:T(8,128)(2,1)S(1)}, u32[]{:S(2)}, u32[]{:S(2)}) collective-permute-start(bf16[4,512,128]{2,1,0:T(8,128)(2,1)S(1)} %pad_maximum_fusion.1), channel_id=1, source_target_pairs={{0,2},{1,3},{2,0},{3,1},{4,6},{5,7},{6,4},{7,5},{8,10},{9,11},{10,... | collective-permute-start | bytes 1572872 | tf_op jit(solution)/shard_map/ppermute | solution.py:26
  23.6 2.7 %collective-permute-start.3 = (f32[32,1152]{1,0:T(8,128)S(1)}, f32[32,1152]{1,0:T(8,128)}, u32[]{:S(2)}, u32[]{:S(2)}) collective-permute-start(f32[32,1152]{1,0:T(8,128)S(1)} %add.67), channel_id=1, source_target_pairs={{0,8},{1,9},{2,10},{3,11},{4,12},{5,13},{6,14},{7,15},{8,0},{9,1},... | collective-permute-start | bytes 442376 | tf_op jit(solution)/shard_map/ppermute | solution.py:26
  26.3 7.5 %collective-permute-done.7 = bf16[4,512,128]{2,1,0:T(8,128)(2,1)S(1)} collective-permute-done((bf16[4,512,128]{2,1,0:T(8,128)(2,1)S(1)}, bf16[4,512,128]{2,1,0:T(8,128)(2,1)S(1)}, u32[]{:S(2)}, u32[]{:S(2)}) %collective-permute-start.7) | collective-permute-done | bytes 524320 | tf_op jit(solution)/shard_map/ppermute | solution.py:26
  34.8 1.8 %fusion.17 = f32[32,144]{1,0:T(8,128)S(1)} fusion(f32[144,1152]{1,0:T(8,128)S(1)} %constant_dynamic-update-slice_fusion, f32[32,1152]{1,0:T(8,128)S(1)} %add.67, f32[32,1152]{1,0:T(8,128)} %collective-permute-done.3), kind=kOutput, calls=%fused_computation.42 | convolution fusion | flops 63774720 | bytes 976896 | tf_op jit(solution)/shard_map/dot_general | solution.py:34
  36.7 2.0 %fusion.16 = f32[32,144]{1,0:T(8,128)S(1)} fusion(f32[144,1152]{1,0:T(8,128)} %collective-permute-done.5, f32[32,1152]{1,0:T(8,128)S(1)} %add.67, f32[32,1152]{1,0:T(8,128)} %collective-permute-done.3), kind=kOutput, calls=%fused_computation.41 | convolution fusion | flops 63774720 | bytes 976896 | tf_op jit(solution)/shard_map/dot_general | solution.py:34
  38.7 1.6 %collective-permute-start.9 = (bf16[32,288]{1,0:T(8,128)(2,1)S(1)}, bf16[32,288]{1,0:T(8,128)(2,1)S(1)}, u32[]{:S(2)}, u32[]{:S(2)}) collective-permute-start(bf16[32,288]{1,0:T(8,128)(2,1)S(1)} %fusion.31), channel_id=1, source_target_pairs={{0,4},{1,5},{2,6},{3,7},{4,0},{5,1},{6,2},{7,3},{8,12},{9,13},{10,... | collective-permute-start | bytes 55304 | tf_op jit(solution)/shard_map/ppermute | solution.py:26
  40.5 2.0 %collective-permute-done.9 = bf16[32,288]{1,0:T(8,128)(2,1)S(1)} collective-permute-done((bf16[32,288]{1,0:T(8,128)(2,1)S(1)}, bf16[32,288]{1,0:T(8,128)(2,1)S(1)}, u32[]{:S(2)}, u32[]{:S(2)}) %collective-permute-start.9) | collective-permute-done | bytes 18464 | tf_op jit(solution)/shard_map/ppermute | solution.py:26
  44.0 3.7 %collective-permute-start.11 = (bf16[32,576]{1,0:T(8,128)(2,1)S(1)}, bf16[32,576]{1,0:T(8,128)(2,1)S(1)}, u32[]{:S(2)}, u32[]{:S(2)}) collective-permute-start(bf16[32,576]{1,0:T(8,128)(2,1)S(1)} %maximum_select_fusion), channel_id=1, source_target_pairs={{24,0},{25,1},{26,2},{27,3},{28,4},{29,5},{30,6},{31,7},{16,8},{17... | collective-permute-start | bytes 110600 | tf_op jit(solution)/shard_map/ppermute | solution.py:22
  47.9 1.9 %collective-permute-done.11 = bf16[32,576]{1,0:T(8,128)(2,1)S(1)} collective-permute-done((bf16[32,576]{1,0:T(8,128)(2,1)S(1)}, bf16[32,576]{1,0:T(8,128)(2,1)S(1)}, u32[]{:S(2)}, u32[]{:S(2)}) %collective-permute-start.11) | collective-permute-done | bytes 36896 | tf_op jit(solution)/shard_map/ppermute | solution.py:22
  51.5 1.7 %shard_map.60 = (f32[32,1408]{1,0:T(8,128)S(1)}, bf16[32,1664]{1,0:T(8,128)(2,1)S(1)}) custom-call(bf16[2,4,512,128]{3,2,1,0:T(8,128)(2,1)S(1)} %pad_maximum_fusion.half_a, bf16[2,4,512,128]{3,2,1,0:T(8,128)(2,1)S(1)} %collective-permute-done.8.half_b, bf16[32,1152]{1,0:T(8,128)(2,1)S(1)} %reshape.23.precond_t, f32[64,128]{1,0:T(8,128)S(1)} %fusion.4.gram), custom_call_target="tpu_custom_call" | custom-call | tf_op jit(solution)/shard_map/pallas_call | solution.py:218
  53.2 1.8 %collective-permute-start.12 = (bf16[32,1664]{1,0:T(8,128)(2,1)S(1)}, bf16[32,1664]{1,0:T(8,128)(2,1)S(1)}, u32[]{:S(2)}, u32[]{:S(2)}) collective-permute-start(bf16[32,1664]{1,0:T(8,128)(2,1)S(1)} %get-tuple-element.18), channel_id=1, source_target_pairs={{0,4},{1,5},{2,6},{3,7},{4,0},{5,1},{6,2},{7,3},{8,12},{9,13},{10,... | collective-permute-start | bytes 319496 | tf_op jit(solution)/shard_map/ppermute | solution.py:26
  55.0 3.0 %collective-permute-done.12 = bf16[32,1664]{1,0:T(8,128)(2,1)S(1)} collective-permute-done((bf16[32,1664]{1,0:T(8,128)(2,1)S(1)}, bf16[32,1664]{1,0:T(8,128)(2,1)S(1)}, u32[]{:S(2)}, u32[]{:S(2)}) %collective-permute-start.12) | collective-permute-done | bytes 106528 | tf_op jit(solution)/shard_map/ppermute | solution.py:26
  58.1 3.2 %collective-permute-start.13 = (bf16[32,1664]{1,0:T(8,128)(2,1)S(1)}, bf16[32,1664]{1,0:T(8,128)(2,1)S(1)}, u32[]{:S(2)}, u32[]{:S(2)}) collective-permute-start(bf16[32,1664]{1,0:T(8,128)(2,1)S(1)} %pad_maximum_fusion.4), channel_id=1, source_target_pairs={{0,8},{1,9},{2,10},{3,11},{4,12},{5,13},{6,14},{7,15},{8,0},{9,1},... | collective-permute-start | bytes 319496 | tf_op jit(solution)/shard_map/ppermute | solution.py:26
  61.7 3.5 %collective-permute-done.13 = bf16[32,1664]{1,0:T(8,128)(2,1)S(1)} collective-permute-done((bf16[32,1664]{1,0:T(8,128)(2,1)S(1)}, bf16[32,1664]{1,0:T(8,128)(2,1)S(1)}, u32[]{:S(2)}, u32[]{:S(2)}) %collective-permute-start.13) | collective-permute-done | bytes 106528 | tf_op jit(solution)/shard_map/ppermute | solution.py:26
  66.9 1.9 %fusion.18 = f32[144,32]{0,1:T(8,128)S(1)} fusion(f32[144,1152]{1,0:T(8,128)} %collective-permute-done.5, f32[32,1664]{1,0:T(8,128)S(1)} %convert_element_type.13, f32[32,1664]{1,0:T(8,128)S(1)} %convert_element_type.12, f32[32,1408]{1,0:T(8,128)S(1)} %get-tuple-element.17), kind=kOutput, calls=%fused_computation.43 | convolution fusion | flops 63774720 | bytes 1124352 | tf_op jit(solution)/shard_map/dot_general | solution.py:34
  69.3 1.6 %collective-permute-start.16 = (f32[32,256]{1,0:T(8,128)S(1)}, f32[32,256]{1,0:T(8,128)S(1)}, u32[]{:S(2)}, u32[]{:S(2)}) collective-permute-start(f32[32,256]{1,0:T(8,128)S(1)} %fusion.29), channel_id=1, source_target_pairs={{0,2},{1,3},{2,0},{3,1},{4,6},{5,7},{6,4},{7,5},{8,10},{9,11},{10,... | collective-permute-start | bytes 98312 | tf_op jit(solution)/shard_map/ppermute | solution.py:26
  71.4 1.9 %collective-permute-done.16 = f32[32,256]{1,0:T(8,128)S(1)} collective-permute-done((f32[32,256]{1,0:T(8,128)S(1)}, f32[32,256]{1,0:T(8,128)S(1)}, u32[]{:S(2)}, u32[]{:S(2)}) %collective-permute-start.16) | collective-permute-done | bytes 32800 | tf_op jit(solution)/shard_map/ppermute | solution.py:26
  73.4 1.9 %collective-permute-done.14 = f32[2,72,128]{2,1,0:T(8,128)S(1)} collective-permute-done((f32[2,72,128]{2,1,0:T(8,128)S(1)}, f32[2,72,128]{2,1,0:T(8,128)S(1)}, u32[]{:S(2)}, u32[]{:S(2)}) %collective-permute-start.14) | collective-permute-done | bytes 73760 | tf_op jit(solution)/shard_map/ppermute | solution.py:26
  (81 shorter events, 15.1 us)
Async XLA Ops:
  0.6 0.9 %copy-start = (bf16[1,2,16,16,128]{4,3,2,1,0:T(8,128)(2,1)S(1)}, bf16[1,2,16,16,128]{4,3,2,1,0:T(8,128)(2,1)}, u32[]{:S(2)}) copy-start(bf16[1,2,16,16,128]{4,3,2,1,0:T(8,128)(2,1)} %param.4) | copy-start | bytes 393220
  1.5 0.9 %copy-start.1 = (bf16[1,2,16,16,128]{4,3,2,1,0:T(8,128)(2,1)S(1)}, bf16[1,2,16,16,128]{4,3,2,1,0:T(8,128)(2,1)}, u32[]{:S(2)}) copy-start(bf16[1,2,16,16,128]{4,3,2,1,0:T(8,128)(2,1)} %param.5) | copy-start | bytes 393220
  2.4 0.8 %copy-start.2 = (f32[1,128,128]{2,1,0:T(8,128)S(1)}, f32[1,128,128]{2,1,0:T(8,128)}, u32[]{:S(2)}) copy-start(f32[1,128,128]{2,1,0:T(8,128)} %param.7) | copy-start | bytes 196612
  5.1 1.7 %collective-permute-start = (f32[2,32,1152]{2,1,0:T(8,128)S(1)}, f32[2,32,1152]{2,1,0:T(8,128)S(1)}, u32[]{:S(2)}, u32[]{:S(2)}) collective-permute-start(f32[2,32,1152]{2,1,0:T(8,128)S(1)} %get-tuple-element.12), channel_id=1, source_target_pairs={{0,1},{1,0},{2,3},{3,2},{4,5},{5,4},{6,7},{7,6},{8,9},{9,8},{10,11... | collective-permute-start | bytes 884744 | tf_op jit(solution)/shard_map/ppermute | solution.py:26
  6.8 4.5 %copy-start.6 = (f32[1,72,1152]{2,1,0:T(8,128)S(1)}, f32[1,72,1152]{2,1,0:T(8,128)}, u32[]{:S(2)}) copy-start(f32[1,72,1152]{2,1,0:T(8,128)} %param.6) | copy-start | bytes 995332
  6.9 11.4 %collective-permute-start.6 = (bf16[2,512,128]{2,1,0:T(8,128)(2,1)S(1)}, bf16[2,512,128]{2,1,0:T(8,128)(2,1)S(1)}, u32[]{:S(2)}, u32[]{:S(2)}) collective-permute-start(bf16[2,512,128]{2,1,0:T(8,128)(2,1)S(1)} %pad_maximum_fusion.2), channel_id=1, source_target_pairs={{16,0},{17,1},{18,2},{19,3},{20,4},{21,5},{22,6},{23,7},{24,8},{25... | collective-permute-start | bytes 786440 | tf_op jit(solution)/shard_map/ppermute | solution.py:22
  9.8 6.7 %collective-permute-start.1 = (f32[32,1152]{1,0:T(8,128)S(1)}, f32[32,1152]{1,0:T(8,128)S(1)}, u32[]{:S(2)}, u32[]{:S(2)}) collective-permute-start(f32[32,1152]{1,0:T(8,128)S(1)} %slice_bitcast_fusion), channel_id=1, source_target_pairs={{0,2},{1,3},{2,0},{3,1},{4,6},{5,7},{6,4},{7,5},{8,10},{9,11},{10,... | collective-permute-start | bytes 442376 | tf_op jit(solution)/shard_map/ppermute | solution.py:26
  11.3 12.2 %collective-permute-start.4 = (f32[72,1152]{1,0:T(8,128)S(1)}, f32[72,1152]{1,0:T(8,128)S(1)}, u32[]{:S(2)}, u32[]{:S(2)}) collective-permute-start(f32[72,1152]{1,0:T(8,128)S(1)} %bitcast.77), channel_id=1, source_target_pairs={{0,2},{1,3},{2,0},{3,1},{4,6},{5,7},{6,4},{7,5},{8,10},{9,11},{10,... | collective-permute-start | bytes 995336 | tf_op jit(solution)/shard_map/ppermute | solution.py:26
  16.6 5.2 %collective-permute-start.2 = (f32[32,1152]{1,0:T(8,128)S(1)}, f32[32,1152]{1,0:T(8,128)S(1)}, u32[]{:S(2)}, u32[]{:S(2)}) collective-permute-start(f32[32,1152]{1,0:T(8,128)S(1)} %fusion.13), channel_id=1, source_target_pairs={{0,4},{1,5},{2,6},{3,7},{4,0},{5,1},{6,2},{7,3},{8,12},{9,13},{10,... | collective-permute-start | bytes 442376 | tf_op jit(solution)/shard_map/ppermute | solution.py:26
  21.8 12.0 %collective-permute-start.7 = (bf16[4,512,128]{2,1,0:T(8,128)(2,1)S(1)}, bf16[4,512,128]{2,1,0:T(8,128)(2,1)S(1)}, u32[]{:S(2)}, u32[]{:S(2)}) collective-permute-start(bf16[4,512,128]{2,1,0:T(8,128)(2,1)S(1)} %pad_maximum_fusion.1), channel_id=1, source_target_pairs={{0,2},{1,3},{2,0},{3,1},{4,6},{5,7},{6,4},{7,5},{8,10},{9,11},{10,... | collective-permute-start | bytes 1572872 | tf_op jit(solution)/shard_map/ppermute | solution.py:26
  23.6 13.1 %collective-permute-start.5 = (f32[144,1152]{1,0:T(8,128)S(1)}, f32[144,1152]{1,0:T(8,128)}, u32[]{:S(2)}, u32[]{:S(2)}) collective-permute-start(f32[144,1152]{1,0:T(8,128)S(1)} %constant_dynamic-update-slice_fusion), channel_id=1, source_target_pairs={{0,1},{1,0},{2,3},{3,2},{4,5},{5,4},{6,7},{7,6},{8,9},{9,8},{10,11... | collective-permute-start | bytes 1990664 | tf_op jit(solution)/shard_map/ppermute | solution.py:26
  23.6 11.2 %collective-permute-start.3 = (f32[32,1152]{1,0:T(8,128)S(1)}, f32[32,1152]{1,0:T(8,128)}, u32[]{:S(2)}, u32[]{:S(2)}) collective-permute-start(f32[32,1152]{1,0:T(8,128)S(1)} %add.67), channel_id=1, source_target_pairs={{0,8},{1,9},{2,10},{3,11},{4,12},{5,13},{6,14},{7,15},{8,0},{9,1},... | collective-permute-start | bytes 442376 | tf_op jit(solution)/shard_map/ppermute | solution.py:26
  34.7 8.0 %collective-permute-start.8 = (bf16[2,4,512,128]{3,2,1,0:T(8,128)(2,1)S(1)}, bf16[2,4,512,128]{3,2,1,0:T(8,128)(2,1)S(1)}, u32[]{:S(2)}, u32[]{:S(2)}) collective-permute-start(bf16[2,4,512,128]{3,2,1,0:T(8,128)(2,1)S(1)} %pad_maximum_fusion.half_a), channel_id=1, source_target_pairs={{0,1},{1,0},{2,3},{3,2},{4,5},{5,4},{6,7},{7,6},{8,9},{9,8},{10,11... | collective-permute-start | bytes 3145736 | tf_op jit(solution)/shard_map/ppermute | solution.py:26
  34.8 1.8 %copy-start.5 = (bf16[4,512,128]{2,1,0:T(8,128)(2,1)S(1)}, bf16[4,512,128]{2,1,0:T(8,128)(2,1)}, u32[]{:S(2)}) copy-start(bf16[4,512,128]{2,1,0:T(8,128)(2,1)} %copy-done.4) | copy-start | bytes 1572868
  38.7 3.8 %collective-permute-start.9 = (bf16[32,288]{1,0:T(8,128)(2,1)S(1)}, bf16[32,288]{1,0:T(8,128)(2,1)S(1)}, u32[]{:S(2)}, u32[]{:S(2)}) collective-permute-start(bf16[32,288]{1,0:T(8,128)(2,1)S(1)} %fusion.31), channel_id=1, source_target_pairs={{0,4},{1,5},{2,6},{3,7},{4,0},{5,1},{6,2},{7,3},{8,12},{9,13},{10,... | collective-permute-start | bytes 55304 | tf_op jit(solution)/shard_map/ppermute | solution.py:26
  43.6 4.1 %collective-permute-start.10 = (bf16[32,576]{1,0:T(8,128)(2,1)S(1)}, bf16[32,576]{1,0:T(8,128)(2,1)S(1)}, u32[]{:S(2)}, u32[]{:S(2)}) collective-permute-start(bf16[32,576]{1,0:T(8,128)(2,1)S(1)} %maximum_select_fusion), channel_id=1, source_target_pairs={{16,0},{17,1},{18,2},{19,3},{20,4},{21,5},{22,6},{23,7},{24,8},{25... | collective-permute-start | bytes 110600 | tf_op jit(solution)/shard_map/ppermute | solution.py:22
  44.0 5.8 %collective-permute-start.11 = (bf16[32,576]{1,0:T(8,128)(2,1)S(1)}, bf16[32,576]{1,0:T(8,128)(2,1)S(1)}, u32[]{:S(2)}, u32[]{:S(2)}) collective-permute-start(bf16[32,576]{1,0:T(8,128)(2,1)S(1)} %maximum_select_fusion), channel_id=1, source_target_pairs={{24,0},{25,1},{26,2},{27,3},{28,4},{29,5},{30,6},{31,7},{16,8},{17... | collective-permute-start | bytes 110600 | tf_op jit(solution)/shard_map/ppermute | solution.py:22
  53.2 4.8 %collective-permute-start.12 = (bf16[32,1664]{1,0:T(8,128)(2,1)S(1)}, bf16[32,1664]{1,0:T(8,128)(2,1)S(1)}, u32[]{:S(2)}, u32[]{:S(2)}) collective-permute-start(bf16[32,1664]{1,0:T(8,128)(2,1)S(1)} %get-tuple-element.18), channel_id=1, source_target_pairs={{0,4},{1,5},{2,6},{3,7},{4,0},{5,1},{6,2},{7,3},{8,12},{9,13},{10,... | collective-permute-start | bytes 319496 | tf_op jit(solution)/shard_map/ppermute | solution.py:26
  58.1 7.1 %collective-permute-start.13 = (bf16[32,1664]{1,0:T(8,128)(2,1)S(1)}, bf16[32,1664]{1,0:T(8,128)(2,1)S(1)}, u32[]{:S(2)}, u32[]{:S(2)}) collective-permute-start(bf16[32,1664]{1,0:T(8,128)(2,1)S(1)} %pad_maximum_fusion.4), channel_id=1, source_target_pairs={{0,8},{1,9},{2,10},{3,11},{4,12},{5,13},{6,14},{7,15},{8,0},{9,1},... | collective-permute-start | bytes 319496 | tf_op jit(solution)/shard_map/ppermute | solution.py:26
  65.9 0.8 %copy-start.3 = (f32[1,128,128]{2,1,0:T(8,128)S(1)}, f32[1,128,128]{2,1,0:T(8,128)}, u32[]{:S(2)}) copy-start(f32[1,128,128]{2,1,0:T(8,128)} %param.7) | copy-start | bytes 196612
  69.3 4.0 %collective-permute-start.16 = (f32[32,256]{1,0:T(8,128)S(1)}, f32[32,256]{1,0:T(8,128)S(1)}, u32[]{:S(2)}, u32[]{:S(2)}) collective-permute-start(f32[32,256]{1,0:T(8,128)S(1)} %fusion.29), channel_id=1, source_target_pairs={{0,2},{1,3},{2,0},{3,1},{4,6},{5,7},{6,4},{7,5},{8,10},{9,11},{10,... | collective-permute-start | bytes 98312 | tf_op jit(solution)/shard_map/ppermute | solution.py:26
  70.9 4.4 %collective-permute-start.14 = (f32[2,72,128]{2,1,0:T(8,128)S(1)}, f32[2,72,128]{2,1,0:T(8,128)S(1)}, u32[]{:S(2)}, u32[]{:S(2)}) collective-permute-start(f32[2,72,128]{2,1,0:T(8,128)S(1)} %slice_bitcast_fusion.2), channel_id=1, source_target_pairs={{0,2},{1,3},{2,0},{3,1},{4,6},{5,7},{6,4},{7,5},{8,10},{9,11},{10,... | collective-permute-start | bytes 221192 | tf_op jit(solution)/shard_map/ppermute | solution.py:26
  73.3 2.0 %collective-permute-start.17 = (f32[2,32,256]{2,1,0:T(8,128)S(1)}, f32[2,32,256]{2,1,0:T(8,128)S(1)}, u32[]{:S(2)}, u32[]{:S(2)}) collective-permute-start(f32[2,32,256]{2,1,0:T(8,128)S(1)} %get-tuple-element.31), channel_id=1, source_target_pairs={{0,1},{1,0},{2,3},{3,2},{4,5},{5,4},{6,7},{7,6},{8,9},{9,8},{10,11... | collective-permute-start | bytes 196616 | tf_op jit(solution)/shard_map/ppermute | solution.py:26
  75.2 1.3 %collective-permute-start.15 = (f32[72,128]{1,0:T(8,128)S(1)}, f32[72,128]{1,0:T(8,128)S(1)}, u32[]{:S(2)}, u32[]{:S(2)}) collective-permute-start(f32[72,128]{1,0:T(8,128)S(1)} %slice_bitcast_fusion.4), channel_id=1, source_target_pairs={{0,1},{1,0},{2,3},{3,2},{4,5},{5,4},{6,7},{7,6},{8,9},{9,8},{10,11... | collective-permute-start | bytes 110600 | tf_op jit(solution)/shard_map/ppermute | solution.py:26
  (1 other events, 0.8 us)

commit v7 on v6

--- a/solution.py
+++ b/solution.py
@@ -83,8 +83,8 @@
         all_rows[:, tap * width : (tap + 1) * width] = (
             both[low : low + width] + both[low + width : low + 2 * width]
         )
-    me = lax.axis_index("pos")
-    mine = 2 * (me & 1) + ((me >> 1) & 1)
+    core, xbit = place_bits()
+    mine = 2 * core + xbit
     quarter = width // 4
     for j in range(4):
         block = all_rows[pl.ds(pl.multiple_of((mine ^ j) * quarter, quarter), quarter), :]
@@ -126,9 +126,74 @@
         out_half[:, low + 2 * width : low + 3 * width] = rest
 
 
+def two_parts(block):
+    high = block.astype(BF16)
+    return jnp.concatenate([high, (block - high.astype(F32)).astype(BF16)], axis=0)
+
+
+def place_bits():
+    me = lax.axis_index("pos")
+    return me & 1, (me >> 1) & 1
+
+
+def precond_kernel(scale, e_t, k_a, k_b, main_a, main_b, precond_t):
+    core, xbit = place_bits()
+    count = e_t.shape[0]
+    rows = k_a.shape[0] // 2
+    parts = two_parts(e_t[...] * scale)
+    total = None
+    for flip, k, main in ((0, k_a, main_a), (1, k_b, main_b)):
+        k_parts = two_parts(k[...])
+        product = dot_nt(parts, k_parts[: 2 * rows]) + dot_nt(parts, k_parts[2 * rows :])
+        product = product[:count] + product[count:]
+        main[...] = product
+        source = lax.broadcasted_iota(jnp.int32, (2 * rows, 4 * rows), 0)
+        target = lax.broadcasted_iota(jnp.int32, (2 * rows, 4 * rows), 1)
+        second = (source >= rows).astype(jnp.int32)
+        block = 2 * (xbit ^ second) + (core ^ flip)
+        one_hot = (source - second * rows + block * rows == target).astype(F32).astype(BF16)
+        placed = jnp.dot(product.astype(BF16), one_hot, preferred_element_type=F32)
+        total = placed if total is None else total + placed
+    precond_t[...] = total.astype(BF16)
+
+
+def update_kernel(scale, cross_t, gram, g_inv, k_a, k_b, main, keep, send):
+    rows = k_a.shape[0] // 2
+    mixed = jnp.dot(gram[...], g_inv[...], precision=HIGH) * (scale * scale)
+    mixed = jnp.concatenate([mixed, mixed], axis=0)
+    parts = two_parts(cross_t[...])
+    for i, k in enumerate((k_a, k_b)):
+        k_parts = two_parts(k[...])
+        product = dot_nt(k_parts[: 2 * rows], parts) + dot_nt(k_parts[2 * rows :], parts)
+        result = main[i] - jnp.dot(product, mixed, precision=HIGH)
+        keep[i] = result[:rows]
+        send[i] = result[rows:]
+
+
+def gram_kernel(half_a, half_b, out, scratch):
+    core, xbit = place_bits()
+    mine = 2 * core + xbit
+    width = half_a.shape[3]
+    quarter = width // 4
+    here = following = None
+    for half in (half_a, half_b):
+        for d in range(2):
+            g = half[d, 2]
+            part = dot_t(g, g)
+            here = part if here is None else here + part
+            part = dot_t(half[d, 3], g)
+            following = part if following is None else following + part
+    last = lax.axis_index("layer") == lax.axis_size("layer") - 1
+    scratch[0] = here
+    scratch[1] = jnp.where(last, 0.0, following)
+    for i in range(2):
+        out[i * quarter : (i + 1) * quarter] = scratch[i, pl.ds(pl.multiple_of(mine * quarter, quarter), quarter), :]
+
+
 VMEM = pl.BlockSpec(memory_space=pltpu.VMEM)
 ANY = pl.BlockSpec(memory_space=pl.ANY)
 PARAMS = pltpu.CompilerParams(vmem_limit_bytes=32 * 1024 * 1024)
+ALONE = pltpu.CompilerParams(vmem_limit_bytes=60 * 1024 * 1024)
 
 
 def per_device(layer_inputs, output_grads, input_inverse, grad_inverse):
@@ -162,57 +227,57 @@
             pltpu.VMEM(g_inv.shape, F32),
             pltpu.SemaphoreType.DMA((3,)),
         ],
-        compiler_params=PARAMS,
+        compiler_params=ALONE,
     )(flat_maps, flat_grads, g_inv)
     h = keep + swap(send, 1)
     k_rows = behind(k_rows, h)
+    k_x = swap(k_rows, 2)
     own = behind(jnp.stack([flat_maps, flat_grads]), h)
+    next_own = after(own)
     h = h[0] + swap(h[1], 2)
+    own, next_own = behind((own, next_own), h)
+    two_own = jnp.stack([own[0], next_own[0], own[1], next_own[1]])
+    two_x = swap(two_own, 2)
     h = h + swap(h, zbits[0])
-    point = h
+    k_rows, k_x = behind((k_rows, k_x), h)
+    k_a = jnp.concatenate([k_rows, k_x], axis=0)
+    k_b = swap(k_a, 1)
     for b in zbits[1:]:
         h = h + swap(h, b)
 
-    k_a = jnp.concatenate([k_rows, swap(k_rows, 2)], axis=0)
-    k_b = swap(k_a, 1)
-
-    next_own = after(own)
-    two_own = behind(jnp.stack([own[0], next_own[0], own[1], next_own[1]]), point)
-    half_a = jnp.stack([two_own, swap(two_own, 2)])
+    main_a, main_b, p_t = pl.pallas_call(
+        functools.partial(precond_kernel, scale),
+        out_shape=[jax.ShapeDtypeStruct((quarter, 2 * rows), F32)] * 2
+        + [jax.ShapeDtypeStruct((quarter, 4 * rows), BF16)],
+        in_specs=[VMEM] * 3,
+        out_specs=[VMEM] * 3,
+        compiler_params=PARAMS,
+    )(h, k_a, k_b)
+
+    two_own, two_x = behind((two_own, two_x), p_t)
+    half_a = jnp.stack([two_own, two_x])
     half_b = swap(half_a, 1)
-
-    h = h * scale
-    main_t = jnp.concatenate(
-        [dot_nt(h, k_a, precision=HIGH), dot_nt(h, k_b, precision=HIGH)], axis=1
-    )
-    p_t = main_t.astype(BF16)
 
     def by_bit(mine, other, b):
         return jnp.where((me & b) == 0, jnp.concatenate([mine, other], 1), jnp.concatenate([other, mine], 1))
 
     for b in zbits[:-1]:
         p_t = by_bit(p_t, swap(p_t, b), b)
+
+    half_a, half_b = behind((half_a, half_b), p_t)
+    gram = pl.pallas_call(
+        gram_kernel,
+        out_shape=jax.ShapeDtypeStruct((2 * quarter, width), F32),
+        in_specs=[VMEM] * 2,
+        out_specs=VMEM,
+        scratch_shapes=[pltpu.VMEM((2, width, width), F32)],
+        compiler_params=PARAMS,
+    )(half_a, half_b)
+    low = cols * quarter
     last = lax.axis_index("layer") == lax.axis_size("layer") - 1
-    early = p_t
-
-    def in_order(p_t):
-        p_t = by_bit(after(p_t), after(p_t, zbits[-1]), zbits[-1])
-        p_t = jnp.where(last, jnp.zeros_like(p_t), p_t)
-        p_t = p_t.reshape(quarter, -1, 2, 2, rows).transpose(0, 1, 3, 2, 4)
-        p_t = jnp.where(xbit == 0, p_t, p_t[:, :, ::-1])
-        p_t = jnp.where(core == 0, p_t, p_t[:, :, :, ::-1])
-        return p_t.reshape(quarter, full)
-
-    low = cols * quarter
-    gram = 0.0
-    for half in (half_a, half_b):
-        here, following = (
-            lax.dynamic_slice_in_dim(half[:, i].reshape(-1, width), low, quarter, 1) for i in (2, 3)
-        )
-        following = jnp.where(last, jnp.zeros_like(following), following)
-        gram = gram + dot_t(jnp.concatenate([here, following], axis=1), half[:, 2].reshape(-1, width))
-
-    p_t = in_order(behind(early, gram))
+    p_same, p_other = behind((after(p_t), after(p_t, zbits[-1])), gram)
+    p_t = by_bit(p_same, p_other, zbits[-1])
+    p_t = jnp.where(last, jnp.zeros_like(p_t), p_t)
 
     out_width = full + 2 * width
     cross_t, cross_half = pl.pallas_call(
@@ -227,7 +292,8 @@
     )(half_a, half_b, p_t, gram)
 
     place = (jnp.arange(width)[None, :] == low + jnp.arange(quarter)[:, None]).astype(F32)
-    main = dot_t(main_t, place, precision=HIGH)
+    main_a, main_b = behind((main_a, main_b), cross_half)
+    main = jnp.stack([dot_t(main_a, place, precision=HIGH), dot_t(main_b, place, precision=HIGH)])
     cross_t, gram = cross_t[:, :full], cross_t[:, full:]
     for b in zbits:
         other = swap(cross_half, b).astype(F32)
@@ -237,17 +303,17 @@
         rest = lax.reduce_precision(gram - high, 8, 7)
         gram = high + rest
         cross_half = jnp.concatenate([cross_t, high, rest], axis=1).astype(BF16)
-    gram = gram * scale
-    h_mine = jnp.dot(gram[:, width:], g_inv, precision=HIGH) * scale
-
-    fix = jnp.concatenate(
-        [dot_nt(k_a, cross_t, precision=HIGH), dot_nt(k_b, cross_t, precision=HIGH)], axis=0
-    )
-    out = main - jnp.dot(fix, h_mine, precision=HIGH)
-    out = out.reshape(2, 2, rows, width)
-    gram = behind(gram, out)
+
+    out, send = pl.pallas_call(
+        functools.partial(update_kernel, scale),
+        out_shape=[jax.ShapeDtypeStruct((2, rows, width), F32)] * 2,
+        in_specs=[VMEM] * 6,
+        out_specs=[VMEM] * 2,
+        compiler_params=PARAMS,
+    )(cross_t, gram[:, width:], g_inv, k_a, k_b, main)
+    gram = behind(gram, out) * scale
     gram = jnp.stack([gram, swap(gram, 2)])
-    out = out[:, 0] + swap(out[:, 1], 2)
+    out = out + swap(send, 2)
     gram = jnp.stack([gram, swap(gram, 1)])
     update = out[0] + swap(out[1], 1)
     gram = jnp.where(xbit == 0, gram, gram[:, ::-1])

time: 77.5 us -> 73.3 us (0.946)
  matrix products: 8.03 us -> 0.56 us
  local copies, waits for them, and re-layouts: 6.43 us -> 1.74 us
  Pallas kernels: 3.47 us -> 7.41 us
  other arithmetic: 2.3 us -> 3.95 us
  starting transfers between devices: 24.5 us -> 25.9 us
  waiting for transfers between devices: 31.4 us -> 32.5 us
    dot_general x6 -> x0, matrix products: 7.03 us -> none  [the longest x4 6.41 us: dot_nt(): lax.dot_general(a, b, (((1,), (1,)), ((), ())), preferred_element_type=F3...]
    unnamed x15 -> x9, local copies, waits for them, and re-layouts: 4.3 us -> 0.83 us
    ppermute x3, waiting for transfers between devices: 1.94 us -> 5.08 us  [after(): return lax.ppermute(block, ('layer', 'pos'), route)]
    ppermute x15, starting transfers between devices: 17.4 us -> 20 us  [swap(): lax.ppermute(block, 'pos', [(i, i ^ bit) for i in range(lax.axis_size('po...]
    pallas_call x0 -> x3, Pallas kernels: none -> 2.52 us  [the longest x1 1.28 us: per_device(): pl.pallas_call(functools.partial(update_kernel, scale), out_shape=[jax.Sh...]
    ppermute x15, waiting for transfers between devices: 29.4 us -> 27.4 us  [swap(): lax.ppermute(block, 'pos', [(i, i ^ bit) for i in range(lax.axis_size('po...]
    pallas_call x1, Pallas kernels: 1.78 us -> 3.2 us  [per_device(): pl.pallas_call(functools.partial(grad_kernel, side), out_shape=[jax.Shape...]
    ppermute x3, starting transfers between devices: 7.07 us -> 5.87 us  [after(): return lax.ppermute(block, ('layer', 'pos'), route)]
  transfers between devices with their start and end apart: 18 -> 18, of which waited for: 12 -> 14; matrix products, arithmetic and copies ran while one was open for 8% -> 4% of each run, Pallas kernels for 0% -> 2%
where the time goes in v7:
time: 73.3 us; the launch traced here: 73 us
  waiting for transfers between devices  32.5 us (44%)
  starting transfers between devices  25.9 us (35%)
  Pallas kernels  7.41 us (10%)
  other arithmetic  3.95 us (5%)
  local copies, waits for them, and re-layouts  1.74 us (2%)
  between operations  0.93 us (1%)
    ppermute x15, waiting for transfers between devices, swap(): lax.ppermute(block, 'pos', [(i, i ^ bit) for i in range(lax.axis_size('po...  27.4 us
    ppermute x15, starting transfers between devices, swap(): lax.ppermute(block, 'pos', [(i, i ^ bit) for i in range(lax.axis_size('po...  20 us
    ppermute x3, starting transfers between devices, after(): return lax.ppermute(block, ('layer', 'pos'), route)  5.87 us
    ppermute x3, waiting for transfers between devices, after(): return lax.ppermute(block, ('layer', 'pos'), route)  5.08 us
    pallas_call x1, Pallas kernels, per_device(): pl.pallas_call(functools.partial(grad_kernel, side), out_shape=[jax.Shape...  3.2 us
    pallas_call x1, Pallas kernels, per_device(): pl.pallas_call(functools.partial(cross_kernel, side), out_shape=[jax.Shap...  1.69 us
  transfers between devices with their start and end apart: 18, of which 14 were waited for; matrix products, arithmetic and copies ran while one was open for 4% of the time, Pallas kernels for 2%

profile of v7, /device:TPU:0, one launch (start us, length us, event | category | flops | bytes accessed | tf_op | source)
XLA Modules:
  0.0 73.0 jit_solution(8318050664690406997)
XLA Ops:
  0.6 3.2 %shard_map.59 = (f32[2,32,1152]{2,1,0:T(8,128)}, f32[2,32,1152]{2,1,0:T(8,128)}) custom-call(bf16[512,128]{1,0:T(8,128)(2,1)} %bitcast.46, bf16[512,128]{1,0:T(8,128)(2,1)} %bitcast.44, f32[128,128]{1,0:T(8,128)} %bitcast.41), custom_call_target="tpu_custom_call" | custom-call | tf_op jit(solution)/shard_map/pallas_call | solution.py:218
  4.4 1.4 %collective-permute-done = f32[2,32,1152]{2,1,0:T(8,128)S(1)} collective-permute-done((f32[2,32,1152]{2,1,0:T(8,128)}, f32[2,32,1152]{2,1,0:T(8,128)S(1)}, u32[]{:S(2)}, u32[]{:S(2)}) %collective-permute-start) | collective-permute-done | bytes 294944 | tf_op jit(solution)/shard_map/ppermute | solution.py:26
  6.8 2.9 %collective-permute-start.2 = (f32[32,1152]{1,0:T(8,128)S(1)}, f32[32,1152]{1,0:T(8,128)S(1)}, u32[]{:S(2)}, u32[]{:S(2)}) collective-permute-start(f32[32,1152]{1,0:T(8,128)S(1)} %slice_bitcast_fusion), channel_id=1, source_target_pairs={{0,2},{1,3},{2,0},{3,1},{4,6},{5,7},{6,4},{7,5},{8,10},{9,11},{10,... | collective-permute-start | bytes 442376 | tf_op jit(solution)/shard_map/ppermute | solution.py:26
  10.8 1.5 %collective-permute-start.1 = (bf16[2,512,128]{2,1,0:T(8,128)(2,1)S(1)}, bf16[2,512,128]{2,1,0:T(8,128)(2,1)S(1)}, u32[]{:S(2)}, u32[]{:S(2)}) collective-permute-start(bf16[2,512,128]{2,1,0:T(8,128)(2,1)S(1)} %pad_maximum_fusion.2), channel_id=1, source_target_pairs={{16,0},{17,1},{18,2},{19,3},{20,4},{21,5},{22,6},{23,7},{24,8},{25... | collective-permute-start | bytes 786440 | tf_op jit(solution)/shard_map/ppermute | solution.py:22
  12.3 2.1 %collective-permute-done.2 = f32[32,1152]{1,0:T(8,128)S(1)} collective-permute-done((f32[32,1152]{1,0:T(8,128)S(1)}, f32[32,1152]{1,0:T(8,128)S(1)}, u32[]{:S(2)}, u32[]{:S(2)}) %collective-permute-start.2) | collective-permute-done | bytes 147488 | tf_op jit(solution)/shard_map/ppermute | solution.py:26
  14.4 2.2 %collective-permute-start.4 = (f32[32,1152]{1,0:T(8,128)S(1)}, f32[32,1152]{1,0:T(8,128)S(1)}, u32[]{:S(2)}, u32[]{:S(2)}) collective-permute-start(f32[32,1152]{1,0:T(8,128)S(1)} %fusion), channel_id=1, source_target_pairs={{0,4},{1,5},{2,6},{3,7},{4,0},{5,1},{6,2},{7,3},{8,12},{9,13},{10,... | collective-permute-start | bytes 442376 | tf_op jit(solution)/shard_map/ppermute | solution.py:26
  16.6 2.2 %collective-permute-done.1 = bf16[2,512,128]{2,1,0:T(8,128)(2,1)S(1)} collective-permute-done((bf16[2,512,128]{2,1,0:T(8,128)(2,1)S(1)}, bf16[2,512,128]{2,1,0:T(8,128)(2,1)S(1)}, u32[]{:S(2)}, u32[]{:S(2)}) %collective-permute-start.1) | collective-permute-done | bytes 262176 | tf_op jit(solution)/shard_map/ppermute | solution.py:22
  21.3 1.8 %collective-permute-start.3 = (bf16[4,512,128]{2,1,0:T(8,128)(2,1)S(1)}, bf16[4,512,128]{2,1,0:T(8,128)(2,1)S(1)}, u32[]{:S(2)}, u32[]{:S(2)}) collective-permute-start(bf16[4,512,128]{2,1,0:T(8,128)(2,1)S(1)} %pad_maximum_fusion.1), channel_id=1, source_target_pairs={{0,2},{1,3},{2,0},{3,1},{4,6},{5,7},{6,4},{7,5},{8,10},{9,11},{10,... | collective-permute-start | bytes 1572872 | tf_op jit(solution)/shard_map/ppermute | solution.py:26
  23.1 2.6 %collective-permute-start.5 = (f32[32,1152]{1,0:T(8,128)S(1)}, f32[32,1152]{1,0:T(8,128)S(1)}, u32[]{:S(2)}, u32[]{:S(2)}) collective-permute-start(f32[32,1152]{1,0:T(8,128)S(1)} %add.58), channel_id=1, source_target_pairs={{0,8},{1,9},{2,10},{3,11},{4,12},{5,13},{6,14},{7,15},{8,0},{9,1},... | collective-permute-start | bytes 442376 | tf_op jit(solution)/shard_map/ppermute | solution.py:26
  25.7 7.4 %collective-permute-done.5 = f32[32,1152]{1,0:T(8,128)S(1)} collective-permute-done((f32[32,1152]{1,0:T(8,128)S(1)}, f32[32,1152]{1,0:T(8,128)S(1)}, u32[]{:S(2)}, u32[]{:S(2)}) %collective-permute-start.5) | collective-permute-done | bytes 147488 | tf_op jit(solution)/shard_map/ppermute | solution.py:26
  33.9 1.8 %collective-permute-done.3 = bf16[4,512,128]{2,1,0:T(8,128)(2,1)S(1)} collective-permute-done((bf16[4,512,128]{2,1,0:T(8,128)(2,1)S(1)}, bf16[4,512,128]{2,1,0:T(8,128)(2,1)S(1)}, u32[]{:S(2)}, u32[]{:S(2)}) %collective-permute-start.3) | collective-permute-done | bytes 524320 | tf_op jit(solution)/shard_map/ppermute | solution.py:26
  35.8 1.9 %collective-permute-start.9 = (bf16[32,288]{1,0:T(8,128)(2,1)S(1)}, bf16[32,288]{1,0:T(8,128)(2,1)}, u32[]{:S(2)}, u32[]{:S(2)}) collective-permute-start(bf16[32,288]{1,0:T(8,128)(2,1)S(1)} %get-tuple-element.34), channel_id=1, source_target_pairs={{0,4},{1,5},{2,6},{3,7},{4,0},{5,1},{6,2},{7,3},{8,12},{9,13},{10,... | collective-permute-start | bytes 55304 | tf_op jit(solution)/shard_map/ppermute | solution.py:26
  37.7 2.1 %collective-permute-done.9 = bf16[32,288]{1,0:T(8,128)(2,1)} collective-permute-done((bf16[32,288]{1,0:T(8,128)(2,1)S(1)}, bf16[32,288]{1,0:T(8,128)(2,1)}, u32[]{:S(2)}, u32[]{:S(2)}) %collective-permute-start.9) | collective-permute-done | bytes 18464 | tf_op jit(solution)/shard_map/ppermute | solution.py:26
  40.7 1.8 %collective-permute-start.10 = (bf16[32,576]{1,0:T(8,128)(2,1)S(1)}, bf16[32,576]{1,0:T(8,128)(2,1)}, u32[]{:S(2)}, u32[]{:S(2)}) collective-permute-start(bf16[32,576]{1,0:T(8,128)(2,1)S(1)} %maximum_select_fusion.1), channel_id=1, source_target_pairs={{16,0},{17,1},{18,2},{19,3},{20,4},{21,5},{22,6},{23,7},{24,8},{25... | collective-permute-start | bytes 110600 | tf_op jit(solution)/shard_map/ppermute | solution.py:22
  42.6 2.5 %collective-permute-start.11 = (bf16[32,576]{1,0:T(8,128)(2,1)S(1)}, bf16[32,576]{1,0:T(8,128)(2,1)}, u32[]{:S(2)}, u32[]{:S(2)}) collective-permute-start(bf16[32,576]{1,0:T(8,128)(2,1)S(1)} %maximum_select_fusion.1), channel_id=1, source_target_pairs={{24,0},{25,1},{26,2},{27,3},{28,4},{29,5},{30,6},{31,7},{16,8},{17... | collective-permute-start | bytes 110600 | tf_op jit(solution)/shard_map/ppermute | solution.py:22
  45.6 2.9 %collective-permute-done.11 = bf16[32,576]{1,0:T(8,128)(2,1)} collective-permute-done((bf16[32,576]{1,0:T(8,128)(2,1)S(1)}, bf16[32,576]{1,0:T(8,128)(2,1)}, u32[]{:S(2)}, u32[]{:S(2)}) %collective-permute-start.11) | collective-permute-done | bytes 36896 | tf_op jit(solution)/shard_map/ppermute | solution.py:22
  49.4 1.7 %shard_map.62 = (f32[32,1408]{1,0:T(8,128)S(1)}, bf16[32,1664]{1,0:T(8,128)(2,1)S(1)}) custom-call(bf16[2,4,512,128]{3,2,1,0:T(8,128)(2,1)S(1)} %pad_maximum_fusion.half_a, bf16[2,4,512,128]{3,2,1,0:T(8,128)(2,1)S(1)} %collective-permute-done.8.half_b, bf16[32,1152]{1,0:T(8,128)(2,1)S(1)} %fusion.1.precond_t, f32[64,128]{1,0:T(8,128)S(1)} %shard_map.61.gram), custom_call_target="tpu_custom_call" | custom-call | tf_op jit(solution)/shard_map/pallas_call | solution.py:283
  51.1 1.6 %collective-permute-start.12 = (bf16[32,1664]{1,0:T(8,128)(2,1)S(1)}, bf16[32,1664]{1,0:T(8,128)(2,1)S(1)}, u32[]{:S(2)}, u32[]{:S(2)}) collective-permute-start(bf16[32,1664]{1,0:T(8,128)(2,1)S(1)} %get-tuple-element.42), channel_id=1, source_target_pairs={{0,4},{1,5},{2,6},{3,7},{4,0},{5,1},{6,2},{7,3},{8,12},{9,13},{10,... | collective-permute-start | bytes 319496 | tf_op jit(solution)/shard_map/ppermute | solution.py:26
  53.3 2.6 %collective-permute-done.12 = bf16[32,1664]{1,0:T(8,128)(2,1)S(1)} collective-permute-done((bf16[32,1664]{1,0:T(8,128)(2,1)S(1)}, bf16[32,1664]{1,0:T(8,128)(2,1)S(1)}, u32[]{:S(2)}, u32[]{:S(2)}) %collective-permute-start.12) | collective-permute-done | bytes 106528 | tf_op jit(solution)/shard_map/ppermute | solution.py:26
  56.0 3.1 %collective-permute-start.13 = (bf16[32,1664]{1,0:T(8,128)(2,1)S(1)}, bf16[32,1664]{1,0:T(8,128)(2,1)S(1)}, u32[]{:S(2)}, u32[]{:S(2)}) collective-permute-start(bf16[32,1664]{1,0:T(8,128)(2,1)S(1)} %pad_maximum_fusion.5), channel_id=1, source_target_pairs={{0,8},{1,9},{2,10},{3,11},{4,12},{5,13},{6,14},{7,15},{8,0},{9,1},... | collective-permute-start | bytes 319496 | tf_op jit(solution)/shard_map/ppermute | solution.py:26
  59.1 3.8 %collective-permute-done.13 = bf16[32,1664]{1,0:T(8,128)(2,1)S(1)} collective-permute-done((bf16[32,1664]{1,0:T(8,128)(2,1)S(1)}, bf16[32,1664]{1,0:T(8,128)(2,1)S(1)}, u32[]{:S(2)}, u32[]{:S(2)}) %collective-permute-start.13) | collective-permute-done | bytes 106528 | tf_op jit(solution)/shard_map/ppermute | solution.py:26
  65.1 1.5 %collective-permute-start.16 = (f32[32,256]{1,0:T(8,128)S(1)}, f32[32,256]{1,0:T(8,128)S(1)}, u32[]{:S(2)}, u32[]{:S(2)}) collective-permute-start(f32[32,256]{1,0:T(8,128)S(1)} %get-tuple-element.59), channel_id=1, source_target_pairs={{0,2},{1,3},{2,0},{3,1},{4,6},{5,7},{6,4},{7,5},{8,10},{9,11},{10,... | collective-permute-start | bytes 98312 | tf_op jit(solution)/shard_map/ppermute | solution.py:26
  67.2 1.9 %collective-permute-done.16 = f32[32,256]{1,0:T(8,128)S(1)} collective-permute-done((f32[32,256]{1,0:T(8,128)S(1)}, f32[32,256]{1,0:T(8,128)S(1)}, u32[]{:S(2)}, u32[]{:S(2)}) %collective-permute-start.16) | collective-permute-done | bytes 32800 | tf_op jit(solution)/shard_map/ppermute | solution.py:26
  69.2 1.8 %collective-permute-done.14 = f32[2,72,128]{2,1,0:T(8,128)S(1)} collective-permute-done((f32[2,72,128]{2,1,0:T(8,128)S(1)}, f32[2,72,128]{2,1,0:T(8,128)S(1)}, u32[]{:S(2)}, u32[]{:S(2)}) %collective-permute-start.14) | collective-permute-done | bytes 73760 | tf_op jit(solution)/shard_map/ppermute | solution.py:26
  (61 shorter events, 13.5 us)
Async XLA Ops:
  3.8 1.9 %collective-permute-start = (f32[2,32,1152]{2,1,0:T(8,128)}, f32[2,32,1152]{2,1,0:T(8,128)S(1)}, u32[]{:S(2)}, u32[]{:S(2)}) collective-permute-start(f32[2,32,1152]{2,1,0:T(8,128)} %get-tuple-element.27), channel_id=1, source_target_pairs={{0,1},{1,0},{2,3},{3,2},{4,5},{5,4},{6,7},{7,6},{8,9},{9,8},{10,11... | collective-permute-start | bytes 884744 | tf_op jit(solution)/shard_map/ppermute | solution.py:26
  6.8 3.0 %copy-start.1 = (bf16[1,2,16,16,128]{4,3,2,1,0:T(8,128)(2,1)S(1)}, bf16[1,2,16,16,128]{4,3,2,1,0:T(8,128)(2,1)}, u32[]{:S(2)}) copy-start(bf16[1,2,16,16,128]{4,3,2,1,0:T(8,128)(2,1)} %param.5) | copy-start | bytes 393220
  6.8 3.0 %copy-start.2 = (bf16[1,2,16,16,128]{4,3,2,1,0:T(8,128)(2,1)S(1)}, bf16[1,2,16,16,128]{4,3,2,1,0:T(8,128)(2,1)}, u32[]{:S(2)}) copy-start(bf16[1,2,16,16,128]{4,3,2,1,0:T(8,128)(2,1)} %param.4) | copy-start | bytes 393220
  6.8 3.0 %copy-start.3 = (f32[1,72,1152]{2,1,0:T(8,128)S(1)}, f32[1,72,1152]{2,1,0:T(8,128)}, u32[]{:S(2)}) copy-start(f32[1,72,1152]{2,1,0:T(8,128)} %param.6) | copy-start | bytes 995332
  6.8 7.6 %collective-permute-start.2 = (f32[32,1152]{1,0:T(8,128)S(1)}, f32[32,1152]{1,0:T(8,128)S(1)}, u32[]{:S(2)}, u32[]{:S(2)}) collective-permute-start(f32[32,1152]{1,0:T(8,128)S(1)} %slice_bitcast_fusion), channel_id=1, source_target_pairs={{0,2},{1,3},{2,0},{3,1},{4,6},{5,7},{6,4},{7,5},{8,10},{9,11},{10,... | collective-permute-start | bytes 442376 | tf_op jit(solution)/shard_map/ppermute | solution.py:26
  9.8 11.2 %collective-permute-start.6 = (f32[72,1152]{1,0:T(8,128)S(1)}, f32[72,1152]{1,0:T(8,128)S(1)}, u32[]{:S(2)}, u32[]{:S(2)}) collective-permute-start(f32[72,1152]{1,0:T(8,128)S(1)} %bitcast.49), channel_id=1, source_target_pairs={{0,2},{1,3},{2,0},{3,1},{4,6},{5,7},{6,4},{7,5},{8,10},{9,11},{10,... | collective-permute-start | bytes 995336 | tf_op jit(solution)/shard_map/ppermute | solution.py:26
  10.8 8.1 %collective-permute-start.1 = (bf16[2,512,128]{2,1,0:T(8,128)(2,1)S(1)}, bf16[2,512,128]{2,1,0:T(8,128)(2,1)S(1)}, u32[]{:S(2)}, u32[]{:S(2)}) collective-permute-start(bf16[2,512,128]{2,1,0:T(8,128)(2,1)S(1)} %pad_maximum_fusion.2), channel_id=1, source_target_pairs={{16,0},{17,1},{18,2},{19,3},{20,4},{21,5},{22,6},{23,7},{24,8},{25... | collective-permute-start | bytes 786440 | tf_op jit(solution)/shard_map/ppermute | solution.py:22
  14.4 5.3 %collective-permute-start.4 = (f32[32,1152]{1,0:T(8,128)S(1)}, f32[32,1152]{1,0:T(8,128)S(1)}, u32[]{:S(2)}, u32[]{:S(2)}) collective-permute-start(f32[32,1152]{1,0:T(8,128)S(1)} %fusion), channel_id=1, source_target_pairs={{0,4},{1,5},{2,6},{3,7},{4,0},{5,1},{6,2},{7,3},{8,12},{9,13},{10,... | collective-permute-start | bytes 442376 | tf_op jit(solution)/shard_map/ppermute | solution.py:26
  21.1 12.1 %collective-permute-start.7 = (f32[144,1152]{1,0:T(8,128)S(1)}, f32[144,1152]{1,0:T(8,128)S(1)}, u32[]{:S(2)}, u32[]{:S(2)}) collective-permute-start(f32[144,1152]{1,0:T(8,128)S(1)} %constant_dynamic-update-slice_fusion.k_a), channel_id=1, source_target_pairs={{0,1},{1,0},{2,3},{3,2},{4,5},{5,4},{6,7},{7,6},{8,9},{9,8},{10,11... | collective-permute-start | bytes 1990664 | tf_op jit(solution)/shard_map/ppermute | solution.py:26
  21.3 14.4 %collective-permute-start.3 = (bf16[4,512,128]{2,1,0:T(8,128)(2,1)S(1)}, bf16[4,512,128]{2,1,0:T(8,128)(2,1)S(1)}, u32[]{:S(2)}, u32[]{:S(2)}) collective-permute-start(bf16[4,512,128]{2,1,0:T(8,128)(2,1)S(1)} %pad_maximum_fusion.1), channel_id=1, source_target_pairs={{0,2},{1,3},{2,0},{3,1},{4,6},{5,7},{6,4},{7,5},{8,10},{9,11},{10,... | collective-permute-start | bytes 1572872 | tf_op jit(solution)/shard_map/ppermute | solution.py:26
  23.1 10.0 %collective-permute-start.5 = (f32[32,1152]{1,0:T(8,128)S(1)}, f32[32,1152]{1,0:T(8,128)S(1)}, u32[]{:S(2)}, u32[]{:S(2)}) collective-permute-start(f32[32,1152]{1,0:T(8,128)S(1)} %add.58), channel_id=1, source_target_pairs={{0,8},{1,9},{2,10},{3,11},{4,12},{5,13},{6,14},{7,15},{8,0},{9,1},... | collective-permute-start | bytes 442376 | tf_op jit(solution)/shard_map/ppermute | solution.py:26
  35.8 9.3 %collective-permute-start.8 = (bf16[2,4,512,128]{3,2,1,0:T(8,128)(2,1)S(1)}, bf16[2,4,512,128]{3,2,1,0:T(8,128)(2,1)S(1)}, u32[]{:S(2)}, u32[]{:S(2)}) collective-permute-start(bf16[2,4,512,128]{3,2,1,0:T(8,128)(2,1)S(1)} %pad_maximum_fusion.half_a), channel_id=1, source_target_pairs={{0,1},{1,0},{2,3},{3,2},{4,5},{5,4},{6,7},{7,6},{8,9},{9,8},{10,11... | collective-permute-start | bytes 3145736 | tf_op jit(solution)/shard_map/ppermute | solution.py:26
  35.8 4.0 %collective-permute-start.9 = (bf16[32,288]{1,0:T(8,128)(2,1)S(1)}, bf16[32,288]{1,0:T(8,128)(2,1)}, u32[]{:S(2)}, u32[]{:S(2)}) collective-permute-start(bf16[32,288]{1,0:T(8,128)(2,1)S(1)} %get-tuple-element.34), channel_id=1, source_target_pairs={{0,4},{1,5},{2,6},{3,7},{4,0},{5,1},{6,2},{7,3},{8,12},{9,13},{10,... | collective-permute-start | bytes 55304 | tf_op jit(solution)/shard_map/ppermute | solution.py:26
  40.7 4.9 %collective-permute-start.10 = (bf16[32,576]{1,0:T(8,128)(2,1)S(1)}, bf16[32,576]{1,0:T(8,128)(2,1)}, u32[]{:S(2)}, u32[]{:S(2)}) collective-permute-start(bf16[32,576]{1,0:T(8,128)(2,1)S(1)} %maximum_select_fusion.1), channel_id=1, source_target_pairs={{16,0},{17,1},{18,2},{19,3},{20,4},{21,5},{22,6},{23,7},{24,8},{25... | collective-permute-start | bytes 110600 | tf_op jit(solution)/shard_map/ppermute | solution.py:22
  42.6 5.9 %collective-permute-start.11 = (bf16[32,576]{1,0:T(8,128)(2,1)S(1)}, bf16[32,576]{1,0:T(8,128)(2,1)}, u32[]{:S(2)}, u32[]{:S(2)}) collective-permute-start(bf16[32,576]{1,0:T(8,128)(2,1)S(1)} %maximum_select_fusion.1), channel_id=1, source_target_pairs={{24,0},{25,1},{26,2},{27,3},{28,4},{29,5},{30,6},{31,7},{16,8},{17... | collective-permute-start | bytes 110600 | tf_op jit(solution)/shard_map/ppermute | solution.py:22
  51.1 4.8 %collective-permute-start.12 = (bf16[32,1664]{1,0:T(8,128)(2,1)S(1)}, bf16[32,1664]{1,0:T(8,128)(2,1)S(1)}, u32[]{:S(2)}, u32[]{:S(2)}) collective-permute-start(bf16[32,1664]{1,0:T(8,128)(2,1)S(1)} %get-tuple-element.42), channel_id=1, source_target_pairs={{0,4},{1,5},{2,6},{3,7},{4,0},{5,1},{6,2},{7,3},{8,12},{9,13},{10,... | collective-permute-start | bytes 319496 | tf_op jit(solution)/shard_map/ppermute | solution.py:26
  56.0 6.9 %collective-permute-start.13 = (bf16[32,1664]{1,0:T(8,128)(2,1)S(1)}, bf16[32,1664]{1,0:T(8,128)(2,1)S(1)}, u32[]{:S(2)}, u32[]{:S(2)}) collective-permute-start(bf16[32,1664]{1,0:T(8,128)(2,1)S(1)} %pad_maximum_fusion.5), channel_id=1, source_target_pairs={{0,8},{1,9},{2,10},{3,11},{4,12},{5,13},{6,14},{7,15},{8,0},{9,1},... | collective-permute-start | bytes 319496 | tf_op jit(solution)/shard_map/ppermute | solution.py:26
  63.0 0.8 %copy-start = (f32[1,128,128]{2,1,0:T(8,128)S(1)}, f32[1,128,128]{2,1,0:T(8,128)}, u32[]{:S(2)}) copy-start(f32[1,128,128]{2,1,0:T(8,128)} %param.7) | copy-start | bytes 196612
  65.1 4.0 %collective-permute-start.16 = (f32[32,256]{1,0:T(8,128)S(1)}, f32[32,256]{1,0:T(8,128)S(1)}, u32[]{:S(2)}, u32[]{:S(2)}) collective-permute-start(f32[32,256]{1,0:T(8,128)S(1)} %get-tuple-element.59), channel_id=1, source_target_pairs={{0,2},{1,3},{2,0},{3,1},{4,6},{5,7},{6,4},{7,5},{8,10},{9,11},{10,... | collective-permute-start | bytes 98312 | tf_op jit(solution)/shard_map/ppermute | solution.py:26
  66.7 4.4 %collective-permute-start.14 = (f32[2,72,128]{2,1,0:T(8,128)S(1)}, f32[2,72,128]{2,1,0:T(8,128)S(1)}, u32[]{:S(2)}, u32[]{:S(2)}) collective-permute-start(f32[2,72,128]{2,1,0:T(8,128)S(1)} %get-tuple-element.48), channel_id=1, source_target_pairs={{0,2},{1,3},{2,0},{3,1},{4,6},{5,7},{6,4},{7,5},{8,10},{9,11},{10,... | collective-permute-start | bytes 221192 | tf_op jit(solution)/shard_map/ppermute | solution.py:26
  69.1 2.0 %collective-permute-start.17 = (f32[2,32,256]{2,1,0:T(8,128)S(1)}, f32[2,32,256]{2,1,0:T(8,128)S(1)}, u32[]{:S(2)}, u32[]{:S(2)}) collective-permute-start(f32[2,32,256]{2,1,0:T(8,128)S(1)} %get-tuple-element.57), channel_id=1, source_target_pairs={{0,1},{1,0},{2,3},{3,2},{4,5},{5,4},{6,7},{7,6},{8,9},{9,8},{10,11... | collective-permute-start | bytes 196616 | tf_op jit(solution)/shard_map/ppermute | solution.py:26
  71.1 1.3 %collective-permute-start.15 = (f32[72,128]{1,0:T(8,128)S(1)}, f32[72,128]{1,0:T(8,128)S(1)}, u32[]{:S(2)}, u32[]{:S(2)}) collective-permute-start(f32[72,128]{1,0:T(8,128)S(1)} %slice_bitcast_fusion.2), channel_id=1, source_target_pairs={{0,1},{1,0},{2,3},{3,2},{4,5},{5,4},{6,7},{7,6},{8,9},{9,8},{10,11... | collective-permute-start | bytes 110600 | tf_op jit(solution)/shard_map/ppermute | solution.py:26

commit v8 on v7

--- a/solution.py
+++ b/solution.py
@@ -54,15 +54,48 @@
     return jnp.concatenate(moved, axis=0)
 
 
-def grad_kernel(side, maps_in, grads_in, g_in, keep, send, all_rows, maps, grads, g_inv, sems):
+def patches(maps, side):
+    count, width = maps.shape
+    wide = maps.astype(F32)
+    x = lax.broadcasted_iota(jnp.int32, (count, 1), 0) % side
+    area = side * side
+    edge = jnp.zeros((side, width), BF16)
+    columns = []
+    for s in range(3):
+        moved = maps
+        if s != 1:
+            inside = (x + (s - 1) >= 0) & (x + (s - 1) < side)
+            moved = jnp.where(inside, pltpu.roll(wide, (1 - s) % count, 0), 0.0).astype(BF16)
+        columns.append(moved)
+    pieces = []
+    for r in range(3):
+        for s in range(3):
+            parts = []
+            for first in range(0, count, area):
+                image = columns[s][first : first + area]
+                if r == 0:
+                    parts += [edge, image[: area - side]]
+                elif r == 1:
+                    parts += [image]
+                else:
+                    parts += [image[side:], edge]
+            pieces.append(jnp.concatenate(parts, axis=0))
+    return jnp.concatenate(pieces, axis=1)
+
+
+def grad_kernel(
+    side, maps_in, grads_in, g_in, k_in, keep, send, k_parts, all_rows, maps, grads, g_inv, k_rows, sems
+):
     copies = [
         pltpu.make_async_copy(source, target, sems.at[i])
-        for i, (source, target) in enumerate([(g_in, g_inv), (grads_in, grads), (maps_in, maps)])
+        for i, (source, target) in enumerate(
+            [(g_in, g_inv), (grads_in, grads), (maps_in, maps), (k_in, k_rows)]
+        )
     ]
     for copy in copies:
         copy.start()
-    for copy in copies:
-        copy.wait()
+    copies[0].wait()
+    copies[1].wait()
     width = maps.shape[1]
     g_t = g_inv[...]
     first = g_t.astype(BF16)
@@ -75,20 +108,20 @@
         return lax.dot_general(part, g, (((0,), (1,)), ((), ())), preferred_element_type=F32)
 
     mixed = mix(first) + (mix(second) + mix(third))
-    high = mixed.astype(BF16).astype(F32)
-    rows = taps_to_rows(jnp.concatenate([high, mixed - high], axis=0), side)
-    both = jnp.dot(rows, maps[...], preferred_element_type=F32)
-    for tap in range(9):
-        low = 2 * width * tap
-        all_rows[:, tap * width : (tap + 1) * width] = (
-            both[low : low + width] + both[low + width : low + 2 * width]
-        )
+    copies[2].wait()
+    both = jnp.dot(two_parts(mixed), patches(maps[...], side), preferred_element_type=F32)
+    all_rows[...] = both[:width] + both[width:]
     core, xbit = place_bits()
     mine = 2 * core + xbit
     quarter = width // 4
     for j in range(4):
         block = all_rows[pl.ds(pl.multiple_of((mine ^ j) * quarter, quarter), quarter), :]
         (keep if j < 2 else send)[j % 2] = block
+    copies[3].wait()
+    k = k_rows[...]
+    high = k.astype(BF16)
+    k_parts[0] = high
+    k_parts[1] = (k - high.astype(F32)).astype(BF16)
 
 
 def cross_kernel(side, half_a, half_b, precond_t, gram, out, out_half):
@@ -139,12 +172,11 @@
 def precond_kernel(scale, e_t, k_a, k_b, main_a, main_b, precond_t):
     core, xbit = place_bits()
     count = e_t.shape[0]
-    rows = k_a.shape[0] // 2
+    rows = k_a.shape[1] // 2
     parts = two_parts(e_t[...] * scale)
     total = None
     for flip, k, main in ((0, k_a, main_a), (1, k_b, main_b)):
-        k_parts = two_parts(k[...])
-        product = dot_nt(parts, k_parts[: 2 * rows]) + dot_nt(parts, k_parts[2 * rows :])
+        product = dot_nt(parts, k[0]) + dot_nt(parts, k[1])
         product = product[:count] + product[count:]
         main[...] = product
         source = lax.broadcasted_iota(jnp.int32, (2 * rows, 4 * rows), 0)
@@ -157,14 +189,13 @@
     precond_t[...] = total.astype(BF16)
 
 
-def update_kernel(scale, cross_t, gram, g_inv, k_a, k_b, main, keep, send):
-    rows = k_a.shape[0] // 2
-    mixed = jnp.dot(gram[...], g_inv[...], precision=HIGH) * (scale * scale)
+def update_kernel(cross_t, gram, g_inv, k_a, k_b, main, keep, send):
+    rows = k_a.shape[1] // 2
+    mixed = jnp.dot(gram[...], g_inv[...], precision=HIGH)
     mixed = jnp.concatenate([mixed, mixed], axis=0)
     parts = two_parts(cross_t[...])
     for i, k in enumerate((k_a, k_b)):
-        k_parts = two_parts(k[...])
-        product = dot_nt(k_parts[: 2 * rows], parts) + dot_nt(k_parts[2 * rows :], parts)
+        product = dot_nt(k[0], parts) + dot_nt(k[1], parts)
         result = main[i] - jnp.dot(product, mixed, precision=HIGH)
         keep[i] = result[:rows]
         send[i] = result[rows:]
@@ -191,9 +222,8 @@
 
 
 VMEM = pl.BlockSpec(memory_space=pltpu.VMEM)
-ANY = pl.BlockSpec(memory_space=pl.ANY)
-PARAMS = pltpu.CompilerParams(vmem_limit_bytes=32 * 1024 * 1024)
-ALONE = pltpu.CompilerParams(vmem_limit_bytes=60 * 1024 * 1024)
+HBM = pl.BlockSpec(memory_space=pltpu.HBM)
+PARAMS = pltpu.CompilerParams(vmem_limit_bytes=16 * 1024 * 1024)
 
 
 def per_device(layer_inputs, output_grads, input_inverse, grad_inverse):
@@ -215,33 +245,38 @@
     flat_maps = maps.reshape(-1, width)
     flat_grads = grads.reshape(-1, width)
 
-    keep, send = pl.pallas_call(
+    keep, send, k_own = pl.pallas_call(
         functools.partial(grad_kernel, side),
-        out_shape=[jax.ShapeDtypeStruct((2, quarter, full), F32)] * 2,
-        in_specs=[ANY] * 3,
-        out_specs=[VMEM] * 2,
+        out_shape=[jax.ShapeDtypeStruct((2, quarter, full), F32)] * 2
+        + [jax.ShapeDtypeStruct((2, rows, full), BF16)],
+        in_specs=[HBM] * 4,
+        out_specs=[VMEM] * 3,
         scratch_shapes=[
             pltpu.VMEM((width, full), F32),
             pltpu.VMEM(flat_maps.shape, BF16),
             pltpu.VMEM(flat_grads.shape, BF16),
             pltpu.VMEM(g_inv.shape, F32),
-            pltpu.SemaphoreType.DMA((3,)),
+            pltpu.VMEM(k_rows.shape, F32),
+            pltpu.SemaphoreType.DMA((4,)),
         ],
-        compiler_params=ALONE,
-    )(flat_maps, flat_grads, g_inv)
+        compiler_params=PARAMS,
+    )(flat_maps, flat_grads, g_inv, k_rows)
     h = keep + swap(send, 1)
-    k_rows = behind(k_rows, h)
-    k_x = swap(k_rows, 2)
+    k_own = behind(k_own, h)
+    k_x = swap(k_own, 2)
     own = behind(jnp.stack([flat_maps, flat_grads]), h)
     next_own = after(own)
     h = h[0] + swap(h[1], 2)
-    own, next_own = behind((own, next_own), h)
+    own, next_own, k_own = behind((own, next_own, k_own), h)
     two_own = jnp.stack([own[0], next_own[0], own[1], next_own[1]])
     two_x = swap(two_own, 2)
+    k_core = swap(k_own, 1)
     h = h + swap(h, zbits[0])
-    k_rows, k_x = behind((k_rows, k_x), h)
-    k_a = jnp.concatenate([k_rows, k_x], axis=0)
-    k_b = swap(k_a, 1)
+    k_own, k_x = behind((k_own, k_x), h)
+    k_a = jnp.concatenate([k_own, k_x], axis=1)
+    third = full // 3
+    k_pieces = [swap(k_x[:, :, i * third : (i + 1) * third], 1) for i in range(3)]
+    k_b = jnp.concatenate([k_core, jnp.concatenate(k_pieces, axis=2)], axis=1)
     for b in zbits[1:]:
         h = h + swap(h, b)
 
@@ -254,17 +289,16 @@
         compiler_params=PARAMS,
     )(h, k_a, k_b)
 
+    def by_bit(mine, other, b):
+        return jnp.where((me & b) == 0, jnp.concatenate([mine, other], 1), jnp.concatenate([other, mine], 1))
+
+    for b in zbits[:-1]:
+        p_t = by_bit(p_t, swap(p_t, b), b)
+
     two_own, two_x = behind((two_own, two_x), p_t)
     half_a = jnp.stack([two_own, two_x])
     half_b = swap(half_a, 1)
 
-    def by_bit(mine, other, b):
-        return jnp.where((me & b) == 0, jnp.concatenate([mine, other], 1), jnp.concatenate([other, mine], 1))
-
-    for b in zbits[:-1]:
-        p_t = by_bit(p_t, swap(p_t, b), b)
-
-    half_a, half_b = behind((half_a, half_b), p_t)
     gram = pl.pallas_call(
         gram_kernel,
         out_shape=jax.ShapeDtypeStruct((2 * quarter, width), F32),
@@ -293,6 +327,7 @@
 
     place = (jnp.arange(width)[None, :] == low + jnp.arange(quarter)[:, None]).astype(F32)
     main_a, main_b = behind((main_a, main_b), cross_half)
+    g_scaled = behind(g_inv, cross_half) * (scale * scale)
     main = jnp.stack([dot_t(main_a, place, precision=HIGH), dot_t(main_b, place, precision=HIGH)])
     cross_t, gram = cross_t[:, :full], cross_t[:, full:]
     for b in zbits:
@@ -305,12 +340,12 @@
         cross_half = jnp.concatenate([cross_t, high, rest], axis=1).astype(BF16)
 
     out, send = pl.pallas_call(
-        functools.partial(update_kernel, scale),
+        update_kernel,
         out_shape=[jax.ShapeDtypeStruct((2, rows, width), F32)] * 2,
         in_specs=[VMEM] * 6,
         out_specs=[VMEM] * 2,
         compiler_params=PARAMS,
-    )(cross_t, gram[:, width:], g_inv, k_a, k_b, main)
+    )(cross_t, gram[:, width:], g_scaled, k_a, k_b, main)
     gram = behind(gram, out) * scale
     gram = jnp.stack([gram, swap(gram, 2)])
     out = out + swap(send, 2)

time: 73.3 us -> 68.7 us (0.937)
  starting transfers between devices: 25.9 us -> 20.6 us
  local copies, waits for them, and re-layouts: 1.74 us -> 4.6 us
  Pallas kernels: 7.41 us -> 5.67 us
    ppermute x15 -> x18, starting transfers between devices: 20 us -> 15.4 us  [swap(): lax.ppermute(block, 'pos', [(i, i ^ bit) for i in range(lax.axis_size('po...]
    unnamed x9 -> x11, local copies, waits for them, and re-layouts: 0.83 us -> 3.65 us
    pallas_call x1, Pallas kernels: 3.2 us -> 1.46 us  [per_device(): pl.pallas_call(functools.partial(grad_kernel, side), out_shape=[jax.Shape...]
    another operation x1, other arithmetic: 0.1 us -> 1.14 us  [per_device(): half_a = jnp.stack([two_own, two_x])]
    add x1, other arithmetic: 1 us -> 0.03 us  [per_device(): h = keep + swap(send, 1)]
    select_n x1, other arithmetic: 0.9 us -> 0.09 us  [by_bit(): jnp.where(me & b == 0, jnp.concatenate([mine, other], 1), jnp.concatenate...]
    ppermute x15 -> x18, waiting for transfers between devices: 27.4 us -> 27.3 us  [swap(): lax.ppermute(block, 'pos', [(i, i ^ bit) for i in range(lax.axis_size('po...]
  transfers between devices with their start and end apart: 18 -> 21, of which waited for: 14 -> 14; matrix products, arithmetic and copies ran while one was open for 4% -> 3% of each run, Pallas kernels for 2% -> 2%
where the time goes in v8:
time: 68.7 us; the launch traced here: 68.3 us
  waiting for transfers between devices  32.7 us (48%)
  starting transfers between devices  20.6 us (30%)
  Pallas kernels  5.67 us (8%)
  local copies, waits for them, and re-layouts  4.6 us (7%)
  other arithmetic  3.25 us (5%)
  between operations  0.96 us (1%)
    ppermute x18, waiting for transfers between devices, swap(): lax.ppermute(block, 'pos', [(i, i ^ bit) for i in range(lax.axis_size('po...  27.3 us
    ppermute x18, starting transfers between devices, swap(): lax.ppermute(block, 'pos', [(i, i ^ bit) for i in range(lax.axis_size('po...  15.4 us
    ppermute x3, waiting for transfers between devices, after(): return lax.ppermute(block, ('layer', 'pos'), route)  5.48 us
    ppermute x3, starting transfers between devices, after(): return lax.ppermute(block, ('layer', 'pos'), route)  5.2 us
    unnamed x11, local copies, waits for them, and re-layouts  3.65 us
    pallas_call x1, Pallas kernels, per_device(): pl.pallas_call(functools.partial(cross_kernel, side), out_shape=[jax.Shap...  1.7 us
    pallas_call x1, Pallas kernels, per_device(): pl.pallas_call(functools.partial(grad_kernel, side), out_shape=[jax.Shape...  1.46 us
  transfers between devices with their start and end apart: 21, of which 14 were waited for; matrix products, arithmetic and copies ran while one was open for 3% of the time, Pallas kernels for 2%

profile of v8, /device:TPU:0, one launch (start us, length us, event | category | flops | bytes accessed | tf_op | source)
XLA Modules:
  0.0 68.3 jit_solution(1147333935443253217)
XLA Ops:
  4.3 1.5 %shard_map.59 = (f32[2,32,1152]{2,1,0:T(8,128)S(1)}, f32[2,32,1152]{2,1,0:T(8,128)S(1)}, bf16[2,72,1152]{2,1,0:T(8,128)(2,1)S(1)}) custom-call(bf16[512,128]{1,0:T(8,128)(2,1)S(1)} %bitcast.43, bf16[512,128]{1,0:T(8,128)(2,1)S(1)} %bitcast.41, f32[128,128]{1,0:T(8,128)S(1)} %bitcast.46, f32[72,1152]{1,0:T(8,128)S(1)} %bitcast.45), custom_call_target="tpu_custom_call" | custom-call | tf_op jit(solution)/shard_map/pallas_call | solution.py:248
  6.2 1.2 %collective-permute-done = f32[2,32,1152]{2,1,0:T(8,128)S(1)} collective-permute-done((f32[2,32,1152]{2,1,0:T(8,128)S(1)}, f32[2,32,1152]{2,1,0:T(8,128)S(1)}, u32[]{:S(2)}, u32[]{:S(2)}) %collective-permute-start) | collective-permute-done | bytes 294944 | tf_op jit(solution)/shard_map/ppermute | solution.py:26
  7.5 2.9 %collective-permute-start.2 = (f32[32,1152]{1,0:T(8,128)S(1)}, f32[32,1152]{1,0:T(8,128)S(1)}, u32[]{:S(2)}, u32[]{:S(2)}) collective-permute-start(f32[32,1152]{1,0:T(8,128)S(1)} %slice_bitcast_fusion), channel_id=1, source_target_pairs={{0,2},{1,3},{2,0},{3,1},{4,6},{5,7},{6,4},{7,5},{8,10},{9,11},{10,... | collective-permute-start | bytes 442376 | tf_op jit(solution)/shard_map/ppermute | solution.py:26
  10.5 1.6 %collective-permute-start.1 = (bf16[2,512,128]{2,1,0:T(8,128)(2,1)S(1)}, bf16[2,512,128]{2,1,0:T(8,128)(2,1)S(1)}, u32[]{:S(2)}, u32[]{:S(2)}) collective-permute-start(bf16[2,512,128]{2,1,0:T(8,128)(2,1)S(1)} %pad_maximum_fusion.2), channel_id=1, source_target_pairs={{16,0},{17,1},{18,2},{19,3},{20,4},{21,5},{22,6},{23,7},{24,8},{25... | collective-permute-start | bytes 786440 | tf_op jit(solution)/shard_map/ppermute | solution.py:22
  12.6 2.3 %collective-permute-done.2 = f32[32,1152]{1,0:T(8,128)S(1)} collective-permute-done((f32[32,1152]{1,0:T(8,128)S(1)}, f32[32,1152]{1,0:T(8,128)S(1)}, u32[]{:S(2)}, u32[]{:S(2)}) %collective-permute-start.2) | collective-permute-done | bytes 147488 | tf_op jit(solution)/shard_map/ppermute | solution.py:26
  14.9 2.1 %collective-permute-start.4 = (f32[32,1152]{1,0:T(8,128)S(1)}, f32[32,1152]{1,0:T(8,128)S(1)}, u32[]{:S(2)}, u32[]{:S(2)}) collective-permute-start(f32[32,1152]{1,0:T(8,128)S(1)} %fusion), channel_id=1, source_target_pairs={{0,4},{1,5},{2,6},{3,7},{4,0},{5,1},{6,2},{7,3},{8,12},{9,13},{10,... | collective-permute-start | bytes 442376 | tf_op jit(solution)/shard_map/ppermute | solution.py:26
  17.0 1.5 %collective-permute-done.1 = bf16[2,512,128]{2,1,0:T(8,128)(2,1)S(1)} collective-permute-done((bf16[2,512,128]{2,1,0:T(8,128)(2,1)S(1)}, bf16[2,512,128]{2,1,0:T(8,128)(2,1)S(1)}, u32[]{:S(2)}, u32[]{:S(2)}) %collective-permute-start.1) | collective-permute-done | bytes 262176 | tf_op jit(solution)/shard_map/ppermute | solution.py:22
  19.1 1.1 %collective-permute-done.4 = f32[32,1152]{1,0:T(8,128)S(1)} collective-permute-done((f32[32,1152]{1,0:T(8,128)S(1)}, f32[32,1152]{1,0:T(8,128)S(1)}, u32[]{:S(2)}, u32[]{:S(2)}) %collective-permute-start.4) | collective-permute-done | bytes 147488 | tf_op jit(solution)/shard_map/ppermute | solution.py:26
  20.2 3.1 %collective-permute-start.5 = (f32[32,1152]{1,0:T(8,128)S(1)}, f32[32,1152]{1,0:T(8,128)S(1)}, u32[]{:S(2)}, u32[]{:S(2)}) collective-permute-start(f32[32,1152]{1,0:T(8,128)S(1)} %add.58), channel_id=1, source_target_pairs={{0,8},{1,9},{2,10},{3,11},{4,12},{5,13},{6,14},{7,15},{8,0},{9,1},... | collective-permute-start | bytes 442376 | tf_op jit(solution)/shard_map/ppermute | solution.py:26
  23.9 5.5 %collective-permute-done.5 = f32[32,1152]{1,0:T(8,128)S(1)} collective-permute-done((f32[32,1152]{1,0:T(8,128)S(1)}, f32[32,1152]{1,0:T(8,128)S(1)}, u32[]{:S(2)}, u32[]{:S(2)}) %collective-permute-start.5) | collective-permute-done | bytes 147488 | tf_op jit(solution)/shard_map/ppermute | solution.py:26
  29.5 1.2 %collective-permute-done.9 = bf16[2,72,384]{2,1,0:T(8,128)(2,1)S(1)} collective-permute-done((bf16[2,72,384]{2,1,0:T(8,128)(2,1)S(1)}, bf16[2,72,384]{2,1,0:T(8,128)(2,1)S(1)}, u32[]{:S(2)}, u32[]{:S(2)}) %collective-permute-start.9) | collective-permute-done | bytes 110624 | tf_op jit(solution)/shard_map/ppermute | solution.py:26
  32.3 3.1 %collective-permute-done.11 = bf16[32,288]{1,0:T(8,128)(2,1)S(1)} collective-permute-done((bf16[32,288]{1,0:T(8,128)(2,1)S(1)}, bf16[32,288]{1,0:T(8,128)(2,1)S(1)}, u32[]{:S(2)}, u32[]{:S(2)}) %collective-permute-start.11) | collective-permute-done | bytes 18464 | tf_op jit(solution)/shard_map/ppermute | solution.py:26
  35.5 1.1 %pad_maximum_fusion.half_a = bf16[2,4,512,128]{3,2,1,0:T(8,128)(2,1)S(1)} fusion(bf16[1,4,512,128]{3,2,1,0:T(8,128)(2,1)} %bitcast.9, bf16[1,4,512,128]{3,2,1,0:T(8,128)(2,1)S(1)} %bitcast.48), kind=kLoop, calls=%fused_computation.2 | loop fusion | flops 524288 | bytes 2097152 | tf_op jit(solution)/shard_map/stack | solution.py:299
  36.7 1.6 %collective-permute-start.13 = (bf16[32,576]{1,0:T(8,128)(2,1)S(1)}, bf16[32,576]{1,0:T(8,128)(2,1)}, u32[]{:S(2)}, u32[]{:S(2)}) collective-permute-start(bf16[32,576]{1,0:T(8,128)(2,1)S(1)} %maximum_select_fusion.1), channel_id=1, source_target_pairs={{16,0},{17,1},{18,2},{19,3},{20,4},{21,5},{22,6},{23,7},{24,8},{25... | collective-permute-start | bytes 110600 | tf_op jit(solution)/shard_map/ppermute | solution.py:22
  38.3 2.0 %collective-permute-start.14 = (bf16[32,576]{1,0:T(8,128)(2,1)S(1)}, bf16[32,576]{1,0:T(8,128)(2,1)}, u32[]{:S(2)}, u32[]{:S(2)}) collective-permute-start(bf16[32,576]{1,0:T(8,128)(2,1)S(1)} %maximum_select_fusion.1), channel_id=1, source_target_pairs={{24,0},{25,1},{26,2},{27,3},{28,4},{29,5},{30,6},{31,7},{16,8},{17... | collective-permute-start | bytes 110600 | tf_op jit(solution)/shard_map/ppermute | solution.py:22
  40.9 3.9 %collective-permute-done.14 = bf16[32,576]{1,0:T(8,128)(2,1)} collective-permute-done((bf16[32,576]{1,0:T(8,128)(2,1)S(1)}, bf16[32,576]{1,0:T(8,128)(2,1)}, u32[]{:S(2)}, u32[]{:S(2)}) %collective-permute-start.14) | collective-permute-done | bytes 36896 | tf_op jit(solution)/shard_map/ppermute | solution.py:22
  45.7 1.7 %shard_map.62 = (f32[32,1408]{1,0:T(8,128)S(1)}, bf16[32,1664]{1,0:T(8,128)(2,1)S(1)}) custom-call(bf16[2,4,512,128]{3,2,1,0:T(8,128)(2,1)S(1)} %pad_maximum_fusion.half_a, bf16[2,4,512,128]{3,2,1,0:T(8,128)(2,1)S(1)} %collective-permute-done.12.half_b, bf16[32,1152]{1,0:T(8,128)(2,1)S(1)} %fusion.1.precond_t, f32[64,128]{1,0:T(8,128)S(1)} %shard_map.61.gram), custom_call_target="tpu_custom_call" | custom-call | tf_op jit(solution)/shard_map/pallas_call | solution.py:317
  48.2 3.9 %collective-permute-done.15 = bf16[32,1664]{1,0:T(8,128)(2,1)S(1)} collective-permute-done((bf16[32,1664]{1,0:T(8,128)(2,1)S(1)}, bf16[32,1664]{1,0:T(8,128)(2,1)S(1)}, u32[]{:S(2)}, u32[]{:S(2)}) %collective-permute-start.15) | collective-permute-done | bytes 106528 | tf_op jit(solution)/shard_map/ppermute | solution.py:26
  52.3 1.9 %collective-permute-start.16 = (bf16[32,1664]{1,0:T(8,128)(2,1)S(1)}, bf16[32,1664]{1,0:T(8,128)(2,1)S(1)}, u32[]{:S(2)}, u32[]{:S(2)}) collective-permute-start(bf16[32,1664]{1,0:T(8,128)(2,1)S(1)} %pad_maximum_fusion.5), channel_id=1, source_target_pairs={{0,8},{1,9},{2,10},{3,11},{4,12},{5,13},{6,14},{7,15},{8,0},{9,1},... | collective-permute-start | bytes 319496 | tf_op jit(solution)/shard_map/ppermute | solution.py:26
  54.2 4.9 %collective-permute-done.16 = bf16[32,1664]{1,0:T(8,128)(2,1)S(1)} collective-permute-done((bf16[32,1664]{1,0:T(8,128)(2,1)S(1)}, bf16[32,1664]{1,0:T(8,128)(2,1)S(1)}, u32[]{:S(2)}, u32[]{:S(2)}) %collective-permute-start.16) | collective-permute-done | bytes 106528 | tf_op jit(solution)/shard_map/ppermute | solution.py:26
  59.2 1.3 %shard_map.63 = (f32[2,72,128]{2,1,0:T(8,128)S(1)}, f32[2,72,128]{2,1,0:T(8,128)S(1)}) custom-call(f32[32,1152]{1,0:T(8,128)S(1)} %slice_add_fusion.cross_t, f32[32,128]{1,0:T(8,128)S(1)} %slice.88.gram, f32[128,128]{1,0:T(8,128)S(1)} %broadcast_multiply_fusion.g_inv, bf16[2,144,1152]{2,1,0:T(8,128)(2,1)S(1)} %constant_dynamic-update-slice_fusion.k_a, ...), custom_call_target="tpu_custom_call" | custom-call | tf_op jit(solution)/shard_map/pallas_call | solution.py:342
  60.5 1.6 %collective-permute-start.19 = (f32[32,256]{1,0:T(8,128)S(1)}, f32[32,256]{1,0:T(8,128)S(1)}, u32[]{:S(2)}, u32[]{:S(2)}) collective-permute-start(f32[32,256]{1,0:T(8,128)S(1)} %get-tuple-element.64), channel_id=1, source_target_pairs={{0,2},{1,3},{2,0},{3,1},{4,6},{5,7},{6,4},{7,5},{8,10},{9,11},{10,... | collective-permute-start | bytes 98312 | tf_op jit(solution)/shard_map/ppermute | solution.py:26
  62.6 1.9 %collective-permute-done.19 = f32[32,256]{1,0:T(8,128)S(1)} collective-permute-done((f32[32,256]{1,0:T(8,128)S(1)}, f32[32,256]{1,0:T(8,128)S(1)}, u32[]{:S(2)}, u32[]{:S(2)}) %collective-permute-start.19) | collective-permute-done | bytes 32800 | tf_op jit(solution)/shard_map/ppermute | solution.py:26
  64.6 1.8 %collective-permute-done.17 = f32[2,72,128]{2,1,0:T(8,128)S(1)} collective-permute-done((f32[2,72,128]{2,1,0:T(8,128)S(1)}, f32[2,72,128]{2,1,0:T(8,128)S(1)}, u32[]{:S(2)}, u32[]{:S(2)}) %collective-permute-start.17) | collective-permute-done | bytes 73760 | tf_op jit(solution)/shard_map/ppermute | solution.py:26
  (72 shorter events, 12.6 us)
Async XLA Ops:
  0.6 0.9 %copy-start = (bf16[1,2,16,16,128]{4,3,2,1,0:T(8,128)(2,1)S(1)}, bf16[1,2,16,16,128]{4,3,2,1,0:T(8,128)(2,1)}, u32[]{:S(2)}) copy-start(bf16[1,2,16,16,128]{4,3,2,1,0:T(8,128)(2,1)} %param.5) | copy-start | bytes 393220
  2.4 1.0 %copy-start.2 = (f32[1,72,1152]{2,1,0:T(8,128)S(1)}, f32[1,72,1152]{2,1,0:T(8,128)}, u32[]{:S(2)}) copy-start(f32[1,72,1152]{2,1,0:T(8,128)} %param.6) | copy-start | bytes 995332
  5.7 1.7 %collective-permute-start = (f32[2,32,1152]{2,1,0:T(8,128)S(1)}, f32[2,32,1152]{2,1,0:T(8,128)S(1)}, u32[]{:S(2)}, u32[]{:S(2)}) collective-permute-start(f32[2,32,1152]{2,1,0:T(8,128)S(1)} %get-tuple-element.28), channel_id=1, source_target_pairs={{0,1},{1,0},{2,3},{3,2},{4,5},{5,4},{6,7},{7,6},{8,9},{9,8},{10,11... | collective-permute-start | bytes 884744 | tf_op jit(solution)/shard_map/ppermute | solution.py:26
  7.5 7.4 %collective-permute-start.2 = (f32[32,1152]{1,0:T(8,128)S(1)}, f32[32,1152]{1,0:T(8,128)S(1)}, u32[]{:S(2)}, u32[]{:S(2)}) collective-permute-start(f32[32,1152]{1,0:T(8,128)S(1)} %slice_bitcast_fusion), channel_id=1, source_target_pairs={{0,2},{1,3},{2,0},{3,1},{4,6},{5,7},{6,4},{7,5},{8,10},{9,11},{10,... | collective-permute-start | bytes 442376 | tf_op jit(solution)/shard_map/ppermute | solution.py:26
  10.5 8.1 %collective-permute-start.1 = (bf16[2,512,128]{2,1,0:T(8,128)(2,1)S(1)}, bf16[2,512,128]{2,1,0:T(8,128)(2,1)S(1)}, u32[]{:S(2)}, u32[]{:S(2)}) collective-permute-start(bf16[2,512,128]{2,1,0:T(8,128)(2,1)S(1)} %pad_maximum_fusion.2), channel_id=1, source_target_pairs={{16,0},{17,1},{18,2},{19,3},{20,4},{21,5},{22,6},{23,7},{24,8},{25... | collective-permute-start | bytes 786440 | tf_op jit(solution)/shard_map/ppermute | solution.py:22
  12.0 11.2 %collective-permute-start.6 = (bf16[2,72,1152]{2,1,0:T(8,128)(2,1)S(1)}, bf16[2,72,1152]{2,1,0:T(8,128)(2,1)S(1)}, u32[]{:S(2)}, u32[]{:S(2)}) collective-permute-start(bf16[2,72,1152]{2,1,0:T(8,128)(2,1)S(1)} %get-tuple-element.35), channel_id=1, source_target_pairs={{0,2},{1,3},{2,0},{3,1},{4,6},{5,7},{6,4},{7,5},{8,10},{9,11},{10,... | collective-permute-start | bytes 995336 | tf_op jit(solution)/shard_map/ppermute | solution.py:26
  14.9 5.3 %collective-permute-start.4 = (f32[32,1152]{1,0:T(8,128)S(1)}, f32[32,1152]{1,0:T(8,128)S(1)}, u32[]{:S(2)}, u32[]{:S(2)}) collective-permute-start(f32[32,1152]{1,0:T(8,128)S(1)} %fusion), channel_id=1, source_target_pairs={{0,4},{1,5},{2,6},{3,7},{4,0},{5,1},{6,2},{7,3},{8,12},{9,13},{10,... | collective-permute-start | bytes 442376 | tf_op jit(solution)/shard_map/ppermute | solution.py:26
  18.6 12.1 %collective-permute-start.7 = (bf16[2,72,1152]{2,1,0:T(8,128)(2,1)S(1)}, bf16[2,72,1152]{2,1,0:T(8,128)(2,1)S(1)}, u32[]{:S(2)}, u32[]{:S(2)}) collective-permute-start(bf16[2,72,1152]{2,1,0:T(8,128)(2,1)S(1)} %get-tuple-element.35), channel_id=1, source_target_pairs={{0,1},{1,0},{2,3},{3,2},{4,5},{5,4},{6,7},{7,6},{8,9},{9,8},{10,11... | collective-permute-start | bytes 995336 | tf_op jit(solution)/shard_map/ppermute | solution.py:26
  18.7 16.8 %collective-permute-start.3 = (bf16[4,512,128]{2,1,0:T(8,128)(2,1)S(1)}, bf16[4,512,128]{2,1,0:T(8,128)(2,1)}, u32[]{:S(2)}, u32[]{:S(2)}) collective-permute-start(bf16[4,512,128]{2,1,0:T(8,128)(2,1)S(1)} %pad_maximum_fusion.1), channel_id=1, source_target_pairs={{0,2},{1,3},{2,0},{3,1},{4,6},{5,7},{6,4},{7,5},{8,10},{9,11},{10,... | collective-permute-start | bytes 1572872 | tf_op jit(solution)/shard_map/ppermute | solution.py:26
  20.2 9.2 %collective-permute-start.5 = (f32[32,1152]{1,0:T(8,128)S(1)}, f32[32,1152]{1,0:T(8,128)S(1)}, u32[]{:S(2)}, u32[]{:S(2)}) collective-permute-start(f32[32,1152]{1,0:T(8,128)S(1)} %add.58), channel_id=1, source_target_pairs={{0,8},{1,9},{2,10},{3,11},{4,12},{5,13},{6,14},{7,15},{8,0},{9,1},... | collective-permute-start | bytes 442376 | tf_op jit(solution)/shard_map/ppermute | solution.py:26
  23.3 6.1 %collective-permute-start.10 = (bf16[2,72,384]{2,1,0:T(8,128)(2,1)S(1)}, bf16[2,72,384]{2,1,0:T(8,128)(2,1)S(1)}, u32[]{:S(2)}, u32[]{:S(2)}) collective-permute-start(bf16[2,72,384]{2,1,0:T(8,128)(2,1)S(1)} %get-tuple-element.55), channel_id=1, source_target_pairs={{0,1},{1,0},{2,3},{3,2},{4,5},{5,4},{6,7},{7,6},{8,9},{9,8},{10,11... | collective-permute-start | bytes 331784 | tf_op jit(solution)/shard_map/ppermute | solution.py:26
  23.4 6.1 %collective-permute-start.8 = (bf16[2,72,384]{2,1,0:T(8,128)(2,1)S(1)}, bf16[2,72,384]{2,1,0:T(8,128)(2,1)S(1)}, u32[]{:S(2)}, u32[]{:S(2)}) collective-permute-start(bf16[2,72,384]{2,1,0:T(8,128)(2,1)S(1)} %get-tuple-element.54), channel_id=1, source_target_pairs={{0,1},{1,0},{2,3},{3,2},{4,5},{5,4},{6,7},{7,6},{8,9},{9,8},{10,11... | collective-permute-start | bytes 331784 | tf_op jit(solution)/shard_map/ppermute | solution.py:26
  29.4 1.3 %collective-permute-start.9 = (bf16[2,72,384]{2,1,0:T(8,128)(2,1)S(1)}, bf16[2,72,384]{2,1,0:T(8,128)(2,1)S(1)}, u32[]{:S(2)}, u32[]{:S(2)}) collective-permute-start(bf16[2,72,384]{2,1,0:T(8,128)(2,1)S(1)} %get-tuple-element.56), channel_id=1, source_target_pairs={{0,1},{1,0},{2,3},{3,2},{4,5},{5,4},{6,7},{7,6},{8,9},{9,8},{10,11... | collective-permute-start | bytes 331784 | tf_op jit(solution)/shard_map/ppermute | solution.py:26
  31.5 3.9 %collective-permute-start.11 = (bf16[32,288]{1,0:T(8,128)(2,1)S(1)}, bf16[32,288]{1,0:T(8,128)(2,1)S(1)}, u32[]{:S(2)}, u32[]{:S(2)}) collective-permute-start(bf16[32,288]{1,0:T(8,128)(2,1)S(1)} %get-tuple-element.37), channel_id=1, source_target_pairs={{0,4},{1,5},{2,6},{3,7},{4,0},{5,1},{6,2},{7,3},{8,12},{9,13},{10,... | collective-permute-start | bytes 55304 | tf_op jit(solution)/shard_map/ppermute | solution.py:26
  36.6 3.7 %collective-permute-start.12 = (bf16[2,4,512,128]{3,2,1,0:T(8,128)(2,1)S(1)}, bf16[2,4,512,128]{3,2,1,0:T(8,128)(2,1)S(1)}, u32[]{:S(2)}, u32[]{:S(2)}) collective-permute-start(bf16[2,4,512,128]{3,2,1,0:T(8,128)(2,1)S(1)} %pad_maximum_fusion.half_a), channel_id=1, source_target_pairs={{0,1},{1,0},{2,3},{3,2},{4,5},{5,4},{6,7},{7,6},{8,9},{9,8},{10,11... | collective-permute-start | bytes 3145736 | tf_op jit(solution)/shard_map/ppermute | solution.py:26
  36.7 4.2 %collective-permute-start.13 = (bf16[32,576]{1,0:T(8,128)(2,1)S(1)}, bf16[32,576]{1,0:T(8,128)(2,1)}, u32[]{:S(2)}, u32[]{:S(2)}) collective-permute-start(bf16[32,576]{1,0:T(8,128)(2,1)S(1)} %maximum_select_fusion.1), channel_id=1, source_target_pairs={{16,0},{17,1},{18,2},{19,3},{20,4},{21,5},{22,6},{23,7},{24,8},{25... | collective-permute-start | bytes 110600 | tf_op jit(solution)/shard_map/ppermute | solution.py:22
  38.3 6.4 %collective-permute-start.14 = (bf16[32,576]{1,0:T(8,128)(2,1)S(1)}, bf16[32,576]{1,0:T(8,128)(2,1)}, u32[]{:S(2)}, u32[]{:S(2)}) collective-permute-start(bf16[32,576]{1,0:T(8,128)(2,1)S(1)} %maximum_select_fusion.1), channel_id=1, source_target_pairs={{24,0},{25,1},{26,2},{27,3},{28,4},{29,5},{30,6},{31,7},{16,8},{17... | collective-permute-start | bytes 110600 | tf_op jit(solution)/shard_map/ppermute | solution.py:22
  45.7 2.0 %copy-start.4 = (f32[1,128,128]{2,1,0:T(8,128)S(1)}, f32[1,128,128]{2,1,0:T(8,128)}, u32[]{:S(2)}) copy-start(f32[1,128,128]{2,1,0:T(8,128)} %param.7) | copy-start | bytes 196612
  47.4 4.8 %collective-permute-start.15 = (bf16[32,1664]{1,0:T(8,128)(2,1)S(1)}, bf16[32,1664]{1,0:T(8,128)(2,1)S(1)}, u32[]{:S(2)}, u32[]{:S(2)}) collective-permute-start(bf16[32,1664]{1,0:T(8,128)(2,1)S(1)} %get-tuple-element.43), channel_id=1, source_target_pairs={{0,4},{1,5},{2,6},{3,7},{4,0},{5,1},{6,2},{7,3},{8,12},{9,13},{10,... | collective-permute-start | bytes 319496 | tf_op jit(solution)/shard_map/ppermute | solution.py:26
  52.3 6.8 %collective-permute-start.16 = (bf16[32,1664]{1,0:T(8,128)(2,1)S(1)}, bf16[32,1664]{1,0:T(8,128)(2,1)S(1)}, u32[]{:S(2)}, u32[]{:S(2)}) collective-permute-start(bf16[32,1664]{1,0:T(8,128)(2,1)S(1)} %pad_maximum_fusion.5), channel_id=1, source_target_pairs={{0,8},{1,9},{2,10},{3,11},{4,12},{5,13},{6,14},{7,15},{8,0},{9,1},... | collective-permute-start | bytes 319496 | tf_op jit(solution)/shard_map/ppermute | solution.py:26
  60.5 4.0 %collective-permute-start.19 = (f32[32,256]{1,0:T(8,128)S(1)}, f32[32,256]{1,0:T(8,128)S(1)}, u32[]{:S(2)}, u32[]{:S(2)}) collective-permute-start(f32[32,256]{1,0:T(8,128)S(1)} %get-tuple-element.64), channel_id=1, source_target_pairs={{0,2},{1,3},{2,0},{3,1},{4,6},{5,7},{6,4},{7,5},{8,10},{9,11},{10,... | collective-permute-start | bytes 98312 | tf_op jit(solution)/shard_map/ppermute | solution.py:26
  62.0 4.4 %collective-permute-start.17 = (f32[2,72,128]{2,1,0:T(8,128)S(1)}, f32[2,72,128]{2,1,0:T(8,128)S(1)}, u32[]{:S(2)}, u32[]{:S(2)}) collective-permute-start(f32[2,72,128]{2,1,0:T(8,128)S(1)} %get-tuple-element.50), channel_id=1, source_target_pairs={{0,2},{1,3},{2,0},{3,1},{4,6},{5,7},{6,4},{7,5},{8,10},{9,11},{10,... | collective-permute-start | bytes 221192 | tf_op jit(solution)/shard_map/ppermute | solution.py:26
  64.5 2.0 %collective-permute-start.20 = (f32[2,32,256]{2,1,0:T(8,128)S(1)}, f32[2,32,256]{2,1,0:T(8,128)S(1)}, u32[]{:S(2)}, u32[]{:S(2)}) collective-permute-start(f32[2,32,256]{2,1,0:T(8,128)S(1)} %get-tuple-element.62), channel_id=1, source_target_pairs={{0,1},{1,0},{2,3},{3,2},{4,5},{5,4},{6,7},{7,6},{8,9},{9,8},{10,11... | collective-permute-start | bytes 196616 | tf_op jit(solution)/shard_map/ppermute | solution.py:26
  66.4 1.3 %collective-permute-start.18 = (f32[72,128]{1,0:T(8,128)S(1)}, f32[72,128]{1,0:T(8,128)S(1)}, u32[]{:S(2)}, u32[]{:S(2)}) collective-permute-start(f32[72,128]{1,0:T(8,128)S(1)} %slice_bitcast_fusion.2), channel_id=1, source_target_pairs={{0,1},{1,0},{2,3},{3,2},{4,5},{5,4},{6,7},{7,6},{8,9},{9,8},{10,11... | collective-permute-start | bytes 110600 | tf_op jit(solution)/shard_map/ppermute | solution.py:26
  (2 other events, 1.7 us)

commit v9 on v8

--- a/solution.py
+++ b/solution.py
@@ -10,6 +10,8 @@
 F32 = jnp.float32
 BF16 = jnp.bfloat16
 HIGH = lax.Precision.HIGHEST
+F16 = jnp.float16
+TOP = 13.0
 
 
 def behind(block, point):
@@ -83,8 +85,13 @@
     return jnp.concatenate(pieces, axis=1)
 
 
+def exponent(block):
+    top = jnp.maximum(jnp.max(jnp.abs(block)), 1e-30)
+    return jnp.ceil(jnp.log2(top))
+
+
 def grad_kernel(
-    side, maps_in, grads_in, g_in, k_in, keep, send, k_parts, all_rows, maps, grads, g_inv, k_rows, sems
+    side, maps_in, grads_in, g_in, k_in, keep, send, k_parts, k_send, all_rows, maps, grads, g_inv, k_rows, sems
 ):
     copies = [
         pltpu.make_async_copy(source, target, sems.at[i])
@@ -110,41 +117,52 @@
     mixed = mix(first) + (mix(second) + mix(third))
     copies[2].wait()
     both = jnp.dot(two_parts(mixed), patches(maps[...], side), preferred_element_type=F32)
-    all_rows[...] = both[:width] + both[width:]
+    both = both[:width] + both[width:]
+    all_rows[...] = both
     core, xbit = place_bits()
     mine = 2 * core + xbit
     quarter = width // 4
+    level = jnp.full((quarter, width), exponent(both), F32)
     for j in range(4):
         block = all_rows[pl.ds(pl.multiple_of((mine ^ j) * quarter, quarter), quarter), :]
-        (keep if j < 2 else send)[j % 2] = block
+        target = keep if j < 2 else send
+        for tap in range(9):
+            target[j % 2, tap] = block[:, tap * width : (tap + 1) * width]
+        target[j % 2, 9] = level
     copies[3].wait()
     k = k_rows[...]
     high = k.astype(BF16)
-    k_parts[0] = high
-    k_parts[1] = (k - high.astype(F32)).astype(BF16)
-
-
-def cross_kernel(side, half_a, half_b, precond_t, gram, out, out_half):
+    rest = (k - high.astype(F32)).astype(BF16)
+    level = jnp.maximum(exponent(k), -99.0)
+    factor = jnp.exp2(jnp.full((1, width), TOP - level, F32))
+    for tap in range(9):
+        part = slice(tap * width, (tap + 1) * width)
+        k_parts[0, tap] = high[:, part]
+        k_parts[1, tap] = rest[:, part]
+        k_send[tap] = k[:, part] * factor
+    k_send[9] = jnp.full((k.shape[0], width), level, F32)
+
+
+def cross_kernel(side, part_0, part_1, part_2, part_3, precond_t, gram, out, out_half):
     quarter = precond_t.shape[0]
-    width = half_a.shape[3]
+    width = part_0.shape[2]
     full = precond_t.shape[1]
     taps = jnp.concatenate([precond_t[:, t * width : (t + 1) * width] for t in range(9)], axis=0)
     both = None
-    for half in (half_a, half_b):
-        for d in range(2):
-            spread = dot_nt(taps, half[d, 1])
-            mapped = None
-            for s in range(3):
-                column = None
-                for r in range(3):
-                    low = quarter * (3 * r + s)
-                    part = shifted(spread[low : low + quarter], r - 1, 0, side)
-                    column = part if column is None else column + part
-                column = shifted(column, 0, s - 1, side)
-                mapped = column if mapped is None else mapped + column
-            mapped = mapped.astype(BF16).astype(F32)
-            part = jnp.dot(taps_to_rows(mapped, side), half[d, 0], preferred_element_type=F32)
-            both = part if both is None else both + part
+    for device in (part_0, part_1, part_2, part_3):
+        spread = dot_nt(taps, device[1])
+        mapped = None
+        for s in range(3):
+            column = None
+            for r in range(3):
+                low = quarter * (3 * r + s)
+                part = shifted(spread[low : low + quarter], r - 1, 0, side)
+                column = part if column is None else column + part
+            column = shifted(column, 0, s - 1, side)
+            mapped = column if mapped is None else mapped + column
+        mapped = mapped.astype(BF16).astype(F32)
+        part = jnp.dot(taps_to_rows(mapped, side), device[0], preferred_element_type=F32)
+        both = part if both is None else both + part
     for tap in range(9):
         part = both[quarter * tap : quarter * (tap + 1)]
         out[:, tap * width : (tap + 1) * width] = part
@@ -169,14 +187,18 @@
     return me & 1, (me >> 1) & 1
 
 
+def taps_to_lanes(block):
+    return jnp.concatenate([block[tap] for tap in range(9)], axis=1)
+
+
 def precond_kernel(scale, e_t, k_a, k_b, main_a, main_b, precond_t):
     core, xbit = place_bits()
-    count = e_t.shape[0]
-    rows = k_a.shape[1] // 2
-    parts = two_parts(e_t[...] * scale)
+    count = e_t.shape[1]
+    rows = k_a.shape[2] // 2
+    parts = two_parts(taps_to_lanes(e_t) * scale)
     total = None
     for flip, k, main in ((0, k_a, main_a), (1, k_b, main_b)):
-        product = dot_nt(parts, k[0]) + dot_nt(parts, k[1])
+        product = dot_nt(parts, taps_to_lanes(k.at[0])) + dot_nt(parts, taps_to_lanes(k.at[1]))
         product = product[:count] + product[count:]
         main[...] = product
         source = lax.broadcasted_iota(jnp.int32, (2 * rows, 4 * rows), 0)
@@ -190,35 +212,31 @@
 
 
 def update_kernel(cross_t, gram, g_inv, k_a, k_b, main, keep, send):
-    rows = k_a.shape[1] // 2
+    rows = k_a.shape[2] // 2
     mixed = jnp.dot(gram[...], g_inv[...], precision=HIGH)
     mixed = jnp.concatenate([mixed, mixed], axis=0)
     parts = two_parts(cross_t[...])
     for i, k in enumerate((k_a, k_b)):
-        product = dot_nt(k[0], parts) + dot_nt(k[1], parts)
+        product = dot_nt(taps_to_lanes(k.at[0]), parts) + dot_nt(taps_to_lanes(k.at[1]), parts)
         result = main[i] - jnp.dot(product, mixed, precision=HIGH)
         keep[i] = result[:rows]
         send[i] = result[rows:]
 
 
-def gram_kernel(half_a, half_b, out, scratch):
+def gram_kernel(grads, next_grads, keep, send, scratch):
     core, xbit = place_bits()
     mine = 2 * core + xbit
-    width = half_a.shape[3]
+    width = grads.shape[1]
     quarter = width // 4
-    here = following = None
-    for half in (half_a, half_b):
-        for d in range(2):
-            g = half[d, 2]
-            part = dot_t(g, g)
-            here = part if here is None else here + part
-            part = dot_t(half[d, 3], g)
-            following = part if following is None else following + part
+    g = grads[...]
     last = lax.axis_index("layer") == lax.axis_size("layer") - 1
-    scratch[0] = here
-    scratch[1] = jnp.where(last, 0.0, following)
-    for i in range(2):
-        out[i * quarter : (i + 1) * quarter] = scratch[i, pl.ds(pl.multiple_of(mine * quarter, quarter), quarter), :]
+    scratch[0] = dot_t(g, g)
+    scratch[1] = jnp.where(last, 0.0, dot_t(next_grads[...], g))
+    for j in range(4):
+        for i in range(2):
+            (keep if j < 2 else send)[j % 2, i * quarter : (i + 1) * quarter] = scratch[
+                i, pl.ds(pl.multiple_of((mine ^ j) * quarter, quarter), quarter), :
+            ]
 
 
 VMEM = pl.BlockSpec(memory_space=pltpu.VMEM)
@@ -245,12 +263,15 @@
     flat_maps = maps.reshape(-1, width)
     flat_grads = grads.reshape(-1, width)
 
-    keep, send, k_own = pl.pallas_call(
+    keep, send, k_own, k_send = pl.pallas_call(
         functools.partial(grad_kernel, side),
-        out_shape=[jax.ShapeDtypeStruct((2, quarter, full), F32)] * 2
-        + [jax.ShapeDtypeStruct((2, rows, full), BF16)],
+        out_shape=[jax.ShapeDtypeStruct((2, 10, quarter, width), F32)] * 2
+        + [
+            jax.ShapeDtypeStruct((2, 9, rows, width), BF16),
+            jax.ShapeDtypeStruct((10, rows, width), F32),
+        ],
         in_specs=[HBM] * 4,
-        out_specs=[VMEM] * 3,
+        out_specs=[VMEM] * 4,
         scratch_shapes=[
             pltpu.VMEM((width, full), F32),
             pltpu.VMEM(flat_maps.shape, BF16),
@@ -261,24 +282,47 @@
         ],
         compiler_params=PARAMS,
     )(flat_maps, flat_grads, g_inv, k_rows)
-    h = keep + swap(send, 1)
-    k_own = behind(k_own, h)
-    k_x = swap(k_own, 2)
+
+    def message(values, level):
+        level = jnp.maximum(level, -99.0)
+        return jnp.concatenate([values * jnp.exp2(TOP - level)[None], level[None]], axis=0).astype(F16)
+
+    def received(parcel):
+        parcel = parcel.astype(F32)
+        return parcel[:9] * jnp.exp2(parcel[9] - TOP)[None], parcel[9]
+
+    other = swap(send, 1)
+    h = keep[:, :9] + other[:, :9]
+    level = jnp.maximum(keep[:, 9], other[:, 9]) + 1
+    k_half = behind(k_send, h).astype(F16)
+    k_others = [swap(k_half, 2), swap(k_half, 1), swap(k_half, 3)]
     own = behind(jnp.stack([flat_maps, flat_grads]), h)
     next_own = after(own)
-    h = h[0] + swap(h[1], 2)
-    own, next_own, k_own = behind((own, next_own, k_own), h)
-    two_own = jnp.stack([own[0], next_own[0], own[1], next_own[1]])
+
+    def add(values, level, bit):
+        more, other_level = received(swap(message(values[1], level[1]) if bit == 2 else message(values, level), bit))
+        if bit == 2:
+            values, level = values[0], level[0]
+        return values + more, jnp.maximum(level, other_level) + 1
+
+    h, level = add(h, level, 2)
+    h, level = add(h, level, zbits[0])
+    next_own = behind(next_own, h)
+    two_own = jnp.stack([flat_maps, next_own[0]])
     two_x = swap(two_own, 2)
-    k_core = swap(k_own, 1)
-    h = h + swap(h, zbits[0])
-    k_own, k_x = behind((k_own, k_x), h)
-    k_a = jnp.concatenate([k_own, k_x], axis=1)
-    third = full // 3
-    k_pieces = [swap(k_x[:, :, i * third : (i + 1) * third], 1) for i in range(3)]
-    k_b = jnp.concatenate([k_core, jnp.concatenate(k_pieces, axis=2)], axis=1)
     for b in zbits[1:]:
-        h = h + swap(h, b)
+        h, level = add(h, level, b)
+
+    def k_pair(parts):
+        return jnp.concatenate(parts, axis=2)
+
+    def k_split(parcel):
+        values, _ = received(parcel)
+        high = lax.reduce_precision(values, 8, 7)
+        return jnp.stack([high, values - high]).astype(BF16)
+
+    k_a = k_pair([k_own, k_split(k_others[0])])
+    k_b = k_pair([k_split(k_others[1]), k_split(k_others[2])])
 
     main_a, main_b, p_t = pl.pallas_call(
         functools.partial(precond_kernel, scale),
@@ -292,25 +336,27 @@
     def by_bit(mine, other, b):
         return jnp.where((me & b) == 0, jnp.concatenate([mine, other], 1), jnp.concatenate([other, mine], 1))
 
+    gram_keep, gram_send = pl.pallas_call(
+        gram_kernel,
+        out_shape=[jax.ShapeDtypeStruct((2, 2 * quarter, width), F32)] * 2,
+        in_specs=[VMEM] * 2,
+        out_specs=[VMEM] * 2,
+        scratch_shapes=[pltpu.VMEM((2, width, width), F32)],
+        compiler_params=PARAMS,
+    )(flat_grads, next_own[1])
+    gram_keep, gram_send, two_own = behind((gram_keep, gram_send, two_own), p_t)
+    core_own = swap(two_own, 1)
+    gram = gram_keep + swap(gram_send, 1)
     for b in zbits[:-1]:
         p_t = by_bit(p_t, swap(p_t, b), b)
 
-    two_own, two_x = behind((two_own, two_x), p_t)
-    half_a = jnp.stack([two_own, two_x])
-    half_b = swap(half_a, 1)
-
-    gram = pl.pallas_call(
-        gram_kernel,
-        out_shape=jax.ShapeDtypeStruct((2 * quarter, width), F32),
-        in_specs=[VMEM] * 2,
-        out_specs=VMEM,
-        scratch_shapes=[pltpu.VMEM((2, width, width), F32)],
-        compiler_params=PARAMS,
-    )(half_a, half_b)
+    two_x = behind(two_x, p_t)
+    core_x = swap(two_x, 1)
+    gram = behind(gram, p_t)
+    gram = gram[0] + swap(gram[1], 2)
     low = cols * quarter
     last = lax.axis_index("layer") == lax.axis_size("layer") - 1
-    p_same, p_other = behind((after(p_t), after(p_t, zbits[-1])), gram)
-    p_t = by_bit(p_same, p_other, zbits[-1])
+    p_t = by_bit(after(p_t), after(p_t, zbits[-1]), zbits[-1])
     p_t = jnp.where(last, jnp.zeros_like(p_t), p_t)
 
     out_width = full + 2 * width
@@ -320,10 +366,10 @@
             jax.ShapeDtypeStruct((quarter, out_width), F32),
             jax.ShapeDtypeStruct((quarter, out_width + 2 * width), BF16),
         ],
-        in_specs=[VMEM] * 4,
+        in_specs=[VMEM] * 6,
         out_specs=[VMEM] * 2,
         compiler_params=PARAMS,
-    )(half_a, half_b, p_t, gram)
+    )(two_own, two_x, core_own, core_x, p_t, gram)
 
     place = (jnp.arange(width)[None, :] == low + jnp.arange(quarter)[:, None]).astype(F32)
     main_a, main_b = behind((main_a, main_b), cross_half)

time: 68.7 us -> 60.3 us (0.88)
  waiting for transfers between devices: 32.7 us -> 22.3 us
  starting transfers between devices: 20.6 us -> 23.9 us
  other arithmetic: 3.25 us -> 1.95 us
    ppermute x18 -> x19, waiting for transfers between devices: 27.3 us -> 20.2 us  [swap(): lax.ppermute(block, 'pos', [(i, i ^ bit) for i in range(lax.axis_size('po...]
    ppermute x18 -> x19, starting transfers between devices: 15.4 us -> 18.9 us  [swap(): lax.ppermute(block, 'pos', [(i, i ^ bit) for i in range(lax.axis_size('po...]
    ppermute x3, waiting for transfers between devices: 5.48 us -> 2.1 us  [after(): return lax.ppermute(block, ('layer', 'pos'), route)]
    select_n x1, other arithmetic: 0.95 us -> 0.09 us  [per_device(): p_t = jnp.where(last, jnp.zeros_like(p_t), p_t)]
    another operation x5 -> x12, other arithmetic: 1.25 us -> 0.41 us  [the longest x3 0.2 us: k_split(): return jnp.stack([high, values - high]).astype(BF16)]
    unnamed x11 -> x14, local copies, waits for them, and re-layouts: 3.65 us -> 3.63 us
  transfers between devices with their start and end apart: 21 -> 22, of which waited for: 14 -> 14; matrix products, arithmetic and copies ran while one was open for 3% -> 4% of each run, Pallas kernels for 2% -> 2%
where the time goes in v9:
time: 60.3 us; the launch traced here: 60 us
  starting transfers between devices  23.9 us (40%)
  waiting for transfers between devices  22.3 us (37%)
  Pallas kernels  5.75 us (10%)
  local copies, waits for them, and re-layouts  4.5 us (7%)
  other arithmetic  1.95 us (3%)
  between operations  1.08 us (2%)
    ppermute x19, waiting for transfers between devices, swap(): lax.ppermute(block, 'pos', [(i, i ^ bit) for i in range(lax.axis_size('po...  20.2 us
    ppermute x19, starting transfers between devices, swap(): lax.ppermute(block, 'pos', [(i, i ^ bit) for i in range(lax.axis_size('po...  18.9 us
    ppermute x3, starting transfers between devices, after(): return lax.ppermute(block, ('layer', 'pos'), route)  4.93 us
    unnamed x14, local copies, waits for them, and re-layouts  3.63 us
    ppermute x3, waiting for transfers between devices, after(): return lax.ppermute(block, ('layer', 'pos'), route)  2.1 us
    pallas_call x1, Pallas kernels, per_device(): pl.pallas_call(functools.partial(grad_kernel, side), out_shape=[jax.Shape...  1.76 us
    pallas_call x1, Pallas kernels, per_device(): pl.pallas_call(functools.partial(cross_kernel, side), out_shape=[jax.Shap...  1.69 us
    pallas_call x1, Pallas kernels, per_device(): pl.pallas_call(update_kernel, out_shape=[jax.ShapeDtypeStruct((2, rows, w...  1.28 us
  transfers between devices with their start and end apart: 22, of which 14 were waited for; matrix products, arithmetic and copies ran while one was open for 4% of the time, Pallas kernels for 2%

profile of v9, /device:TPU:0, one launch (start us, length us, event | category | flops | bytes accessed | tf_op | source)
XLA Modules:
  0.0 60.0 jit_solution(16075341302108915079)
XLA Ops:
  4.3 1.8 %shard_map.59 = (f32[2,10,32,128]{3,2,1,0:T(8,128)S(1)}, f32[2,10,32,128]{3,2,1,0:T(8,128)S(1)}, bf16[2,9,72,128]{3,2,1,0:T(8,128)(2,1)S(1)}, f32[10,72,128]{2,1,0:T(8,128)S(1)}) custom-call(bf16[512,128]{1,0:T(8,128)(2,1)S(1)} %bitcast.96, bf16[512,128]{1,0:T(8,128)(2,1)S(1)} %bitcast.93, f32[128,128]{1,0:T(8,128)S(1)} %bitcast.100, f32[72,1152]{1,0:T(8,128)S(1)} %bitcast.99), custom_call_target="tpu_custom_call" | custom-call | tf_op jit(solution)/shard_map/pallas_call | solution.py:266
  6.6 1.3 %collective-permute-done = f32[2,10,32,128]{3,2,1,0:T(8,128)S(1)} collective-permute-done((f32[2,10,32,128]{3,2,1,0:T(8,128)S(1)}, f32[2,10,32,128]{3,2,1,0:T(8,128)S(1)}, u32[]{:S(2)}, u32[]{:S(2)}) %collective-permute-start) | collective-permute-done | bytes 327712 | tf_op jit(solution)/shard_map/ppermute | solution.py:28
  8.0 2.9 %collective-permute-start.2 = (f16[10,32,128]{2,1,0:T(8,128)(2,1)S(1)}, f16[10,32,128]{2,1,0:T(8,128)(2,1)S(1)}, u32[]{:S(2)}, u32[]{:S(2)}) collective-permute-start(f16[10,32,128]{2,1,0:T(8,128)(2,1)S(1)} %pad_maximum_fusion.5), channel_id=1, source_target_pairs={{0,2},{1,3},{2,0},{3,1},{4,6},{5,7},{6,4},{7,5},{8,10},{9,11},{10,... | collective-permute-start | bytes 245768 | tf_op jit(solution)/shard_map/ppermute | solution.py:28
  10.9 2.7 %collective-permute-done.2 = f16[10,32,128]{2,1,0:T(8,128)(2,1)S(1)} collective-permute-done((f16[10,32,128]{2,1,0:T(8,128)(2,1)S(1)}, f16[10,32,128]{2,1,0:T(8,128)(2,1)S(1)}, u32[]{:S(2)}, u32[]{:S(2)}) %collective-permute-start.2) | collective-permute-done | bytes 81952 | tf_op jit(solution)/shard_map/ppermute | solution.py:28
  13.8 1.9 %collective-permute-start.3 = (f16[10,32,128]{2,1,0:T(8,128)(2,1)S(1)}, f16[10,32,128]{2,1,0:T(8,128)(2,1)S(1)}, u32[]{:S(2)}, u32[]{:S(2)}) collective-permute-start(f16[10,32,128]{2,1,0:T(8,128)(2,1)S(1)} %pad_maximum_fusion.6), channel_id=1, source_target_pairs={{0,4},{1,5},{2,6},{3,7},{4,0},{5,1},{6,2},{7,3},{8,12},{9,13},{10,... | collective-permute-start | bytes 245768 | tf_op jit(solution)/shard_map/ppermute | solution.py:28
  15.7 1.6 %collective-permute-start.5 = (f16[10,72,128]{2,1,0:T(8,128)(2,1)S(1)}, f16[10,72,128]{2,1,0:T(8,128)(2,1)S(1)}, u32[]{:S(2)}, u32[]{:S(2)}) collective-permute-start(f16[10,72,128]{2,1,0:T(8,128)(2,1)S(1)} %convert_element_type.38), channel_id=1, source_target_pairs={{0,2},{1,3},{2,0},{3,1},{4,6},{5,7},{6,4},{7,5},{8,10},{9,11},{10,... | collective-permute-start | bytes 552968 | tf_op jit(solution)/shard_map/ppermute | solution.py:28
  17.9 1.5 %collective-permute-start.1 = (bf16[2,512,128]{2,1,0:T(8,128)(2,1)S(1)}, bf16[2,512,128]{2,1,0:T(8,128)(2,1)S(1)}, u32[]{:S(2)}, u32[]{:S(2)}) collective-permute-start(bf16[2,512,128]{2,1,0:T(8,128)(2,1)S(1)} %pad_maximum_fusion.1), channel_id=1, source_target_pairs={{16,0},{17,1},{18,2},{19,3},{20,4},{21,5},{22,6},{23,7},{24,8},{25... | collective-permute-start | bytes 786440 | tf_op jit(solution)/shard_map/ppermute | solution.py:24
  19.5 2.7 %collective-permute-start.4 = (f16[10,32,128]{2,1,0:T(8,128)(2,1)S(1)}, f16[10,32,128]{2,1,0:T(8,128)(2,1)S(1)}, u32[]{:S(2)}, u32[]{:S(2)}) collective-permute-start(f16[10,32,128]{2,1,0:T(8,128)(2,1)S(1)} %pad_maximum_fusion.7), channel_id=1, source_target_pairs={{0,8},{1,9},{2,10},{3,11},{4,12},{5,13},{6,14},{7,15},{8,0},{9,1},... | collective-permute-start | bytes 245768 | tf_op jit(solution)/shard_map/ppermute | solution.py:28
  22.5 1.7 %collective-permute-done.7 = f16[10,72,128]{2,1,0:T(8,128)(2,1)S(1)} collective-permute-done((f16[10,72,128]{2,1,0:T(8,128)(2,1)S(1)}, f16[10,72,128]{2,1,0:T(8,128)(2,1)S(1)}, u32[]{:S(2)}, u32[]{:S(2)}) %collective-permute-start.7) | collective-permute-done | bytes 184352 | tf_op jit(solution)/shard_map/ppermute | solution.py:28
  24.7 1.6 %collective-permute-done.4 = f16[10,32,128]{2,1,0:T(8,128)(2,1)S(1)} collective-permute-done((f16[10,32,128]{2,1,0:T(8,128)(2,1)S(1)}, f16[10,32,128]{2,1,0:T(8,128)(2,1)S(1)}, u32[]{:S(2)}, u32[]{:S(2)}) %collective-permute-start.4) | collective-permute-done | bytes 81952 | tf_op jit(solution)/shard_map/ppermute | solution.py:28
  27.4 1.6 %collective-permute-start.8 = (bf16[2,512,128]{2,1,0:T(8,128)(2,1)S(1)}, bf16[2,512,128]{2,1,0:T(8,128)(2,1)S(1)}, u32[]{:S(2)}, u32[]{:S(2)}) collective-permute-start(bf16[2,512,128]{2,1,0:T(8,128)(2,1)S(1)} %pad_maximum_fusion.part_0), channel_id=1, source_target_pairs={{0,2},{1,3},{2,0},{3,1},{4,6},{5,7},{6,4},{7,5},{8,10},{9,11},{10,... | collective-permute-start | bytes 786440 | tf_op jit(solution)/shard_map/ppermute | solution.py:28
  29.5 1.4 %collective-permute-done.9 = bf16[32,288]{1,0:T(8,128)(2,1)S(1)} collective-permute-done((bf16[32,288]{1,0:T(8,128)(2,1)S(1)}, bf16[32,288]{1,0:T(8,128)(2,1)S(1)}, u32[]{:S(2)}, u32[]{:S(2)}) %collective-permute-start.9) | collective-permute-done | bytes 18464 | tf_op jit(solution)/shard_map/ppermute | solution.py:28
  31.0 2.4 %collective-permute-start.13 = (bf16[32,576]{1,0:T(8,128)(2,1)S(1)}, bf16[32,576]{1,0:T(8,128)(2,1)S(1)}, u32[]{:S(2)}, u32[]{:S(2)}) collective-permute-start(bf16[32,576]{1,0:T(8,128)(2,1)S(1)} %maximum_select_fusion.1), channel_id=1, source_target_pairs={{24,0},{25,1},{26,2},{27,3},{28,4},{29,5},{30,6},{31,7},{16,8},{17... | collective-permute-start | bytes 110600 | tf_op jit(solution)/shard_map/ppermute | solution.py:24
  33.3 1.0 %collective-permute-start.12 = (bf16[32,576]{1,0:T(8,128)(2,1)S(1)}, bf16[32,576]{1,0:T(8,128)(2,1)S(1)}, u32[]{:S(2)}, u32[]{:S(2)}) collective-permute-start(bf16[32,576]{1,0:T(8,128)(2,1)S(1)} %maximum_select_fusion.1), channel_id=1, source_target_pairs={{16,0},{17,1},{18,2},{19,3},{20,4},{21,5},{22,6},{23,7},{24,8},{25... | collective-permute-start | bytes 110600 | tf_op jit(solution)/shard_map/ppermute | solution.py:24
  34.4 1.1 %collective-permute-start.15 = (f32[64,128]{1,0:T(8,128)S(1)}, f32[64,128]{1,0:T(8,128)S(1)}, u32[]{:S(2)}, u32[]{:S(2)}) collective-permute-start(f32[64,128]{1,0:T(8,128)S(1)} %slice_bitcast_fusion.5), channel_id=1, source_target_pairs={{0,2},{1,3},{2,0},{3,1},{4,6},{5,7},{6,4},{7,5},{8,10},{9,11},{10,... | collective-permute-start | bytes 98312 | tf_op jit(solution)/shard_map/ppermute | solution.py:28
  35.5 1.8 %collective-permute-done.13 = bf16[32,576]{1,0:T(8,128)(2,1)S(1)} collective-permute-done((bf16[32,576]{1,0:T(8,128)(2,1)S(1)}, bf16[32,576]{1,0:T(8,128)(2,1)S(1)}, u32[]{:S(2)}, u32[]{:S(2)}) %collective-permute-start.13) | collective-permute-done | bytes 36896 | tf_op jit(solution)/shard_map/ppermute | solution.py:24
  38.4 1.7 %shard_map.62 = (f32[32,1408]{1,0:T(8,128)S(1)}, bf16[32,1664]{1,0:T(8,128)(2,1)S(1)}) custom-call(bf16[2,512,128]{2,1,0:T(8,128)(2,1)S(1)} %pad_maximum_fusion.part_0, bf16[2,512,128]{2,1,0:T(8,128)(2,1)S(1)} %collective-permute-done.8.part_1, bf16[2,512,128]{2,1,0:T(8,128)(2,1)S(1)} %collective-permute-done.10.part_2, ...), custom_call_target="tpu_custom_call" | custom-call | tf_op jit(solution)/shard_map/pallas_call | solution.py:363
  40.1 1.5 %collective-permute-start.16 = (bf16[32,1664]{1,0:T(8,128)(2,1)S(1)}, bf16[32,1664]{1,0:T(8,128)(2,1)S(1)}, u32[]{:S(2)}, u32[]{:S(2)}) collective-permute-start(bf16[32,1664]{1,0:T(8,128)(2,1)S(1)} %get-tuple-element.43), channel_id=1, source_target_pairs={{0,4},{1,5},{2,6},{3,7},{4,0},{5,1},{6,2},{7,3},{8,12},{9,13},{10,... | collective-permute-start | bytes 319496 | tf_op jit(solution)/shard_map/ppermute | solution.py:28
  42.2 2.7 %collective-permute-done.16 = bf16[32,1664]{1,0:T(8,128)(2,1)S(1)} collective-permute-done((bf16[32,1664]{1,0:T(8,128)(2,1)S(1)}, bf16[32,1664]{1,0:T(8,128)(2,1)S(1)}, u32[]{:S(2)}, u32[]{:S(2)}) %collective-permute-start.16) | collective-permute-done | bytes 106528 | tf_op jit(solution)/shard_map/ppermute | solution.py:28
  45.0 1.8 %collective-permute-start.17 = (bf16[32,1664]{1,0:T(8,128)(2,1)S(1)}, bf16[32,1664]{1,0:T(8,128)(2,1)S(1)}, u32[]{:S(2)}, u32[]{:S(2)}) collective-permute-start(bf16[32,1664]{1,0:T(8,128)(2,1)S(1)} %pad_maximum_fusion.4), channel_id=1, source_target_pairs={{0,8},{1,9},{2,10},{3,11},{4,12},{5,13},{6,14},{7,15},{8,0},{9,1},... | collective-permute-start | bytes 319496 | tf_op jit(solution)/shard_map/ppermute | solution.py:28
  46.8 4.9 %collective-permute-done.17 = bf16[32,1664]{1,0:T(8,128)(2,1)S(1)} collective-permute-done((bf16[32,1664]{1,0:T(8,128)(2,1)S(1)}, bf16[32,1664]{1,0:T(8,128)(2,1)S(1)}, u32[]{:S(2)}, u32[]{:S(2)}) %collective-permute-start.17) | collective-permute-done | bytes 106528 | tf_op jit(solution)/shard_map/ppermute | solution.py:28
  51.9 1.3 %shard_map.63 = (f32[2,72,128]{2,1,0:T(8,128)S(1)}, f32[2,72,128]{2,1,0:T(8,128)S(1)}) custom-call(f32[32,1152]{1,0:T(8,128)S(1)} %slice_add_fusion.1.cross_t, f32[32,128]{1,0:T(8,128)S(1)} %slice.171.gram, f32[128,128]{1,0:T(8,128)S(1)} %broadcast_multiply_fusion.g_inv, bf16[2,9,144,128]{3,2,1,0:T(8,128)(2,1)S(1)} %get-tuple-element.76.k_a, ...), custom_call_target="tpu_custom_call" | custom-call | tf_op jit(solution)/shard_map/pallas_call | solution.py:388
  53.4 1.9 %collective-permute-start.18 = (f32[2,72,128]{2,1,0:T(8,128)S(1)}, f32[2,72,128]{2,1,0:T(8,128)S(1)}, u32[]{:S(2)}, u32[]{:S(2)}) collective-permute-start(f32[2,72,128]{2,1,0:T(8,128)S(1)} %get-tuple-element.50), channel_id=1, source_target_pairs={{0,2},{1,3},{2,0},{3,1},{4,6},{5,7},{6,4},{7,5},{8,10},{9,11},{10,... | collective-permute-start | bytes 221192 | tf_op jit(solution)/shard_map/ppermute | solution.py:28
  55.3 1.9 %collective-permute-done.20 = f32[32,256]{1,0:T(8,128)S(1)} collective-permute-done((f32[32,256]{1,0:T(8,128)S(1)}, f32[32,256]{1,0:T(8,128)S(1)}, u32[]{:S(2)}, u32[]{:S(2)}) %collective-permute-start.20) | collective-permute-done | bytes 32800 | tf_op jit(solution)/shard_map/ppermute | solution.py:28
  (99 shorter events, 12.3 us)
Async XLA Ops:
  6.0 1.8 %collective-permute-start = (f32[2,10,32,128]{3,2,1,0:T(8,128)S(1)}, f32[2,10,32,128]{3,2,1,0:T(8,128)S(1)}, u32[]{:S(2)}, u32[]{:S(2)}) collective-permute-start(f32[2,10,32,128]{3,2,1,0:T(8,128)S(1)} %get-tuple-element.28), channel_id=1, source_target_pairs={{0,1},{1,0},{2,3},{3,2},{4,5},{5,4},{6,7},{7,6},{8,9},{9,8},{10,11... | collective-permute-start | bytes 983048 | tf_op jit(solution)/shard_map/ppermute | solution.py:28
  7.8 3.1 %copy-start.1 = (bf16[1,2,16,16,128]{4,3,2,1,0:T(8,128)(2,1)S(1)}, bf16[1,2,16,16,128]{4,3,2,1,0:T(8,128)(2,1)}, u32[]{:S(2)}) copy-start(bf16[1,2,16,16,128]{4,3,2,1,0:T(8,128)(2,1)} %param.5) | copy-start | bytes 393220
  8.0 5.7 %collective-permute-start.2 = (f16[10,32,128]{2,1,0:T(8,128)(2,1)S(1)}, f16[10,32,128]{2,1,0:T(8,128)(2,1)S(1)}, u32[]{:S(2)}, u32[]{:S(2)}) collective-permute-start(f16[10,32,128]{2,1,0:T(8,128)(2,1)S(1)} %pad_maximum_fusion.5), channel_id=1, source_target_pairs={{0,2},{1,3},{2,0},{3,1},{4,6},{5,7},{6,4},{7,5},{8,10},{9,11},{10,... | collective-permute-start | bytes 245768 | tf_op jit(solution)/shard_map/ppermute | solution.py:28
  13.8 5.7 %collective-permute-start.3 = (f16[10,32,128]{2,1,0:T(8,128)(2,1)S(1)}, f16[10,32,128]{2,1,0:T(8,128)(2,1)S(1)}, u32[]{:S(2)}, u32[]{:S(2)}) collective-permute-start(f16[10,32,128]{2,1,0:T(8,128)(2,1)S(1)} %pad_maximum_fusion.6), channel_id=1, source_target_pairs={{0,4},{1,5},{2,6},{3,7},{4,0},{5,1},{6,2},{7,3},{8,12},{9,13},{10,... | collective-permute-start | bytes 245768 | tf_op jit(solution)/shard_map/ppermute | solution.py:28
  15.7 6.7 %collective-permute-start.5 = (f16[10,72,128]{2,1,0:T(8,128)(2,1)S(1)}, f16[10,72,128]{2,1,0:T(8,128)(2,1)S(1)}, u32[]{:S(2)}, u32[]{:S(2)}) collective-permute-start(f16[10,72,128]{2,1,0:T(8,128)(2,1)S(1)} %convert_element_type.38), channel_id=1, source_target_pairs={{0,2},{1,3},{2,0},{3,1},{4,6},{5,7},{6,4},{7,5},{8,10},{9,11},{10,... | collective-permute-start | bytes 552968 | tf_op jit(solution)/shard_map/ppermute | solution.py:28
  17.2 7.0 %collective-permute-start.7 = (f16[10,72,128]{2,1,0:T(8,128)(2,1)S(1)}, f16[10,72,128]{2,1,0:T(8,128)(2,1)S(1)}, u32[]{:S(2)}, u32[]{:S(2)}) collective-permute-start(f16[10,72,128]{2,1,0:T(8,128)(2,1)S(1)} %convert_element_type.38), channel_id=1, source_target_pairs={{0,3},{1,2},{2,1},{3,0},{4,7},{5,6},{6,5},{7,4},{8,11},{9,10},{10,... | collective-permute-start | bytes 552968 | tf_op jit(solution)/shard_map/ppermute | solution.py:28
  17.2 7.2 %collective-permute-start.6 = (f16[10,72,128]{2,1,0:T(8,128)(2,1)S(1)}, f16[10,72,128]{2,1,0:T(8,128)(2,1)S(1)}, u32[]{:S(2)}, u32[]{:S(2)}) collective-permute-start(f16[10,72,128]{2,1,0:T(8,128)(2,1)S(1)} %convert_element_type.38), channel_id=1, source_target_pairs={{0,1},{1,0},{2,3},{3,2},{4,5},{5,4},{6,7},{7,6},{8,9},{9,8},{10,11... | collective-permute-start | bytes 552968 | tf_op jit(solution)/shard_map/ppermute | solution.py:28
  17.9 9.2 %collective-permute-start.1 = (bf16[2,512,128]{2,1,0:T(8,128)(2,1)S(1)}, bf16[2,512,128]{2,1,0:T(8,128)(2,1)S(1)}, u32[]{:S(2)}, u32[]{:S(2)}) collective-permute-start(bf16[2,512,128]{2,1,0:T(8,128)(2,1)S(1)} %pad_maximum_fusion.1), channel_id=1, source_target_pairs={{16,0},{17,1},{18,2},{19,3},{20,4},{21,5},{22,6},{23,7},{24,8},{25... | collective-permute-start | bytes 786440 | tf_op jit(solution)/shard_map/ppermute | solution.py:24
  19.5 6.7 %collective-permute-start.4 = (f16[10,32,128]{2,1,0:T(8,128)(2,1)S(1)}, f16[10,32,128]{2,1,0:T(8,128)(2,1)S(1)}, u32[]{:S(2)}, u32[]{:S(2)}) collective-permute-start(f16[10,32,128]{2,1,0:T(8,128)(2,1)S(1)} %pad_maximum_fusion.7), channel_id=1, source_target_pairs={{0,8},{1,9},{2,10},{3,11},{4,12},{5,13},{6,14},{7,15},{8,0},{9,1},... | collective-permute-start | bytes 245768 | tf_op jit(solution)/shard_map/ppermute | solution.py:28
  27.0 3.8 %collective-permute-start.9 = (bf16[32,288]{1,0:T(8,128)(2,1)S(1)}, bf16[32,288]{1,0:T(8,128)(2,1)S(1)}, u32[]{:S(2)}, u32[]{:S(2)}) collective-permute-start(bf16[32,288]{1,0:T(8,128)(2,1)S(1)} %get-tuple-element.36), channel_id=1, source_target_pairs={{0,4},{1,5},{2,6},{3,7},{4,0},{5,1},{6,2},{7,3},{8,12},{9,13},{10,... | collective-permute-start | bytes 55304 | tf_op jit(solution)/shard_map/ppermute | solution.py:28
  27.4 8.1 %collective-permute-start.8 = (bf16[2,512,128]{2,1,0:T(8,128)(2,1)S(1)}, bf16[2,512,128]{2,1,0:T(8,128)(2,1)S(1)}, u32[]{:S(2)}, u32[]{:S(2)}) collective-permute-start(bf16[2,512,128]{2,1,0:T(8,128)(2,1)S(1)} %pad_maximum_fusion.part_0), channel_id=1, source_target_pairs={{0,2},{1,3},{2,0},{3,1},{4,6},{5,7},{6,4},{7,5},{8,10},{9,11},{10,... | collective-permute-start | bytes 786440 | tf_op jit(solution)/shard_map/ppermute | solution.py:28
  29.0 9.4 %collective-permute-start.10 = (bf16[2,512,128]{2,1,0:T(8,128)(2,1)S(1)}, bf16[2,512,128]{2,1,0:T(8,128)(2,1)S(1)}, u32[]{:S(2)}, u32[]{:S(2)}) collective-permute-start(bf16[2,512,128]{2,1,0:T(8,128)(2,1)S(1)} %pad_maximum_fusion.part_0), channel_id=1, source_target_pairs={{0,1},{1,0},{2,3},{3,2},{4,5},{5,4},{6,7},{7,6},{8,9},{9,8},{10,11... | collective-permute-start | bytes 786440 | tf_op jit(solution)/shard_map/ppermute | solution.py:28
  29.0 5.4 %collective-permute-start.14 = (f32[2,64,128]{2,1,0:T(8,128)S(1)}, f32[2,64,128]{2,1,0:T(8,128)S(1)}, u32[]{:S(2)}, u32[]{:S(2)}) collective-permute-start(f32[2,64,128]{2,1,0:T(8,128)S(1)} %get-tuple-element.40), channel_id=1, source_target_pairs={{0,1},{1,0},{2,3},{3,2},{4,5},{5,4},{6,7},{7,6},{8,9},{9,8},{10,11... | collective-permute-start | bytes 196616 | tf_op jit(solution)/shard_map/ppermute | solution.py:28
  31.0 6.4 %collective-permute-start.13 = (bf16[32,576]{1,0:T(8,128)(2,1)S(1)}, bf16[32,576]{1,0:T(8,128)(2,1)S(1)}, u32[]{:S(2)}, u32[]{:S(2)}) collective-permute-start(bf16[32,576]{1,0:T(8,128)(2,1)S(1)} %maximum_select_fusion.1), channel_id=1, source_target_pairs={{24,0},{25,1},{26,2},{27,3},{28,4},{29,5},{30,6},{31,7},{16,8},{17... | collective-permute-start | bytes 110600 | tf_op jit(solution)/shard_map/ppermute | solution.py:24
  33.3 4.3 %collective-permute-start.12 = (bf16[32,576]{1,0:T(8,128)(2,1)S(1)}, bf16[32,576]{1,0:T(8,128)(2,1)S(1)}, u32[]{:S(2)}, u32[]{:S(2)}) collective-permute-start(bf16[32,576]{1,0:T(8,128)(2,1)S(1)} %maximum_select_fusion.1), channel_id=1, source_target_pairs={{16,0},{17,1},{18,2},{19,3},{20,4},{21,5},{22,6},{23,7},{24,8},{25... | collective-permute-start | bytes 110600 | tf_op jit(solution)/shard_map/ppermute | solution.py:24
  34.4 4.0 %collective-permute-start.15 = (f32[64,128]{1,0:T(8,128)S(1)}, f32[64,128]{1,0:T(8,128)S(1)}, u32[]{:S(2)}, u32[]{:S(2)}) collective-permute-start(f32[64,128]{1,0:T(8,128)S(1)} %slice_bitcast_fusion.5), channel_id=1, source_target_pairs={{0,2},{1,3},{2,0},{3,1},{4,6},{5,7},{6,4},{7,5},{8,10},{9,11},{10,... | collective-permute-start | bytes 98312 | tf_op jit(solution)/shard_map/ppermute | solution.py:28
  35.5 2.9 %collective-permute-start.11 = (bf16[2,512,128]{2,1,0:T(8,128)(2,1)S(1)}, bf16[2,512,128]{2,1,0:T(8,128)(2,1)S(1)}, u32[]{:S(2)}, u32[]{:S(2)}) collective-permute-start(bf16[2,512,128]{2,1,0:T(8,128)(2,1)S(1)} %collective-permute-done.8.part_1), channel_id=1, source_target_pairs={{0,1},{1,0},{2,3},{3,2},{4,5},{5,4},{6,7},{7,6},{8,9},{9,8},{10,11... | collective-permute-start | bytes 786440 | tf_op jit(solution)/shard_map/ppermute | solution.py:28
  37.7 3.8 %copy-start.6 = (f32[1,128,128]{2,1,0:T(8,128)S(1)}, f32[1,128,128]{2,1,0:T(8,128)}, u32[]{:S(2)}) copy-start(f32[1,128,128]{2,1,0:T(8,128)} %param.7) | copy-start | bytes 196612
  40.1 4.8 %collective-permute-start.16 = (bf16[32,1664]{1,0:T(8,128)(2,1)S(1)}, bf16[32,1664]{1,0:T(8,128)(2,1)S(1)}, u32[]{:S(2)}, u32[]{:S(2)}) collective-permute-start(bf16[32,1664]{1,0:T(8,128)(2,1)S(1)} %get-tuple-element.43), channel_id=1, source_target_pairs={{0,4},{1,5},{2,6},{3,7},{4,0},{5,1},{6,2},{7,3},{8,12},{9,13},{10,... | collective-permute-start | bytes 319496 | tf_op jit(solution)/shard_map/ppermute | solution.py:28
  45.0 6.8 %collective-permute-start.17 = (bf16[32,1664]{1,0:T(8,128)(2,1)S(1)}, bf16[32,1664]{1,0:T(8,128)(2,1)S(1)}, u32[]{:S(2)}, u32[]{:S(2)}) collective-permute-start(bf16[32,1664]{1,0:T(8,128)(2,1)S(1)} %pad_maximum_fusion.4), channel_id=1, source_target_pairs={{0,8},{1,9},{2,10},{3,11},{4,12},{5,13},{6,14},{7,15},{8,0},{9,1},... | collective-permute-start | bytes 319496 | tf_op jit(solution)/shard_map/ppermute | solution.py:28
  53.2 4.0 %collective-permute-start.20 = (f32[32,256]{1,0:T(8,128)S(1)}, f32[32,256]{1,0:T(8,128)S(1)}, u32[]{:S(2)}, u32[]{:S(2)}) collective-permute-start(f32[32,256]{1,0:T(8,128)S(1)} %get-tuple-element.73), channel_id=1, source_target_pairs={{0,2},{1,3},{2,0},{3,1},{4,6},{5,7},{6,4},{7,5},{8,10},{9,11},{10,... | collective-permute-start | bytes 98312 | tf_op jit(solution)/shard_map/ppermute | solution.py:28
  53.4 4.6 %collective-permute-start.18 = (f32[2,72,128]{2,1,0:T(8,128)S(1)}, f32[2,72,128]{2,1,0:T(8,128)S(1)}, u32[]{:S(2)}, u32[]{:S(2)}) collective-permute-start(f32[2,72,128]{2,1,0:T(8,128)S(1)} %get-tuple-element.50), channel_id=1, source_target_pairs={{0,2},{1,3},{2,0},{3,1},{4,6},{5,7},{6,4},{7,5},{8,10},{9,11},{10,... | collective-permute-start | bytes 221192 | tf_op jit(solution)/shard_map/ppermute | solution.py:28
  57.2 1.3 %collective-permute-start.21 = (f32[2,32,256]{2,1,0:T(8,128)S(1)}, f32[2,32,256]{2,1,0:T(8,128)S(1)}, u32[]{:S(2)}, u32[]{:S(2)}) collective-permute-start(f32[2,32,256]{2,1,0:T(8,128)S(1)} %get-tuple-element.71), channel_id=1, source_target_pairs={{0,1},{1,0},{2,3},{3,2},{4,5},{5,4},{6,7},{7,6},{8,9},{9,8},{10,11... | collective-permute-start | bytes 196616 | tf_op jit(solution)/shard_map/ppermute | solution.py:28
  58.0 1.4 %collective-permute-start.19 = (f32[72,128]{1,0:T(8,128)S(1)}, f32[72,128]{1,0:T(8,128)S(1)}, u32[]{:S(2)}, u32[]{:S(2)}) collective-permute-start(f32[72,128]{1,0:T(8,128)S(1)} %slice_bitcast_fusion.3), channel_id=1, source_target_pairs={{0,1},{1,0},{2,3},{3,2},{4,5},{5,4},{6,7},{7,6},{8,9},{9,8},{10,11... | collective-permute-start | bytes 110600 | tf_op jit(solution)/shard_map/ppermute | solution.py:28
  (5 other events, 6.7 us)

commit v10 on v9

--- a/solution.py
+++ b/solution.py
@@ -143,10 +143,9 @@
     k_send[9] = jnp.full((k.shape[0], width), level, F32)
 
 
-def cross_kernel(side, part_0, part_1, part_2, part_3, precond_t, gram, out, out_half):
+def cross_kernel(side, part_0, part_1, part_2, part_3, precond_t, out, out_half):
     quarter = precond_t.shape[0]
     width = part_0.shape[2]
-    full = precond_t.shape[1]
     taps = jnp.concatenate([precond_t[:, t * width : (t + 1) * width] for t in range(9)], axis=0)
     both = None
     for device in (part_0, part_1, part_2, part_3):
@@ -167,14 +166,6 @@
         part = both[quarter * tap : quarter * (tap + 1)]
         out[:, tap * width : (tap + 1) * width] = part
         out_half[:, tap * width : (tap + 1) * width] = part.astype(BF16)
-    for i in range(2):
-        part = gram[i * quarter : (i + 1) * quarter]
-        high = part.astype(BF16)
-        rest = (part - high.astype(F32)).astype(BF16)
-        low = full + i * width
-        out[:, low : low + width] = high.astype(F32) + rest.astype(F32)
-        out_half[:, low : low + width] = high
-        out_half[:, low + 2 * width : low + 3 * width] = rest
 
 
 def two_parts(block):
@@ -211,10 +202,9 @@
     precond_t[...] = total.astype(BF16)
 
 
-def update_kernel(cross_t, gram, g_inv, k_a, k_b, main, keep, send):
+def update_kernel(cross_t, mixed_in, k_a, k_b, main, keep, send):
     rows = k_a.shape[2] // 2
-    mixed = jnp.dot(gram[...], g_inv[...], precision=HIGH)
-    mixed = jnp.concatenate([mixed, mixed], axis=0)
+    mixed = jnp.concatenate([mixed_in[...], mixed_in[...]], axis=0)
     parts = two_parts(cross_t[...])
     for i, k in enumerate((k_a, k_b)):
         product = dot_nt(taps_to_lanes(k.at[0]), parts) + dot_nt(taps_to_lanes(k.at[1]), parts)
@@ -223,20 +213,11 @@
         send[i] = result[rows:]
 
 
-def gram_kernel(grads, next_grads, keep, send, scratch):
-    core, xbit = place_bits()
-    mine = 2 * core + xbit
-    width = grads.shape[1]
-    quarter = width // 4
+def gram_kernel(grads, next_grads, out):
     g = grads[...]
     last = lax.axis_index("layer") == lax.axis_size("layer") - 1
-    scratch[0] = dot_t(g, g)
-    scratch[1] = jnp.where(last, 0.0, dot_t(next_grads[...], g))
-    for j in range(4):
-        for i in range(2):
-            (keep if j < 2 else send)[j % 2, i * quarter : (i + 1) * quarter] = scratch[
-                i, pl.ds(pl.multiple_of((mine ^ j) * quarter, quarter), quarter), :
-            ]
+    out[0] = dot_t(g, g)
+    out[1] = jnp.where(last, 0.0, dot_t(g, next_grads[...]))
 
 
 VMEM = pl.BlockSpec(memory_space=pltpu.VMEM)
@@ -281,7 +262,7 @@
             pltpu.SemaphoreType.DMA((4,)),
         ],
         compiler_params=PARAMS,
-    )(flat_maps, flat_grads, g_inv, k_rows)
+    )(*(pltpu.with_memory_space_constraint(a, pltpu.HBM) for a in (flat_maps, flat_grads, g_inv, k_rows)))
 
     def message(values, level):
         level = jnp.maximum(level, -99.0)
@@ -307,6 +288,7 @@
 
     h, level = add(h, level, 2)
     h, level = add(h, level, zbits[0])
+    h, k_others[0], k_others[1] = lax.optimization_barrier((h, k_others[0], k_others[1]))
     next_own = behind(next_own, h)
     two_own = jnp.stack([flat_maps, next_own[0]])
     two_x = swap(two_own, 2)
@@ -336,71 +318,59 @@
     def by_bit(mine, other, b):
         return jnp.where((me & b) == 0, jnp.concatenate([mine, other], 1), jnp.concatenate([other, mine], 1))
 
-    gram_keep, gram_send = pl.pallas_call(
+    gram = pl.pallas_call(
         gram_kernel,
-        out_shape=[jax.ShapeDtypeStruct((2, 2 * quarter, width), F32)] * 2,
+        out_shape=jax.ShapeDtypeStruct((2, width, width), F32),
         in_specs=[VMEM] * 2,
-        out_specs=[VMEM] * 2,
-        scratch_shapes=[pltpu.VMEM((2, width, width), F32)],
+        out_specs=VMEM,
         compiler_params=PARAMS,
     )(flat_grads, next_own[1])
-    gram_keep, gram_send, two_own = behind((gram_keep, gram_send, two_own), p_t)
+    gram, two_own = behind((gram, two_own), p_t)
     core_own = swap(two_own, 1)
-    gram = gram_keep + swap(gram_send, 1)
     for b in zbits[:-1]:
+        gram = gram + swap(gram, b)
         p_t = by_bit(p_t, swap(p_t, b), b)
 
-    two_x = behind(two_x, p_t)
+    two_x, gram = behind((two_x, gram), p_t)
     core_x = swap(two_x, 1)
-    gram = behind(gram, p_t)
-    gram = gram[0] + swap(gram[1], 2)
+    gram = gram + swap(gram, zbits[-1])
     low = cols * quarter
     last = lax.axis_index("layer") == lax.axis_size("layer") - 1
     p_t = by_bit(after(p_t), after(p_t, zbits[-1]), zbits[-1])
     p_t = jnp.where(last, jnp.zeros_like(p_t), p_t)
 
-    out_width = full + 2 * width
     cross_t, cross_half = pl.pallas_call(
         functools.partial(cross_kernel, side),
-        out_shape=[
-            jax.ShapeDtypeStruct((quarter, out_width), F32),
-            jax.ShapeDtypeStruct((quarter, out_width + 2 * width), BF16),
-        ],
-        in_specs=[VMEM] * 6,
+        out_shape=[jax.ShapeDtypeStruct((quarter, full), F32), jax.ShapeDtypeStruct((quarter, full), BF16)],
+        in_specs=[VMEM] * 5,
         out_specs=[VMEM] * 2,
         compiler_params=PARAMS,
-    )(two_own, two_x, core_own, core_x, p_t, gram)
-
+    )(two_own, two_x, core_own, core_x, p_t)
+
+    gram = behind(gram, cross_half)
+    gram = gram + swap(gram, 1)
     place = (jnp.arange(width)[None, :] == low + jnp.arange(quarter)[:, None]).astype(F32)
     main_a, main_b = behind((main_a, main_b), cross_half)
-    g_scaled = behind(g_inv, cross_half) * (scale * scale)
     main = jnp.stack([dot_t(main_a, place, precision=HIGH), dot_t(main_b, place, precision=HIGH)])
-    cross_t, gram = cross_t[:, :full], cross_t[:, full:]
-    for b in zbits:
-        other = swap(cross_half, b).astype(F32)
-        cross_t = cross_t + other[:, :full]
-        gram = gram + (other[:, full:out_width] + other[:, out_width:])
-        high = lax.reduce_precision(gram, 8, 7)
-        rest = lax.reduce_precision(gram - high, 8, 7)
-        gram = high + rest
-        cross_half = jnp.concatenate([cross_t, high, rest], axis=1).astype(BF16)
+    for i, b in enumerate(zbits):
+        cross_t = cross_t + swap(cross_half, b).astype(F32)
+        cross_half = cross_t.astype(BF16)
+        if i == 0:
+            gram = behind(gram, cross_half)
+            gram = gram + swap(gram, 2)
+            mixed = dot_t(gram[1], g_inv, precision=HIGH) * (scale * scale)
+            mixed = lax.dynamic_slice_in_dim(mixed, low, quarter, 0)
 
     out, send = pl.pallas_call(
         update_kernel,
         out_shape=[jax.ShapeDtypeStruct((2, rows, width), F32)] * 2,
-        in_specs=[VMEM] * 6,
+        in_specs=[VMEM] * 5,
         out_specs=[VMEM] * 2,
         compiler_params=PARAMS,
-    )(cross_t, gram[:, width:], g_scaled, k_a, k_b, main)
-    gram = behind(gram, out) * scale
-    gram = jnp.stack([gram, swap(gram, 2)])
+    )(cross_t, mixed, k_a, k_b, main)
     out = out + swap(send, 2)
-    gram = jnp.stack([gram, swap(gram, 1)])
     update = out[0] + swap(out[1], 1)
-    gram = jnp.where(xbit == 0, gram, gram[:, ::-1])
-    gram = jnp.where(core == 0, gram, gram[::-1])
-    gram = gram.reshape(width, 2, width).transpose(1, 2, 0)
-    return (update[None], gram[None])
+    return (update[None], (gram * scale)[None])
 
 
 def solution(mesh):

time: 60.3 us -> 67.4 us (1.12)
  waiting for transfers between devices: 22.3 us -> 35.3 us
  local copies, waits for them, and re-layouts: 4.5 us -> 0.04 us
  starting transfers between devices: 23.9 us -> 21.2 us
    ppermute x19, waiting for transfers between devices: 20.2 us -> 33 us  [swap(): lax.ppermute(block, 'pos', [(i, i ^ bit) for i in range(lax.axis_size('po...]
    unnamed x14 -> x6, local copies, waits for them, and re-layouts: 3.63 us -> 0.02 us
    ppermute x19, starting transfers between devices: 18.9 us -> 17.4 us  [swap(): lax.ppermute(block, 'pos', [(i, i ^ bit) for i in range(lax.axis_size('po...]
    ppermute x3, starting transfers between devices: 4.93 us -> 3.87 us  [after(): return lax.ppermute(block, ('layer', 'pos'), route)]
    reshape x2 -> x0, local copies, waits for them, and re-layouts: 0.83 us -> none  [per_device(): gram = gram.reshape(width, 2, width).transpose(1, 2, 0)]
    broadcast_in_dim x1 -> x2, other arithmetic: 0.62 us -> 1.3 us  [per_device(): return (update[None], (gram * scale)[None])]
  transfers between devices with their start and end apart: 22 -> 22, of which waited for: 14 -> 13; matrix products, arithmetic and copies ran while one was open for 4% -> 2% of each run, Pallas kernels for 2% -> 2%
where the time goes in v10:
time: 67.4 us; the launch traced here: 67.2 us
  waiting for transfers between devices  35.3 us (52%)
  starting transfers between devices  21.2 us (31%)
  Pallas kernels  6.22 us (9%)
  other arithmetic  2.51 us (4%)
  between operations  1.07 us (2%)
  matrix products  0.84 us (1%)
    ppermute x19, waiting for transfers between devices, swap(): lax.ppermute(block, 'pos', [(i, i ^ bit) for i in range(lax.axis_size('po...  33 us
    ppermute x19, starting transfers between devices, swap(): lax.ppermute(block, 'pos', [(i, i ^ bit) for i in range(lax.axis_size('po...  17.4 us
    ppermute x3, starting transfers between devices, after(): return lax.ppermute(block, ('layer', 'pos'), route)  3.87 us
    ppermute x3, waiting for transfers between devices, after(): return lax.ppermute(block, ('layer', 'pos'), route)  2.31 us
    pallas_call x1, Pallas kernels, per_device(): pl.pallas_call(functools.partial(grad_kernel, side), out_shape=[jax.Shape...  2.21 us
    pallas_call x1, Pallas kernels, per_device(): pl.pallas_call(functools.partial(cross_kernel, side), out_shape=[jax.Shap...  1.68 us
  transfers between devices with their start and end apart: 22, of which 13 were waited for; matrix products, arithmetic and copies ran while one was open for 2% of the time, Pallas kernels for 2%

profile of v10, /device:TPU:0, one launch (start us, length us, event | category | flops | bytes accessed | tf_op | source)
XLA Modules:
  0.0 67.2 jit_solution(17755745112891826015)
XLA Ops:
  0.6 2.2 %shard_map.59 = (f32[2,10,32,128]{3,2,1,0:T(8,128)S(1)}, f32[2,10,32,128]{3,2,1,0:T(8,128)S(1)}, bf16[2,9,72,128]{3,2,1,0:T(8,128)(2,1)S(1)}, f32[10,72,128]{2,1,0:T(8,128)S(1)}) custom-call(bf16[512,128]{1,0:T(8,128)(2,1)} %bitcast.87, bf16[512,128]{1,0:T(8,128)(2,1)} %bitcast.84, f32[128,128]{1,0:T(8,128)} %bitcast.91, f32[72,1152]{1,0:T(8,128)} %bitcast.90), custom_call_target="tpu_custom_call" | custom-call | tf_op jit(solution)/shard_map/pallas_call | solution.py:247
  3.4 1.3 %collective-permute-done = f32[2,10,32,128]{3,2,1,0:T(8,128)S(1)} collective-permute-done((f32[2,10,32,128]{3,2,1,0:T(8,128)S(1)}, f32[2,10,32,128]{3,2,1,0:T(8,128)S(1)}, u32[]{:S(2)}, u32[]{:S(2)}) %collective-permute-start) | collective-permute-done | bytes 327712 | tf_op jit(solution)/shard_map/ppermute | solution.py:28
  4.8 2.9 %collective-permute-start.2 = (f16[10,32,128]{2,1,0:T(8,128)(2,1)S(1)}, f16[10,32,128]{2,1,0:T(8,128)(2,1)S(1)}, u32[]{:S(2)}, u32[]{:S(2)}) collective-permute-start(f16[10,32,128]{2,1,0:T(8,128)(2,1)S(1)} %pad_maximum_fusion.3), channel_id=1, source_target_pairs={{0,2},{1,3},{2,0},{3,1},{4,6},{5,7},{6,4},{7,5},{8,10},{9,11},{10,... | collective-permute-start | bytes 245768 | tf_op jit(solution)/shard_map/ppermute | solution.py:28
  7.7 2.7 %collective-permute-done.2 = f16[10,32,128]{2,1,0:T(8,128)(2,1)S(1)} collective-permute-done((f16[10,32,128]{2,1,0:T(8,128)(2,1)S(1)}, f16[10,32,128]{2,1,0:T(8,128)(2,1)S(1)}, u32[]{:S(2)}, u32[]{:S(2)}) %collective-permute-start.2) | collective-permute-done | bytes 81952 | tf_op jit(solution)/shard_map/ppermute | solution.py:28
  10.6 1.9 %collective-permute-start.3 = (f16[10,32,128]{2,1,0:T(8,128)(2,1)S(1)}, f16[10,32,128]{2,1,0:T(8,128)(2,1)S(1)}, u32[]{:S(2)}, u32[]{:S(2)}) collective-permute-start(f16[10,32,128]{2,1,0:T(8,128)(2,1)S(1)} %pad_maximum_fusion.4), channel_id=1, source_target_pairs={{0,4},{1,5},{2,6},{3,7},{4,0},{5,1},{6,2},{7,3},{8,12},{9,13},{10,... | collective-permute-start | bytes 245768 | tf_op jit(solution)/shard_map/ppermute | solution.py:28
  12.5 1.6 %collective-permute-start.4 = (f16[10,72,128]{2,1,0:T(8,128)(2,1)S(1)}, f16[10,72,128]{2,1,0:T(8,128)(2,1)S(1)}, u32[]{:S(2)}, u32[]{:S(2)}) collective-permute-start(f16[10,72,128]{2,1,0:T(8,128)(2,1)S(1)} %convert_element_type.39), channel_id=1, source_target_pairs={{0,2},{1,3},{2,0},{3,1},{4,6},{5,7},{6,4},{7,5},{8,10},{9,11},{10,... | collective-permute-start | bytes 552968 | tf_op jit(solution)/shard_map/ppermute | solution.py:28
  14.8 1.5 %collective-permute-start.1 = (bf16[2,512,128]{2,1,0:T(8,128)(2,1)S(1)}, bf16[2,512,128]{2,1,0:T(8,128)(2,1)S(1)}, u32[]{:S(2)}, u32[]{:S(2)}) collective-permute-start(bf16[2,512,128]{2,1,0:T(8,128)(2,1)S(1)} %pad_maximum_fusion.1), channel_id=1, source_target_pairs={{16,0},{17,1},{18,2},{19,3},{20,4},{21,5},{22,6},{23,7},{24,8},{25... | collective-permute-start | bytes 786440 | tf_op jit(solution)/shard_map/ppermute | solution.py:24
  16.4 2.9 %collective-permute-done.4 = f16[10,72,128]{2,1,0:T(8,128)(2,1)S(1)} collective-permute-done((f16[10,72,128]{2,1,0:T(8,128)(2,1)S(1)}, f16[10,72,128]{2,1,0:T(8,128)(2,1)S(1)}, u32[]{:S(2)}, u32[]{:S(2)}) %collective-permute-start.4) | collective-permute-done | bytes 184352 | tf_op jit(solution)/shard_map/ppermute | solution.py:28
  19.5 1.6 %collective-permute-done.7 = f16[10,72,128]{2,1,0:T(8,128)(2,1)S(1)} collective-permute-done((f16[10,72,128]{2,1,0:T(8,128)(2,1)S(1)}, f16[10,72,128]{2,1,0:T(8,128)(2,1)S(1)}, u32[]{:S(2)}, u32[]{:S(2)}) %collective-permute-start.7) | collective-permute-done | bytes 184352 | tf_op jit(solution)/shard_map/ppermute | solution.py:28
  21.3 2.7 %collective-permute-start.6 = (f16[10,32,128]{2,1,0:T(8,128)(2,1)S(1)}, f16[10,32,128]{2,1,0:T(8,128)(2,1)S(1)}, u32[]{:S(2)}, u32[]{:S(2)}) collective-permute-start(f16[10,32,128]{2,1,0:T(8,128)(2,1)S(1)} %pad_maximum_fusion.5), channel_id=1, source_target_pairs={{0,8},{1,9},{2,10},{3,11},{4,12},{5,13},{6,14},{7,15},{8,0},{9,1},... | collective-permute-start | bytes 245768 | tf_op jit(solution)/shard_map/ppermute | solution.py:28
  25.0 4.2 %collective-permute-done.6 = f16[10,32,128]{2,1,0:T(8,128)(2,1)S(1)} collective-permute-done((f16[10,32,128]{2,1,0:T(8,128)(2,1)S(1)}, f16[10,32,128]{2,1,0:T(8,128)(2,1)S(1)}, u32[]{:S(2)}, u32[]{:S(2)}) %collective-permute-start.6) | collective-permute-done | bytes 81952 | tf_op jit(solution)/shard_map/ppermute | solution.py:28
  30.3 2.1 %collective-permute-start.9 = (f32[2,128,128]{2,1,0:T(8,128)S(1)}, f32[2,128,128]{2,1,0:T(8,128)S(1)}, u32[]{:S(2)}, u32[]{:S(2)}) collective-permute-start(f32[2,128,128]{2,1,0:T(8,128)S(1)} %shard_map.60), channel_id=1, source_target_pairs={{0,4},{1,5},{2,6},{3,7},{4,0},{5,1},{6,2},{7,3},{8,12},{9,13},{10,... | collective-permute-start | bytes 393224 | tf_op jit(solution)/shard_map/ppermute | solution.py:28
  32.4 1.6 %collective-permute-done.10 = bf16[32,288]{1,0:T(8,128)(2,1)S(1)} collective-permute-done((bf16[32,288]{1,0:T(8,128)(2,1)S(1)}, bf16[32,288]{1,0:T(8,128)(2,1)S(1)}, u32[]{:S(2)}, u32[]{:S(2)}) %collective-permute-start.10) | collective-permute-done | bytes 18464 | tf_op jit(solution)/shard_map/ppermute | solution.py:28
  34.2 1.6 %collective-permute-start.13 = (bf16[32,576]{1,0:T(8,128)(2,1)S(1)}, bf16[32,576]{1,0:T(8,128)(2,1)S(1)}, u32[]{:S(2)}, u32[]{:S(2)}) collective-permute-start(bf16[32,576]{1,0:T(8,128)(2,1)S(1)} %maximum_select_fusion.1), channel_id=1, source_target_pairs={{16,0},{17,1},{18,2},{19,3},{20,4},{21,5},{22,6},{23,7},{24,8},{25... | collective-permute-start | bytes 110600 | tf_op jit(solution)/shard_map/ppermute | solution.py:24
  36.7 2.6 %collective-permute-start.17 = (f32[2,128,128]{2,1,0:T(8,128)S(1)}, f32[2,128,128]{2,1,0:T(8,128)S(1)}, u32[]{:S(2)}, u32[]{:S(2)}) collective-permute-start(f32[2,128,128]{2,1,0:T(8,128)S(1)} %add.92), channel_id=1, source_target_pairs={{0,8},{1,9},{2,10},{3,11},{4,12},{5,13},{6,14},{7,15},{8,0},{9,1},... | collective-permute-start | bytes 393224 | tf_op jit(solution)/shard_map/ppermute | solution.py:28
  39.2 2.3 %collective-permute-done.14 = bf16[32,576]{1,0:T(8,128)(2,1)S(1)} collective-permute-done((bf16[32,576]{1,0:T(8,128)(2,1)S(1)}, bf16[32,576]{1,0:T(8,128)(2,1)S(1)}, u32[]{:S(2)}, u32[]{:S(2)}) %collective-permute-start.14) | collective-permute-done | bytes 36896 | tf_op jit(solution)/shard_map/ppermute | solution.py:24
  41.7 4.6 %collective-permute-done.17 = f32[2,128,128]{2,1,0:T(8,128)S(1)} collective-permute-done((f32[2,128,128]{2,1,0:T(8,128)S(1)}, f32[2,128,128]{2,1,0:T(8,128)S(1)}, u32[]{:S(2)}, u32[]{:S(2)}) %collective-permute-start.17) | collective-permute-done | bytes 131104 | tf_op jit(solution)/shard_map/ppermute | solution.py:28
  46.3 1.7 %shard_map.62 = (f32[32,1152]{1,0:T(8,128)S(1)}, bf16[32,1152]{1,0:T(8,128)(2,1)S(1)}) custom-call(bf16[2,512,128]{2,1,0:T(8,128)(2,1)S(1)} %pad_maximum_fusion.part_0, bf16[2,512,128]{2,1,0:T(8,128)(2,1)S(1)} %collective-permute-done.8.part_1, bf16[2,512,128]{2,1,0:T(8,128)(2,1)S(1)} %collective-permute-done.11.part_2, ...), custom_call_target="tpu_custom_call" | custom-call | tf_op jit(solution)/shard_map/pallas_call | solution.py:342
  48.7 3.7 %collective-permute-done.15 = bf16[32,1152]{1,0:T(8,128)(2,1)S(1)} collective-permute-done((bf16[32,1152]{1,0:T(8,128)(2,1)S(1)}, bf16[32,1152]{1,0:T(8,128)(2,1)S(1)}, u32[]{:S(2)}, u32[]{:S(2)}) %collective-permute-start.15) | collective-permute-done | bytes 73760 | tf_op jit(solution)/shard_map/ppermute | solution.py:28
  52.4 1.0 %collective-permute-start.16 = (bf16[32,1152]{1,0:T(8,128)(2,1)S(1)}, bf16[32,1152]{1,0:T(8,128)(2,1)S(1)}, u32[]{:S(2)}, u32[]{:S(2)}) collective-permute-start(bf16[32,1152]{1,0:T(8,128)(2,1)S(1)} %fusion.14), channel_id=1, source_target_pairs={{0,8},{1,9},{2,10},{3,11},{4,12},{5,13},{6,14},{7,15},{8,0},{9,1},... | collective-permute-start | bytes 221192 | tf_op jit(solution)/shard_map/ppermute | solution.py:28
  53.7 4.4 %collective-permute-done.16 = bf16[32,1152]{1,0:T(8,128)(2,1)S(1)} collective-permute-done((bf16[32,1152]{1,0:T(8,128)(2,1)S(1)}, bf16[32,1152]{1,0:T(8,128)(2,1)S(1)}, u32[]{:S(2)}, u32[]{:S(2)}) %collective-permute-start.16) | collective-permute-done | bytes 73760 | tf_op jit(solution)/shard_map/ppermute | solution.py:28
  59.5 1.3 %shard_map.63 = (f32[2,72,128]{2,1,0:T(8,128)S(1)}, f32[2,72,128]{2,1,0:T(8,128)S(1)}) custom-call(f32[32,1152]{1,0:T(8,128)S(1)} %convert_add_fusion.cross_t, f32[32,128]{1,0:T(8,128)S(1)} %dynamic-slice_multiply_fusion.mixed_in, bf16[2,9,144,128]{3,2,1,0:T(8,128)(2,1)S(1)} %get-tuple-element.70.k_a, bf16[2,9,144,128]{3,2,1,0:T(8,128)(2,1)S(1)} %get-tuple-element.71.k_b, ...), custom_call_target="tpu_custom_call" | custom-call | tf_op jit(solution)/shard_map/pallas_call | solution.py:364
  61.1 4.2 %collective-permute-done.20 = f32[2,72,128]{2,1,0:T(8,128)S(1)} collective-permute-done((f32[2,72,128]{2,1,0:T(8,128)S(1)}, f32[2,72,128]{2,1,0:T(8,128)S(1)}, u32[]{:S(2)}, u32[]{:S(2)}) %collective-permute-start.20) | collective-permute-done | bytes 73760 | tf_op jit(solution)/shard_map/ppermute | solution.py:28
  65.4 1.2 %collective-permute-done.21 = f32[72,128]{1,0:T(8,128)S(1)} collective-permute-done((f32[72,128]{1,0:T(8,128)S(1)}, f32[72,128]{1,0:T(8,128)S(1)}, u32[]{:S(2)}, u32[]{:S(2)}) %collective-permute-start.21) | collective-permute-done | bytes 36896 | tf_op jit(solution)/shard_map/ppermute | solution.py:28
  (80 shorter events, 8.3 us)
Async XLA Ops:
  2.9 1.8 %collective-permute-start = (f32[2,10,32,128]{3,2,1,0:T(8,128)S(1)}, f32[2,10,32,128]{3,2,1,0:T(8,128)S(1)}, u32[]{:S(2)}, u32[]{:S(2)}) collective-permute-start(f32[2,10,32,128]{3,2,1,0:T(8,128)S(1)} %get-tuple-element.28), channel_id=1, source_target_pairs={{0,1},{1,0},{2,3},{3,2},{4,5},{5,4},{6,7},{7,6},{8,9},{9,8},{10,11... | collective-permute-start | bytes 983048 | tf_op jit(solution)/shard_map/ppermute | solution.py:28
  4.7 7.8 %copy-start = (bf16[1,2,16,16,128]{4,3,2,1,0:T(8,128)(2,1)S(1)}, bf16[1,2,16,16,128]{4,3,2,1,0:T(8,128)(2,1)}, u32[]{:S(2)}) copy-start(bf16[1,2,16,16,128]{4,3,2,1,0:T(8,128)(2,1)} %param.5) | copy-start | bytes 393220
  4.7 7.8 %copy-start.1 = (bf16[1,2,16,16,128]{4,3,2,1,0:T(8,128)(2,1)S(1)}, bf16[1,2,16,16,128]{4,3,2,1,0:T(8,128)(2,1)}, u32[]{:S(2)}) copy-start(bf16[1,2,16,16,128]{4,3,2,1,0:T(8,128)(2,1)} %param.4) | copy-start | bytes 393220
  4.8 5.7 %collective-permute-start.2 = (f16[10,32,128]{2,1,0:T(8,128)(2,1)S(1)}, f16[10,32,128]{2,1,0:T(8,128)(2,1)S(1)}, u32[]{:S(2)}, u32[]{:S(2)}) collective-permute-start(f16[10,32,128]{2,1,0:T(8,128)(2,1)S(1)} %pad_maximum_fusion.3), channel_id=1, source_target_pairs={{0,2},{1,3},{2,0},{3,1},{4,6},{5,7},{6,4},{7,5},{8,10},{9,11},{10,... | collective-permute-start | bytes 245768 | tf_op jit(solution)/shard_map/ppermute | solution.py:28
  10.6 5.7 %collective-permute-start.3 = (f16[10,32,128]{2,1,0:T(8,128)(2,1)S(1)}, f16[10,32,128]{2,1,0:T(8,128)(2,1)S(1)}, u32[]{:S(2)}, u32[]{:S(2)}) collective-permute-start(f16[10,32,128]{2,1,0:T(8,128)(2,1)S(1)} %pad_maximum_fusion.4), channel_id=1, source_target_pairs={{0,4},{1,5},{2,6},{3,7},{4,0},{5,1},{6,2},{7,3},{8,12},{9,13},{10,... | collective-permute-start | bytes 245768 | tf_op jit(solution)/shard_map/ppermute | solution.py:28
  12.5 6.7 %collective-permute-start.4 = (f16[10,72,128]{2,1,0:T(8,128)(2,1)S(1)}, f16[10,72,128]{2,1,0:T(8,128)(2,1)S(1)}, u32[]{:S(2)}, u32[]{:S(2)}) collective-permute-start(f16[10,72,128]{2,1,0:T(8,128)(2,1)S(1)} %convert_element_type.39), channel_id=1, source_target_pairs={{0,2},{1,3},{2,0},{3,1},{4,6},{5,7},{6,4},{7,5},{8,10},{9,11},{10,... | collective-permute-start | bytes 552968 | tf_op jit(solution)/shard_map/ppermute | solution.py:28
  14.1 5.2 %collective-permute-start.5 = (f16[10,72,128]{2,1,0:T(8,128)(2,1)S(1)}, f16[10,72,128]{2,1,0:T(8,128)(2,1)S(1)}, u32[]{:S(2)}, u32[]{:S(2)}) collective-permute-start(f16[10,72,128]{2,1,0:T(8,128)(2,1)S(1)} %convert_element_type.39), channel_id=1, source_target_pairs={{0,1},{1,0},{2,3},{3,2},{4,5},{5,4},{6,7},{7,6},{8,9},{9,8},{10,11... | collective-permute-start | bytes 552968 | tf_op jit(solution)/shard_map/ppermute | solution.py:28
  14.1 7.0 %collective-permute-start.7 = (f16[10,72,128]{2,1,0:T(8,128)(2,1)S(1)}, f16[10,72,128]{2,1,0:T(8,128)(2,1)S(1)}, u32[]{:S(2)}, u32[]{:S(2)}) collective-permute-start(f16[10,72,128]{2,1,0:T(8,128)(2,1)S(1)} %convert_element_type.39), channel_id=1, source_target_pairs={{0,3},{1,2},{2,1},{3,0},{4,7},{5,6},{6,5},{7,4},{8,11},{9,10},{10,... | collective-permute-start | bytes 552968 | tf_op jit(solution)/shard_map/ppermute | solution.py:28
  14.8 9.4 %collective-permute-start.1 = (bf16[2,512,128]{2,1,0:T(8,128)(2,1)S(1)}, bf16[2,512,128]{2,1,0:T(8,128)(2,1)S(1)}, u32[]{:S(2)}, u32[]{:S(2)}) collective-permute-start(bf16[2,512,128]{2,1,0:T(8,128)(2,1)S(1)} %pad_maximum_fusion.1), channel_id=1, source_target_pairs={{16,0},{17,1},{18,2},{19,3},{20,4},{21,5},{22,6},{23,7},{24,8},{25... | collective-permute-start | bytes 786440 | tf_op jit(solution)/shard_map/ppermute | solution.py:24
  21.3 7.9 %collective-permute-start.6 = (f16[10,32,128]{2,1,0:T(8,128)(2,1)S(1)}, f16[10,32,128]{2,1,0:T(8,128)(2,1)S(1)}, u32[]{:S(2)}, u32[]{:S(2)}) collective-permute-start(f16[10,32,128]{2,1,0:T(8,128)(2,1)S(1)} %pad_maximum_fusion.5), channel_id=1, source_target_pairs={{0,8},{1,9},{2,10},{3,11},{4,12},{5,13},{6,14},{7,15},{8,0},{9,1},... | collective-permute-start | bytes 245768 | tf_op jit(solution)/shard_map/ppermute | solution.py:28
  24.2 12.4 %collective-permute-start.8 = (bf16[2,512,128]{2,1,0:T(8,128)(2,1)S(1)}, bf16[2,512,128]{2,1,0:T(8,128)(2,1)S(1)}, u32[]{:S(2)}, u32[]{:S(2)}) collective-permute-start(bf16[2,512,128]{2,1,0:T(8,128)(2,1)S(1)} %pad_maximum_fusion.part_0), channel_id=1, source_target_pairs={{0,2},{1,3},{2,0},{3,1},{4,6},{5,7},{6,4},{7,5},{8,10},{9,11},{10,... | collective-permute-start | bytes 786440 | tf_op jit(solution)/shard_map/ppermute | solution.py:28
  30.0 4.0 %collective-permute-start.10 = (bf16[32,288]{1,0:T(8,128)(2,1)S(1)}, bf16[32,288]{1,0:T(8,128)(2,1)S(1)}, u32[]{:S(2)}, u32[]{:S(2)}) collective-permute-start(bf16[32,288]{1,0:T(8,128)(2,1)S(1)} %get-tuple-element.37), channel_id=1, source_target_pairs={{0,4},{1,5},{2,6},{3,7},{4,0},{5,1},{6,2},{7,3},{8,12},{9,13},{10,... | collective-permute-start | bytes 55304 | tf_op jit(solution)/shard_map/ppermute | solution.py:28
  30.3 6.2 %collective-permute-start.9 = (f32[2,128,128]{2,1,0:T(8,128)S(1)}, f32[2,128,128]{2,1,0:T(8,128)S(1)}, u32[]{:S(2)}, u32[]{:S(2)}) collective-permute-start(f32[2,128,128]{2,1,0:T(8,128)S(1)} %shard_map.60), channel_id=1, source_target_pairs={{0,4},{1,5},{2,6},{3,7},{4,0},{5,1},{6,2},{7,3},{8,12},{9,13},{10,... | collective-permute-start | bytes 393224 | tf_op jit(solution)/shard_map/ppermute | solution.py:28
  32.4 13.8 %collective-permute-start.11 = (bf16[2,512,128]{2,1,0:T(8,128)(2,1)S(1)}, bf16[2,512,128]{2,1,0:T(8,128)(2,1)S(1)}, u32[]{:S(2)}, u32[]{:S(2)}) collective-permute-start(bf16[2,512,128]{2,1,0:T(8,128)(2,1)S(1)} %pad_maximum_fusion.part_0), channel_id=1, source_target_pairs={{0,1},{1,0},{2,3},{3,2},{4,5},{5,4},{6,7},{7,6},{8,9},{9,8},{10,11... | collective-permute-start | bytes 786440 | tf_op jit(solution)/shard_map/ppermute | solution.py:28
  34.2 5.1 %collective-permute-start.13 = (bf16[32,576]{1,0:T(8,128)(2,1)S(1)}, bf16[32,576]{1,0:T(8,128)(2,1)S(1)}, u32[]{:S(2)}, u32[]{:S(2)}) collective-permute-start(bf16[32,576]{1,0:T(8,128)(2,1)S(1)} %maximum_select_fusion.1), channel_id=1, source_target_pairs={{16,0},{17,1},{18,2},{19,3},{20,4},{21,5},{22,6},{23,7},{24,8},{25... | collective-permute-start | bytes 110600 | tf_op jit(solution)/shard_map/ppermute | solution.py:24
  35.8 5.8 %collective-permute-start.14 = (bf16[32,576]{1,0:T(8,128)(2,1)S(1)}, bf16[32,576]{1,0:T(8,128)(2,1)S(1)}, u32[]{:S(2)}, u32[]{:S(2)}) collective-permute-start(bf16[32,576]{1,0:T(8,128)(2,1)S(1)} %maximum_select_fusion.1), channel_id=1, source_target_pairs={{24,0},{25,1},{26,2},{27,3},{28,4},{29,5},{30,6},{31,7},{16,8},{17... | collective-permute-start | bytes 110600 | tf_op jit(solution)/shard_map/ppermute | solution.py:24
  36.6 9.7 %collective-permute-start.12 = (bf16[2,512,128]{2,1,0:T(8,128)(2,1)S(1)}, bf16[2,512,128]{2,1,0:T(8,128)(2,1)S(1)}, u32[]{:S(2)}, u32[]{:S(2)}) collective-permute-start(bf16[2,512,128]{2,1,0:T(8,128)(2,1)S(1)} %collective-permute-done.8.part_1), channel_id=1, source_target_pairs={{0,1},{1,0},{2,3},{3,2},{4,5},{5,4},{6,7},{7,6},{8,9},{9,8},{10,11... | collective-permute-start | bytes 786440 | tf_op jit(solution)/shard_map/ppermute | solution.py:28
  36.7 9.6 %collective-permute-start.17 = (f32[2,128,128]{2,1,0:T(8,128)S(1)}, f32[2,128,128]{2,1,0:T(8,128)S(1)}, u32[]{:S(2)}, u32[]{:S(2)}) collective-permute-start(f32[2,128,128]{2,1,0:T(8,128)S(1)} %add.92), channel_id=1, source_target_pairs={{0,8},{1,9},{2,10},{3,11},{4,12},{5,13},{6,14},{7,15},{8,0},{9,1},... | collective-permute-start | bytes 393224 | tf_op jit(solution)/shard_map/ppermute | solution.py:28
  48.0 4.4 %collective-permute-start.15 = (bf16[32,1152]{1,0:T(8,128)(2,1)S(1)}, bf16[32,1152]{1,0:T(8,128)(2,1)S(1)}, u32[]{:S(2)}, u32[]{:S(2)}) collective-permute-start(bf16[32,1152]{1,0:T(8,128)(2,1)S(1)} %get-tuple-element.42), channel_id=1, source_target_pairs={{0,4},{1,5},{2,6},{3,7},{4,0},{5,1},{6,2},{7,3},{8,12},{9,13},{10,... | collective-permute-start | bytes 221192 | tf_op jit(solution)/shard_map/ppermute | solution.py:28
  48.1 5.4 %collective-permute-start.18 = (f32[2,128,128]{2,1,0:T(8,128)S(1)}, f32[2,128,128]{2,1,0:T(8,128)S(1)}, u32[]{:S(2)}, u32[]{:S(2)}) collective-permute-start(f32[2,128,128]{2,1,0:T(8,128)S(1)} %add.95), channel_id=1, source_target_pairs={{0,1},{1,0},{2,3},{3,2},{4,5},{5,4},{6,7},{7,6},{8,9},{9,8},{10,11... | collective-permute-start | bytes 393224 | tf_op jit(solution)/shard_map/ppermute | solution.py:28
  52.4 5.6 %collective-permute-start.16 = (bf16[32,1152]{1,0:T(8,128)(2,1)S(1)}, bf16[32,1152]{1,0:T(8,128)(2,1)S(1)}, u32[]{:S(2)}, u32[]{:S(2)}) collective-permute-start(bf16[32,1152]{1,0:T(8,128)(2,1)S(1)} %fusion.14), channel_id=1, source_target_pairs={{0,8},{1,9},{2,10},{3,11},{4,12},{5,13},{6,14},{7,15},{8,0},{9,1},... | collective-permute-start | bytes 221192 | tf_op jit(solution)/shard_map/ppermute | solution.py:28
  53.5 5.0 %collective-permute-start.19 = (f32[2,128,128]{2,1,0:T(8,128)S(1)}, f32[2,128,128]{2,1,0:T(8,128)S(1)}, u32[]{:S(2)}, u32[]{:S(2)}) collective-permute-start(f32[2,128,128]{2,1,0:T(8,128)S(1)} %add.96), channel_id=1, source_target_pairs={{0,2},{1,3},{2,0},{3,1},{4,6},{5,7},{6,4},{7,5},{8,10},{9,11},{10,... | collective-permute-start | bytes 393224 | tf_op jit(solution)/shard_map/ppermute | solution.py:28
  60.9 4.4 %collective-permute-start.20 = (f32[2,72,128]{2,1,0:T(8,128)S(1)}, f32[2,72,128]{2,1,0:T(8,128)S(1)}, u32[]{:S(2)}, u32[]{:S(2)}) collective-permute-start(f32[2,72,128]{2,1,0:T(8,128)S(1)} %get-tuple-element.51), channel_id=1, source_target_pairs={{0,2},{1,3},{2,0},{3,1},{4,6},{5,7},{6,4},{7,5},{8,10},{9,11},{10,... | collective-permute-start | bytes 221192 | tf_op jit(solution)/shard_map/ppermute | solution.py:28
  65.3 1.3 %collective-permute-start.21 = (f32[72,128]{1,0:T(8,128)S(1)}, f32[72,128]{1,0:T(8,128)S(1)}, u32[]{:S(2)}, u32[]{:S(2)}) collective-permute-start(f32[72,128]{1,0:T(8,128)S(1)} %slice_bitcast_fusion.5), channel_id=1, source_target_pairs={{0,1},{1,0},{2,3},{3,2},{4,5},{5,4},{6,7},{7,6},{8,9},{9,8},{10,11... | collective-permute-start | bytes 110600 | tf_op jit(solution)/shard_map/ppermute | solution.py:28
  (1 other events, 5.8 us)

commit v11 on v10

--- a/solution.py
+++ b/solution.py
@@ -213,11 +213,21 @@
         send[i] = result[rows:]
 
 
-def gram_kernel(grads, next_grads, out):
+def gram_kernel(grads, next_grads, *refs):
+    outs, scratch = refs[:4], refs[4]
+    core, xbit = place_bits()
+    mine = 2 * core + xbit
+    width = grads.shape[1]
+    quarter = width // 4
     g = grads[...]
     last = lax.axis_index("layer") == lax.axis_size("layer") - 1
-    out[0] = dot_t(g, g)
-    out[1] = jnp.where(last, 0.0, dot_t(g, next_grads[...]))
+    scratch[0] = dot_t(g, g)
+    scratch[1] = jnp.where(last, 0.0, dot_t(next_grads[...], g))
+    for j in range(4):
+        for i in range(2):
+            outs[j][i * quarter : (i + 1) * quarter] = scratch[
+                i, pl.ds(pl.multiple_of((mine ^ j) * quarter, quarter), quarter), :
+            ]
 
 
 VMEM = pl.BlockSpec(memory_space=pltpu.VMEM)
@@ -288,7 +298,6 @@
 
     h, level = add(h, level, 2)
     h, level = add(h, level, zbits[0])
-    h, k_others[0], k_others[1] = lax.optimization_barrier((h, k_others[0], k_others[1]))
     next_own = behind(next_own, h)
     two_own = jnp.stack([flat_maps, next_own[0]])
     two_x = swap(two_own, 2)
@@ -318,22 +327,25 @@
     def by_bit(mine, other, b):
         return jnp.where((me & b) == 0, jnp.concatenate([mine, other], 1), jnp.concatenate([other, mine], 1))
 
-    gram = pl.pallas_call(
+    grams = pl.pallas_call(
         gram_kernel,
-        out_shape=jax.ShapeDtypeStruct((2, width, width), F32),
+        out_shape=[jax.ShapeDtypeStruct((2 * quarter, width), F32)] * 4,
         in_specs=[VMEM] * 2,
-        out_specs=VMEM,
+        out_specs=[VMEM] * 4,
+        scratch_shapes=[pltpu.VMEM((2, width, width), F32)],
         compiler_params=PARAMS,
     )(flat_grads, next_own[1])
-    gram, two_own = behind((gram, two_own), p_t)
+    grams = behind(grams, p_t)
+    grams = [grams[0]] + [swap(grams[j], bits) for j, bits in ((1, 2), (2, 1), (3, 3))]
+    for b in zbits[:-1]:
+        p_t = by_bit(p_t, swap(p_t, b), b)
+
+    two_own, two_x, grams = behind((two_own, two_x, grams), p_t)
     core_own = swap(two_own, 1)
+    core_x = swap(two_x, 1)
+    gram = (grams[0] + grams[1]) + (grams[2] + grams[3])
     for b in zbits[:-1]:
         gram = gram + swap(gram, b)
-        p_t = by_bit(p_t, swap(p_t, b), b)
-
-    two_x, gram = behind((two_x, gram), p_t)
-    core_x = swap(two_x, 1)
-    gram = gram + swap(gram, zbits[-1])
     low = cols * quarter
     last = lax.axis_index("layer") == lax.axis_size("layer") - 1
     p_t = by_bit(after(p_t), after(p_t, zbits[-1]), zbits[-1])
@@ -348,7 +360,7 @@
     )(two_own, two_x, core_own, core_x, p_t)
 
     gram = behind(gram, cross_half)
-    gram = gram + swap(gram, 1)
+    gram = gram + swap(gram, zbits[-1])
     place = (jnp.arange(width)[None, :] == low + jnp.arange(quarter)[:, None]).astype(F32)
     main_a, main_b = behind((main_a, main_b), cross_half)
     main = jnp.stack([dot_t(main_a, place, precision=HIGH), dot_t(main_b, place, precision=HIGH)])
@@ -357,9 +369,8 @@
         cross_half = cross_t.astype(BF16)
         if i == 0:
             gram = behind(gram, cross_half)
-            gram = gram + swap(gram, 2)
-            mixed = dot_t(gram[1], g_inv, precision=HIGH) * (scale * scale)
-            mixed = lax.dynamic_slice_in_dim(mixed, low, quarter, 0)
+            mixed = jnp.dot(gram[quarter:], g_inv, precision=HIGH) * (scale * scale)
+            grams = [gram] + [swap(gram, bits) for bits in (2, 1, 3)]
 
     out, send = pl.pallas_call(
         update_kernel,
@@ -370,7 +381,12 @@
     )(cross_t, mixed, k_a, k_b, main)
     out = out + swap(send, 2)
     update = out[0] + swap(out[1], 1)
-    return (update[None], (gram * scale)[None])
+
+    grams = jnp.stack(behind(grams, out)).reshape(2, 2, 2, quarter, width) * scale
+    grams = jnp.where(xbit == 0, grams, grams[:, ::-1])
+    grams = jnp.where(core == 0, grams, grams[::-1])
+    grams = grams.transpose(2, 4, 0, 1, 3).reshape(2, width, width)
+    return (update[None], grams[None])
 
 
 def solution(mesh):

time: 67.4 us -> 62 us (0.920)
  waiting for transfers between devices: 35.3 us -> 21.5 us
  starting transfers between devices: 21.2 us -> 29.7 us
  local copies, waits for them, and re-layouts: 0.04 us -> 0.81 us
  other arithmetic: 2.51 us -> 1.83 us
    ppermute x19 -> x23, waiting for transfers between devices: 33 us -> 20.1 us  [swap(): lax.ppermute(block, 'pos', [(i, i ^ bit) for i in range(lax.axis_size('po...]
    ppermute x19 -> x23, starting transfers between devices: 17.4 us -> 23.2 us  [swap(): lax.ppermute(block, 'pos', [(i, i ^ bit) for i in range(lax.axis_size('po...]
    ppermute x3, starting transfers between devices: 3.87 us -> 6.48 us  [after(): return lax.ppermute(block, ('layer', 'pos'), route)]
    ppermute x3, waiting for transfers between devices: 2.31 us -> 1.37 us  [after(): return lax.ppermute(block, ('layer', 'pos'), route)]
    unnamed x6 -> x7, local copies, waits for them, and re-layouts: 0.02 us -> 0.78 us
    broadcast_in_dim x2 -> x1, other arithmetic: 1.3 us -> 0.62 us  [per_device(): return (update[None], grams[None])]
  transfers between devices with their start and end apart: 22 -> 26, of which waited for: 13 -> 13; matrix products, arithmetic and copies ran while one was open for 2% -> 4% of each run, Pallas kernels for 2% -> 2%
where the time goes in v11:
time: 62 us; the launch traced here: 61.8 us
  starting transfers between devices  29.7 us (48%)
  waiting for transfers between devices  21.5 us (35%)
  Pallas kernels  6.22 us (10%)
  other arithmetic  1.83 us (3%)
  between operations  1.05 us (2%)
  local copies, waits for them, and re-layouts  0.81 us (1%)
  matrix products  0.72 us (1%)
    ppermute x23, starting transfers between devices, swap(): lax.ppermute(block, 'pos', [(i, i ^ bit) for i in range(lax.axis_size('po...  23.2 us
    ppermute x23, waiting for transfers between devices, swap(): lax.ppermute(block, 'pos', [(i, i ^ bit) for i in range(lax.axis_size('po...  20.1 us
    ppermute x3, starting transfers between devices, after(): return lax.ppermute(block, ('layer', 'pos'), route)  6.48 us
    pallas_call x1, Pallas kernels, per_device(): pl.pallas_call(functools.partial(grad_kernel, side), out_shape=[jax.Shape...  2.21 us
    pallas_call x1, Pallas kernels, per_device(): pl.pallas_call(functools.partial(cross_kernel, side), out_shape=[jax.Shap...  1.68 us
    ppermute x3, waiting for transfers between devices, after(): return lax.ppermute(block, ('layer', 'pos'), route)  1.37 us
    pallas_call x1, Pallas kernels, per_device(): pl.pallas_call(update_kernel, out_shape=[jax.ShapeDtypeStruct((2, rows, w...  1.31 us
  transfers between devices with their start and end apart: 26, of which 13 were waited for; matrix products, arithmetic and copies ran while one was open for 4% of the time, Pallas kernels for 2%

profile of v11, /device:TPU:0, one launch (start us, length us, event | category | flops | bytes accessed | tf_op | source)
XLA Modules:
  0.0 61.8 jit_solution(4215731435418869645)
XLA Ops:
  0.6 2.2 %shard_map.59 = (f32[2,10,32,128]{3,2,1,0:T(8,128)S(1)}, f32[2,10,32,128]{3,2,1,0:T(8,128)S(1)}, bf16[2,9,72,128]{3,2,1,0:T(8,128)(2,1)S(1)}, f32[10,72,128]{2,1,0:T(8,128)S(1)}) custom-call(bf16[512,128]{1,0:T(8,128)(2,1)} %bitcast.91, bf16[512,128]{1,0:T(8,128)(2,1)} %bitcast.88, f32[128,128]{1,0:T(8,128)} %bitcast.97, f32[72,1152]{1,0:T(8,128)} %bitcast.96), custom_call_target="tpu_custom_call" | custom-call | tf_op jit(solution)/shard_map/pallas_call | solution.py:257
  3.4 1.3 %collective-permute-done = f32[2,10,32,128]{3,2,1,0:T(8,128)S(1)} collective-permute-done((f32[2,10,32,128]{3,2,1,0:T(8,128)S(1)}, f32[2,10,32,128]{3,2,1,0:T(8,128)S(1)}, u32[]{:S(2)}, u32[]{:S(2)}) %collective-permute-start) | collective-permute-done | bytes 327712 | tf_op jit(solution)/shard_map/ppermute | solution.py:28
  4.8 2.9 %collective-permute-start.2 = (f16[10,32,128]{2,1,0:T(8,128)(2,1)S(1)}, f16[10,32,128]{2,1,0:T(8,128)(2,1)S(1)}, u32[]{:S(2)}, u32[]{:S(2)}) collective-permute-start(f16[10,32,128]{2,1,0:T(8,128)(2,1)S(1)} %pad_maximum_fusion.4), channel_id=1, source_target_pairs={{0,2},{1,3},{2,0},{3,1},{4,6},{5,7},{6,4},{7,5},{8,10},{9,11},{10,... | collective-permute-start | bytes 245768 | tf_op jit(solution)/shard_map/ppermute | solution.py:28
  7.7 2.7 %collective-permute-done.2 = f16[10,32,128]{2,1,0:T(8,128)(2,1)S(1)} collective-permute-done((f16[10,32,128]{2,1,0:T(8,128)(2,1)S(1)}, f16[10,32,128]{2,1,0:T(8,128)(2,1)S(1)}, u32[]{:S(2)}, u32[]{:S(2)}) %collective-permute-start.2) | collective-permute-done | bytes 81952 | tf_op jit(solution)/shard_map/ppermute | solution.py:28
  10.6 1.9 %collective-permute-start.3 = (f16[10,32,128]{2,1,0:T(8,128)(2,1)S(1)}, f16[10,32,128]{2,1,0:T(8,128)(2,1)S(1)}, u32[]{:S(2)}, u32[]{:S(2)}) collective-permute-start(f16[10,32,128]{2,1,0:T(8,128)(2,1)S(1)} %pad_maximum_fusion.5), channel_id=1, source_target_pairs={{0,4},{1,5},{2,6},{3,7},{4,0},{5,1},{6,2},{7,3},{8,12},{9,13},{10,... | collective-permute-start | bytes 245768 | tf_op jit(solution)/shard_map/ppermute | solution.py:28
  12.7 1.5 %collective-permute-start.7 = (f16[10,72,128]{2,1,0:T(8,128)(2,1)S(1)}, f16[10,72,128]{2,1,0:T(8,128)(2,1)S(1)}, u32[]{:S(2)}, u32[]{:S(2)}) collective-permute-start(f16[10,72,128]{2,1,0:T(8,128)(2,1)S(1)} %convert_element_type.40), channel_id=1, source_target_pairs={{0,1},{1,0},{2,3},{3,2},{4,5},{5,4},{6,7},{7,6},{8,9},{9,8},{10,11... | collective-permute-start | bytes 552968 | tf_op jit(solution)/shard_map/ppermute | solution.py:28
  14.8 1.5 %collective-permute-start.1 = (bf16[2,512,128]{2,1,0:T(8,128)(2,1)S(1)}, bf16[2,512,128]{2,1,0:T(8,128)(2,1)S(1)}, u32[]{:S(2)}, u32[]{:S(2)}) collective-permute-start(bf16[2,512,128]{2,1,0:T(8,128)(2,1)S(1)} %pad_maximum_fusion), channel_id=1, source_target_pairs={{16,0},{17,1},{18,2},{19,3},{20,4},{21,5},{22,6},{23,7},{24,8},{25... | collective-permute-start | bytes 786440 | tf_op jit(solution)/shard_map/ppermute | solution.py:24
  16.4 2.7 %collective-permute-start.5 = (f16[10,32,128]{2,1,0:T(8,128)(2,1)S(1)}, f16[10,32,128]{2,1,0:T(8,128)(2,1)S(1)}, u32[]{:S(2)}, u32[]{:S(2)}) collective-permute-start(f16[10,32,128]{2,1,0:T(8,128)(2,1)S(1)} %pad_maximum_fusion.6), channel_id=1, source_target_pairs={{0,8},{1,9},{2,10},{3,11},{4,12},{5,13},{6,14},{7,15},{8,0},{9,1},... | collective-permute-start | bytes 245768 | tf_op jit(solution)/shard_map/ppermute | solution.py:28
  19.8 3.7 %collective-permute-done.6 = f16[10,72,128]{2,1,0:T(8,128)(2,1)S(1)} collective-permute-done((f16[10,72,128]{2,1,0:T(8,128)(2,1)S(1)}, f16[10,72,128]{2,1,0:T(8,128)(2,1)S(1)}, u32[]{:S(2)}, u32[]{:S(2)}) %collective-permute-start.6) | collective-permute-done | bytes 184352 | tf_op jit(solution)/shard_map/ppermute | solution.py:28
  25.8 1.5 %collective-permute-start.9 = (f32[64,128]{1,0:T(8,128)S(1)}, f32[64,128]{1,0:T(8,128)S(1)}, u32[]{:S(2)}, u32[]{:S(2)}) collective-permute-start(f32[64,128]{1,0:T(8,128)S(1)} %get-tuple-element.51), channel_id=1, source_target_pairs={{0,2},{1,3},{2,0},{3,1},{4,6},{5,7},{6,4},{7,5},{8,10},{9,11},{10,... | collective-permute-start | bytes 98312 | tf_op jit(solution)/shard_map/ppermute | solution.py:28
  28.0 1.1 %collective-permute-done.12 = bf16[32,288]{1,0:T(8,128)(2,1)S(1)} collective-permute-done((bf16[32,288]{1,0:T(8,128)(2,1)S(1)}, bf16[32,288]{1,0:T(8,128)(2,1)S(1)}, u32[]{:S(2)}, u32[]{:S(2)}) %collective-permute-start.12) | collective-permute-done | bytes 18464 | tf_op jit(solution)/shard_map/ppermute | solution.py:28
  29.2 3.4 %collective-permute-start.16 = (bf16[32,576]{1,0:T(8,128)(2,1)S(1)}, bf16[32,576]{1,0:T(8,128)(2,1)S(1)}, u32[]{:S(2)}, u32[]{:S(2)}) collective-permute-start(bf16[32,576]{1,0:T(8,128)(2,1)S(1)} %maximum_select_fusion.1), channel_id=1, source_target_pairs={{24,0},{25,1},{26,2},{27,3},{28,4},{29,5},{30,6},{31,7},{16,8},{17... | collective-permute-start | bytes 110600 | tf_op jit(solution)/shard_map/ppermute | solution.py:24
  33.3 1.5 %collective-permute-start.15 = (bf16[32,576]{1,0:T(8,128)(2,1)S(1)}, bf16[32,576]{1,0:T(8,128)(2,1)S(1)}, u32[]{:S(2)}, u32[]{:S(2)}) collective-permute-start(bf16[32,576]{1,0:T(8,128)(2,1)S(1)} %maximum_select_fusion.1), channel_id=1, source_target_pairs={{16,0},{17,1},{18,2},{19,3},{20,4},{21,5},{22,6},{23,7},{24,8},{25... | collective-permute-start | bytes 110600 | tf_op jit(solution)/shard_map/ppermute | solution.py:24
  35.9 1.4 %collective-permute-done.15 = bf16[32,576]{1,0:T(8,128)(2,1)S(1)} collective-permute-done((bf16[32,576]{1,0:T(8,128)(2,1)S(1)}, bf16[32,576]{1,0:T(8,128)(2,1)S(1)}, u32[]{:S(2)}, u32[]{:S(2)}) %collective-permute-start.15) | collective-permute-done | bytes 36896 | tf_op jit(solution)/shard_map/ppermute | solution.py:24
  37.4 2.0 %collective-permute-done.19 = f32[64,128]{1,0:T(8,128)S(1)} collective-permute-done((f32[64,128]{1,0:T(8,128)S(1)}, f32[64,128]{1,0:T(8,128)S(1)}, u32[]{:S(2)}, u32[]{:S(2)}) %collective-permute-start.19) | collective-permute-done | bytes 32800 | tf_op jit(solution)/shard_map/ppermute | solution.py:28
  39.4 1.7 %shard_map.62 = (f32[32,1152]{1,0:T(8,128)S(1)}, bf16[32,1152]{1,0:T(8,128)(2,1)S(1)}) custom-call(bf16[2,512,128]{2,1,0:T(8,128)(2,1)S(1)} %pad_maximum_fusion.1.part_0, bf16[2,512,128]{2,1,0:T(8,128)(2,1)S(1)} %collective-permute-done.4.part_1, bf16[2,512,128]{2,1,0:T(8,128)(2,1)S(1)} %collective-permute-done.13.part_2, ...), custom_call_target="tpu_custom_call" | custom-call | tf_op jit(solution)/shard_map/pallas_call | solution.py:354
  42.2 2.7 %collective-permute-start.20 = (f32[64,128]{1,0:T(8,128)S(1)}, f32[64,128]{1,0:T(8,128)S(1)}, u32[]{:S(2)}, u32[]{:S(2)}) collective-permute-start(f32[64,128]{1,0:T(8,128)S(1)} %add.97), channel_id=1, source_target_pairs={{0,8},{1,9},{2,10},{3,11},{4,12},{5,13},{6,14},{7,15},{8,0},{9,1},... | collective-permute-start | bytes 98312 | tf_op jit(solution)/shard_map/ppermute | solution.py:28
  44.8 2.2 %collective-permute-done.20 = f32[64,128]{1,0:T(8,128)S(1)} collective-permute-done((f32[64,128]{1,0:T(8,128)S(1)}, f32[64,128]{1,0:T(8,128)S(1)}, u32[]{:S(2)}, u32[]{:S(2)}) %collective-permute-start.20) | collective-permute-done | bytes 32800 | tf_op jit(solution)/shard_map/ppermute | solution.py:28
  47.1 2.7 %collective-permute-start.18 = (bf16[32,1152]{1,0:T(8,128)(2,1)S(1)}, bf16[32,1152]{1,0:T(8,128)(2,1)S(1)}, u32[]{:S(2)}, u32[]{:S(2)}) collective-permute-start(bf16[32,1152]{1,0:T(8,128)(2,1)S(1)} %fusion.14), channel_id=1, source_target_pairs={{0,8},{1,9},{2,10},{3,11},{4,12},{5,13},{6,14},{7,15},{8,0},{9,1},... | collective-permute-start | bytes 221192 | tf_op jit(solution)/shard_map/ppermute | solution.py:28
  49.9 2.5 %collective-permute-done.18 = bf16[32,1152]{1,0:T(8,128)(2,1)S(1)} collective-permute-done((bf16[32,1152]{1,0:T(8,128)(2,1)S(1)}, bf16[32,1152]{1,0:T(8,128)(2,1)S(1)}, u32[]{:S(2)}, u32[]{:S(2)}) %collective-permute-start.18) | collective-permute-done | bytes 73760 | tf_op jit(solution)/shard_map/ppermute | solution.py:28
  52.4 1.3 %shard_map.63 = (f32[2,72,128]{2,1,0:T(8,128)S(1)}, f32[2,72,128]{2,1,0:T(8,128)S(1)}) custom-call(f32[32,1152]{1,0:T(8,128)S(1)} %convert_add_fusion.cross_t, f32[32,128]{1,0:T(8,128)S(1)} %convolution_multiply_fusion.mixed_in, bf16[2,9,144,128]{3,2,1,0:T(8,128)(2,1)S(1)} %get-tuple-element.94.k_a, bf16[2,9,144,128]{3,2,1,0:T(8,128)(2,1)S(1)} %get-tuple-element.95.k_b, ...), custom_call_target="tpu_custom_call" | custom-call | tf_op jit(solution)/shard_map/pallas_call | solution.py:375
  54.6 1.4 %collective-permute-start.24 = (f32[64,128]{1,0:T(8,128)S(1)}, f32[64,128]{1,0:T(8,128)S(1)}, u32[]{:S(2)}, u32[]{:S(2)}) collective-permute-start(f32[64,128]{1,0:T(8,128)S(1)} %add.98), channel_id=1, source_target_pairs={{0,1},{1,0},{2,3},{3,2},{4,5},{5,4},{6,7},{7,6},{8,9},{9,8},{10,11... | collective-permute-start | bytes 98312 | tf_op jit(solution)/shard_map/ppermute | solution.py:28
  56.7 1.8 %collective-permute-done.21 = f32[2,72,128]{2,1,0:T(8,128)S(1)} collective-permute-done((f32[2,72,128]{2,1,0:T(8,128)S(1)}, f32[2,72,128]{2,1,0:T(8,128)S(1)}, u32[]{:S(2)}, u32[]{:S(2)}) %collective-permute-start.21) | collective-permute-done | bytes 73760 | tf_op jit(solution)/shard_map/ppermute | solution.py:28
  58.6 1.3 %collective-permute-done.23 = f32[64,128]{1,0:T(8,128)S(1)} collective-permute-done((f32[64,128]{1,0:T(8,128)S(1)}, f32[64,128]{1,0:T(8,128)S(1)}, u32[]{:S(2)}, u32[]{:S(2)}) %collective-permute-start.23) | collective-permute-done | bytes 32800 | tf_op jit(solution)/shard_map/ppermute | solution.py:28
  (90 shorter events, 12.0 us)
Async XLA Ops:
  4.8 5.7 %collective-permute-start.2 = (f16[10,32,128]{2,1,0:T(8,128)(2,1)S(1)}, f16[10,32,128]{2,1,0:T(8,128)(2,1)S(1)}, u32[]{:S(2)}, u32[]{:S(2)}) collective-permute-start(f16[10,32,128]{2,1,0:T(8,128)(2,1)S(1)} %pad_maximum_fusion.4), channel_id=1, source_target_pairs={{0,2},{1,3},{2,0},{3,1},{4,6},{5,7},{6,4},{7,5},{8,10},{9,11},{10,... | collective-permute-start | bytes 245768 | tf_op jit(solution)/shard_map/ppermute | solution.py:28
  10.6 5.7 %collective-permute-start.3 = (f16[10,32,128]{2,1,0:T(8,128)(2,1)S(1)}, f16[10,32,128]{2,1,0:T(8,128)(2,1)S(1)}, u32[]{:S(2)}, u32[]{:S(2)}) collective-permute-start(f16[10,32,128]{2,1,0:T(8,128)(2,1)S(1)} %pad_maximum_fusion.5), channel_id=1, source_target_pairs={{0,4},{1,5},{2,6},{3,7},{4,0},{5,1},{6,2},{7,3},{8,12},{9,13},{10,... | collective-permute-start | bytes 245768 | tf_op jit(solution)/shard_map/ppermute | solution.py:28
  12.6 7.0 %collective-permute-start.8 = (f16[10,72,128]{2,1,0:T(8,128)(2,1)S(1)}, f16[10,72,128]{2,1,0:T(8,128)(2,1)S(1)}, u32[]{:S(2)}, u32[]{:S(2)}) collective-permute-start(f16[10,72,128]{2,1,0:T(8,128)(2,1)S(1)} %convert_element_type.40), channel_id=1, source_target_pairs={{0,3},{1,2},{2,1},{3,0},{4,7},{5,6},{6,5},{7,4},{8,11},{9,10},{10,... | collective-permute-start | bytes 552968 | tf_op jit(solution)/shard_map/ppermute | solution.py:28
  12.7 6.9 %collective-permute-start.7 = (f16[10,72,128]{2,1,0:T(8,128)(2,1)S(1)}, f16[10,72,128]{2,1,0:T(8,128)(2,1)S(1)}, u32[]{:S(2)}, u32[]{:S(2)}) collective-permute-start(f16[10,72,128]{2,1,0:T(8,128)(2,1)S(1)} %convert_element_type.40), channel_id=1, source_target_pairs={{0,1},{1,0},{2,3},{3,2},{4,5},{5,4},{6,7},{7,6},{8,9},{9,8},{10,11... | collective-permute-start | bytes 552968 | tf_op jit(solution)/shard_map/ppermute | solution.py:28
  14.2 9.3 %collective-permute-start.6 = (f16[10,72,128]{2,1,0:T(8,128)(2,1)S(1)}, f16[10,72,128]{2,1,0:T(8,128)(2,1)S(1)}, u32[]{:S(2)}, u32[]{:S(2)}) collective-permute-start(f16[10,72,128]{2,1,0:T(8,128)(2,1)S(1)} %convert_element_type.40), channel_id=1, source_target_pairs={{0,2},{1,3},{2,0},{3,1},{4,6},{5,7},{6,4},{7,5},{8,10},{9,11},{10,... | collective-permute-start | bytes 552968 | tf_op jit(solution)/shard_map/ppermute | solution.py:28
  14.8 9.0 %collective-permute-start.1 = (bf16[2,512,128]{2,1,0:T(8,128)(2,1)S(1)}, bf16[2,512,128]{2,1,0:T(8,128)(2,1)S(1)}, u32[]{:S(2)}, u32[]{:S(2)}) collective-permute-start(bf16[2,512,128]{2,1,0:T(8,128)(2,1)S(1)} %pad_maximum_fusion), channel_id=1, source_target_pairs={{16,0},{17,1},{18,2},{19,3},{20,4},{21,5},{22,6},{23,7},{24,8},{25... | collective-permute-start | bytes 786440 | tf_op jit(solution)/shard_map/ppermute | solution.py:24
  16.4 7.3 %collective-permute-start.5 = (f16[10,32,128]{2,1,0:T(8,128)(2,1)S(1)}, f16[10,32,128]{2,1,0:T(8,128)(2,1)S(1)}, u32[]{:S(2)}, u32[]{:S(2)}) collective-permute-start(f16[10,32,128]{2,1,0:T(8,128)(2,1)S(1)} %pad_maximum_fusion.6), channel_id=1, source_target_pairs={{0,8},{1,9},{2,10},{3,11},{4,12},{5,13},{6,14},{7,15},{8,0},{9,1},... | collective-permute-start | bytes 245768 | tf_op jit(solution)/shard_map/ppermute | solution.py:28
  23.9 10.9 %collective-permute-start.4 = (bf16[2,512,128]{2,1,0:T(8,128)(2,1)S(1)}, bf16[2,512,128]{2,1,0:T(8,128)(2,1)S(1)}, u32[]{:S(2)}, u32[]{:S(2)}) collective-permute-start(bf16[2,512,128]{2,1,0:T(8,128)(2,1)S(1)} %pad_maximum_fusion.1.part_0), channel_id=1, source_target_pairs={{0,2},{1,3},{2,0},{3,1},{4,6},{5,7},{6,4},{7,5},{8,10},{9,11},{10,... | collective-permute-start | bytes 786440 | tf_op jit(solution)/shard_map/ppermute | solution.py:28
  25.2 3.8 %collective-permute-start.12 = (bf16[32,288]{1,0:T(8,128)(2,1)S(1)}, bf16[32,288]{1,0:T(8,128)(2,1)S(1)}, u32[]{:S(2)}, u32[]{:S(2)}) collective-permute-start(bf16[32,288]{1,0:T(8,128)(2,1)S(1)} %get-tuple-element.49), channel_id=1, source_target_pairs={{0,4},{1,5},{2,6},{3,7},{4,0},{5,1},{6,2},{7,3},{8,12},{9,13},{10,... | collective-permute-start | bytes 55304 | tf_op jit(solution)/shard_map/ppermute | solution.py:28
  25.8 7.4 %collective-permute-start.9 = (f32[64,128]{1,0:T(8,128)S(1)}, f32[64,128]{1,0:T(8,128)S(1)}, u32[]{:S(2)}, u32[]{:S(2)}) collective-permute-start(f32[64,128]{1,0:T(8,128)S(1)} %get-tuple-element.51), channel_id=1, source_target_pairs={{0,2},{1,3},{2,0},{3,1},{4,6},{5,7},{6,4},{7,5},{8,10},{9,11},{10,... | collective-permute-start | bytes 98312 | tf_op jit(solution)/shard_map/ppermute | solution.py:28
  27.3 7.5 %collective-permute-start.10 = (f32[64,128]{1,0:T(8,128)S(1)}, f32[64,128]{1,0:T(8,128)S(1)}, u32[]{:S(2)}, u32[]{:S(2)}) collective-permute-start(f32[64,128]{1,0:T(8,128)S(1)} %get-tuple-element.52), channel_id=1, source_target_pairs={{0,1},{1,0},{2,3},{3,2},{4,5},{5,4},{6,7},{7,6},{8,9},{9,8},{10,11... | collective-permute-start | bytes 98312 | tf_op jit(solution)/shard_map/ppermute | solution.py:28
  27.3 7.5 %collective-permute-start.11 = (f32[64,128]{1,0:T(8,128)S(1)}, f32[64,128]{1,0:T(8,128)S(1)}, u32[]{:S(2)}, u32[]{:S(2)}) collective-permute-start(f32[64,128]{1,0:T(8,128)S(1)} %get-tuple-element.53), channel_id=1, source_target_pairs={{0,3},{1,2},{2,1},{3,0},{4,7},{5,6},{6,5},{7,4},{8,11},{9,10},{10,... | collective-permute-start | bytes 98312 | tf_op jit(solution)/shard_map/ppermute | solution.py:28
  29.2 6.7 %collective-permute-start.16 = (bf16[32,576]{1,0:T(8,128)(2,1)S(1)}, bf16[32,576]{1,0:T(8,128)(2,1)S(1)}, u32[]{:S(2)}, u32[]{:S(2)}) collective-permute-start(bf16[32,576]{1,0:T(8,128)(2,1)S(1)} %maximum_select_fusion.1), channel_id=1, source_target_pairs={{24,0},{25,1},{26,2},{27,3},{28,4},{29,5},{30,6},{31,7},{16,8},{17... | collective-permute-start | bytes 110600 | tf_op jit(solution)/shard_map/ppermute | solution.py:24
  33.3 4.0 %collective-permute-start.15 = (bf16[32,576]{1,0:T(8,128)(2,1)S(1)}, bf16[32,576]{1,0:T(8,128)(2,1)S(1)}, u32[]{:S(2)}, u32[]{:S(2)}) collective-permute-start(bf16[32,576]{1,0:T(8,128)(2,1)S(1)} %maximum_select_fusion.1), channel_id=1, source_target_pairs={{16,0},{17,1},{18,2},{19,3},{20,4},{21,5},{22,6},{23,7},{24,8},{25... | collective-permute-start | bytes 110600 | tf_op jit(solution)/shard_map/ppermute | solution.py:24
  34.8 4.6 %collective-permute-start.13 = (bf16[2,512,128]{2,1,0:T(8,128)(2,1)S(1)}, bf16[2,512,128]{2,1,0:T(8,128)(2,1)S(1)}, u32[]{:S(2)}, u32[]{:S(2)}) collective-permute-start(bf16[2,512,128]{2,1,0:T(8,128)(2,1)S(1)} %pad_maximum_fusion.1.part_0), channel_id=1, source_target_pairs={{0,1},{1,0},{2,3},{3,2},{4,5},{5,4},{6,7},{7,6},{8,9},{9,8},{10,11... | collective-permute-start | bytes 786440 | tf_op jit(solution)/shard_map/ppermute | solution.py:28
  34.9 4.5 %collective-permute-start.14 = (bf16[2,512,128]{2,1,0:T(8,128)(2,1)S(1)}, bf16[2,512,128]{2,1,0:T(8,128)(2,1)S(1)}, u32[]{:S(2)}, u32[]{:S(2)}) collective-permute-start(bf16[2,512,128]{2,1,0:T(8,128)(2,1)S(1)} %collective-permute-done.4.part_1), channel_id=1, source_target_pairs={{0,1},{1,0},{2,3},{3,2},{4,5},{5,4},{6,7},{7,6},{8,9},{9,8},{10,11... | collective-permute-start | bytes 786440 | tf_op jit(solution)/shard_map/ppermute | solution.py:28
  35.4 4.0 %collective-permute-start.19 = (f32[64,128]{1,0:T(8,128)S(1)}, f32[64,128]{1,0:T(8,128)S(1)}, u32[]{:S(2)}, u32[]{:S(2)}) collective-permute-start(f32[64,128]{1,0:T(8,128)S(1)} %add_add_fusion), channel_id=1, source_target_pairs={{0,4},{1,5},{2,6},{3,7},{4,0},{5,1},{6,2},{7,3},{8,12},{9,13},{10,... | collective-permute-start | bytes 98312 | tf_op jit(solution)/shard_map/ppermute | solution.py:28
  41.1 6.0 %collective-permute-start.17 = (bf16[32,1152]{1,0:T(8,128)(2,1)S(1)}, bf16[32,1152]{1,0:T(8,128)(2,1)S(1)}, u32[]{:S(2)}, u32[]{:S(2)}) collective-permute-start(bf16[32,1152]{1,0:T(8,128)(2,1)S(1)} %get-tuple-element.57), channel_id=1, source_target_pairs={{0,4},{1,5},{2,6},{3,7},{4,0},{5,1},{6,2},{7,3},{8,12},{9,13},{10,... | collective-permute-start | bytes 221192 | tf_op jit(solution)/shard_map/ppermute | solution.py:28
  42.2 4.9 %collective-permute-start.20 = (f32[64,128]{1,0:T(8,128)S(1)}, f32[64,128]{1,0:T(8,128)S(1)}, u32[]{:S(2)}, u32[]{:S(2)}) collective-permute-start(f32[64,128]{1,0:T(8,128)S(1)} %add.97), channel_id=1, source_target_pairs={{0,8},{1,9},{2,10},{3,11},{4,12},{5,13},{6,14},{7,15},{8,0},{9,1},... | collective-permute-start | bytes 98312 | tf_op jit(solution)/shard_map/ppermute | solution.py:28
  47.1 5.3 %collective-permute-start.18 = (bf16[32,1152]{1,0:T(8,128)(2,1)S(1)}, bf16[32,1152]{1,0:T(8,128)(2,1)S(1)}, u32[]{:S(2)}, u32[]{:S(2)}) collective-permute-start(bf16[32,1152]{1,0:T(8,128)(2,1)S(1)} %fusion.14), channel_id=1, source_target_pairs={{0,8},{1,9},{2,10},{3,11},{4,12},{5,13},{6,14},{7,15},{8,0},{9,1},... | collective-permute-start | bytes 221192 | tf_op jit(solution)/shard_map/ppermute | solution.py:28
  53.8 4.8 %collective-permute-start.21 = (f32[2,72,128]{2,1,0:T(8,128)S(1)}, f32[2,72,128]{2,1,0:T(8,128)S(1)}, u32[]{:S(2)}, u32[]{:S(2)}) collective-permute-start(f32[2,72,128]{2,1,0:T(8,128)S(1)} %get-tuple-element.69), channel_id=1, source_target_pairs={{0,2},{1,3},{2,0},{3,1},{4,6},{5,7},{6,4},{7,5},{8,10},{9,11},{10,... | collective-permute-start | bytes 221192 | tf_op jit(solution)/shard_map/ppermute | solution.py:28
  54.6 4.0 %collective-permute-start.25 = (f32[64,128]{1,0:T(8,128)S(1)}, f32[64,128]{1,0:T(8,128)S(1)}, u32[]{:S(2)}, u32[]{:S(2)}) collective-permute-start(f32[64,128]{1,0:T(8,128)S(1)} %add.98), channel_id=1, source_target_pairs={{0,3},{1,2},{2,1},{3,0},{4,7},{5,6},{6,5},{7,4},{8,11},{9,10},{10,... | collective-permute-start | bytes 98312 | tf_op jit(solution)/shard_map/ppermute | solution.py:28
  54.6 4.0 %collective-permute-start.24 = (f32[64,128]{1,0:T(8,128)S(1)}, f32[64,128]{1,0:T(8,128)S(1)}, u32[]{:S(2)}, u32[]{:S(2)}) collective-permute-start(f32[64,128]{1,0:T(8,128)S(1)} %add.98), channel_id=1, source_target_pairs={{0,1},{1,0},{2,3},{3,2},{4,5},{5,4},{6,7},{7,6},{8,9},{9,8},{10,11... | collective-permute-start | bytes 98312 | tf_op jit(solution)/shard_map/ppermute | solution.py:28
  56.0 3.9 %collective-permute-start.23 = (f32[64,128]{1,0:T(8,128)S(1)}, f32[64,128]{1,0:T(8,128)S(1)}, u32[]{:S(2)}, u32[]{:S(2)}) collective-permute-start(f32[64,128]{1,0:T(8,128)S(1)} %add.98), channel_id=1, source_target_pairs={{0,2},{1,3},{2,0},{3,1},{4,6},{5,7},{6,4},{7,5},{8,10},{9,11},{10,... | collective-permute-start | bytes 98312 | tf_op jit(solution)/shard_map/ppermute | solution.py:28
  (5 other events, 27.3 us)

commit v12 on v11

--- a/solution.py
+++ b/solution.py
@@ -122,28 +122,29 @@
     core, xbit = place_bits()
     mine = 2 * core + xbit
     quarter = width // 4
-    level = jnp.full((quarter, width), exponent(both), F32)
+    level = jnp.full((8, width), exponent(both), F32)
     for j in range(4):
         block = all_rows[pl.ds(pl.multiple_of((mine ^ j) * quarter, quarter), quarter), :]
         target = keep if j < 2 else send
         for tap in range(9):
-            target[j % 2, tap] = block[:, tap * width : (tap + 1) * width]
-        target[j % 2, 9] = level
+            target[j % 2, tap * quarter : (tap + 1) * quarter] = block[:, tap * width : (tap + 1) * width]
+        target[j % 2, 9 * quarter :] = level
     copies[3].wait()
     k = k_rows[...]
     high = k.astype(BF16)
     rest = (k - high.astype(F32)).astype(BF16)
     level = jnp.maximum(exponent(k), -99.0)
     factor = jnp.exp2(jnp.full((1, width), TOP - level, F32))
+    rows = k.shape[0]
     for tap in range(9):
         part = slice(tap * width, (tap + 1) * width)
         k_parts[0, tap] = high[:, part]
         k_parts[1, tap] = rest[:, part]
-        k_send[tap] = k[:, part] * factor
-    k_send[9] = jnp.full((k.shape[0], width), level, F32)
-
-
-def cross_kernel(side, part_0, part_1, part_2, part_3, precond_t, out, out_half):
+        k_send[tap * rows : (tap + 1) * rows] = k[:, part] * factor
+    k_send[9 * rows :] = jnp.full((8, width), level, F32)
+
+
+def cross_kernel(side, part_0, part_1, part_2, part_3, precond_t, gram_0, gram_1, gram_2, gram_3, out, gram, levels):
     quarter = precond_t.shape[0]
     width = part_0.shape[2]
     taps = jnp.concatenate([precond_t[:, t * width : (t + 1) * width] for t in range(9)], axis=0)
@@ -162,10 +163,11 @@
         mapped = mapped.astype(BF16).astype(F32)
         part = jnp.dot(taps_to_rows(mapped, side), device[0], preferred_element_type=F32)
         both = part if both is None else both + part
-    for tap in range(9):
-        part = both[quarter * tap : quarter * (tap + 1)]
-        out[:, tap * width : (tap + 1) * width] = part
-        out_half[:, tap * width : (tap + 1) * width] = part.astype(BF16)
+    out[...] = both
+    grams = (gram_0[...] + gram_1[...]) + (gram_2[...] + gram_3[...])
+    gram[...] = grams
+    levels[0] = jnp.full((8, width), exponent(both), F32)
+    levels[1] = jnp.full((8, width), exponent(grams), F32)
 
 
 def two_parts(block):
@@ -182,11 +184,16 @@
     return jnp.concatenate([block[tap] for tap in range(9)], axis=1)
 
 
+def rows_to_lanes(block):
+    count = block.shape[0] // 9
+    return jnp.concatenate([block[tap * count : (tap + 1) * count] for tap in range(9)], axis=1)
+
+
 def precond_kernel(scale, e_t, k_a, k_b, main_a, main_b, precond_t):
     core, xbit = place_bits()
-    count = e_t.shape[1]
+    count = e_t.shape[0] // 9
     rows = k_a.shape[2] // 2
-    parts = two_parts(taps_to_lanes(e_t) * scale)
+    parts = two_parts(rows_to_lanes(e_t) * scale)
     total = None
     for flip, k, main in ((0, k_a, main_a), (1, k_b, main_b)):
         product = dot_nt(parts, taps_to_lanes(k.at[0])) + dot_nt(parts, taps_to_lanes(k.at[1]))
@@ -202,15 +209,16 @@
     precond_t[...] = total.astype(BF16)
 
 
-def update_kernel(cross_t, mixed_in, k_a, k_b, main, keep, send):
+def update_kernel(cross_t, mixed_in, k_a, k_b, main, gram, keep, send):
     rows = k_a.shape[2] // 2
     mixed = jnp.concatenate([mixed_in[...], mixed_in[...]], axis=0)
-    parts = two_parts(cross_t[...])
+    parts = two_parts(rows_to_lanes(cross_t))
     for i, k in enumerate((k_a, k_b)):
         product = dot_nt(taps_to_lanes(k.at[0]), parts) + dot_nt(taps_to_lanes(k.at[1]), parts)
         result = main[i] - jnp.dot(product, mixed, precision=HIGH)
         keep[i] = result[:rows]
-        send[i] = result[rows:]
+        send[i * rows : (i + 1) * rows] = result[rows:]
+    send[2 * rows :] = gram[...]
 
 
 def gram_kernel(grads, next_grads, *refs):
@@ -256,10 +264,10 @@
 
     keep, send, k_own, k_send = pl.pallas_call(
         functools.partial(grad_kernel, side),
-        out_shape=[jax.ShapeDtypeStruct((2, 10, quarter, width), F32)] * 2
+        out_shape=[jax.ShapeDtypeStruct((2, 9 * quarter + 8, width), F32)] * 2
         + [
             jax.ShapeDtypeStruct((2, 9, rows, width), BF16),
-            jax.ShapeDtypeStruct((10, rows, width), F32),
+            jax.ShapeDtypeStruct((9 * rows + 8, width), F32),
         ],
         in_specs=[HBM] * 4,
         out_specs=[VMEM] * 4,
@@ -274,41 +282,45 @@
         compiler_params=PARAMS,
     )(*(pltpu.with_memory_space_constraint(a, pltpu.HBM) for a in (flat_maps, flat_grads, g_inv, k_rows)))
 
-    def message(values, level):
-        level = jnp.maximum(level, -99.0)
-        return jnp.concatenate([values * jnp.exp2(TOP - level)[None], level[None]], axis=0).astype(F16)
-
-    def received(parcel):
+    def packed(groups):
+        groups = [(values, jnp.maximum(level, -99.0)) for values, level in groups]
+        scaled = [lax.reduce_precision(values * jnp.exp2(TOP - level[:1]), 5, 10) for values, level in groups]
+        return jnp.concatenate(scaled + [level for _, level in groups], axis=0)
+
+    def opened(parcel, sizes):
         parcel = parcel.astype(F32)
-        return parcel[:9] * jnp.exp2(parcel[9] - TOP)[None], parcel[9]
-
+        groups = []
+        start, at = 0, sum(sizes)
+        for size in sizes:
+            level = parcel[at : at + 8]
+            groups.append((parcel[start : start + size] * jnp.exp2(level[:1] - TOP), level))
+            start, at = start + size, at + 8
+        return groups
+
+    def summed(values, level, sent, bit):
+        (more, other_level), = opened(swap(packed([sent]).astype(F16), bit), [9 * quarter])
+        return values + more, jnp.maximum(level, other_level) + 1
+
+    wide = 9 * quarter
     other = swap(send, 1)
-    h = keep[:, :9] + other[:, :9]
-    level = jnp.maximum(keep[:, 9], other[:, 9]) + 1
+    h = keep[:, :wide] + other[:, :wide]
+    level = jnp.maximum(keep[:, wide:], other[:, wide:]) + 1
     k_half = behind(k_send, h).astype(F16)
     k_others = [swap(k_half, 2), swap(k_half, 1), swap(k_half, 3)]
+    h, level = summed(h[0], level[0], (h[1], level[1]), 2)
+    h, level = summed(h, level, (h, level), zbits[0])
     own = behind(jnp.stack([flat_maps, flat_grads]), h)
     next_own = after(own)
-
-    def add(values, level, bit):
-        more, other_level = received(swap(message(values[1], level[1]) if bit == 2 else message(values, level), bit))
-        if bit == 2:
-            values, level = values[0], level[0]
-        return values + more, jnp.maximum(level, other_level) + 1
-
-    h, level = add(h, level, 2)
-    h, level = add(h, level, zbits[0])
-    next_own = behind(next_own, h)
     two_own = jnp.stack([flat_maps, next_own[0]])
-    two_x = swap(two_own, 2)
     for b in zbits[1:]:
-        h, level = add(h, level, b)
+        h, level = summed(h, level, (h, level), b)
 
     def k_pair(parts):
         return jnp.concatenate(parts, axis=2)
 
     def k_split(parcel):
-        values, _ = received(parcel)
+        (values, _), = opened(parcel, [9 * rows])
+        values = values.reshape(9, rows, width)
         high = lax.reduce_precision(values, 8, 7)
         return jnp.stack([high, values - high]).astype(BF16)
 
@@ -327,6 +339,7 @@
     def by_bit(mine, other, b):
         return jnp.where((me & b) == 0, jnp.concatenate([mine, other], 1), jnp.concatenate([other, mine], 1))
 
+    two_x = swap(behind(two_own, p_t), 2)
     grams = pl.pallas_call(
         gram_kernel,
         out_shape=[jax.ShapeDtypeStruct((2 * quarter, width), F32)] * 4,
@@ -340,49 +353,58 @@
     for b in zbits[:-1]:
         p_t = by_bit(p_t, swap(p_t, b), b)
 
-    two_own, two_x, grams = behind((two_own, two_x, grams), p_t)
+    two_own, two_x = behind((two_own, two_x), p_t)
     core_own = swap(two_own, 1)
     core_x = swap(two_x, 1)
-    gram = (grams[0] + grams[1]) + (grams[2] + grams[3])
-    for b in zbits[:-1]:
-        gram = gram + swap(gram, b)
     low = cols * quarter
     last = lax.axis_index("layer") == lax.axis_size("layer") - 1
     p_t = by_bit(after(p_t), after(p_t, zbits[-1]), zbits[-1])
     p_t = jnp.where(last, jnp.zeros_like(p_t), p_t)
 
-    cross_t, cross_half = pl.pallas_call(
+    cross_t, gram, levels = pl.pallas_call(
         functools.partial(cross_kernel, side),
-        out_shape=[jax.ShapeDtypeStruct((quarter, full), F32), jax.ShapeDtypeStruct((quarter, full), BF16)],
-        in_specs=[VMEM] * 5,
+        out_shape=[
+            jax.ShapeDtypeStruct((wide, width), F32),
+            jax.ShapeDtypeStruct((2 * quarter, width), F32),
+            jax.ShapeDtypeStruct((2, 8, width), F32),
+        ],
+        in_specs=[VMEM] * 9,
+        out_specs=[VMEM] * 3,
+        compiler_params=PARAMS,
+    )(two_own, two_x, core_own, core_x, p_t, *grams)
+
+    place = (jnp.arange(width)[None, :] == low + jnp.arange(quarter)[:, None]).astype(F32)
+    main_a, main_b = behind((main_a, main_b), cross_t)
+    main = jnp.stack([dot_t(main_a, place, precision=HIGH), dot_t(main_b, place, precision=HIGH)])
+    sizes = [wide, 2 * quarter]
+    cross_level, gram_level = levels[0], levels[1]
+    for b in zbits:
+        mine = packed([(cross_t, cross_level), (gram, gram_level)])
+        (more, level), (more_gram, level_gram) = opened(swap(mine.astype(F16), b), sizes)
+        cross_t = cross_t + more
+        gram = opened(mine, sizes)[1][0] + more_gram
+        cross_level = jnp.maximum(cross_level, level) + 1
+        gram_level = jnp.maximum(gram_level, level_gram) + 1
+    mixed = jnp.dot(gram[quarter:], g_inv, precision=HIGH) * (scale * scale)
+
+    out, send = pl.pallas_call(
+        update_kernel,
+        out_shape=[
+            jax.ShapeDtypeStruct((2, rows, width), F32),
+            jax.ShapeDtypeStruct((2 * rows + 2 * quarter, width), F32),
+        ],
+        in_specs=[VMEM] * 6,
         out_specs=[VMEM] * 2,
         compiler_params=PARAMS,
-    )(two_own, two_x, core_own, core_x, p_t)
-
-    gram = behind(gram, cross_half)
-    gram = gram + swap(gram, zbits[-1])
-    place = (jnp.arange(width)[None, :] == low + jnp.arange(quarter)[:, None]).astype(F32)
-    main_a, main_b = behind((main_a, main_b), cross_half)
-    main = jnp.stack([dot_t(main_a, place, precision=HIGH), dot_t(main_b, place, precision=HIGH)])
-    for i, b in enumerate(zbits):
-        cross_t = cross_t + swap(cross_half, b).astype(F32)
-        cross_half = cross_t.astype(BF16)
-        if i == 0:
-            gram = behind(gram, cross_half)
-            mixed = jnp.dot(gram[quarter:], g_inv, precision=HIGH) * (scale * scale)
-            grams = [gram] + [swap(gram, bits) for bits in (2, 1, 3)]
-
-    out, send = pl.pallas_call(
-        update_kernel,
-        out_shape=[jax.ShapeDtypeStruct((2, rows, width), F32)] * 2,
-        in_specs=[VMEM] * 5,
-        out_specs=[VMEM] * 2,
-        compiler_params=PARAMS,
-    )(cross_t, mixed, k_a, k_b, main)
-    out = out + swap(send, 2)
-    update = out[0] + swap(out[1], 1)
-
-    grams = jnp.stack(behind(grams, out)).reshape(2, 2, 2, quarter, width) * scale
+    )(cross_t, mixed, k_a, k_b, main, gram)
+    other = swap(send, 2)
+    keep = out[0] + other[:rows]
+    send = jnp.concatenate([out[1] + other[rows : 2 * rows], gram, other[2 * rows :]], axis=0)
+    other = swap(send, 1)
+    update = keep + other[:rows]
+    grams = jnp.concatenate([send[rows:], other[rows:]], axis=0)
+
+    grams = grams.reshape(2, 2, 2, quarter, width) * scale
     grams = jnp.where(xbit == 0, grams, grams[:, ::-1])
     grams = jnp.where(core == 0, grams, grams[::-1])
     grams = grams.transpose(2, 4, 0, 1, 3).reshape(2, width, width)

time: 62 us -> 64.9 us (1.047)
  waiting for transfers between devices: 21.5 us -> 32 us
  starting transfers between devices: 29.7 us -> 21.2 us
  other arithmetic: 1.83 us -> 2.5 us
    ppermute x23 -> x18, waiting for transfers between devices: 20.1 us -> 27.1 us  [swap(): lax.ppermute(block, 'pos', [(i, i ^ bit) for i in range(lax.axis_size('po...]
    ppermute x23 -> x18, starting transfers between devices: 23.2 us -> 16.8 us  [swap(): lax.ppermute(block, 'pos', [(i, i ^ bit) for i in range(lax.axis_size('po...]
    ppermute x3, waiting for transfers between devices: 1.37 us -> 4.84 us  [after(): return lax.ppermute(block, ('layer', 'pos'), route)]
    ppermute x3, starting transfers between devices: 6.48 us -> 4.37 us  [after(): return lax.ppermute(block, ('layer', 'pos'), route)]
  transfers between devices with their start and end apart: 26 -> 21, of which waited for: 13 -> 12; matrix products, arithmetic and copies ran while one was open for 4% -> 2% of each run, Pallas kernels for 2% -> 2%
where the time goes in v12:
time: 64.9 us; the launch traced here: 64.7 us
  waiting for transfers between devices  32 us (49%)
  starting transfers between devices  21.2 us (33%)
  Pallas kernels  6.4 us (10%)
  other arithmetic  2.5 us (4%)
  between operations  1.16 us (2%)
  local copies, waits for them, and re-layouts  0.81 us (1%)
  matrix products  0.72 us (1%)
    ppermute x18, waiting for transfers between devices, swap(): lax.ppermute(block, 'pos', [(i, i ^ bit) for i in range(lax.axis_size('po...  27.1 us
    ppermute x18, starting transfers between devices, swap(): lax.ppermute(block, 'pos', [(i, i ^ bit) for i in range(lax.axis_size('po...  16.8 us
    ppermute x3, waiting for transfers between devices, after(): return lax.ppermute(block, ('layer', 'pos'), route)  4.84 us
    ppermute x3, starting transfers between devices, after(): return lax.ppermute(block, ('layer', 'pos'), route)  4.37 us
    pallas_call x1, Pallas kernels, per_device(): pl.pallas_call(functools.partial(grad_kernel, side), out_shape=[jax.Shape...  2.21 us
    pallas_call x1, Pallas kernels, per_device(): pl.pallas_call(functools.partial(cross_kernel, side), out_shape=[jax.Shap...  1.87 us
    pallas_call x1, Pallas kernels, per_device(): pl.pallas_call(update_kernel, out_shape=[jax.ShapeDtypeStruct((2, rows, w...  1.31 us
  transfers between devices with their start and end apart: 21, of which 12 were waited for; matrix products, arithmetic and copies ran while one was open for 2% of the time, Pallas kernels for 2%

profile of v12, /device:TPU:0, one launch (start us, length us, event | category | flops | bytes accessed | tf_op | source)
XLA Modules:
  0.0 64.7 jit_solution(15937288734790174389)
XLA Ops:
  0.6 2.2 %shard_map.59 = (f32[2,296,128]{2,1,0:T(8,128)S(1)}, f32[2,296,128]{2,1,0:T(8,128)S(1)}, bf16[2,9,72,128]{3,2,1,0:T(8,128)(2,1)S(1)}, f32[656,128]{1,0:T(8,128)S(1)}) custom-call(bf16[512,128]{1,0:T(8,128)(2,1)} %bitcast.114, bf16[512,128]{1,0:T(8,128)(2,1)} %bitcast.108, f32[128,128]{1,0:T(8,128)} %bitcast.120, f32[72,1152]{1,0:T(8,128)} %bitcast.119), custom_call_target="tpu_custom_call" | custom-call | tf_op jit(solution)/shard_map/pallas_call | solution.py:265
  3.4 1.2 %collective-permute-done = f32[2,296,128]{2,1,0:T(8,128)S(1)} collective-permute-done((f32[2,296,128]{2,1,0:T(8,128)S(1)}, f32[2,296,128]{2,1,0:T(8,128)S(1)}, u32[]{:S(2)}, u32[]{:S(2)}) %collective-permute-start) | collective-permute-done | bytes 303136 | tf_op jit(solution)/shard_map/ppermute | solution.py:28
  4.8 2.9 %collective-permute-start.1 = (f16[296,128]{1,0:T(8,128)(2,1)S(1)}, f16[296,128]{1,0:T(8,128)(2,1)S(1)}, u32[]{:S(2)}, u32[]{:S(2)}) collective-permute-start(f16[296,128]{1,0:T(8,128)(2,1)S(1)} %pad_maximum_fusion.7), channel_id=1, source_target_pairs={{0,2},{1,3},{2,0},{3,1},{4,6},{5,7},{6,4},{7,5},{8,10},{9,11},{10,... | collective-permute-start | bytes 227336 | tf_op jit(solution)/shard_map/ppermute | solution.py:28
  7.7 2.6 %collective-permute-done.1 = f16[296,128]{1,0:T(8,128)(2,1)S(1)} collective-permute-done((f16[296,128]{1,0:T(8,128)(2,1)S(1)}, f16[296,128]{1,0:T(8,128)(2,1)S(1)}, u32[]{:S(2)}, u32[]{:S(2)}) %collective-permute-start.1) | collective-permute-done | bytes 75808 | tf_op jit(solution)/shard_map/ppermute | solution.py:28
  10.5 1.9 %collective-permute-start.2 = (f16[296,128]{1,0:T(8,128)(2,1)S(1)}, f16[296,128]{1,0:T(8,128)(2,1)S(1)}, u32[]{:S(2)}, u32[]{:S(2)}) collective-permute-start(f16[296,128]{1,0:T(8,128)(2,1)S(1)} %pad_maximum_fusion.8), channel_id=1, source_target_pairs={{0,4},{1,5},{2,6},{3,7},{4,0},{5,1},{6,2},{7,3},{8,12},{9,13},{10,... | collective-permute-start | bytes 227336 | tf_op jit(solution)/shard_map/ppermute | solution.py:28
  12.6 1.6 %collective-permute-start.7 = (f16[656,128]{1,0:T(8,128)(2,1)S(1)}, f16[656,128]{1,0:T(8,128)(2,1)S(1)}, u32[]{:S(2)}, u32[]{:S(2)}) collective-permute-start(f16[656,128]{1,0:T(8,128)(2,1)S(1)} %convert_element_type.39), channel_id=1, source_target_pairs={{0,3},{1,2},{2,1},{3,0},{4,7},{5,6},{6,5},{7,4},{8,11},{9,10},{10,... | collective-permute-start | bytes 503816 | tf_op jit(solution)/shard_map/ppermute | solution.py:28
  15.2 2.9 %collective-permute-start.4 = (f16[296,128]{1,0:T(8,128)(2,1)S(1)}, f16[296,128]{1,0:T(8,128)(2,1)S(1)}, u32[]{:S(2)}, u32[]{:S(2)}) collective-permute-start(f16[296,128]{1,0:T(8,128)(2,1)S(1)} %pad_maximum_fusion.9), channel_id=1, source_target_pairs={{0,8},{1,9},{2,10},{3,11},{4,12},{5,13},{6,14},{7,15},{8,0},{9,1},... | collective-permute-start | bytes 227336 | tf_op jit(solution)/shard_map/ppermute | solution.py:28
  18.1 1.5 %collective-permute-start.3 = (bf16[2,512,128]{2,1,0:T(8,128)(2,1)S(1)}, bf16[2,512,128]{2,1,0:T(8,128)(2,1)S(1)}, u32[]{:S(2)}, u32[]{:S(2)}) collective-permute-start(bf16[2,512,128]{2,1,0:T(8,128)(2,1)S(1)} %pad_maximum_fusion), channel_id=1, source_target_pairs={{16,0},{17,1},{18,2},{19,3},{20,4},{21,5},{22,6},{23,7},{24,8},{25... | collective-permute-start | bytes 786440 | tf_op jit(solution)/shard_map/ppermute | solution.py:24
  19.8 3.0 %collective-permute-done.5 = f16[656,128]{1,0:T(8,128)(2,1)S(1)} collective-permute-done((f16[656,128]{1,0:T(8,128)(2,1)S(1)}, f16[656,128]{1,0:T(8,128)(2,1)S(1)}, u32[]{:S(2)}, u32[]{:S(2)}) %collective-permute-start.5) | collective-permute-done | bytes 167968 | tf_op jit(solution)/shard_map/ppermute | solution.py:28
  24.0 1.3 %collective-permute-done.3 = bf16[2,512,128]{2,1,0:T(8,128)(2,1)S(1)} collective-permute-done((bf16[2,512,128]{2,1,0:T(8,128)(2,1)S(1)}, bf16[2,512,128]{2,1,0:T(8,128)(2,1)S(1)}, u32[]{:S(2)}, u32[]{:S(2)}) %collective-permute-start.3) | collective-permute-done | bytes 262176 | tf_op jit(solution)/shard_map/ppermute | solution.py:24
  25.4 1.6 %collective-permute-start.8 = (bf16[2,512,128]{2,1,0:T(8,128)(2,1)S(1)}, bf16[2,512,128]{2,1,0:T(8,128)(2,1)S(1)}, u32[]{:S(2)}, u32[]{:S(2)}) collective-permute-start(bf16[2,512,128]{2,1,0:T(8,128)(2,1)S(1)} %pad_maximum_fusion.1.part_0), channel_id=1, source_target_pairs={{0,2},{1,3},{2,0},{3,1},{4,6},{5,7},{6,4},{7,5},{8,10},{9,11},{10,... | collective-permute-start | bytes 786440 | tf_op jit(solution)/shard_map/ppermute | solution.py:28
  27.7 3.1 %collective-permute-done.9 = bf16[32,288]{1,0:T(8,128)(2,1)S(1)} collective-permute-done((bf16[32,288]{1,0:T(8,128)(2,1)S(1)}, bf16[32,288]{1,0:T(8,128)(2,1)S(1)}, u32[]{:S(2)}, u32[]{:S(2)}) %collective-permute-start.9) | collective-permute-done | bytes 18464 | tf_op jit(solution)/shard_map/ppermute | solution.py:28
  30.9 1.6 %collective-permute-start.12 = (bf16[32,576]{1,0:T(8,128)(2,1)S(1)}, bf16[32,576]{1,0:T(8,128)(2,1)S(1)}, u32[]{:S(2)}, u32[]{:S(2)}) collective-permute-start(bf16[32,576]{1,0:T(8,128)(2,1)S(1)} %maximum_select_fusion.1), channel_id=1, source_target_pairs={{16,0},{17,1},{18,2},{19,3},{20,4},{21,5},{22,6},{23,7},{24,8},{25... | collective-permute-start | bytes 110600 | tf_op jit(solution)/shard_map/ppermute | solution.py:24
  32.4 1.3 %collective-permute-start.13 = (bf16[32,576]{1,0:T(8,128)(2,1)S(1)}, bf16[32,576]{1,0:T(8,128)(2,1)S(1)}, u32[]{:S(2)}, u32[]{:S(2)}) collective-permute-start(bf16[32,576]{1,0:T(8,128)(2,1)S(1)} %maximum_select_fusion.1), channel_id=1, source_target_pairs={{24,0},{25,1},{26,2},{27,3},{28,4},{29,5},{30,6},{31,7},{16,8},{17... | collective-permute-start | bytes 110600 | tf_op jit(solution)/shard_map/ppermute | solution.py:24
  35.1 3.6 %collective-permute-done.13 = bf16[32,576]{1,0:T(8,128)(2,1)S(1)} collective-permute-done((bf16[32,576]{1,0:T(8,128)(2,1)S(1)}, bf16[32,576]{1,0:T(8,128)(2,1)S(1)}, u32[]{:S(2)}, u32[]{:S(2)}) %collective-permute-start.13) | collective-permute-done | bytes 36896 | tf_op jit(solution)/shard_map/ppermute | solution.py:24
  38.8 3.2 %collective-permute-done.16.gram_3 = f32[64,128]{1,0:T(8,128)S(1)} collective-permute-done((f32[64,128]{1,0:T(8,128)S(1)}, f32[64,128]{1,0:T(8,128)S(1)}, u32[]{:S(2)}, u32[]{:S(2)}) %collective-permute-start.16) | collective-permute-done | bytes 32800 | tf_op jit(solution)/shard_map/ppermute | solution.py:28
  42.0 1.9 %shard_map.62 = (f32[288,128]{1,0:T(8,128)S(1)}, f32[64,128]{1,0:T(8,128)S(1)}, f32[2,8,128]{2,1,0:T(8,128)S(1)}) custom-call(bf16[2,512,128]{2,1,0:T(8,128)(2,1)S(1)} %pad_maximum_fusion.1.part_0, bf16[2,512,128]{2,1,0:T(8,128)(2,1)S(1)} %collective-permute-done.8.part_1, bf16[2,512,128]{2,1,0:T(8,128)(2,1)S(1)} %collective-permute-done.10.part_2, ...), custom_call_target="tpu_custom_call" | custom-call | tf_op jit(solution)/shard_map/pallas_call | solution.py:364
  45.2 3.6 %collective-permute-done.17 = f16[368,128]{1,0:T(8,128)(2,1)S(1)} collective-permute-done((f16[368,128]{1,0:T(8,128)(2,1)S(1)}, f16[368,128]{1,0:T(8,128)(2,1)S(1)}, u32[]{:S(2)}, u32[]{:S(2)}) %collective-permute-start.17) | collective-permute-done | bytes 94240 | tf_op jit(solution)/shard_map/ppermute | solution.py:28
  49.1 1.0 %collective-permute-start.18 = (f16[368,128]{1,0:T(8,128)(2,1)S(1)}, f16[368,128]{1,0:T(8,128)(2,1)S(1)}, u32[]{:S(2)}, u32[]{:S(2)}) collective-permute-start(f16[368,128]{1,0:T(8,128)(2,1)S(1)} %pad_maximum_fusion.6), channel_id=1, source_target_pairs={{0,8},{1,9},{2,10},{3,11},{4,12},{5,13},{6,14},{7,15},{8,0},{9,1},... | collective-permute-start | bytes 282632 | tf_op jit(solution)/shard_map/ppermute | solution.py:28
  50.0 5.4 %collective-permute-done.18 = f16[368,128]{1,0:T(8,128)(2,1)S(1)} collective-permute-done((f16[368,128]{1,0:T(8,128)(2,1)S(1)}, f16[368,128]{1,0:T(8,128)(2,1)S(1)}, u32[]{:S(2)}, u32[]{:S(2)}) %collective-permute-start.18) | collective-permute-done | bytes 94240 | tf_op jit(solution)/shard_map/ppermute | solution.py:28
  55.8 1.3 %shard_map.63 = (f32[2,72,128]{2,1,0:T(8,128)S(1)}, f32[208,128]{1,0:T(8,128)S(1)}) custom-call(f32[288,128]{1,0:T(8,128)S(1)} %fusion.3.cross_t, f32[32,128]{1,0:T(8,128)S(1)} %convolution_multiply_fusion.mixed_in, bf16[2,9,144,128]{3,2,1,0:T(8,128)(2,1)S(1)} %maximum_maximum_fusion.k_a, bf16[2,9,144,128]{3,2,1,0:T(8,128)(2,1)S(1)} %maximum_maximum_fusion.1.k_b, ...), custom_call_target="tpu_custom_call" | custom-call | tf_op jit(solution)/shard_map/pallas_call | solution.py:390
  57.1 1.4 %collective-permute-start.19 = (f32[208,128]{1,0:T(8,128)S(1)}, f32[208,128]{1,0:T(8,128)S(1)}, u32[]{:S(2)}, u32[]{:S(2)}) collective-permute-start(f32[208,128]{1,0:T(8,128)S(1)} %get-tuple-element.55), channel_id=1, source_target_pairs={{0,2},{1,3},{2,0},{3,1},{4,6},{5,7},{6,4},{7,5},{8,10},{9,11},{10,... | collective-permute-start | bytes 319496 | tf_op jit(solution)/shard_map/ppermute | solution.py:28
  58.5 3.4 %collective-permute-done.19 = f32[208,128]{1,0:T(8,128)S(1)} collective-permute-done((f32[208,128]{1,0:T(8,128)S(1)}, f32[208,128]{1,0:T(8,128)S(1)}, u32[]{:S(2)}, u32[]{:S(2)}) %collective-permute-start.19) | collective-permute-done | bytes 106528 | tf_op jit(solution)/shard_map/ppermute | solution.py:28
  62.0 1.3 %collective-permute-done.20 = f32[200,128]{1,0:T(8,128)S(1)} collective-permute-done((f32[200,128]{1,0:T(8,128)S(1)}, f32[200,128]{1,0:T(8,128)S(1)}, u32[]{:S(2)}, u32[]{:S(2)}) %collective-permute-start.20) | collective-permute-done | bytes 102432 | tf_op jit(solution)/shard_map/ppermute | solution.py:28
  (101 shorter events, 8.8 us)
Async XLA Ops:
  2.8 1.7 %collective-permute-start = (f32[2,296,128]{2,1,0:T(8,128)S(1)}, f32[2,296,128]{2,1,0:T(8,128)S(1)}, u32[]{:S(2)}, u32[]{:S(2)}) collective-permute-start(f32[2,296,128]{2,1,0:T(8,128)S(1)} %get-tuple-element.30), channel_id=1, source_target_pairs={{0,1},{1,0},{2,3},{3,2},{4,5},{5,4},{6,7},{7,6},{8,9},{9,8},{10,11... | collective-permute-start | bytes 909320 | tf_op jit(solution)/shard_map/ppermute | solution.py:28
  4.7 7.8 %copy-start = (bf16[1,2,16,16,128]{4,3,2,1,0:T(8,128)(2,1)S(1)}, bf16[1,2,16,16,128]{4,3,2,1,0:T(8,128)(2,1)}, u32[]{:S(2)}) copy-start(bf16[1,2,16,16,128]{4,3,2,1,0:T(8,128)(2,1)} %param.5) | copy-start | bytes 393220
  4.7 7.8 %copy-start.1 = (bf16[1,2,16,16,128]{4,3,2,1,0:T(8,128)(2,1)S(1)}, bf16[1,2,16,16,128]{4,3,2,1,0:T(8,128)(2,1)}, u32[]{:S(2)}) copy-start(bf16[1,2,16,16,128]{4,3,2,1,0:T(8,128)(2,1)} %param.4) | copy-start | bytes 393220
  4.8 5.5 %collective-permute-start.1 = (f16[296,128]{1,0:T(8,128)(2,1)S(1)}, f16[296,128]{1,0:T(8,128)(2,1)S(1)}, u32[]{:S(2)}, u32[]{:S(2)}) collective-permute-start(f16[296,128]{1,0:T(8,128)(2,1)S(1)} %pad_maximum_fusion.7), channel_id=1, source_target_pairs={{0,2},{1,3},{2,0},{3,1},{4,6},{5,7},{6,4},{7,5},{8,10},{9,11},{10,... | collective-permute-start | bytes 227336 | tf_op jit(solution)/shard_map/ppermute | solution.py:28
  10.5 4.4 %collective-permute-start.2 = (f16[296,128]{1,0:T(8,128)(2,1)S(1)}, f16[296,128]{1,0:T(8,128)(2,1)S(1)}, u32[]{:S(2)}, u32[]{:S(2)}) collective-permute-start(f16[296,128]{1,0:T(8,128)(2,1)S(1)} %pad_maximum_fusion.8), channel_id=1, source_target_pairs={{0,4},{1,5},{2,6},{3,7},{4,0},{5,1},{6,2},{7,3},{8,12},{9,13},{10,... | collective-permute-start | bytes 227336 | tf_op jit(solution)/shard_map/ppermute | solution.py:28
  12.5 7.1 %collective-permute-start.6 = (f16[656,128]{1,0:T(8,128)(2,1)S(1)}, f16[656,128]{1,0:T(8,128)(2,1)S(1)}, u32[]{:S(2)}, u32[]{:S(2)}) collective-permute-start(f16[656,128]{1,0:T(8,128)(2,1)S(1)} %convert_element_type.39), channel_id=1, source_target_pairs={{0,1},{1,0},{2,3},{3,2},{4,5},{5,4},{6,7},{7,6},{8,9},{9,8},{10,11... | collective-permute-start | bytes 503816 | tf_op jit(solution)/shard_map/ppermute | solution.py:28
  12.6 7.1 %collective-permute-start.7 = (f16[656,128]{1,0:T(8,128)(2,1)S(1)}, f16[656,128]{1,0:T(8,128)(2,1)S(1)}, u32[]{:S(2)}, u32[]{:S(2)}) collective-permute-start(f16[656,128]{1,0:T(8,128)(2,1)S(1)} %convert_element_type.39), channel_id=1, source_target_pairs={{0,3},{1,2},{2,1},{3,0},{4,7},{5,6},{6,5},{7,4},{8,11},{9,10},{10,... | collective-permute-start | bytes 503816 | tf_op jit(solution)/shard_map/ppermute | solution.py:28
  14.2 8.6 %collective-permute-start.5 = (f16[656,128]{1,0:T(8,128)(2,1)S(1)}, f16[656,128]{1,0:T(8,128)(2,1)S(1)}, u32[]{:S(2)}, u32[]{:S(2)}) collective-permute-start(f16[656,128]{1,0:T(8,128)(2,1)S(1)} %convert_element_type.39), channel_id=1, source_target_pairs={{0,2},{1,3},{2,0},{3,1},{4,6},{5,7},{6,4},{7,5},{8,10},{9,11},{10,... | collective-permute-start | bytes 503816 | tf_op jit(solution)/shard_map/ppermute | solution.py:28
  15.2 8.0 %collective-permute-start.4 = (f16[296,128]{1,0:T(8,128)(2,1)S(1)}, f16[296,128]{1,0:T(8,128)(2,1)S(1)}, u32[]{:S(2)}, u32[]{:S(2)}) collective-permute-start(f16[296,128]{1,0:T(8,128)(2,1)S(1)} %pad_maximum_fusion.9), channel_id=1, source_target_pairs={{0,8},{1,9},{2,10},{3,11},{4,12},{5,13},{6,14},{7,15},{8,0},{9,1},... | collective-permute-start | bytes 227336 | tf_op jit(solution)/shard_map/ppermute | solution.py:28
  18.1 7.2 %collective-permute-start.3 = (bf16[2,512,128]{2,1,0:T(8,128)(2,1)S(1)}, bf16[2,512,128]{2,1,0:T(8,128)(2,1)S(1)}, u32[]{:S(2)}, u32[]{:S(2)}) collective-permute-start(bf16[2,512,128]{2,1,0:T(8,128)(2,1)S(1)} %pad_maximum_fusion), channel_id=1, source_target_pairs={{16,0},{17,1},{18,2},{19,3},{20,4},{21,5},{22,6},{23,7},{24,8},{25... | collective-permute-start | bytes 786440 | tf_op jit(solution)/shard_map/ppermute | solution.py:24
  25.4 8.3 %collective-permute-start.8 = (bf16[2,512,128]{2,1,0:T(8,128)(2,1)S(1)}, bf16[2,512,128]{2,1,0:T(8,128)(2,1)S(1)}, u32[]{:S(2)}, u32[]{:S(2)}) collective-permute-start(bf16[2,512,128]{2,1,0:T(8,128)(2,1)S(1)} %pad_maximum_fusion.1.part_0), channel_id=1, source_target_pairs={{0,2},{1,3},{2,0},{3,1},{4,6},{5,7},{6,4},{7,5},{8,10},{9,11},{10,... | collective-permute-start | bytes 786440 | tf_op jit(solution)/shard_map/ppermute | solution.py:28
  26.9 3.8 %collective-permute-start.9 = (bf16[32,288]{1,0:T(8,128)(2,1)S(1)}, bf16[32,288]{1,0:T(8,128)(2,1)S(1)}, u32[]{:S(2)}, u32[]{:S(2)}) collective-permute-start(bf16[32,288]{1,0:T(8,128)(2,1)S(1)} %get-tuple-element.35), channel_id=1, source_target_pairs={{0,4},{1,5},{2,6},{3,7},{4,0},{5,1},{6,2},{7,3},{8,12},{9,13},{10,... | collective-permute-start | bytes 55304 | tf_op jit(solution)/shard_map/ppermute | solution.py:28
  30.9 4.3 %collective-permute-start.12 = (bf16[32,576]{1,0:T(8,128)(2,1)S(1)}, bf16[32,576]{1,0:T(8,128)(2,1)S(1)}, u32[]{:S(2)}, u32[]{:S(2)}) collective-permute-start(bf16[32,576]{1,0:T(8,128)(2,1)S(1)} %maximum_select_fusion.1), channel_id=1, source_target_pairs={{16,0},{17,1},{18,2},{19,3},{20,4},{21,5},{22,6},{23,7},{24,8},{25... | collective-permute-start | bytes 110600 | tf_op jit(solution)/shard_map/ppermute | solution.py:24
  32.4 6.2 %collective-permute-start.13 = (bf16[32,576]{1,0:T(8,128)(2,1)S(1)}, bf16[32,576]{1,0:T(8,128)(2,1)S(1)}, u32[]{:S(2)}, u32[]{:S(2)}) collective-permute-start(bf16[32,576]{1,0:T(8,128)(2,1)S(1)} %maximum_select_fusion.1), channel_id=1, source_target_pairs={{24,0},{25,1},{26,2},{27,3},{28,4},{29,5},{30,6},{31,7},{16,8},{17... | collective-permute-start | bytes 110600 | tf_op jit(solution)/shard_map/ppermute | solution.py:24
  33.7 8.3 %collective-permute-start.10 = (bf16[2,512,128]{2,1,0:T(8,128)(2,1)S(1)}, bf16[2,512,128]{2,1,0:T(8,128)(2,1)S(1)}, u32[]{:S(2)}, u32[]{:S(2)}) collective-permute-start(bf16[2,512,128]{2,1,0:T(8,128)(2,1)S(1)} %pad_maximum_fusion.1.part_0), channel_id=1, source_target_pairs={{0,1},{1,0},{2,3},{3,2},{4,5},{5,4},{6,7},{7,6},{8,9},{9,8},{10,11... | collective-permute-start | bytes 786440 | tf_op jit(solution)/shard_map/ppermute | solution.py:28
  33.7 8.3 %collective-permute-start.11 = (bf16[2,512,128]{2,1,0:T(8,128)(2,1)S(1)}, bf16[2,512,128]{2,1,0:T(8,128)(2,1)S(1)}, u32[]{:S(2)}, u32[]{:S(2)}) collective-permute-start(bf16[2,512,128]{2,1,0:T(8,128)(2,1)S(1)} %collective-permute-done.8.part_1), channel_id=1, source_target_pairs={{0,1},{1,0},{2,3},{3,2},{4,5},{5,4},{6,7},{7,6},{8,9},{9,8},{10,11... | collective-permute-start | bytes 786440 | tf_op jit(solution)/shard_map/ppermute | solution.py:28
  34.5 4.3 %collective-permute-start.14 = (f32[64,128]{1,0:T(8,128)S(1)}, f32[64,128]{1,0:T(8,128)S(1)}, u32[]{:S(2)}, u32[]{:S(2)}) collective-permute-start(f32[64,128]{1,0:T(8,128)S(1)} %get-tuple-element.44), channel_id=1, source_target_pairs={{0,2},{1,3},{2,0},{3,1},{4,6},{5,7},{6,4},{7,5},{8,10},{9,11},{10,... | collective-permute-start | bytes 98312 | tf_op jit(solution)/shard_map/ppermute | solution.py:28
  35.1 3.7 %collective-permute-start.15 = (f32[64,128]{1,0:T(8,128)S(1)}, f32[64,128]{1,0:T(8,128)S(1)}, u32[]{:S(2)}, u32[]{:S(2)}) collective-permute-start(f32[64,128]{1,0:T(8,128)S(1)} %get-tuple-element.45), channel_id=1, source_target_pairs={{0,1},{1,0},{2,3},{3,2},{4,5},{5,4},{6,7},{7,6},{8,9},{9,8},{10,11... | collective-permute-start | bytes 98312 | tf_op jit(solution)/shard_map/ppermute | solution.py:28
  38.7 3.3 %collective-permute-start.16 = (f32[64,128]{1,0:T(8,128)S(1)}, f32[64,128]{1,0:T(8,128)S(1)}, u32[]{:S(2)}, u32[]{:S(2)}) collective-permute-start(f32[64,128]{1,0:T(8,128)S(1)} %get-tuple-element.46), channel_id=1, source_target_pairs={{0,3},{1,2},{2,1},{3,0},{4,7},{5,6},{6,5},{7,4},{8,11},{9,10},{10,... | collective-permute-start | bytes 98312 | tf_op jit(solution)/shard_map/ppermute | solution.py:28
  44.1 4.6 %collective-permute-start.17 = (f16[368,128]{1,0:T(8,128)(2,1)S(1)}, f16[368,128]{1,0:T(8,128)(2,1)S(1)}, u32[]{:S(2)}, u32[]{:S(2)}) collective-permute-start(f16[368,128]{1,0:T(8,128)(2,1)S(1)} %pad_maximum_fusion.5), channel_id=1, source_target_pairs={{0,4},{1,5},{2,6},{3,7},{4,0},{5,1},{6,2},{7,3},{8,12},{9,13},{10,... | collective-permute-start | bytes 282632 | tf_op jit(solution)/shard_map/ppermute | solution.py:28
  48.8 6.7 %copy-start.2 = (f32[1,128,128]{2,1,0:T(8,128)S(1)}, f32[1,128,128]{2,1,0:T(8,128)}, u32[]{:S(2)}) copy-start(f32[1,128,128]{2,1,0:T(8,128)} %param.7) | copy-start | bytes 196612
  49.1 6.4 %collective-permute-start.18 = (f16[368,128]{1,0:T(8,128)(2,1)S(1)}, f16[368,128]{1,0:T(8,128)(2,1)S(1)}, u32[]{:S(2)}, u32[]{:S(2)}) collective-permute-start(f16[368,128]{1,0:T(8,128)(2,1)S(1)} %pad_maximum_fusion.6), channel_id=1, source_target_pairs={{0,8},{1,9},{2,10},{3,11},{4,12},{5,13},{6,14},{7,15},{8,0},{9,1},... | collective-permute-start | bytes 282632 | tf_op jit(solution)/shard_map/ppermute | solution.py:28
  57.1 4.8 %collective-permute-start.19 = (f32[208,128]{1,0:T(8,128)S(1)}, f32[208,128]{1,0:T(8,128)S(1)}, u32[]{:S(2)}, u32[]{:S(2)}) collective-permute-start(f32[208,128]{1,0:T(8,128)S(1)} %get-tuple-element.55), channel_id=1, source_target_pairs={{0,2},{1,3},{2,0},{3,1},{4,6},{5,7},{6,4},{7,5},{8,10},{9,11},{10,... | collective-permute-start | bytes 319496 | tf_op jit(solution)/shard_map/ppermute | solution.py:28
  61.9 1.4 %collective-permute-start.20 = (f32[200,128]{1,0:T(8,128)S(1)}, f32[200,128]{1,0:T(8,128)S(1)}, u32[]{:S(2)}, u32[]{:S(2)}) collective-permute-start(f32[200,128]{1,0:T(8,128)S(1)} %pad_maximum_fusion.4), channel_id=1, source_target_pairs={{0,1},{1,0},{2,3},{3,2},{4,5},{5,4},{6,7},{7,6},{8,9},{9,8},{10,11... | collective-permute-start | bytes 307208 | tf_op jit(solution)/shard_map/ppermute | solution.py:28

commit v13 on v12

--- a/solution.py
+++ b/solution.py
@@ -91,7 +91,7 @@
 
 
 def grad_kernel(
-    side, maps_in, grads_in, g_in, k_in, keep, send, k_parts, k_send, all_rows, maps, grads, g_inv, k_rows, sems
+    side, maps_in, grads_in, g_in, k_in, keep, send, k_parts, all_rows, maps, grads, g_inv, k_rows, sems
 ):
     copies = [
         pltpu.make_async_copy(source, target, sems.at[i])
@@ -122,13 +122,23 @@
     core, xbit = place_bits()
     mine = 2 * core + xbit
     quarter = width // 4
-    level = jnp.full((8, width), exponent(both), F32)
+    level = jnp.maximum(exponent(both), -99.0)
+    factor = jnp.exp2(jnp.full((1, width), TOP - level, F32))
+    level = jnp.full((8, width), level, F32)
+    size = 9 * quarter + 8
     for j in range(4):
         block = all_rows[pl.ds(pl.multiple_of((mine ^ j) * quarter, quarter), quarter), :]
-        target = keep if j < 2 else send
         for tap in range(9):
-            target[j % 2, tap * quarter : (tap + 1) * quarter] = block[:, tap * width : (tap + 1) * width]
-        target[j % 2, 9 * quarter :] = level
+            part = block[:, tap * width : (tap + 1) * width]
+            if j < 2:
+                keep[j, tap * quarter : (tap + 1) * quarter] = part
+            else:
+                low = (j - 2) * size + tap * quarter
+                send[low : low + quarter] = part * factor
+        if j < 2:
+            keep[j, size - 8 :] = level
+        else:
+            send[(j - 1) * size - 8 : (j - 1) * size] = level
     copies[3].wait()
     k = k_rows[...]
     high = k.astype(BF16)
@@ -140,8 +150,9 @@
         part = slice(tap * width, (tap + 1) * width)
         k_parts[0, tap] = high[:, part]
         k_parts[1, tap] = rest[:, part]
-        k_send[tap * rows : (tap + 1) * rows] = k[:, part] * factor
-    k_send[9 * rows :] = jnp.full((8, width), level, F32)
+        low = 2 * size + tap * rows
+        send[low : low + rows] = k[:, part] * factor
+    send[2 * size + 9 * rows :] = jnp.full((8, width), level, F32)
 
 
 def cross_kernel(side, part_0, part_1, part_2, part_3, precond_t, gram_0, gram_1, gram_2, gram_3, out, gram, levels):
@@ -221,6 +232,22 @@
     send[2 * rows :] = gram[...]
 
 
+def finish_kernel(scale, keep, mine, other, update, grams, scratch):
+    core, xbit = place_bits()
+    first = 2 * core + xbit
+    rows, width = update.shape
+    quarter = width // 4
+    update[...] = keep[...] + other[:rows]
+    for j in range(4):
+        source = mine if j < 2 else other
+        for i in range(2):
+            low = rows + 2 * quarter * (j % 2) + i * quarter
+            place = pl.ds(pl.multiple_of((first ^ j) * quarter, quarter), quarter)
+            scratch[i, place, :] = source[low : low + quarter] * scale
+    grams[0] = scratch[0]
+    grams[1] = scratch[1].T
+
+
 def gram_kernel(grads, next_grads, *refs):
     outs, scratch = refs[:4], refs[4]
     core, xbit = place_bits()
@@ -262,15 +289,16 @@
     flat_maps = maps.reshape(-1, width)
     flat_grads = grads.reshape(-1, width)
 
-    keep, send, k_own, k_send = pl.pallas_call(
+    wide = 9 * quarter
+    keep, send, k_own = pl.pallas_call(
         functools.partial(grad_kernel, side),
-        out_shape=[jax.ShapeDtypeStruct((2, 9 * quarter + 8, width), F32)] * 2
-        + [
+        out_shape=[
+            jax.ShapeDtypeStruct((2, wide + 8, width), F32),
+            jax.ShapeDtypeStruct((2 * (wide + 8) + 9 * rows + 8, width), F32),
             jax.ShapeDtypeStruct((2, 9, rows, width), BF16),
-            jax.ShapeDtypeStruct((9 * rows + 8, width), F32),
         ],
         in_specs=[HBM] * 4,
-        out_specs=[VMEM] * 4,
+        out_specs=[VMEM] * 3,
         scratch_shapes=[
             pltpu.VMEM((width, full), F32),
             pltpu.VMEM(flat_maps.shape, BF16),
@@ -301,17 +329,24 @@
         (more, other_level), = opened(swap(packed([sent]).astype(F16), bit), [9 * quarter])
         return values + more, jnp.maximum(level, other_level) + 1
 
-    wide = 9 * quarter
-    other = swap(send, 1)
-    h = keep[:, :wide] + other[:, :wide]
-    level = jnp.maximum(keep[:, wide:], other[:, wide:]) + 1
-    k_half = behind(k_send, h).astype(F16)
-    k_others = [swap(k_half, 2), swap(k_half, 1), swap(k_half, 3)]
+    sent = send.astype(F16)
+    other = swap(sent, 1)
+    e_rows = 2 * (wide + 8)
+    h, level = [], []
+    for j in range(2):
+        (more, other_level), = opened(other[j * (wide + 8) : (j + 1) * (wide + 8)], [wide])
+        h.append(keep[j, :wide] + more)
+        level.append(jnp.maximum(keep[j, wide:], other_level) + 1)
+    k_core = other[e_rows:]
+    k_sent = jnp.concatenate(behind((sent[e_rows:], k_core), h[0]), axis=0)
+    k_x, k_diagonal = jnp.split(swap(k_sent, 2), 2, axis=0)
+    own = behind(jnp.stack([flat_maps, flat_grads]), h[0])
+    next_own = after(own)
     h, level = summed(h[0], level[0], (h[1], level[1]), 2)
     h, level = summed(h, level, (h, level), zbits[0])
-    own = behind(jnp.stack([flat_maps, flat_grads]), h)
-    next_own = after(own)
+    next_own = behind(next_own, h)
     two_own = jnp.stack([flat_maps, next_own[0]])
+    two_x = swap(two_own, 2)
     for b in zbits[1:]:
         h, level = summed(h, level, (h, level), b)
 
@@ -324,8 +359,8 @@
         high = lax.reduce_precision(values, 8, 7)
         return jnp.stack([high, values - high]).astype(BF16)
 
-    k_a = k_pair([k_own, k_split(k_others[0])])
-    k_b = k_pair([k_split(k_others[1]), k_split(k_others[2])])
+    k_a = k_pair([k_own, k_split(k_x)])
+    k_b = k_pair([k_split(k_core), k_split(k_diagonal)])
 
     main_a, main_b, p_t = pl.pallas_call(
         functools.partial(precond_kernel, scale),
@@ -339,7 +374,6 @@
     def by_bit(mine, other, b):
         return jnp.where((me & b) == 0, jnp.concatenate([mine, other], 1), jnp.concatenate([other, mine], 1))
 
-    two_x = swap(behind(two_own, p_t), 2)
     grams = pl.pallas_call(
         gram_kernel,
         out_shape=[jax.ShapeDtypeStruct((2 * quarter, width), F32)] * 4,
@@ -400,14 +434,14 @@
     other = swap(send, 2)
     keep = out[0] + other[:rows]
     send = jnp.concatenate([out[1] + other[rows : 2 * rows], gram, other[2 * rows :]], axis=0)
-    other = swap(send, 1)
-    update = keep + other[:rows]
-    grams = jnp.concatenate([send[rows:], other[rows:]], axis=0)
-
-    grams = grams.reshape(2, 2, 2, quarter, width) * scale
-    grams = jnp.where(xbit == 0, grams, grams[:, ::-1])
-    grams = jnp.where(core == 0, grams, grams[::-1])
-    grams = grams.transpose(2, 4, 0, 1, 3).reshape(2, width, width)
+    update, grams = pl.pallas_call(
+        functools.partial(finish_kernel, scale),
+        out_shape=[jax.ShapeDtypeStruct((rows, width), F32), jax.ShapeDtypeStruct((2, width, width), F32)],
+        in_specs=[VMEM] * 3,
+        out_specs=[VMEM] * 2,
+        scratch_shapes=[pltpu.VMEM((2, width, width), F32)],
+        compiler_params=PARAMS,
+    )(keep, send, swap(send, 1))
     return (update[None], grams[None])
 
 

time: 64.9 us -> 66.5 us (1.025)
  starting transfers between devices: 21.2 us -> 25.7 us
  waiting for transfers between devices: 32 us -> 29.2 us
  Pallas kernels: 6.4 us -> 7.21 us
    ppermute x18 -> x16, starting transfers between devices: 16.8 us -> 21.9 us  [swap(): lax.ppermute(block, 'pos', [(i, i ^ bit) for i in range(lax.axis_size('po...]
    ppermute x3, waiting for transfers between devices: 4.84 us -> 1.64 us  [after(): return lax.ppermute(block, ('layer', 'pos'), route)]
    pallas_call x0 -> x1, Pallas kernels: none -> 0.78 us  [per_device(): pl.pallas_call(functools.partial(finish_kernel, scale), out_shape=[jax.Sh...]
    ppermute x18 -> x16, waiting for transfers between devices: 27.1 us -> 27.5 us  [swap(): lax.ppermute(block, 'pos', [(i, i ^ bit) for i in range(lax.axis_size('po...]
  transfers between devices with their start and end apart: 21 -> 19, of which waited for: 12 -> 12; matrix products, arithmetic and copies ran while one was open for 2% -> 2% of each run, Pallas kernels for 2% -> 2%
where the time goes in v13:
time: 66.5 us; the launch traced here: 66.4 us
  waiting for transfers between devices  29.2 us (44%)
  starting transfers between devices  25.7 us (39%)
  Pallas kernels  7.21 us (11%)
  other arithmetic  2 us (3%)
  between operations  1.11 us (2%)
  matrix products  0.72 us (1%)
    ppermute x16, waiting for transfers between devices, swap(): lax.ppermute(block, 'pos', [(i, i ^ bit) for i in range(lax.axis_size('po...  27.5 us
    ppermute x16, starting transfers between devices, swap(): lax.ppermute(block, 'pos', [(i, i ^ bit) for i in range(lax.axis_size('po...  21.9 us
    ppermute x3, starting transfers between devices, after(): return lax.ppermute(block, ('layer', 'pos'), route)  3.82 us
    pallas_call x1, Pallas kernels, per_device(): pl.pallas_call(functools.partial(grad_kernel, side), out_shape=[jax.Shape...  2.24 us
    pallas_call x1, Pallas kernels, per_device(): pl.pallas_call(functools.partial(cross_kernel, side), out_shape=[jax.Shap...  1.87 us
    ppermute x3, waiting for transfers between devices, after(): return lax.ppermute(block, ('layer', 'pos'), route)  1.64 us
  transfers between devices with their start and end apart: 19, of which 12 were waited for; matrix products, arithmetic and copies ran while one was open for 2% of the time, Pallas kernels for 2%

profile of v13, /device:TPU:0, one launch (start us, length us, event | category | flops | bytes accessed | tf_op | source)
XLA Modules:
  0.0 66.4 jit_solution(17908958296016230129)
XLA Ops:
  0.6 2.2 %shard_map.59 = (f32[2,296,128]{2,1,0:T(8,128)S(1)}, f32[1248,128]{1,0:T(8,128)S(1)}, bf16[2,9,72,128]{3,2,1,0:T(8,128)(2,1)S(1)}) custom-call(bf16[512,128]{1,0:T(8,128)(2,1)} %bitcast.96, bf16[512,128]{1,0:T(8,128)(2,1)} %bitcast.90, f32[128,128]{1,0:T(8,128)} %bitcast.100, f32[72,1152]{1,0:T(8,128)} %bitcast.99), custom_call_target="tpu_custom_call" | custom-call | tf_op jit(solution)/shard_map/pallas_call | solution.py:293
  4.9 2.9 %collective-permute-start.2 = (f16[296,128]{1,0:T(8,128)(2,1)S(1)}, f16[296,128]{1,0:T(8,128)(2,1)S(1)}, u32[]{:S(2)}, u32[]{:S(2)}) collective-permute-start(f16[296,128]{1,0:T(8,128)(2,1)S(1)} %pad_maximum_fusion.7), channel_id=1, source_target_pairs={{0,2},{1,3},{2,0},{3,1},{4,6},{5,7},{6,4},{7,5},{8,10},{9,11},{10,... | collective-permute-start | bytes 227336 | tf_op jit(solution)/shard_map/ppermute | solution.py:28
  7.9 2.5 %collective-permute-done.2 = f16[296,128]{1,0:T(8,128)(2,1)S(1)} collective-permute-done((f16[296,128]{1,0:T(8,128)(2,1)S(1)}, f16[296,128]{1,0:T(8,128)(2,1)S(1)}, u32[]{:S(2)}, u32[]{:S(2)}) %collective-permute-start.2) | collective-permute-done | bytes 75808 | tf_op jit(solution)/shard_map/ppermute | solution.py:28
  10.7 1.9 %collective-permute-start.3 = (f16[296,128]{1,0:T(8,128)(2,1)S(1)}, f16[296,128]{1,0:T(8,128)(2,1)S(1)}, u32[]{:S(2)}, u32[]{:S(2)}) collective-permute-start(f16[296,128]{1,0:T(8,128)(2,1)S(1)} %pad_maximum_fusion.8), channel_id=1, source_target_pairs={{0,4},{1,5},{2,6},{3,7},{4,0},{5,1},{6,2},{7,3},{8,12},{9,13},{10,... | collective-permute-start | bytes 227336 | tf_op jit(solution)/shard_map/ppermute | solution.py:28
  12.6 1.6 %collective-permute-start.1 = (bf16[2,512,128]{2,1,0:T(8,128)(2,1)S(1)}, bf16[2,512,128]{2,1,0:T(8,128)(2,1)S(1)}, u32[]{:S(2)}, u32[]{:S(2)}) collective-permute-start(bf16[2,512,128]{2,1,0:T(8,128)(2,1)S(1)} %pad_maximum_fusion.1), channel_id=1, source_target_pairs={{16,0},{17,1},{18,2},{19,3},{20,4},{21,5},{22,6},{23,7},{24,8},{25... | collective-permute-start | bytes 786440 | tf_op jit(solution)/shard_map/ppermute | solution.py:24
  15.3 2.9 %collective-permute-start.5 = (f16[296,128]{1,0:T(8,128)(2,1)S(1)}, f16[296,128]{1,0:T(8,128)(2,1)S(1)}, u32[]{:S(2)}, u32[]{:S(2)}) collective-permute-start(f16[296,128]{1,0:T(8,128)(2,1)S(1)} %pad_maximum_fusion.9), channel_id=1, source_target_pairs={{0,8},{1,9},{2,10},{3,11},{4,12},{5,13},{6,14},{7,15},{8,0},{9,1},... | collective-permute-start | bytes 227336 | tf_op jit(solution)/shard_map/ppermute | solution.py:28
  18.3 1.6 %collective-permute-start.6 = (f16[1312,128]{1,0:T(8,128)(2,1)S(1)}, f16[1312,128]{1,0:T(8,128)(2,1)S(1)}, u32[]{:S(2)}, u32[]{:S(2)}) collective-permute-start(f16[1312,128]{1,0:T(8,128)(2,1)S(1)} %pad_maximum_fusion), channel_id=1, source_target_pairs={{0,2},{1,3},{2,0},{3,1},{4,6},{5,7},{6,4},{7,5},{8,10},{9,11},{10,... | collective-permute-start | bytes 1007624 | tf_op jit(solution)/shard_map/ppermute | solution.py:28
  20.8 1.8 %collective-permute-start.4 = (bf16[2,512,128]{2,1,0:T(8,128)(2,1)S(1)}, bf16[2,512,128]{2,1,0:T(8,128)(2,1)S(1)}, u32[]{:S(2)}, u32[]{:S(2)}) collective-permute-start(bf16[2,512,128]{2,1,0:T(8,128)(2,1)S(1)} %pad_maximum_fusion.2.part_0), channel_id=1, source_target_pairs={{0,2},{1,3},{2,0},{3,1},{4,6},{5,7},{6,4},{7,5},{8,10},{9,11},{10,... | collective-permute-start | bytes 786440 | tf_op jit(solution)/shard_map/ppermute | solution.py:28
  22.6 5.9 %collective-permute-done.6 = f16[1312,128]{1,0:T(8,128)(2,1)S(1)} collective-permute-done((f16[1312,128]{1,0:T(8,128)(2,1)S(1)}, f16[1312,128]{1,0:T(8,128)(2,1)S(1)}, u32[]{:S(2)}, u32[]{:S(2)}) %collective-permute-start.6) | collective-permute-done | bytes 335904 | tf_op jit(solution)/shard_map/ppermute | solution.py:28
  29.7 1.6 %collective-permute-start.7 = (bf16[32,288]{1,0:T(8,128)(2,1)S(1)}, bf16[32,288]{1,0:T(8,128)(2,1)S(1)}, u32[]{:S(2)}, u32[]{:S(2)}) collective-permute-start(bf16[32,288]{1,0:T(8,128)(2,1)S(1)} %get-tuple-element.38), channel_id=1, source_target_pairs={{0,4},{1,5},{2,6},{3,7},{4,0},{5,1},{6,2},{7,3},{8,12},{9,13},{10,... | collective-permute-start | bytes 55304 | tf_op jit(solution)/shard_map/ppermute | solution.py:28
  31.3 2.2 %collective-permute-done.7 = bf16[32,288]{1,0:T(8,128)(2,1)S(1)} collective-permute-done((bf16[32,288]{1,0:T(8,128)(2,1)S(1)}, bf16[32,288]{1,0:T(8,128)(2,1)S(1)}, u32[]{:S(2)}, u32[]{:S(2)}) %collective-permute-start.7) | collective-permute-done | bytes 18464 | tf_op jit(solution)/shard_map/ppermute | solution.py:28
  33.6 1.4 %collective-permute-start.11 = (bf16[32,576]{1,0:T(8,128)(2,1)S(1)}, bf16[32,576]{1,0:T(8,128)(2,1)S(1)}, u32[]{:S(2)}, u32[]{:S(2)}) collective-permute-start(bf16[32,576]{1,0:T(8,128)(2,1)S(1)} %maximum_select_fusion.1), channel_id=1, source_target_pairs={{24,0},{25,1},{26,2},{27,3},{28,4},{29,5},{30,6},{31,7},{16,8},{17... | collective-permute-start | bytes 110600 | tf_op jit(solution)/shard_map/ppermute | solution.py:24
  37.9 1.6 %collective-permute-done.11 = bf16[32,576]{1,0:T(8,128)(2,1)S(1)} collective-permute-done((bf16[32,576]{1,0:T(8,128)(2,1)S(1)}, bf16[32,576]{1,0:T(8,128)(2,1)S(1)}, u32[]{:S(2)}, u32[]{:S(2)}) %collective-permute-start.11) | collective-permute-done | bytes 36896 | tf_op jit(solution)/shard_map/ppermute | solution.py:24
  39.5 1.6 %collective-permute-start.14 = (f32[64,128]{1,0:T(8,128)S(1)}, f32[64,128]{1,0:T(8,128)S(1)}, u32[]{:S(2)}, u32[]{:S(2)}) collective-permute-start(f32[64,128]{1,0:T(8,128)S(1)} %get-tuple-element.48), channel_id=1, source_target_pairs={{0,3},{1,2},{2,1},{3,0},{4,7},{5,6},{6,5},{7,4},{8,11},{9,10},{10,... | collective-permute-start | bytes 98312 | tf_op jit(solution)/shard_map/ppermute | solution.py:28
  41.2 1.6 %collective-permute-done.14.gram_3 = f32[64,128]{1,0:T(8,128)S(1)} collective-permute-done((f32[64,128]{1,0:T(8,128)S(1)}, f32[64,128]{1,0:T(8,128)S(1)}, u32[]{:S(2)}, u32[]{:S(2)}) %collective-permute-start.14) | collective-permute-done | bytes 32800 | tf_op jit(solution)/shard_map/ppermute | solution.py:28
  42.8 1.9 %shard_map.62 = (f32[288,128]{1,0:T(8,128)S(1)}, f32[64,128]{1,0:T(8,128)S(1)}, f32[2,8,128]{2,1,0:T(8,128)S(1)}) custom-call(bf16[2,512,128]{2,1,0:T(8,128)(2,1)S(1)} %pad_maximum_fusion.2.part_0, bf16[2,512,128]{2,1,0:T(8,128)(2,1)S(1)} %collective-permute-done.4.part_1, bf16[2,512,128]{2,1,0:T(8,128)(2,1)S(1)} %collective-permute-done.8.part_2, ...), custom_call_target="tpu_custom_call" | custom-call | tf_op jit(solution)/shard_map/pallas_call | solution.py:398
  44.9 1.7 %collective-permute-start.15 = (f16[368,128]{1,0:T(8,128)(2,1)S(1)}, f16[368,128]{1,0:T(8,128)(2,1)S(1)}, u32[]{:S(2)}, u32[]{:S(2)}) collective-permute-start(f16[368,128]{1,0:T(8,128)(2,1)S(1)} %pad_maximum_fusion.5), channel_id=1, source_target_pairs={{0,4},{1,5},{2,6},{3,7},{4,0},{5,1},{6,2},{7,3},{8,12},{9,13},{10,... | collective-permute-start | bytes 282632 | tf_op jit(solution)/shard_map/ppermute | solution.py:28
  47.2 3.0 %collective-permute-done.15 = f16[368,128]{1,0:T(8,128)(2,1)S(1)} collective-permute-done((f16[368,128]{1,0:T(8,128)(2,1)S(1)}, f16[368,128]{1,0:T(8,128)(2,1)S(1)}, u32[]{:S(2)}, u32[]{:S(2)}) %collective-permute-start.15) | collective-permute-done | bytes 94240 | tf_op jit(solution)/shard_map/ppermute | solution.py:28
  50.4 2.1 %collective-permute-start.16 = (f16[368,128]{1,0:T(8,128)(2,1)S(1)}, f16[368,128]{1,0:T(8,128)(2,1)S(1)}, u32[]{:S(2)}, u32[]{:S(2)}) collective-permute-start(f16[368,128]{1,0:T(8,128)(2,1)S(1)} %pad_maximum_fusion.6), channel_id=1, source_target_pairs={{0,8},{1,9},{2,10},{3,11},{4,12},{5,13},{6,14},{7,15},{8,0},{9,1},... | collective-permute-start | bytes 282632 | tf_op jit(solution)/shard_map/ppermute | solution.py:28
  52.5 5.3 %collective-permute-done.16 = f16[368,128]{1,0:T(8,128)(2,1)S(1)} collective-permute-done((f16[368,128]{1,0:T(8,128)(2,1)S(1)}, f16[368,128]{1,0:T(8,128)(2,1)S(1)}, u32[]{:S(2)}, u32[]{:S(2)}) %collective-permute-start.16) | collective-permute-done | bytes 94240 | tf_op jit(solution)/shard_map/ppermute | solution.py:28
  58.1 1.3 %shard_map.63 = (f32[2,72,128]{2,1,0:T(8,128)S(1)}, f32[208,128]{1,0:T(8,128)S(1)}) custom-call(f32[288,128]{1,0:T(8,128)S(1)} %fusion.3.cross_t, f32[32,128]{1,0:T(8,128)S(1)} %convolution_multiply_fusion.mixed_in, bf16[2,9,144,128]{3,2,1,0:T(8,128)(2,1)S(1)} %maximum_maximum_fusion.k_a, bf16[2,9,144,128]{3,2,1,0:T(8,128)(2,1)S(1)} %maximum_maximum_fusion.1.k_b, ...), custom_call_target="tpu_custom_call" | custom-call | tf_op jit(solution)/shard_map/pallas_call | solution.py:424
  59.4 1.6 %collective-permute-start.17 = (f32[208,128]{1,0:T(8,128)S(1)}, f32[208,128]{1,0:T(8,128)S(1)}, u32[]{:S(2)}, u32[]{:S(2)}) collective-permute-start(f32[208,128]{1,0:T(8,128)S(1)} %get-tuple-element.57), channel_id=1, source_target_pairs={{0,2},{1,3},{2,0},{3,1},{4,6},{5,7},{6,4},{7,5},{8,10},{9,11},{10,... | collective-permute-start | bytes 319496 | tf_op jit(solution)/shard_map/ppermute | solution.py:28
  61.0 3.2 %collective-permute-done.17 = f32[208,128]{1,0:T(8,128)S(1)} collective-permute-done((f32[208,128]{1,0:T(8,128)S(1)}, f32[208,128]{1,0:T(8,128)S(1)}, u32[]{:S(2)}, u32[]{:S(2)}) %collective-permute-start.17) | collective-permute-done | bytes 106528 | tf_op jit(solution)/shard_map/ppermute | solution.py:28
  64.3 1.3 %collective-permute-done.18.other = f32[200,128]{1,0:T(8,128)S(1)} collective-permute-done((f32[200,128]{1,0:T(8,128)S(1)}, f32[200,128]{1,0:T(8,128)S(1)}, u32[]{:S(2)}, u32[]{:S(2)}) %collective-permute-start.18) | collective-permute-done | bytes 102432 | tf_op jit(solution)/shard_map/ppermute | solution.py:28
  (95 shorter events, 10.6 us)
Async XLA Ops:
  2.9 0.9 %copy-start = (bf16[1,2,16,16,128]{4,3,2,1,0:T(8,128)(2,1)S(1)}, bf16[1,2,16,16,128]{4,3,2,1,0:T(8,128)(2,1)}, u32[]{:S(2)}) copy-start(bf16[1,2,16,16,128]{4,3,2,1,0:T(8,128)(2,1)} %param.5) | copy-start | bytes 393220
  2.9 1.0 %copy-start.1 = (bf16[1,2,16,16,128]{4,3,2,1,0:T(8,128)(2,1)S(1)}, bf16[1,2,16,16,128]{4,3,2,1,0:T(8,128)(2,1)}, u32[]{:S(2)}) copy-start(bf16[1,2,16,16,128]{4,3,2,1,0:T(8,128)(2,1)} %param.4) | copy-start | bytes 393220
  3.0 1.8 %collective-permute-start = (f16[1248,128]{1,0:T(8,128)(2,1)S(1)}, f16[1248,128]{1,0:T(8,128)(2,1)S(1)}, u32[]{:S(2)}, u32[]{:S(2)}) collective-permute-start(f16[1248,128]{1,0:T(8,128)(2,1)S(1)} %convert_element_type.42), channel_id=1, source_target_pairs={{0,1},{1,0},{2,3},{3,2},{4,5},{5,4},{6,7},{7,6},{8,9},{9,8},{10,11... | collective-permute-start | bytes 958472 | tf_op jit(solution)/shard_map/ppermute | solution.py:28
  4.9 5.5 %collective-permute-start.2 = (f16[296,128]{1,0:T(8,128)(2,1)S(1)}, f16[296,128]{1,0:T(8,128)(2,1)S(1)}, u32[]{:S(2)}, u32[]{:S(2)}) collective-permute-start(f16[296,128]{1,0:T(8,128)(2,1)S(1)} %pad_maximum_fusion.7), channel_id=1, source_target_pairs={{0,2},{1,3},{2,0},{3,1},{4,6},{5,7},{6,4},{7,5},{8,10},{9,11},{10,... | collective-permute-start | bytes 227336 | tf_op jit(solution)/shard_map/ppermute | solution.py:28
  10.7 4.4 %collective-permute-start.3 = (f16[296,128]{1,0:T(8,128)(2,1)S(1)}, f16[296,128]{1,0:T(8,128)(2,1)S(1)}, u32[]{:S(2)}, u32[]{:S(2)}) collective-permute-start(f16[296,128]{1,0:T(8,128)(2,1)S(1)} %pad_maximum_fusion.8), channel_id=1, source_target_pairs={{0,4},{1,5},{2,6},{3,7},{4,0},{5,1},{6,2},{7,3},{8,12},{9,13},{10,... | collective-permute-start | bytes 227336 | tf_op jit(solution)/shard_map/ppermute | solution.py:28
  12.6 8.1 %collective-permute-start.1 = (bf16[2,512,128]{2,1,0:T(8,128)(2,1)S(1)}, bf16[2,512,128]{2,1,0:T(8,128)(2,1)S(1)}, u32[]{:S(2)}, u32[]{:S(2)}) collective-permute-start(bf16[2,512,128]{2,1,0:T(8,128)(2,1)S(1)} %pad_maximum_fusion.1), channel_id=1, source_target_pairs={{16,0},{17,1},{18,2},{19,3},{20,4},{21,5},{22,6},{23,7},{24,8},{25... | collective-permute-start | bytes 786440 | tf_op jit(solution)/shard_map/ppermute | solution.py:24
  15.3 5.3 %collective-permute-start.5 = (f16[296,128]{1,0:T(8,128)(2,1)S(1)}, f16[296,128]{1,0:T(8,128)(2,1)S(1)}, u32[]{:S(2)}, u32[]{:S(2)}) collective-permute-start(f16[296,128]{1,0:T(8,128)(2,1)S(1)} %pad_maximum_fusion.9), channel_id=1, source_target_pairs={{0,8},{1,9},{2,10},{3,11},{4,12},{5,13},{6,14},{7,15},{8,0},{9,1},... | collective-permute-start | bytes 227336 | tf_op jit(solution)/shard_map/ppermute | solution.py:28
  18.3 10.2 %collective-permute-start.6 = (f16[1312,128]{1,0:T(8,128)(2,1)S(1)}, f16[1312,128]{1,0:T(8,128)(2,1)S(1)}, u32[]{:S(2)}, u32[]{:S(2)}) collective-permute-start(f16[1312,128]{1,0:T(8,128)(2,1)S(1)} %pad_maximum_fusion), channel_id=1, source_target_pairs={{0,2},{1,3},{2,0},{3,1},{4,6},{5,7},{6,4},{7,5},{8,10},{9,11},{10,... | collective-permute-start | bytes 1007624 | tf_op jit(solution)/shard_map/ppermute | solution.py:28
  20.8 15.1 %collective-permute-start.4 = (bf16[2,512,128]{2,1,0:T(8,128)(2,1)S(1)}, bf16[2,512,128]{2,1,0:T(8,128)(2,1)S(1)}, u32[]{:S(2)}, u32[]{:S(2)}) collective-permute-start(bf16[2,512,128]{2,1,0:T(8,128)(2,1)S(1)} %pad_maximum_fusion.2.part_0), channel_id=1, source_target_pairs={{0,2},{1,3},{2,0},{3,1},{4,6},{5,7},{6,4},{7,5},{8,10},{9,11},{10,... | collective-permute-start | bytes 786440 | tf_op jit(solution)/shard_map/ppermute | solution.py:28
  29.7 3.8 %collective-permute-start.7 = (bf16[32,288]{1,0:T(8,128)(2,1)S(1)}, bf16[32,288]{1,0:T(8,128)(2,1)S(1)}, u32[]{:S(2)}, u32[]{:S(2)}) collective-permute-start(bf16[32,288]{1,0:T(8,128)(2,1)S(1)} %get-tuple-element.38), channel_id=1, source_target_pairs={{0,4},{1,5},{2,6},{3,7},{4,0},{5,1},{6,2},{7,3},{8,12},{9,13},{10,... | collective-permute-start | bytes 55304 | tf_op jit(solution)/shard_map/ppermute | solution.py:28
  33.6 5.9 %collective-permute-start.11 = (bf16[32,576]{1,0:T(8,128)(2,1)S(1)}, bf16[32,576]{1,0:T(8,128)(2,1)S(1)}, u32[]{:S(2)}, u32[]{:S(2)}) collective-permute-start(bf16[32,576]{1,0:T(8,128)(2,1)S(1)} %maximum_select_fusion.1), channel_id=1, source_target_pairs={{24,0},{25,1},{26,2},{27,3},{28,4},{29,5},{30,6},{31,7},{16,8},{17... | collective-permute-start | bytes 110600 | tf_op jit(solution)/shard_map/ppermute | solution.py:24
  35.0 4.5 %collective-permute-start.10 = (bf16[32,576]{1,0:T(8,128)(2,1)S(1)}, bf16[32,576]{1,0:T(8,128)(2,1)S(1)}, u32[]{:S(2)}, u32[]{:S(2)}) collective-permute-start(bf16[32,576]{1,0:T(8,128)(2,1)S(1)} %maximum_select_fusion.1), channel_id=1, source_target_pairs={{16,0},{17,1},{18,2},{19,3},{20,4},{21,5},{22,6},{23,7},{24,8},{25... | collective-permute-start | bytes 110600 | tf_op jit(solution)/shard_map/ppermute | solution.py:24
  35.9 7.0 %collective-permute-start.8 = (bf16[2,512,128]{2,1,0:T(8,128)(2,1)S(1)}, bf16[2,512,128]{2,1,0:T(8,128)(2,1)S(1)}, u32[]{:S(2)}, u32[]{:S(2)}) collective-permute-start(bf16[2,512,128]{2,1,0:T(8,128)(2,1)S(1)} %pad_maximum_fusion.2.part_0), channel_id=1, source_target_pairs={{0,1},{1,0},{2,3},{3,2},{4,5},{5,4},{6,7},{7,6},{8,9},{9,8},{10,11... | collective-permute-start | bytes 786440 | tf_op jit(solution)/shard_map/ppermute | solution.py:28
  35.9 7.0 %collective-permute-start.9 = (bf16[2,512,128]{2,1,0:T(8,128)(2,1)S(1)}, bf16[2,512,128]{2,1,0:T(8,128)(2,1)S(1)}, u32[]{:S(2)}, u32[]{:S(2)}) collective-permute-start(bf16[2,512,128]{2,1,0:T(8,128)(2,1)S(1)} %collective-permute-done.4.part_1), channel_id=1, source_target_pairs={{0,1},{1,0},{2,3},{3,2},{4,5},{5,4},{6,7},{7,6},{8,9},{9,8},{10,11... | collective-permute-start | bytes 786440 | tf_op jit(solution)/shard_map/ppermute | solution.py:28
  36.7 4.5 %collective-permute-start.12 = (f32[64,128]{1,0:T(8,128)S(1)}, f32[64,128]{1,0:T(8,128)S(1)}, u32[]{:S(2)}, u32[]{:S(2)}) collective-permute-start(f32[64,128]{1,0:T(8,128)S(1)} %get-tuple-element.46), channel_id=1, source_target_pairs={{0,2},{1,3},{2,0},{3,1},{4,6},{5,7},{6,4},{7,5},{8,10},{9,11},{10,... | collective-permute-start | bytes 98312 | tf_op jit(solution)/shard_map/ppermute | solution.py:28
  39.5 1.7 %collective-permute-start.13 = (f32[64,128]{1,0:T(8,128)S(1)}, f32[64,128]{1,0:T(8,128)S(1)}, u32[]{:S(2)}, u32[]{:S(2)}) collective-permute-start(f32[64,128]{1,0:T(8,128)S(1)} %get-tuple-element.47), channel_id=1, source_target_pairs={{0,1},{1,0},{2,3},{3,2},{4,5},{5,4},{6,7},{7,6},{8,9},{9,8},{10,11... | collective-permute-start | bytes 98312 | tf_op jit(solution)/shard_map/ppermute | solution.py:28
  39.5 3.3 %collective-permute-start.14 = (f32[64,128]{1,0:T(8,128)S(1)}, f32[64,128]{1,0:T(8,128)S(1)}, u32[]{:S(2)}, u32[]{:S(2)}) collective-permute-start(f32[64,128]{1,0:T(8,128)S(1)} %get-tuple-element.48), channel_id=1, source_target_pairs={{0,3},{1,2},{2,1},{3,0},{4,7},{5,6},{6,5},{7,4},{8,11},{9,10},{10,... | collective-permute-start | bytes 98312 | tf_op jit(solution)/shard_map/ppermute | solution.py:28
  44.9 5.2 %collective-permute-start.15 = (f16[368,128]{1,0:T(8,128)(2,1)S(1)}, f16[368,128]{1,0:T(8,128)(2,1)S(1)}, u32[]{:S(2)}, u32[]{:S(2)}) collective-permute-start(f16[368,128]{1,0:T(8,128)(2,1)S(1)} %pad_maximum_fusion.5), channel_id=1, source_target_pairs={{0,4},{1,5},{2,6},{3,7},{4,0},{5,1},{6,2},{7,3},{8,12},{9,13},{10,... | collective-permute-start | bytes 282632 | tf_op jit(solution)/shard_map/ppermute | solution.py:28
  50.4 7.5 %copy-start.2 = (f32[1,128,128]{2,1,0:T(8,128)S(1)}, f32[1,128,128]{2,1,0:T(8,128)}, u32[]{:S(2)}) copy-start(f32[1,128,128]{2,1,0:T(8,128)} %param.7) | copy-start | bytes 196612
  50.4 7.3 %collective-permute-start.16 = (f16[368,128]{1,0:T(8,128)(2,1)S(1)}, f16[368,128]{1,0:T(8,128)(2,1)S(1)}, u32[]{:S(2)}, u32[]{:S(2)}) collective-permute-start(f16[368,128]{1,0:T(8,128)(2,1)S(1)} %pad_maximum_fusion.6), channel_id=1, source_target_pairs={{0,8},{1,9},{2,10},{3,11},{4,12},{5,13},{6,14},{7,15},{8,0},{9,1},... | collective-permute-start | bytes 282632 | tf_op jit(solution)/shard_map/ppermute | solution.py:28
  59.4 4.8 %collective-permute-start.17 = (f32[208,128]{1,0:T(8,128)S(1)}, f32[208,128]{1,0:T(8,128)S(1)}, u32[]{:S(2)}, u32[]{:S(2)}) collective-permute-start(f32[208,128]{1,0:T(8,128)S(1)} %get-tuple-element.57), channel_id=1, source_target_pairs={{0,2},{1,3},{2,0},{3,1},{4,6},{5,7},{6,4},{7,5},{8,10},{9,11},{10,... | collective-permute-start | bytes 319496 | tf_op jit(solution)/shard_map/ppermute | solution.py:28
  64.2 1.4 %collective-permute-start.18 = (f32[200,128]{1,0:T(8,128)S(1)}, f32[200,128]{1,0:T(8,128)S(1)}, u32[]{:S(2)}, u32[]{:S(2)}) collective-permute-start(f32[200,128]{1,0:T(8,128)S(1)} %pad_maximum_fusion.4.mine), channel_id=1, source_target_pairs={{0,1},{1,0},{2,3},{3,2},{4,5},{5,4},{6,7},{7,6},{8,9},{9,8},{10,11... | collective-permute-start | bytes 307208 | tf_op jit(solution)/shard_map/ppermute | solution.py:28

commit v14 on v9

--- a/solution.py
+++ b/solution.py
@@ -281,7 +281,7 @@
             pltpu.SemaphoreType.DMA((4,)),
         ],
         compiler_params=PARAMS,
-    )(flat_maps, flat_grads, g_inv, k_rows)
+    )(*(pltpu.with_memory_space_constraint(a, pltpu.HBM) for a in (flat_maps, flat_grads, g_inv, k_rows)))
 
     def message(values, level):
         level = jnp.maximum(level, -99.0)

time: 60.3 us -> 57 us (0.945)
  local copies, waits for them, and re-layouts: 4.5 us -> 0.88 us
    unnamed x14 -> x6, local copies, waits for them, and re-layouts: 3.63 us -> 0.02 us
where the time goes in v14:
time: 57 us; the launch traced here: 56.8 us
  starting transfers between devices  23.9 us (42%)
  waiting for transfers between devices  22.3 us (39%)
  Pallas kernels  6.2 us (11%)
  other arithmetic  1.95 us (3%)
  between operations  1.07 us (2%)
  local copies, waits for them, and re-layouts  0.88 us (2%)
    ppermute x19, waiting for transfers between devices, swap(): lax.ppermute(block, 'pos', [(i, i ^ bit) for i in range(lax.axis_size('po...  20.2 us
    ppermute x19, starting transfers between devices, swap(): lax.ppermute(block, 'pos', [(i, i ^ bit) for i in range(lax.axis_size('po...  18.9 us
    ppermute x3, starting transfers between devices, after(): return lax.ppermute(block, ('layer', 'pos'), route)  4.93 us
    pallas_call x1, Pallas kernels, per_device(): pl.pallas_call(functools.partial(grad_kernel, side), out_shape=[jax.Shape...  2.21 us
    ppermute x3, waiting for transfers between devices, after(): return lax.ppermute(block, ('layer', 'pos'), route)  2.1 us
    pallas_call x1, Pallas kernels, per_device(): pl.pallas_call(functools.partial(cross_kernel, side), out_shape=[jax.Shap...  1.69 us
    pallas_call x1, Pallas kernels, per_device(): pl.pallas_call(update_kernel, out_shape=[jax.ShapeDtypeStruct((2, rows, w...  1.28 us
  transfers between devices with their start and end apart: 22, of which 14 were waited for; matrix products, arithmetic and copies ran while one was open for 4% of the time, Pallas kernels for 2%

profile of v14, /device:TPU:0, one launch (start us, length us, event | category | flops | bytes accessed | tf_op | source)
XLA Modules:
  0.0 56.8 jit_solution(4682978368034916307)
XLA Ops:
  0.6 2.2 %shard_map.59 = (f32[2,10,32,128]{3,2,1,0:T(8,128)S(1)}, f32[2,10,32,128]{3,2,1,0:T(8,128)S(1)}, bf16[2,9,72,128]{3,2,1,0:T(8,128)(2,1)S(1)}, f32[10,72,128]{2,1,0:T(8,128)S(1)}) custom-call(bf16[512,128]{1,0:T(8,128)(2,1)} %bitcast.96, bf16[512,128]{1,0:T(8,128)(2,1)} %bitcast.93, f32[128,128]{1,0:T(8,128)} %bitcast.100, f32[72,1152]{1,0:T(8,128)} %bitcast.99), custom_call_target="tpu_custom_call" | custom-call | tf_op jit(solution)/shard_map/pallas_call | solution.py:266
  3.4 1.3 %collective-permute-done = f32[2,10,32,128]{3,2,1,0:T(8,128)S(1)} collective-permute-done((f32[2,10,32,128]{3,2,1,0:T(8,128)S(1)}, f32[2,10,32,128]{3,2,1,0:T(8,128)S(1)}, u32[]{:S(2)}, u32[]{:S(2)}) %collective-permute-start) | collective-permute-done | bytes 327712 | tf_op jit(solution)/shard_map/ppermute | solution.py:28
  4.8 2.9 %collective-permute-start.2 = (f16[10,32,128]{2,1,0:T(8,128)(2,1)S(1)}, f16[10,32,128]{2,1,0:T(8,128)(2,1)S(1)}, u32[]{:S(2)}, u32[]{:S(2)}) collective-permute-start(f16[10,32,128]{2,1,0:T(8,128)(2,1)S(1)} %pad_maximum_fusion.5), channel_id=1, source_target_pairs={{0,2},{1,3},{2,0},{3,1},{4,6},{5,7},{6,4},{7,5},{8,10},{9,11},{10,... | collective-permute-start | bytes 245768 | tf_op jit(solution)/shard_map/ppermute | solution.py:28
  7.7 2.7 %collective-permute-done.2 = f16[10,32,128]{2,1,0:T(8,128)(2,1)S(1)} collective-permute-done((f16[10,32,128]{2,1,0:T(8,128)(2,1)S(1)}, f16[10,32,128]{2,1,0:T(8,128)(2,1)S(1)}, u32[]{:S(2)}, u32[]{:S(2)}) %collective-permute-start.2) | collective-permute-done | bytes 81952 | tf_op jit(solution)/shard_map/ppermute | solution.py:28
  10.6 1.9 %collective-permute-start.3 = (f16[10,32,128]{2,1,0:T(8,128)(2,1)S(1)}, f16[10,32,128]{2,1,0:T(8,128)(2,1)S(1)}, u32[]{:S(2)}, u32[]{:S(2)}) collective-permute-start(f16[10,32,128]{2,1,0:T(8,128)(2,1)S(1)} %pad_maximum_fusion.6), channel_id=1, source_target_pairs={{0,4},{1,5},{2,6},{3,7},{4,0},{5,1},{6,2},{7,3},{8,12},{9,13},{10,... | collective-permute-start | bytes 245768 | tf_op jit(solution)/shard_map/ppermute | solution.py:28
  12.5 1.6 %collective-permute-start.5 = (f16[10,72,128]{2,1,0:T(8,128)(2,1)S(1)}, f16[10,72,128]{2,1,0:T(8,128)(2,1)S(1)}, u32[]{:S(2)}, u32[]{:S(2)}) collective-permute-start(f16[10,72,128]{2,1,0:T(8,128)(2,1)S(1)} %convert_element_type.38), channel_id=1, source_target_pairs={{0,2},{1,3},{2,0},{3,1},{4,6},{5,7},{6,4},{7,5},{8,10},{9,11},{10,... | collective-permute-start | bytes 552968 | tf_op jit(solution)/shard_map/ppermute | solution.py:28
  14.7 1.5 %collective-permute-start.1 = (bf16[2,512,128]{2,1,0:T(8,128)(2,1)S(1)}, bf16[2,512,128]{2,1,0:T(8,128)(2,1)S(1)}, u32[]{:S(2)}, u32[]{:S(2)}) collective-permute-start(bf16[2,512,128]{2,1,0:T(8,128)(2,1)S(1)} %pad_maximum_fusion.1), channel_id=1, source_target_pairs={{16,0},{17,1},{18,2},{19,3},{20,4},{21,5},{22,6},{23,7},{24,8},{25... | collective-permute-start | bytes 786440 | tf_op jit(solution)/shard_map/ppermute | solution.py:24
  16.4 2.7 %collective-permute-start.4 = (f16[10,32,128]{2,1,0:T(8,128)(2,1)S(1)}, f16[10,32,128]{2,1,0:T(8,128)(2,1)S(1)}, u32[]{:S(2)}, u32[]{:S(2)}) collective-permute-start(f16[10,32,128]{2,1,0:T(8,128)(2,1)S(1)} %pad_maximum_fusion.7), channel_id=1, source_target_pairs={{0,8},{1,9},{2,10},{3,11},{4,12},{5,13},{6,14},{7,15},{8,0},{9,1},... | collective-permute-start | bytes 245768 | tf_op jit(solution)/shard_map/ppermute | solution.py:28
  19.4 1.7 %collective-permute-done.7 = f16[10,72,128]{2,1,0:T(8,128)(2,1)S(1)} collective-permute-done((f16[10,72,128]{2,1,0:T(8,128)(2,1)S(1)}, f16[10,72,128]{2,1,0:T(8,128)(2,1)S(1)}, u32[]{:S(2)}, u32[]{:S(2)}) %collective-permute-start.7) | collective-permute-done | bytes 184352 | tf_op jit(solution)/shard_map/ppermute | solution.py:28
  21.5 1.6 %collective-permute-done.4 = f16[10,32,128]{2,1,0:T(8,128)(2,1)S(1)} collective-permute-done((f16[10,32,128]{2,1,0:T(8,128)(2,1)S(1)}, f16[10,32,128]{2,1,0:T(8,128)(2,1)S(1)}, u32[]{:S(2)}, u32[]{:S(2)}) %collective-permute-start.4) | collective-permute-done | bytes 81952 | tf_op jit(solution)/shard_map/ppermute | solution.py:28
  24.2 1.6 %collective-permute-start.8 = (bf16[2,512,128]{2,1,0:T(8,128)(2,1)S(1)}, bf16[2,512,128]{2,1,0:T(8,128)(2,1)S(1)}, u32[]{:S(2)}, u32[]{:S(2)}) collective-permute-start(bf16[2,512,128]{2,1,0:T(8,128)(2,1)S(1)} %pad_maximum_fusion.part_0), channel_id=1, source_target_pairs={{0,2},{1,3},{2,0},{3,1},{4,6},{5,7},{6,4},{7,5},{8,10},{9,11},{10,... | collective-permute-start | bytes 786440 | tf_op jit(solution)/shard_map/ppermute | solution.py:28
  26.3 1.4 %collective-permute-done.9 = bf16[32,288]{1,0:T(8,128)(2,1)S(1)} collective-permute-done((bf16[32,288]{1,0:T(8,128)(2,1)S(1)}, bf16[32,288]{1,0:T(8,128)(2,1)S(1)}, u32[]{:S(2)}, u32[]{:S(2)}) %collective-permute-start.9) | collective-permute-done | bytes 18464 | tf_op jit(solution)/shard_map/ppermute | solution.py:28
  27.8 2.4 %collective-permute-start.13 = (bf16[32,576]{1,0:T(8,128)(2,1)S(1)}, bf16[32,576]{1,0:T(8,128)(2,1)S(1)}, u32[]{:S(2)}, u32[]{:S(2)}) collective-permute-start(bf16[32,576]{1,0:T(8,128)(2,1)S(1)} %maximum_select_fusion.1), channel_id=1, source_target_pairs={{24,0},{25,1},{26,2},{27,3},{28,4},{29,5},{30,6},{31,7},{16,8},{17... | collective-permute-start | bytes 110600 | tf_op jit(solution)/shard_map/ppermute | solution.py:24
  30.2 1.0 %collective-permute-start.12 = (bf16[32,576]{1,0:T(8,128)(2,1)S(1)}, bf16[32,576]{1,0:T(8,128)(2,1)S(1)}, u32[]{:S(2)}, u32[]{:S(2)}) collective-permute-start(bf16[32,576]{1,0:T(8,128)(2,1)S(1)} %maximum_select_fusion.1), channel_id=1, source_target_pairs={{16,0},{17,1},{18,2},{19,3},{20,4},{21,5},{22,6},{23,7},{24,8},{25... | collective-permute-start | bytes 110600 | tf_op jit(solution)/shard_map/ppermute | solution.py:24
  31.2 1.1 %collective-permute-start.15 = (f32[64,128]{1,0:T(8,128)S(1)}, f32[64,128]{1,0:T(8,128)S(1)}, u32[]{:S(2)}, u32[]{:S(2)}) collective-permute-start(f32[64,128]{1,0:T(8,128)S(1)} %slice_bitcast_fusion.5), channel_id=1, source_target_pairs={{0,2},{1,3},{2,0},{3,1},{4,6},{5,7},{6,4},{7,5},{8,10},{9,11},{10,... | collective-permute-start | bytes 98312 | tf_op jit(solution)/shard_map/ppermute | solution.py:28
  32.4 1.8 %collective-permute-done.13 = bf16[32,576]{1,0:T(8,128)(2,1)S(1)} collective-permute-done((bf16[32,576]{1,0:T(8,128)(2,1)S(1)}, bf16[32,576]{1,0:T(8,128)(2,1)S(1)}, u32[]{:S(2)}, u32[]{:S(2)}) %collective-permute-start.13) | collective-permute-done | bytes 36896 | tf_op jit(solution)/shard_map/ppermute | solution.py:24
  35.2 1.7 %shard_map.62 = (f32[32,1408]{1,0:T(8,128)S(1)}, bf16[32,1664]{1,0:T(8,128)(2,1)S(1)}) custom-call(bf16[2,512,128]{2,1,0:T(8,128)(2,1)S(1)} %pad_maximum_fusion.part_0, bf16[2,512,128]{2,1,0:T(8,128)(2,1)S(1)} %collective-permute-done.8.part_1, bf16[2,512,128]{2,1,0:T(8,128)(2,1)S(1)} %collective-permute-done.10.part_2, ...), custom_call_target="tpu_custom_call" | custom-call | tf_op jit(solution)/shard_map/pallas_call | solution.py:363
  36.9 1.5 %collective-permute-start.16 = (bf16[32,1664]{1,0:T(8,128)(2,1)S(1)}, bf16[32,1664]{1,0:T(8,128)(2,1)S(1)}, u32[]{:S(2)}, u32[]{:S(2)}) collective-permute-start(bf16[32,1664]{1,0:T(8,128)(2,1)S(1)} %get-tuple-element.43), channel_id=1, source_target_pairs={{0,4},{1,5},{2,6},{3,7},{4,0},{5,1},{6,2},{7,3},{8,12},{9,13},{10,... | collective-permute-start | bytes 319496 | tf_op jit(solution)/shard_map/ppermute | solution.py:28
  39.0 2.7 %collective-permute-done.16 = bf16[32,1664]{1,0:T(8,128)(2,1)S(1)} collective-permute-done((bf16[32,1664]{1,0:T(8,128)(2,1)S(1)}, bf16[32,1664]{1,0:T(8,128)(2,1)S(1)}, u32[]{:S(2)}, u32[]{:S(2)}) %collective-permute-start.16) | collective-permute-done | bytes 106528 | tf_op jit(solution)/shard_map/ppermute | solution.py:28
  41.8 1.8 %collective-permute-start.17 = (bf16[32,1664]{1,0:T(8,128)(2,1)S(1)}, bf16[32,1664]{1,0:T(8,128)(2,1)S(1)}, u32[]{:S(2)}, u32[]{:S(2)}) collective-permute-start(bf16[32,1664]{1,0:T(8,128)(2,1)S(1)} %pad_maximum_fusion.4), channel_id=1, source_target_pairs={{0,8},{1,9},{2,10},{3,11},{4,12},{5,13},{6,14},{7,15},{8,0},{9,1},... | collective-permute-start | bytes 319496 | tf_op jit(solution)/shard_map/ppermute | solution.py:28
  43.7 4.9 %collective-permute-done.17 = bf16[32,1664]{1,0:T(8,128)(2,1)S(1)} collective-permute-done((bf16[32,1664]{1,0:T(8,128)(2,1)S(1)}, bf16[32,1664]{1,0:T(8,128)(2,1)S(1)}, u32[]{:S(2)}, u32[]{:S(2)}) %collective-permute-start.17) | collective-permute-done | bytes 106528 | tf_op jit(solution)/shard_map/ppermute | solution.py:28
  48.7 1.3 %shard_map.63 = (f32[2,72,128]{2,1,0:T(8,128)S(1)}, f32[2,72,128]{2,1,0:T(8,128)S(1)}) custom-call(f32[32,1152]{1,0:T(8,128)S(1)} %slice_add_fusion.1.cross_t, f32[32,128]{1,0:T(8,128)S(1)} %slice.171.gram, f32[128,128]{1,0:T(8,128)S(1)} %broadcast_multiply_fusion.g_inv, bf16[2,9,144,128]{3,2,1,0:T(8,128)(2,1)S(1)} %get-tuple-element.76.k_a, ...), custom_call_target="tpu_custom_call" | custom-call | tf_op jit(solution)/shard_map/pallas_call | solution.py:388
  50.2 1.9 %collective-permute-start.18 = (f32[2,72,128]{2,1,0:T(8,128)S(1)}, f32[2,72,128]{2,1,0:T(8,128)S(1)}, u32[]{:S(2)}, u32[]{:S(2)}) collective-permute-start(f32[2,72,128]{2,1,0:T(8,128)S(1)} %get-tuple-element.50), channel_id=1, source_target_pairs={{0,2},{1,3},{2,0},{3,1},{4,6},{5,7},{6,4},{7,5},{8,10},{9,11},{10,... | collective-permute-start | bytes 221192 | tf_op jit(solution)/shard_map/ppermute | solution.py:28
  52.1 1.9 %collective-permute-done.20 = f32[32,256]{1,0:T(8,128)S(1)} collective-permute-done((f32[32,256]{1,0:T(8,128)S(1)}, f32[32,256]{1,0:T(8,128)S(1)}, u32[]{:S(2)}, u32[]{:S(2)}) %collective-permute-start.20) | collective-permute-done | bytes 32800 | tf_op jit(solution)/shard_map/ppermute | solution.py:28
  (91 shorter events, 8.7 us)
Async XLA Ops:
  2.9 1.8 %collective-permute-start = (f32[2,10,32,128]{3,2,1,0:T(8,128)S(1)}, f32[2,10,32,128]{3,2,1,0:T(8,128)S(1)}, u32[]{:S(2)}, u32[]{:S(2)}) collective-permute-start(f32[2,10,32,128]{3,2,1,0:T(8,128)S(1)} %get-tuple-element.28), channel_id=1, source_target_pairs={{0,1},{1,0},{2,3},{3,2},{4,5},{5,4},{6,7},{7,6},{8,9},{9,8},{10,11... | collective-permute-start | bytes 983048 | tf_op jit(solution)/shard_map/ppermute | solution.py:28
  4.6 3.1 %copy-start = (bf16[1,2,16,16,128]{4,3,2,1,0:T(8,128)(2,1)S(1)}, bf16[1,2,16,16,128]{4,3,2,1,0:T(8,128)(2,1)}, u32[]{:S(2)}) copy-start(bf16[1,2,16,16,128]{4,3,2,1,0:T(8,128)(2,1)} %param.5) | copy-start | bytes 393220
  4.8 5.7 %collective-permute-start.2 = (f16[10,32,128]{2,1,0:T(8,128)(2,1)S(1)}, f16[10,32,128]{2,1,0:T(8,128)(2,1)S(1)}, u32[]{:S(2)}, u32[]{:S(2)}) collective-permute-start(f16[10,32,128]{2,1,0:T(8,128)(2,1)S(1)} %pad_maximum_fusion.5), channel_id=1, source_target_pairs={{0,2},{1,3},{2,0},{3,1},{4,6},{5,7},{6,4},{7,5},{8,10},{9,11},{10,... | collective-permute-start | bytes 245768 | tf_op jit(solution)/shard_map/ppermute | solution.py:28
  10.6 5.7 %collective-permute-start.3 = (f16[10,32,128]{2,1,0:T(8,128)(2,1)S(1)}, f16[10,32,128]{2,1,0:T(8,128)(2,1)S(1)}, u32[]{:S(2)}, u32[]{:S(2)}) collective-permute-start(f16[10,32,128]{2,1,0:T(8,128)(2,1)S(1)} %pad_maximum_fusion.6), channel_id=1, source_target_pairs={{0,4},{1,5},{2,6},{3,7},{4,0},{5,1},{6,2},{7,3},{8,12},{9,13},{10,... | collective-permute-start | bytes 245768 | tf_op jit(solution)/shard_map/ppermute | solution.py:28
  12.5 6.7 %collective-permute-start.5 = (f16[10,72,128]{2,1,0:T(8,128)(2,1)S(1)}, f16[10,72,128]{2,1,0:T(8,128)(2,1)S(1)}, u32[]{:S(2)}, u32[]{:S(2)}) collective-permute-start(f16[10,72,128]{2,1,0:T(8,128)(2,1)S(1)} %convert_element_type.38), channel_id=1, source_target_pairs={{0,2},{1,3},{2,0},{3,1},{4,6},{5,7},{6,4},{7,5},{8,10},{9,11},{10,... | collective-permute-start | bytes 552968 | tf_op jit(solution)/shard_map/ppermute | solution.py:28
  14.1 7.0 %collective-permute-start.7 = (f16[10,72,128]{2,1,0:T(8,128)(2,1)S(1)}, f16[10,72,128]{2,1,0:T(8,128)(2,1)S(1)}, u32[]{:S(2)}, u32[]{:S(2)}) collective-permute-start(f16[10,72,128]{2,1,0:T(8,128)(2,1)S(1)} %convert_element_type.38), channel_id=1, source_target_pairs={{0,3},{1,2},{2,1},{3,0},{4,7},{5,6},{6,5},{7,4},{8,11},{9,10},{10,... | collective-permute-start | bytes 552968 | tf_op jit(solution)/shard_map/ppermute | solution.py:28
  14.1 7.2 %collective-permute-start.6 = (f16[10,72,128]{2,1,0:T(8,128)(2,1)S(1)}, f16[10,72,128]{2,1,0:T(8,128)(2,1)S(1)}, u32[]{:S(2)}, u32[]{:S(2)}) collective-permute-start(f16[10,72,128]{2,1,0:T(8,128)(2,1)S(1)} %convert_element_type.38), channel_id=1, source_target_pairs={{0,1},{1,0},{2,3},{3,2},{4,5},{5,4},{6,7},{7,6},{8,9},{9,8},{10,11... | collective-permute-start | bytes 552968 | tf_op jit(solution)/shard_map/ppermute | solution.py:28
  14.7 9.2 %collective-permute-start.1 = (bf16[2,512,128]{2,1,0:T(8,128)(2,1)S(1)}, bf16[2,512,128]{2,1,0:T(8,128)(2,1)S(1)}, u32[]{:S(2)}, u32[]{:S(2)}) collective-permute-start(bf16[2,512,128]{2,1,0:T(8,128)(2,1)S(1)} %pad_maximum_fusion.1), channel_id=1, source_target_pairs={{16,0},{17,1},{18,2},{19,3},{20,4},{21,5},{22,6},{23,7},{24,8},{25... | collective-permute-start | bytes 786440 | tf_op jit(solution)/shard_map/ppermute | solution.py:24
  16.4 6.7 %collective-permute-start.4 = (f16[10,32,128]{2,1,0:T(8,128)(2,1)S(1)}, f16[10,32,128]{2,1,0:T(8,128)(2,1)S(1)}, u32[]{:S(2)}, u32[]{:S(2)}) collective-permute-start(f16[10,32,128]{2,1,0:T(8,128)(2,1)S(1)} %pad_maximum_fusion.7), channel_id=1, source_target_pairs={{0,8},{1,9},{2,10},{3,11},{4,12},{5,13},{6,14},{7,15},{8,0},{9,1},... | collective-permute-start | bytes 245768 | tf_op jit(solution)/shard_map/ppermute | solution.py:28
  23.9 3.8 %collective-permute-start.9 = (bf16[32,288]{1,0:T(8,128)(2,1)S(1)}, bf16[32,288]{1,0:T(8,128)(2,1)S(1)}, u32[]{:S(2)}, u32[]{:S(2)}) collective-permute-start(bf16[32,288]{1,0:T(8,128)(2,1)S(1)} %get-tuple-element.36), channel_id=1, source_target_pairs={{0,4},{1,5},{2,6},{3,7},{4,0},{5,1},{6,2},{7,3},{8,12},{9,13},{10,... | collective-permute-start | bytes 55304 | tf_op jit(solution)/shard_map/ppermute | solution.py:28
  24.2 8.1 %collective-permute-start.8 = (bf16[2,512,128]{2,1,0:T(8,128)(2,1)S(1)}, bf16[2,512,128]{2,1,0:T(8,128)(2,1)S(1)}, u32[]{:S(2)}, u32[]{:S(2)}) collective-permute-start(bf16[2,512,128]{2,1,0:T(8,128)(2,1)S(1)} %pad_maximum_fusion.part_0), channel_id=1, source_target_pairs={{0,2},{1,3},{2,0},{3,1},{4,6},{5,7},{6,4},{7,5},{8,10},{9,11},{10,... | collective-permute-start | bytes 786440 | tf_op jit(solution)/shard_map/ppermute | solution.py:28
  25.8 9.4 %collective-permute-start.10 = (bf16[2,512,128]{2,1,0:T(8,128)(2,1)S(1)}, bf16[2,512,128]{2,1,0:T(8,128)(2,1)S(1)}, u32[]{:S(2)}, u32[]{:S(2)}) collective-permute-start(bf16[2,512,128]{2,1,0:T(8,128)(2,1)S(1)} %pad_maximum_fusion.part_0), channel_id=1, source_target_pairs={{0,1},{1,0},{2,3},{3,2},{4,5},{5,4},{6,7},{7,6},{8,9},{9,8},{10,11... | collective-permute-start | bytes 786440 | tf_op jit(solution)/shard_map/ppermute | solution.py:28
  25.8 5.4 %collective-permute-start.14 = (f32[2,64,128]{2,1,0:T(8,128)S(1)}, f32[2,64,128]{2,1,0:T(8,128)S(1)}, u32[]{:S(2)}, u32[]{:S(2)}) collective-permute-start(f32[2,64,128]{2,1,0:T(8,128)S(1)} %get-tuple-element.40), channel_id=1, source_target_pairs={{0,1},{1,0},{2,3},{3,2},{4,5},{5,4},{6,7},{7,6},{8,9},{9,8},{10,11... | collective-permute-start | bytes 196616 | tf_op jit(solution)/shard_map/ppermute | solution.py:28
  27.8 6.4 %collective-permute-start.13 = (bf16[32,576]{1,0:T(8,128)(2,1)S(1)}, bf16[32,576]{1,0:T(8,128)(2,1)S(1)}, u32[]{:S(2)}, u32[]{:S(2)}) collective-permute-start(bf16[32,576]{1,0:T(8,128)(2,1)S(1)} %maximum_select_fusion.1), channel_id=1, source_target_pairs={{24,0},{25,1},{26,2},{27,3},{28,4},{29,5},{30,6},{31,7},{16,8},{17... | collective-permute-start | bytes 110600 | tf_op jit(solution)/shard_map/ppermute | solution.py:24
  30.2 4.3 %collective-permute-start.12 = (bf16[32,576]{1,0:T(8,128)(2,1)S(1)}, bf16[32,576]{1,0:T(8,128)(2,1)S(1)}, u32[]{:S(2)}, u32[]{:S(2)}) collective-permute-start(bf16[32,576]{1,0:T(8,128)(2,1)S(1)} %maximum_select_fusion.1), channel_id=1, source_target_pairs={{16,0},{17,1},{18,2},{19,3},{20,4},{21,5},{22,6},{23,7},{24,8},{25... | collective-permute-start | bytes 110600 | tf_op jit(solution)/shard_map/ppermute | solution.py:24
  31.2 4.0 %collective-permute-start.15 = (f32[64,128]{1,0:T(8,128)S(1)}, f32[64,128]{1,0:T(8,128)S(1)}, u32[]{:S(2)}, u32[]{:S(2)}) collective-permute-start(f32[64,128]{1,0:T(8,128)S(1)} %slice_bitcast_fusion.5), channel_id=1, source_target_pairs={{0,2},{1,3},{2,0},{3,1},{4,6},{5,7},{6,4},{7,5},{8,10},{9,11},{10,... | collective-permute-start | bytes 98312 | tf_op jit(solution)/shard_map/ppermute | solution.py:28
  32.4 2.9 %collective-permute-start.11 = (bf16[2,512,128]{2,1,0:T(8,128)(2,1)S(1)}, bf16[2,512,128]{2,1,0:T(8,128)(2,1)S(1)}, u32[]{:S(2)}, u32[]{:S(2)}) collective-permute-start(bf16[2,512,128]{2,1,0:T(8,128)(2,1)S(1)} %collective-permute-done.8.part_1), channel_id=1, source_target_pairs={{0,1},{1,0},{2,3},{3,2},{4,5},{5,4},{6,7},{7,6},{8,9},{9,8},{10,11... | collective-permute-start | bytes 786440 | tf_op jit(solution)/shard_map/ppermute | solution.py:28
  34.6 3.8 %copy-start.2 = (f32[1,128,128]{2,1,0:T(8,128)S(1)}, f32[1,128,128]{2,1,0:T(8,128)}, u32[]{:S(2)}) copy-start(f32[1,128,128]{2,1,0:T(8,128)} %param.7) | copy-start | bytes 196612
  36.9 4.8 %collective-permute-start.16 = (bf16[32,1664]{1,0:T(8,128)(2,1)S(1)}, bf16[32,1664]{1,0:T(8,128)(2,1)S(1)}, u32[]{:S(2)}, u32[]{:S(2)}) collective-permute-start(bf16[32,1664]{1,0:T(8,128)(2,1)S(1)} %get-tuple-element.43), channel_id=1, source_target_pairs={{0,4},{1,5},{2,6},{3,7},{4,0},{5,1},{6,2},{7,3},{8,12},{9,13},{10,... | collective-permute-start | bytes 319496 | tf_op jit(solution)/shard_map/ppermute | solution.py:28
  41.8 6.8 %collective-permute-start.17 = (bf16[32,1664]{1,0:T(8,128)(2,1)S(1)}, bf16[32,1664]{1,0:T(8,128)(2,1)S(1)}, u32[]{:S(2)}, u32[]{:S(2)}) collective-permute-start(bf16[32,1664]{1,0:T(8,128)(2,1)S(1)} %pad_maximum_fusion.4), channel_id=1, source_target_pairs={{0,8},{1,9},{2,10},{3,11},{4,12},{5,13},{6,14},{7,15},{8,0},{9,1},... | collective-permute-start | bytes 319496 | tf_op jit(solution)/shard_map/ppermute | solution.py:28
  50.0 4.0 %collective-permute-start.20 = (f32[32,256]{1,0:T(8,128)S(1)}, f32[32,256]{1,0:T(8,128)S(1)}, u32[]{:S(2)}, u32[]{:S(2)}) collective-permute-start(f32[32,256]{1,0:T(8,128)S(1)} %get-tuple-element.73), channel_id=1, source_target_pairs={{0,2},{1,3},{2,0},{3,1},{4,6},{5,7},{6,4},{7,5},{8,10},{9,11},{10,... | collective-permute-start | bytes 98312 | tf_op jit(solution)/shard_map/ppermute | solution.py:28
  50.2 4.6 %collective-permute-start.18 = (f32[2,72,128]{2,1,0:T(8,128)S(1)}, f32[2,72,128]{2,1,0:T(8,128)S(1)}, u32[]{:S(2)}, u32[]{:S(2)}) collective-permute-start(f32[2,72,128]{2,1,0:T(8,128)S(1)} %get-tuple-element.50), channel_id=1, source_target_pairs={{0,2},{1,3},{2,0},{3,1},{4,6},{5,7},{6,4},{7,5},{8,10},{9,11},{10,... | collective-permute-start | bytes 221192 | tf_op jit(solution)/shard_map/ppermute | solution.py:28
  54.0 1.3 %collective-permute-start.21 = (f32[2,32,256]{2,1,0:T(8,128)S(1)}, f32[2,32,256]{2,1,0:T(8,128)S(1)}, u32[]{:S(2)}, u32[]{:S(2)}) collective-permute-start(f32[2,32,256]{2,1,0:T(8,128)S(1)} %get-tuple-element.71), channel_id=1, source_target_pairs={{0,1},{1,0},{2,3},{3,2},{4,5},{5,4},{6,7},{7,6},{8,9},{9,8},{10,11... | collective-permute-start | bytes 196616 | tf_op jit(solution)/shard_map/ppermute | solution.py:28
  54.8 1.4 %collective-permute-start.19 = (f32[72,128]{1,0:T(8,128)S(1)}, f32[72,128]{1,0:T(8,128)S(1)}, u32[]{:S(2)}, u32[]{:S(2)}) collective-permute-start(f32[72,128]{1,0:T(8,128)S(1)} %slice_bitcast_fusion.3), channel_id=1, source_target_pairs={{0,1},{1,0},{2,3},{3,2},{4,5},{5,4},{6,7},{7,6},{8,9},{9,8},{10,11... | collective-permute-start | bytes 110600 | tf_op jit(solution)/shard_map/ppermute | solution.py:28
  (1 other events, 3.1 us)

commit v15 on v14

--- a/solution.py
+++ b/solution.py
@@ -211,16 +211,35 @@
     precond_t[...] = total.astype(BF16)
 
 
-def update_kernel(cross_t, gram, g_inv, k_a, k_b, main, keep, send):
+def update_kernel(cross_t, gram, g_inv, k_a, k_b, main, keep, send_x, send_core, send_diagonal):
     rows = k_a.shape[2] // 2
-    mixed = jnp.dot(gram[...], g_inv[...], precision=HIGH)
+    width = main.shape[2]
+    mixed = jnp.dot(gram[:, width:], g_inv[...], precision=HIGH)
     mixed = jnp.concatenate([mixed, mixed], axis=0)
     parts = two_parts(cross_t[...])
-    for i, k in enumerate((k_a, k_b)):
+    quarter = gram.shape[0]
+    for i, (k, targets) in enumerate(((k_a, (keep, send_x)), (k_b, (send_core, send_diagonal)))):
         product = dot_nt(taps_to_lanes(k.at[0]), parts) + dot_nt(taps_to_lanes(k.at[1]), parts)
         result = main[i] - jnp.dot(product, mixed, precision=HIGH)
-        keep[i] = result[:rows]
-        send[i] = result[rows:]
+        targets[0][:rows] = result[:rows]
+        targets[1][:rows] = result[rows:]
+    for target in (keep, send_x, send_core, send_diagonal):
+        target[rows : rows + quarter] = gram[:, :width]
+        target[rows + quarter :] = gram[:, width:]
+
+
+def finish_kernel(scale, mine, from_x, from_core, from_diagonal, update, grams, scratch):
+    core, xbit = place_bits()
+    first = 2 * core + xbit
+    rows, width = update.shape
+    quarter = width // 4
+    update[...] = (mine[:rows] + from_x[:rows]) + (from_core[:rows] + from_diagonal[:rows])
+    for j, source in enumerate((mine, from_x, from_core, from_diagonal)):
+        place = pl.ds(pl.multiple_of((first ^ j) * quarter, quarter), quarter)
+        for i in range(2):
+            scratch[i, place, :] = source[rows + i * quarter : rows + (i + 1) * quarter] * scale
+    grams[0] = scratch[0]
+    grams[1] = scratch[1].T
 
 
 def gram_kernel(grads, next_grads, keep, send, scratch):
@@ -385,22 +404,23 @@
         gram = high + rest
         cross_half = jnp.concatenate([cross_t, high, rest], axis=1).astype(BF16)
 
-    out, send = pl.pallas_call(
+    parcels = pl.pallas_call(
         update_kernel,
-        out_shape=[jax.ShapeDtypeStruct((2, rows, width), F32)] * 2,
+        out_shape=[jax.ShapeDtypeStruct((rows + 2 * quarter, width), F32)] * 4,
         in_specs=[VMEM] * 6,
+        out_specs=[VMEM] * 4,
+        compiler_params=PARAMS,
+    )(cross_t, gram, g_scaled, k_a, k_b, main)
+    parcels = [parcels[0]] + [swap(parcels[j], bits) for j, bits in ((1, 2), (2, 1), (3, 3))]
+    update, grams = pl.pallas_call(
+        functools.partial(finish_kernel, scale),
+        out_shape=[jax.ShapeDtypeStruct((rows, width), F32), jax.ShapeDtypeStruct((2, width, width), F32)],
+        in_specs=[VMEM] * 4,
         out_specs=[VMEM] * 2,
-        compiler_params=PARAMS,
-    )(cross_t, gram[:, width:], g_scaled, k_a, k_b, main)
-    gram = behind(gram, out) * scale
-    gram = jnp.stack([gram, swap(gram, 2)])
-    out = out + swap(send, 2)
-    gram = jnp.stack([gram, swap(gram, 1)])
-    update = out[0] + swap(out[1], 1)
-    gram = jnp.where(xbit == 0, gram, gram[:, ::-1])
-    gram = jnp.where(core == 0, gram, gram[::-1])
-    gram = gram.reshape(width, 2, width).transpose(1, 2, 0)
-    return (update[None], gram[None])
+        scratch_shapes=[pltpu.VMEM((2, width, width), F32)],
+        compiler_params=PARAMS,
+    )(*parcels)
+    return (update[None], grams[None])
 
 
 def solution(mesh):

time: 57 us -> 56 us (0.982)
  local copies, waits for them, and re-layouts: 0.88 us -> 0.04 us
  Pallas kernels: 6.2 us -> 6.97 us
  other arithmetic: 1.95 us -> 1.26 us
    reshape x2 -> x0, local copies, waits for them, and re-layouts: 0.83 us -> none  [per_device(): gram = gram.reshape(width, 2, width).transpose(1, 2, 0)]
    pallas_call x1 -> x2, Pallas kernels: 1.28 us -> 2.05 us  [the longest x1 1.28 us: per_device(): pl.pallas_call(update_kernel, out_shape=[jax.ShapeDtypeStruct((rows + 2 *...]
    broadcast_in_dim x1 -> x0, other arithmetic: 0.62 us -> none  [per_device(): return (update[None], gram[None])]
    ppermute x19 -> x18, waiting for transfers between devices: 20.2 us -> 19.9 us  [swap(): lax.ppermute(block, 'pos', [(i, i ^ bit) for i in range(lax.axis_size('po...]
    ppermute x19 -> x18, starting transfers between devices: 18.9 us -> 18.9 us  [swap(): lax.ppermute(block, 'pos', [(i, i ^ bit) for i in range(lax.axis_size('po...]
  transfers between devices with their start and end apart: 22 -> 21, of which waited for: 14 -> 12; matrix products, arithmetic and copies ran while one was open for 4% -> 3% of each run, Pallas kernels for 2% -> 2%
where the time goes in v15:
time: 56 us; the launch traced here: 55.7 us
  starting transfers between devices  23.8 us (42%)
  waiting for transfers between devices  22 us (39%)
  Pallas kernels  6.97 us (12%)
  other arithmetic  1.26 us (2%)
  between operations  0.99 us (2%)
  matrix products  0.56 us (1%)
    ppermute x18, waiting for transfers between devices, swap(): lax.ppermute(block, 'pos', [(i, i ^ bit) for i in range(lax.axis_size('po...  19.9 us
    ppermute x18, starting transfers between devices, swap(): lax.ppermute(block, 'pos', [(i, i ^ bit) for i in range(lax.axis_size('po...  18.9 us
    ppermute x3, starting transfers between devices, after(): return lax.ppermute(block, ('layer', 'pos'), route)  4.93 us
    pallas_call x1, Pallas kernels, per_device(): pl.pallas_call(functools.partial(grad_kernel, side), out_shape=[jax.Shape...  2.21 us
    ppermute x3, waiting for transfers between devices, after(): return lax.ppermute(block, ('layer', 'pos'), route)  2.1 us
    pallas_call x1, Pallas kernels, per_device(): pl.pallas_call(functools.partial(cross_kernel, side), out_shape=[jax.Shap...  1.69 us
    pallas_call x1, Pallas kernels, per_device(): pl.pallas_call(update_kernel, out_shape=[jax.ShapeDtypeStruct((rows + 2 *...  1.28 us
  transfers between devices with their start and end apart: 21, of which 12 were waited for; matrix products, arithmetic and copies ran while one was open for 3% of the time, Pallas kernels for 2%

profile of v15, /device:TPU:0, one launch (start us, length us, event | category | flops | bytes accessed | tf_op | source)
XLA Modules:
  0.0 55.7 jit_solution(9724903447604821855)
XLA Ops:
  0.6 2.2 %shard_map.59 = (f32[2,10,32,128]{3,2,1,0:T(8,128)S(1)}, f32[2,10,32,128]{3,2,1,0:T(8,128)S(1)}, bf16[2,9,72,128]{3,2,1,0:T(8,128)(2,1)S(1)}, f32[10,72,128]{2,1,0:T(8,128)S(1)}) custom-call(bf16[512,128]{1,0:T(8,128)(2,1)} %bitcast.77, bf16[512,128]{1,0:T(8,128)(2,1)} %bitcast.74, f32[128,128]{1,0:T(8,128)} %bitcast.81, f32[72,1152]{1,0:T(8,128)} %bitcast.80), custom_call_target="tpu_custom_call" | custom-call | tf_op jit(solution)/shard_map/pallas_call | solution.py:285
  3.4 1.3 %collective-permute-done = f32[2,10,32,128]{3,2,1,0:T(8,128)S(1)} collective-permute-done((f32[2,10,32,128]{3,2,1,0:T(8,128)S(1)}, f32[2,10,32,128]{3,2,1,0:T(8,128)S(1)}, u32[]{:S(2)}, u32[]{:S(2)}) %collective-permute-start) | collective-permute-done | bytes 327712 | tf_op jit(solution)/shard_map/ppermute | solution.py:28
  4.8 2.9 %collective-permute-start.2 = (f16[10,32,128]{2,1,0:T(8,128)(2,1)S(1)}, f16[10,32,128]{2,1,0:T(8,128)(2,1)S(1)}, u32[]{:S(2)}, u32[]{:S(2)}) collective-permute-start(f16[10,32,128]{2,1,0:T(8,128)(2,1)S(1)} %pad_maximum_fusion.4), channel_id=1, source_target_pairs={{0,2},{1,3},{2,0},{3,1},{4,6},{5,7},{6,4},{7,5},{8,10},{9,11},{10,... | collective-permute-start | bytes 245768 | tf_op jit(solution)/shard_map/ppermute | solution.py:28
  7.7 2.7 %collective-permute-done.2 = f16[10,32,128]{2,1,0:T(8,128)(2,1)S(1)} collective-permute-done((f16[10,32,128]{2,1,0:T(8,128)(2,1)S(1)}, f16[10,32,128]{2,1,0:T(8,128)(2,1)S(1)}, u32[]{:S(2)}, u32[]{:S(2)}) %collective-permute-start.2) | collective-permute-done | bytes 81952 | tf_op jit(solution)/shard_map/ppermute | solution.py:28
  10.6 1.9 %collective-permute-start.3 = (f16[10,32,128]{2,1,0:T(8,128)(2,1)S(1)}, f16[10,32,128]{2,1,0:T(8,128)(2,1)S(1)}, u32[]{:S(2)}, u32[]{:S(2)}) collective-permute-start(f16[10,32,128]{2,1,0:T(8,128)(2,1)S(1)} %pad_maximum_fusion.5), channel_id=1, source_target_pairs={{0,4},{1,5},{2,6},{3,7},{4,0},{5,1},{6,2},{7,3},{8,12},{9,13},{10,... | collective-permute-start | bytes 245768 | tf_op jit(solution)/shard_map/ppermute | solution.py:28
  12.5 1.6 %collective-permute-start.5 = (f16[10,72,128]{2,1,0:T(8,128)(2,1)S(1)}, f16[10,72,128]{2,1,0:T(8,128)(2,1)S(1)}, u32[]{:S(2)}, u32[]{:S(2)}) collective-permute-start(f16[10,72,128]{2,1,0:T(8,128)(2,1)S(1)} %convert_element_type.38), channel_id=1, source_target_pairs={{0,2},{1,3},{2,0},{3,1},{4,6},{5,7},{6,4},{7,5},{8,10},{9,11},{10,... | collective-permute-start | bytes 552968 | tf_op jit(solution)/shard_map/ppermute | solution.py:28
  14.7 1.5 %collective-permute-start.1 = (bf16[2,512,128]{2,1,0:T(8,128)(2,1)S(1)}, bf16[2,512,128]{2,1,0:T(8,128)(2,1)S(1)}, u32[]{:S(2)}, u32[]{:S(2)}) collective-permute-start(bf16[2,512,128]{2,1,0:T(8,128)(2,1)S(1)} %pad_maximum_fusion.1), channel_id=1, source_target_pairs={{16,0},{17,1},{18,2},{19,3},{20,4},{21,5},{22,6},{23,7},{24,8},{25... | collective-permute-start | bytes 786440 | tf_op jit(solution)/shard_map/ppermute | solution.py:24
  16.4 2.7 %collective-permute-start.4 = (f16[10,32,128]{2,1,0:T(8,128)(2,1)S(1)}, f16[10,32,128]{2,1,0:T(8,128)(2,1)S(1)}, u32[]{:S(2)}, u32[]{:S(2)}) collective-permute-start(f16[10,32,128]{2,1,0:T(8,128)(2,1)S(1)} %pad_maximum_fusion.6), channel_id=1, source_target_pairs={{0,8},{1,9},{2,10},{3,11},{4,12},{5,13},{6,14},{7,15},{8,0},{9,1},... | collective-permute-start | bytes 245768 | tf_op jit(solution)/shard_map/ppermute | solution.py:28
  19.4 1.7 %collective-permute-done.7 = f16[10,72,128]{2,1,0:T(8,128)(2,1)S(1)} collective-permute-done((f16[10,72,128]{2,1,0:T(8,128)(2,1)S(1)}, f16[10,72,128]{2,1,0:T(8,128)(2,1)S(1)}, u32[]{:S(2)}, u32[]{:S(2)}) %collective-permute-start.7) | collective-permute-done | bytes 184352 | tf_op jit(solution)/shard_map/ppermute | solution.py:28
  21.5 1.6 %collective-permute-done.4 = f16[10,32,128]{2,1,0:T(8,128)(2,1)S(1)} collective-permute-done((f16[10,32,128]{2,1,0:T(8,128)(2,1)S(1)}, f16[10,32,128]{2,1,0:T(8,128)(2,1)S(1)}, u32[]{:S(2)}, u32[]{:S(2)}) %collective-permute-start.4) | collective-permute-done | bytes 81952 | tf_op jit(solution)/shard_map/ppermute | solution.py:28
  24.2 1.6 %collective-permute-start.8 = (bf16[2,512,128]{2,1,0:T(8,128)(2,1)S(1)}, bf16[2,512,128]{2,1,0:T(8,128)(2,1)S(1)}, u32[]{:S(2)}, u32[]{:S(2)}) collective-permute-start(bf16[2,512,128]{2,1,0:T(8,128)(2,1)S(1)} %pad_maximum_fusion.part_0), channel_id=1, source_target_pairs={{0,2},{1,3},{2,0},{3,1},{4,6},{5,7},{6,4},{7,5},{8,10},{9,11},{10,... | collective-permute-start | bytes 786440 | tf_op jit(solution)/shard_map/ppermute | solution.py:28
  26.3 1.4 %collective-permute-done.9 = bf16[32,288]{1,0:T(8,128)(2,1)S(1)} collective-permute-done((bf16[32,288]{1,0:T(8,128)(2,1)S(1)}, bf16[32,288]{1,0:T(8,128)(2,1)S(1)}, u32[]{:S(2)}, u32[]{:S(2)}) %collective-permute-start.9) | collective-permute-done | bytes 18464 | tf_op jit(solution)/shard_map/ppermute | solution.py:28
  27.8 2.4 %collective-permute-start.13 = (bf16[32,576]{1,0:T(8,128)(2,1)S(1)}, bf16[32,576]{1,0:T(8,128)(2,1)S(1)}, u32[]{:S(2)}, u32[]{:S(2)}) collective-permute-start(bf16[32,576]{1,0:T(8,128)(2,1)S(1)} %maximum_select_fusion.1), channel_id=1, source_target_pairs={{24,0},{25,1},{26,2},{27,3},{28,4},{29,5},{30,6},{31,7},{16,8},{17... | collective-permute-start | bytes 110600 | tf_op jit(solution)/shard_map/ppermute | solution.py:24
  30.2 1.0 %collective-permute-start.12 = (bf16[32,576]{1,0:T(8,128)(2,1)S(1)}, bf16[32,576]{1,0:T(8,128)(2,1)S(1)}, u32[]{:S(2)}, u32[]{:S(2)}) collective-permute-start(bf16[32,576]{1,0:T(8,128)(2,1)S(1)} %maximum_select_fusion.1), channel_id=1, source_target_pairs={{16,0},{17,1},{18,2},{19,3},{20,4},{21,5},{22,6},{23,7},{24,8},{25... | collective-permute-start | bytes 110600 | tf_op jit(solution)/shard_map/ppermute | solution.py:24
  31.2 1.1 %collective-permute-start.15 = (f32[64,128]{1,0:T(8,128)S(1)}, f32[64,128]{1,0:T(8,128)S(1)}, u32[]{:S(2)}, u32[]{:S(2)}) collective-permute-start(f32[64,128]{1,0:T(8,128)S(1)} %slice_bitcast_fusion.3), channel_id=1, source_target_pairs={{0,2},{1,3},{2,0},{3,1},{4,6},{5,7},{6,4},{7,5},{8,10},{9,11},{10,... | collective-permute-start | bytes 98312 | tf_op jit(solution)/shard_map/ppermute | solution.py:28
  32.4 1.8 %collective-permute-done.13 = bf16[32,576]{1,0:T(8,128)(2,1)S(1)} collective-permute-done((bf16[32,576]{1,0:T(8,128)(2,1)S(1)}, bf16[32,576]{1,0:T(8,128)(2,1)S(1)}, u32[]{:S(2)}, u32[]{:S(2)}) %collective-permute-start.13) | collective-permute-done | bytes 36896 | tf_op jit(solution)/shard_map/ppermute | solution.py:24
  35.2 1.7 %shard_map.62 = (f32[32,1408]{1,0:T(8,128)S(1)}, bf16[32,1664]{1,0:T(8,128)(2,1)S(1)}) custom-call(bf16[2,512,128]{2,1,0:T(8,128)(2,1)S(1)} %pad_maximum_fusion.part_0, bf16[2,512,128]{2,1,0:T(8,128)(2,1)S(1)} %collective-permute-done.8.part_1, bf16[2,512,128]{2,1,0:T(8,128)(2,1)S(1)} %collective-permute-done.10.part_2, ...), custom_call_target="tpu_custom_call" | custom-call | tf_op jit(solution)/shard_map/pallas_call | solution.py:382
  36.9 1.5 %collective-permute-start.16 = (bf16[32,1664]{1,0:T(8,128)(2,1)S(1)}, bf16[32,1664]{1,0:T(8,128)(2,1)S(1)}, u32[]{:S(2)}, u32[]{:S(2)}) collective-permute-start(bf16[32,1664]{1,0:T(8,128)(2,1)S(1)} %get-tuple-element.46), channel_id=1, source_target_pairs={{0,4},{1,5},{2,6},{3,7},{4,0},{5,1},{6,2},{7,3},{8,12},{9,13},{10,... | collective-permute-start | bytes 319496 | tf_op jit(solution)/shard_map/ppermute | solution.py:28
  39.0 2.7 %collective-permute-done.16 = bf16[32,1664]{1,0:T(8,128)(2,1)S(1)} collective-permute-done((bf16[32,1664]{1,0:T(8,128)(2,1)S(1)}, bf16[32,1664]{1,0:T(8,128)(2,1)S(1)}, u32[]{:S(2)}, u32[]{:S(2)}) %collective-permute-start.16) | collective-permute-done | bytes 106528 | tf_op jit(solution)/shard_map/ppermute | solution.py:28
  41.8 1.8 %collective-permute-start.17 = (bf16[32,1664]{1,0:T(8,128)(2,1)S(1)}, bf16[32,1664]{1,0:T(8,128)(2,1)S(1)}, u32[]{:S(2)}, u32[]{:S(2)}) collective-permute-start(bf16[32,1664]{1,0:T(8,128)(2,1)S(1)} %pad_maximum_fusion.3), channel_id=1, source_target_pairs={{0,8},{1,9},{2,10},{3,11},{4,12},{5,13},{6,14},{7,15},{8,0},{9,1},... | collective-permute-start | bytes 319496 | tf_op jit(solution)/shard_map/ppermute | solution.py:28
  43.7 4.9 %collective-permute-done.17 = bf16[32,1664]{1,0:T(8,128)(2,1)S(1)} collective-permute-done((bf16[32,1664]{1,0:T(8,128)(2,1)S(1)}, bf16[32,1664]{1,0:T(8,128)(2,1)S(1)}, u32[]{:S(2)}, u32[]{:S(2)}) %collective-permute-start.17) | collective-permute-done | bytes 106528 | tf_op jit(solution)/shard_map/ppermute | solution.py:28
  48.7 1.3 %shard_map.63 = (f32[136,128]{1,0:T(8,128)S(1)}, f32[136,128]{1,0:T(8,128)S(1)}, f32[136,128]{1,0:T(8,128)S(1)}, f32[136,128]{1,0:T(8,128)S(1)}) custom-call(f32[32,1152]{1,0:T(8,128)S(1)} %slice_add_fusion.1.cross_t, f32[32,256]{1,0:T(8,128)S(1)} %reduce-precision_add_fusion.gram, f32[128,128]{1,0:T(8,128)S(1)} %broadcast_multiply_fusion.g_inv, ...), custom_call_target="tpu_custom_call" | custom-call | tf_op jit(solution)/shard_map/pallas_call | solution.py:407
  50.2 2.0 %collective-permute-start.20 = (f32[136,128]{1,0:T(8,128)S(1)}, f32[136,128]{1,0:T(8,128)S(1)}, u32[]{:S(2)}, u32[]{:S(2)}) collective-permute-start(f32[136,128]{1,0:T(8,128)S(1)} %get-tuple-element.55), channel_id=1, source_target_pairs={{0,3},{1,2},{2,1},{3,0},{4,7},{5,6},{6,5},{7,4},{8,11},{9,10},{10,... | collective-permute-start | bytes 208904 | tf_op jit(solution)/shard_map/ppermute | solution.py:28
  52.2 2.7 %collective-permute-done.18.from_x = f32[136,128]{1,0:T(8,128)S(1)} collective-permute-done((f32[136,128]{1,0:T(8,128)S(1)}, f32[136,128]{1,0:T(8,128)S(1)}, u32[]{:S(2)}, u32[]{:S(2)}) %collective-permute-start.18) | collective-permute-done | bytes 69664 | tf_op jit(solution)/shard_map/ppermute | solution.py:28
  (79 shorter events, 6.7 us)
Async XLA Ops:
  2.9 1.8 %collective-permute-start = (f32[2,10,32,128]{3,2,1,0:T(8,128)S(1)}, f32[2,10,32,128]{3,2,1,0:T(8,128)S(1)}, u32[]{:S(2)}, u32[]{:S(2)}) collective-permute-start(f32[2,10,32,128]{3,2,1,0:T(8,128)S(1)} %get-tuple-element.31), channel_id=1, source_target_pairs={{0,1},{1,0},{2,3},{3,2},{4,5},{5,4},{6,7},{7,6},{8,9},{9,8},{10,11... | collective-permute-start | bytes 983048 | tf_op jit(solution)/shard_map/ppermute | solution.py:28
  4.6 3.1 %copy-start = (bf16[1,2,16,16,128]{4,3,2,1,0:T(8,128)(2,1)S(1)}, bf16[1,2,16,16,128]{4,3,2,1,0:T(8,128)(2,1)}, u32[]{:S(2)}) copy-start(bf16[1,2,16,16,128]{4,3,2,1,0:T(8,128)(2,1)} %param.5) | copy-start | bytes 393220
  4.6 3.1 %copy-start.1 = (bf16[1,2,16,16,128]{4,3,2,1,0:T(8,128)(2,1)S(1)}, bf16[1,2,16,16,128]{4,3,2,1,0:T(8,128)(2,1)}, u32[]{:S(2)}) copy-start(bf16[1,2,16,16,128]{4,3,2,1,0:T(8,128)(2,1)} %param.4) | copy-start | bytes 393220
  4.8 5.7 %collective-permute-start.2 = (f16[10,32,128]{2,1,0:T(8,128)(2,1)S(1)}, f16[10,32,128]{2,1,0:T(8,128)(2,1)S(1)}, u32[]{:S(2)}, u32[]{:S(2)}) collective-permute-start(f16[10,32,128]{2,1,0:T(8,128)(2,1)S(1)} %pad_maximum_fusion.4), channel_id=1, source_target_pairs={{0,2},{1,3},{2,0},{3,1},{4,6},{5,7},{6,4},{7,5},{8,10},{9,11},{10,... | collective-permute-start | bytes 245768 | tf_op jit(solution)/shard_map/ppermute | solution.py:28
  10.6 5.7 %collective-permute-start.3 = (f16[10,32,128]{2,1,0:T(8,128)(2,1)S(1)}, f16[10,32,128]{2,1,0:T(8,128)(2,1)S(1)}, u32[]{:S(2)}, u32[]{:S(2)}) collective-permute-start(f16[10,32,128]{2,1,0:T(8,128)(2,1)S(1)} %pad_maximum_fusion.5), channel_id=1, source_target_pairs={{0,4},{1,5},{2,6},{3,7},{4,0},{5,1},{6,2},{7,3},{8,12},{9,13},{10,... | collective-permute-start | bytes 245768 | tf_op jit(solution)/shard_map/ppermute | solution.py:28
  12.5 6.7 %collective-permute-start.5 = (f16[10,72,128]{2,1,0:T(8,128)(2,1)S(1)}, f16[10,72,128]{2,1,0:T(8,128)(2,1)S(1)}, u32[]{:S(2)}, u32[]{:S(2)}) collective-permute-start(f16[10,72,128]{2,1,0:T(8,128)(2,1)S(1)} %convert_element_type.38), channel_id=1, source_target_pairs={{0,2},{1,3},{2,0},{3,1},{4,6},{5,7},{6,4},{7,5},{8,10},{9,11},{10,... | collective-permute-start | bytes 552968 | tf_op jit(solution)/shard_map/ppermute | solution.py:28
  14.1 7.0 %collective-permute-start.7 = (f16[10,72,128]{2,1,0:T(8,128)(2,1)S(1)}, f16[10,72,128]{2,1,0:T(8,128)(2,1)S(1)}, u32[]{:S(2)}, u32[]{:S(2)}) collective-permute-start(f16[10,72,128]{2,1,0:T(8,128)(2,1)S(1)} %convert_element_type.38), channel_id=1, source_target_pairs={{0,3},{1,2},{2,1},{3,0},{4,7},{5,6},{6,5},{7,4},{8,11},{9,10},{10,... | collective-permute-start | bytes 552968 | tf_op jit(solution)/shard_map/ppermute | solution.py:28
  14.1 7.2 %collective-permute-start.6 = (f16[10,72,128]{2,1,0:T(8,128)(2,1)S(1)}, f16[10,72,128]{2,1,0:T(8,128)(2,1)S(1)}, u32[]{:S(2)}, u32[]{:S(2)}) collective-permute-start(f16[10,72,128]{2,1,0:T(8,128)(2,1)S(1)} %convert_element_type.38), channel_id=1, source_target_pairs={{0,1},{1,0},{2,3},{3,2},{4,5},{5,4},{6,7},{7,6},{8,9},{9,8},{10,11... | collective-permute-start | bytes 552968 | tf_op jit(solution)/shard_map/ppermute | solution.py:28
  14.7 9.2 %collective-permute-start.1 = (bf16[2,512,128]{2,1,0:T(8,128)(2,1)S(1)}, bf16[2,512,128]{2,1,0:T(8,128)(2,1)S(1)}, u32[]{:S(2)}, u32[]{:S(2)}) collective-permute-start(bf16[2,512,128]{2,1,0:T(8,128)(2,1)S(1)} %pad_maximum_fusion.1), channel_id=1, source_target_pairs={{16,0},{17,1},{18,2},{19,3},{20,4},{21,5},{22,6},{23,7},{24,8},{25... | collective-permute-start | bytes 786440 | tf_op jit(solution)/shard_map/ppermute | solution.py:24
  16.4 6.7 %collective-permute-start.4 = (f16[10,32,128]{2,1,0:T(8,128)(2,1)S(1)}, f16[10,32,128]{2,1,0:T(8,128)(2,1)S(1)}, u32[]{:S(2)}, u32[]{:S(2)}) collective-permute-start(f16[10,32,128]{2,1,0:T(8,128)(2,1)S(1)} %pad_maximum_fusion.6), channel_id=1, source_target_pairs={{0,8},{1,9},{2,10},{3,11},{4,12},{5,13},{6,14},{7,15},{8,0},{9,1},... | collective-permute-start | bytes 245768 | tf_op jit(solution)/shard_map/ppermute | solution.py:28
  23.9 3.8 %collective-permute-start.9 = (bf16[32,288]{1,0:T(8,128)(2,1)S(1)}, bf16[32,288]{1,0:T(8,128)(2,1)S(1)}, u32[]{:S(2)}, u32[]{:S(2)}) collective-permute-start(bf16[32,288]{1,0:T(8,128)(2,1)S(1)} %get-tuple-element.39), channel_id=1, source_target_pairs={{0,4},{1,5},{2,6},{3,7},{4,0},{5,1},{6,2},{7,3},{8,12},{9,13},{10,... | collective-permute-start | bytes 55304 | tf_op jit(solution)/shard_map/ppermute | solution.py:28
  24.2 8.1 %collective-permute-start.8 = (bf16[2,512,128]{2,1,0:T(8,128)(2,1)S(1)}, bf16[2,512,128]{2,1,0:T(8,128)(2,1)S(1)}, u32[]{:S(2)}, u32[]{:S(2)}) collective-permute-start(bf16[2,512,128]{2,1,0:T(8,128)(2,1)S(1)} %pad_maximum_fusion.part_0), channel_id=1, source_target_pairs={{0,2},{1,3},{2,0},{3,1},{4,6},{5,7},{6,4},{7,5},{8,10},{9,11},{10,... | collective-permute-start | bytes 786440 | tf_op jit(solution)/shard_map/ppermute | solution.py:28
  25.8 9.4 %collective-permute-start.10 = (bf16[2,512,128]{2,1,0:T(8,128)(2,1)S(1)}, bf16[2,512,128]{2,1,0:T(8,128)(2,1)S(1)}, u32[]{:S(2)}, u32[]{:S(2)}) collective-permute-start(bf16[2,512,128]{2,1,0:T(8,128)(2,1)S(1)} %pad_maximum_fusion.part_0), channel_id=1, source_target_pairs={{0,1},{1,0},{2,3},{3,2},{4,5},{5,4},{6,7},{7,6},{8,9},{9,8},{10,11... | collective-permute-start | bytes 786440 | tf_op jit(solution)/shard_map/ppermute | solution.py:28
  25.8 5.4 %collective-permute-start.14 = (f32[2,64,128]{2,1,0:T(8,128)S(1)}, f32[2,64,128]{2,1,0:T(8,128)S(1)}, u32[]{:S(2)}, u32[]{:S(2)}) collective-permute-start(f32[2,64,128]{2,1,0:T(8,128)S(1)} %get-tuple-element.43), channel_id=1, source_target_pairs={{0,1},{1,0},{2,3},{3,2},{4,5},{5,4},{6,7},{7,6},{8,9},{9,8},{10,11... | collective-permute-start | bytes 196616 | tf_op jit(solution)/shard_map/ppermute | solution.py:28
  27.8 6.4 %collective-permute-start.13 = (bf16[32,576]{1,0:T(8,128)(2,1)S(1)}, bf16[32,576]{1,0:T(8,128)(2,1)S(1)}, u32[]{:S(2)}, u32[]{:S(2)}) collective-permute-start(bf16[32,576]{1,0:T(8,128)(2,1)S(1)} %maximum_select_fusion.1), channel_id=1, source_target_pairs={{24,0},{25,1},{26,2},{27,3},{28,4},{29,5},{30,6},{31,7},{16,8},{17... | collective-permute-start | bytes 110600 | tf_op jit(solution)/shard_map/ppermute | solution.py:24
  30.2 4.3 %collective-permute-start.12 = (bf16[32,576]{1,0:T(8,128)(2,1)S(1)}, bf16[32,576]{1,0:T(8,128)(2,1)S(1)}, u32[]{:S(2)}, u32[]{:S(2)}) collective-permute-start(bf16[32,576]{1,0:T(8,128)(2,1)S(1)} %maximum_select_fusion.1), channel_id=1, source_target_pairs={{16,0},{17,1},{18,2},{19,3},{20,4},{21,5},{22,6},{23,7},{24,8},{25... | collective-permute-start | bytes 110600 | tf_op jit(solution)/shard_map/ppermute | solution.py:24
  31.2 4.0 %collective-permute-start.15 = (f32[64,128]{1,0:T(8,128)S(1)}, f32[64,128]{1,0:T(8,128)S(1)}, u32[]{:S(2)}, u32[]{:S(2)}) collective-permute-start(f32[64,128]{1,0:T(8,128)S(1)} %slice_bitcast_fusion.3), channel_id=1, source_target_pairs={{0,2},{1,3},{2,0},{3,1},{4,6},{5,7},{6,4},{7,5},{8,10},{9,11},{10,... | collective-permute-start | bytes 98312 | tf_op jit(solution)/shard_map/ppermute | solution.py:28
  32.4 2.9 %collective-permute-start.11 = (bf16[2,512,128]{2,1,0:T(8,128)(2,1)S(1)}, bf16[2,512,128]{2,1,0:T(8,128)(2,1)S(1)}, u32[]{:S(2)}, u32[]{:S(2)}) collective-permute-start(bf16[2,512,128]{2,1,0:T(8,128)(2,1)S(1)} %collective-permute-done.8.part_1), channel_id=1, source_target_pairs={{0,1},{1,0},{2,3},{3,2},{4,5},{5,4},{6,7},{7,6},{8,9},{9,8},{10,11... | collective-permute-start | bytes 786440 | tf_op jit(solution)/shard_map/ppermute | solution.py:28
  34.6 3.8 %copy-start.2 = (f32[1,128,128]{2,1,0:T(8,128)S(1)}, f32[1,128,128]{2,1,0:T(8,128)}, u32[]{:S(2)}) copy-start(f32[1,128,128]{2,1,0:T(8,128)} %param.7) | copy-start | bytes 196612
  36.9 4.8 %collective-permute-start.16 = (bf16[32,1664]{1,0:T(8,128)(2,1)S(1)}, bf16[32,1664]{1,0:T(8,128)(2,1)S(1)}, u32[]{:S(2)}, u32[]{:S(2)}) collective-permute-start(bf16[32,1664]{1,0:T(8,128)(2,1)S(1)} %get-tuple-element.46), channel_id=1, source_target_pairs={{0,4},{1,5},{2,6},{3,7},{4,0},{5,1},{6,2},{7,3},{8,12},{9,13},{10,... | collective-permute-start | bytes 319496 | tf_op jit(solution)/shard_map/ppermute | solution.py:28
  41.8 6.8 %collective-permute-start.17 = (bf16[32,1664]{1,0:T(8,128)(2,1)S(1)}, bf16[32,1664]{1,0:T(8,128)(2,1)S(1)}, u32[]{:S(2)}, u32[]{:S(2)}) collective-permute-start(bf16[32,1664]{1,0:T(8,128)(2,1)S(1)} %pad_maximum_fusion.3), channel_id=1, source_target_pairs={{0,8},{1,9},{2,10},{3,11},{4,12},{5,13},{6,14},{7,15},{8,0},{9,1},... | collective-permute-start | bytes 319496 | tf_op jit(solution)/shard_map/ppermute | solution.py:28
  50.0 4.9 %collective-permute-start.18 = (f32[136,128]{1,0:T(8,128)S(1)}, f32[136,128]{1,0:T(8,128)S(1)}, u32[]{:S(2)}, u32[]{:S(2)}) collective-permute-start(f32[136,128]{1,0:T(8,128)S(1)} %get-tuple-element.53), channel_id=1, source_target_pairs={{0,2},{1,3},{2,0},{3,1},{4,6},{5,7},{6,4},{7,5},{8,10},{9,11},{10,... | collective-permute-start | bytes 208904 | tf_op jit(solution)/shard_map/ppermute | solution.py:28
  50.2 4.8 %collective-permute-start.19 = (f32[136,128]{1,0:T(8,128)S(1)}, f32[136,128]{1,0:T(8,128)S(1)}, u32[]{:S(2)}, u32[]{:S(2)}) collective-permute-start(f32[136,128]{1,0:T(8,128)S(1)} %get-tuple-element.54), channel_id=1, source_target_pairs={{0,1},{1,0},{2,3},{3,2},{4,5},{5,4},{6,7},{7,6},{8,9},{9,8},{10,11... | collective-permute-start | bytes 208904 | tf_op jit(solution)/shard_map/ppermute | solution.py:28
  50.2 4.8 %collective-permute-start.20 = (f32[136,128]{1,0:T(8,128)S(1)}, f32[136,128]{1,0:T(8,128)S(1)}, u32[]{:S(2)}, u32[]{:S(2)}) collective-permute-start(f32[136,128]{1,0:T(8,128)S(1)} %get-tuple-element.55), channel_id=1, source_target_pairs={{0,3},{1,2},{2,1},{3,0},{4,7},{5,6},{6,5},{7,4},{8,11},{9,10},{10,... | collective-permute-start | bytes 208904 | tf_op jit(solution)/shard_map/ppermute | solution.py:28

commit v16 on v13

--- a/solution.py
+++ b/solution.py
@@ -155,7 +155,7 @@
     send[2 * size + 9 * rows :] = jnp.full((8, width), level, F32)
 
 
-def cross_kernel(side, part_0, part_1, part_2, part_3, precond_t, gram_0, gram_1, gram_2, gram_3, out, gram, levels):
+def cross_kernel(side, part_0, part_1, part_2, part_3, precond_t, gram, out, levels):
     quarter = precond_t.shape[0]
     width = part_0.shape[2]
     taps = jnp.concatenate([precond_t[:, t * width : (t + 1) * width] for t in range(9)], axis=0)
@@ -175,10 +175,10 @@
         part = jnp.dot(taps_to_rows(mapped, side), device[0], preferred_element_type=F32)
         both = part if both is None else both + part
     out[...] = both
-    grams = (gram_0[...] + gram_1[...]) + (gram_2[...] + gram_3[...])
-    gram[...] = grams
-    levels[0] = jnp.full((8, width), exponent(both), F32)
-    levels[1] = jnp.full((8, width), exponent(grams), F32)
+    level = jnp.maximum(exponent(both), -99.0)
+    gram_level = jnp.maximum(exponent(gram[...]), -99.0)
+    levels[0] = jnp.full((8, width), level, F32)
+    levels[1] = jnp.full((8, width), gram_level, F32)
 
 
 def two_parts(block):
@@ -220,36 +220,38 @@
     precond_t[...] = total.astype(BF16)
 
 
-def update_kernel(cross_t, mixed_in, k_a, k_b, main, gram, keep, send):
+def update_kernel(cross_t, gram, g_inv, k_a, k_b, main, keep, send_x, send_core, send_diagonal):
     rows = k_a.shape[2] // 2
-    mixed = jnp.concatenate([mixed_in[...], mixed_in[...]], axis=0)
+    width = main.shape[2]
+    mixed = jnp.dot(gram[gram.shape[0] // 2 :], g_inv[...], precision=HIGH)
+    mixed = jnp.concatenate([mixed, mixed], axis=0)
     parts = two_parts(rows_to_lanes(cross_t))
-    for i, k in enumerate((k_a, k_b)):
+    quarter = gram.shape[0] // 2
+    for i, (k, targets) in enumerate(((k_a, (keep, send_x)), (k_b, (send_core, send_diagonal)))):
         product = dot_nt(taps_to_lanes(k.at[0]), parts) + dot_nt(taps_to_lanes(k.at[1]), parts)
         result = main[i] - jnp.dot(product, mixed, precision=HIGH)
-        keep[i] = result[:rows]
-        send[i * rows : (i + 1) * rows] = result[rows:]
-    send[2 * rows :] = gram[...]
-
-
-def finish_kernel(scale, keep, mine, other, update, grams, scratch):
+        targets[0][:rows] = result[:rows]
+        targets[1][:rows] = result[rows:]
+    for target in (keep, send_x, send_core, send_diagonal):
+        target[rows : rows + quarter] = gram[:quarter]
+        target[rows + quarter :] = gram[quarter:]
+
+
+def finish_kernel(scale, mine, from_x, from_core, from_diagonal, update, grams, scratch):
     core, xbit = place_bits()
     first = 2 * core + xbit
     rows, width = update.shape
     quarter = width // 4
-    update[...] = keep[...] + other[:rows]
-    for j in range(4):
-        source = mine if j < 2 else other
+    update[...] = (mine[:rows] + from_x[:rows]) + (from_core[:rows] + from_diagonal[:rows])
+    for j, source in enumerate((mine, from_x, from_core, from_diagonal)):
+        place = pl.ds(pl.multiple_of((first ^ j) * quarter, quarter), quarter)
         for i in range(2):
-            low = rows + 2 * quarter * (j % 2) + i * quarter
-            place = pl.ds(pl.multiple_of((first ^ j) * quarter, quarter), quarter)
-            scratch[i, place, :] = source[low : low + quarter] * scale
+            scratch[i, place, :] = source[rows + i * quarter : rows + (i + 1) * quarter] * scale
     grams[0] = scratch[0]
     grams[1] = scratch[1].T
 
 
-def gram_kernel(grads, next_grads, *refs):
-    outs, scratch = refs[:4], refs[4]
+def gram_kernel(grads, next_grads, keep, send, scratch):
     core, xbit = place_bits()
     mine = 2 * core + xbit
     width = grads.shape[1]
@@ -260,7 +262,7 @@
     scratch[1] = jnp.where(last, 0.0, dot_t(next_grads[...], g))
     for j in range(4):
         for i in range(2):
-            outs[j][i * quarter : (i + 1) * quarter] = scratch[
+            (keep if j < 2 else send)[j % 2, i * quarter : (i + 1) * quarter] = scratch[
                 i, pl.ds(pl.multiple_of((mine ^ j) * quarter, quarter), quarter), :
             ]
 
@@ -338,15 +340,15 @@
         h.append(keep[j, :wide] + more)
         level.append(jnp.maximum(keep[j, wide:], other_level) + 1)
     k_core = other[e_rows:]
-    k_sent = jnp.concatenate(behind((sent[e_rows:], k_core), h[0]), axis=0)
-    k_x, k_diagonal = jnp.split(swap(k_sent, 2), 2, axis=0)
-    own = behind(jnp.stack([flat_maps, flat_grads]), h[0])
+    k_sent, k_late = behind((sent[e_rows:], k_core), h[0])
+    k_x, k_diagonal = swap(k_sent, 2), swap(k_late, 2)
+    own = behind(jnp.stack([flat_maps, flat_grads]), sent)
     next_own = after(own)
     h, level = summed(h[0], level[0], (h[1], level[1]), 2)
     h, level = summed(h, level, (h, level), zbits[0])
     next_own = behind(next_own, h)
     two_own = jnp.stack([flat_maps, next_own[0]])
-    two_x = swap(two_own, 2)
+    two_x = swap(behind(two_own, h), 2)
     for b in zbits[1:]:
         h, level = summed(h, level, (h, level), b)
 
@@ -374,74 +376,70 @@
     def by_bit(mine, other, b):
         return jnp.where((me & b) == 0, jnp.concatenate([mine, other], 1), jnp.concatenate([other, mine], 1))
 
-    grams = pl.pallas_call(
+    gram_keep, gram_send = pl.pallas_call(
         gram_kernel,
-        out_shape=[jax.ShapeDtypeStruct((2 * quarter, width), F32)] * 4,
+        out_shape=[jax.ShapeDtypeStruct((2, 2 * quarter, width), F32)] * 2,
         in_specs=[VMEM] * 2,
-        out_specs=[VMEM] * 4,
+        out_specs=[VMEM] * 2,
         scratch_shapes=[pltpu.VMEM((2, width, width), F32)],
         compiler_params=PARAMS,
     )(flat_grads, next_own[1])
-    grams = behind(grams, p_t)
-    grams = [grams[0]] + [swap(grams[j], bits) for j, bits in ((1, 2), (2, 1), (3, 3))]
+    gram_keep, gram_send = behind((gram_keep, gram_send), p_t)
+    gram = gram_keep + swap(gram_send, 1)
     for b in zbits[:-1]:
         p_t = by_bit(p_t, swap(p_t, b), b)
 
-    two_own, two_x = behind((two_own, two_x), p_t)
+    two_x = behind(two_x, p_t)
+    core_x = swap(two_x, 1)
+    two_own = behind(two_own, p_t)
     core_own = swap(two_own, 1)
-    core_x = swap(two_x, 1)
+    gram = behind(gram, p_t)
+    gram = gram[0] + swap(gram[1], 2)
     low = cols * quarter
     last = lax.axis_index("layer") == lax.axis_size("layer") - 1
     p_t = by_bit(after(p_t), after(p_t, zbits[-1]), zbits[-1])
     p_t = jnp.where(last, jnp.zeros_like(p_t), p_t)
 
-    cross_t, gram, levels = pl.pallas_call(
+    wide = 9 * quarter
+    cross_t, levels = pl.pallas_call(
         functools.partial(cross_kernel, side),
-        out_shape=[
-            jax.ShapeDtypeStruct((wide, width), F32),
-            jax.ShapeDtypeStruct((2 * quarter, width), F32),
-            jax.ShapeDtypeStruct((2, 8, width), F32),
-        ],
-        in_specs=[VMEM] * 9,
-        out_specs=[VMEM] * 3,
-        compiler_params=PARAMS,
-    )(two_own, two_x, core_own, core_x, p_t, *grams)
+        out_shape=[jax.ShapeDtypeStruct((wide, width), F32), jax.ShapeDtypeStruct((2, 8, width), F32)],
+        in_specs=[VMEM] * 6,
+        out_specs=[VMEM] * 2,
+        compiler_params=PARAMS,
+    )(two_own, two_x, core_own, core_x, p_t, gram)
 
     place = (jnp.arange(width)[None, :] == low + jnp.arange(quarter)[:, None]).astype(F32)
     main_a, main_b = behind((main_a, main_b), cross_t)
+    g_scaled = behind(g_inv, cross_t) * (scale * scale)
     main = jnp.stack([dot_t(main_a, place, precision=HIGH), dot_t(main_b, place, precision=HIGH)])
-    sizes = [wide, 2 * quarter]
-    cross_level, gram_level = levels[0], levels[1]
+    level, gram_level = levels[0], levels[1]
+    edge = wide + 2 * quarter
     for b in zbits:
-        mine = packed([(cross_t, cross_level), (gram, gram_level)])
-        (more, level), (more_gram, level_gram) = opened(swap(mine.astype(F16), b), sizes)
-        cross_t = cross_t + more
-        gram = opened(mine, sizes)[1][0] + more_gram
-        cross_level = jnp.maximum(cross_level, level) + 1
-        gram_level = jnp.maximum(gram_level, level_gram) + 1
-    mixed = jnp.dot(gram[quarter:], g_inv, precision=HIGH) * (scale * scale)
-
-    out, send = pl.pallas_call(
+        scaled = lax.reduce_precision(gram * jnp.exp2(TOP - gram_level[:1]), 5, 10)
+        mine = jnp.concatenate([cross_t * jnp.exp2(TOP - level[:1]), scaled, level, gram_level], axis=0)
+        other = swap(mine.astype(F16), b).astype(F32)
+        cross_t = cross_t + other[:wide] * jnp.exp2(other[edge : edge + 1] - TOP)
+        gram = scaled * jnp.exp2(gram_level[:1] - TOP) + other[wide:edge] * jnp.exp2(other[edge + 8 : edge + 9] - TOP)
+        level = jnp.maximum(level, other[edge : edge + 8]) + 1
+        gram_level = jnp.maximum(gram_level, other[edge + 8 :]) + 1
+
+    parcels = pl.pallas_call(
         update_kernel,
-        out_shape=[
-            jax.ShapeDtypeStruct((2, rows, width), F32),
-            jax.ShapeDtypeStruct((2 * rows + 2 * quarter, width), F32),
-        ],
+        out_shape=[jax.ShapeDtypeStruct((rows + 2 * quarter, width), F32)] * 4,
         in_specs=[VMEM] * 6,
-        out_specs=[VMEM] * 2,
-        compiler_params=PARAMS,
-    )(cross_t, mixed, k_a, k_b, main, gram)
-    other = swap(send, 2)
-    keep = out[0] + other[:rows]
-    send = jnp.concatenate([out[1] + other[rows : 2 * rows], gram, other[2 * rows :]], axis=0)
+        out_specs=[VMEM] * 4,
+        compiler_params=PARAMS,
+    )(cross_t, gram, g_scaled, k_a, k_b, main)
+    parcels = [parcels[0]] + [swap(parcels[j], bits) for j, bits in ((1, 2), (2, 1), (3, 3))]
     update, grams = pl.pallas_call(
         functools.partial(finish_kernel, scale),
         out_shape=[jax.ShapeDtypeStruct((rows, width), F32), jax.ShapeDtypeStruct((2, width, width), F32)],
-        in_specs=[VMEM] * 3,
+        in_specs=[VMEM] * 4,
         out_specs=[VMEM] * 2,
         scratch_shapes=[pltpu.VMEM((2, width, width), F32)],
         compiler_params=PARAMS,
-    )(keep, send, swap(send, 1))
+    )(*parcels)
     return (update[None], grams[None])
 
 

time: 66.5 us -> 55.1 us (0.83)
  waiting for transfers between devices: 29.2 us -> 19.4 us
  starting transfers between devices: 25.7 us -> 24.7 us
    ppermute x16 -> x17, waiting for transfers between devices: 27.5 us -> 18 us  [swap(): lax.ppermute(block, 'pos', [(i, i ^ bit) for i in range(lax.axis_size('po...]
    ppermute x16 -> x17, starting transfers between devices: 21.9 us -> 18 us  [swap(): lax.ppermute(block, 'pos', [(i, i ^ bit) for i in range(lax.axis_size('po...]
    ppermute x3, starting transfers between devices: 3.82 us -> 6.74 us  [after(): return lax.ppermute(block, ('layer', 'pos'), route)]
  transfers between devices with their start and end apart: 19 -> 20, of which waited for: 12 -> 11; matrix products, arithmetic and copies ran while one was open for 2% -> 3% of each run, Pallas kernels for 2% -> 1%
where the time goes in v16:
time: 55.1 us; the launch traced here: 54.9 us
  starting transfers between devices  24.7 us (45%)
  waiting for transfers between devices  19.4 us (35%)
  Pallas kernels  7.21 us (13%)
  other arithmetic  1.76 us (3%)
  between operations  1.14 us (2%)
  matrix products  0.56 us (1%)
    ppermute x17, waiting for transfers between devices, swap(): lax.ppermute(block, 'pos', [(i, i ^ bit) for i in range(lax.axis_size('po...  18 us
    ppermute x17, starting transfers between devices, swap(): lax.ppermute(block, 'pos', [(i, i ^ bit) for i in range(lax.axis_size('po...  18 us
    ppermute x3, starting transfers between devices, after(): return lax.ppermute(block, ('layer', 'pos'), route)  6.74 us
    pallas_call x1, Pallas kernels, per_device(): pl.pallas_call(functools.partial(grad_kernel, side), out_shape=[jax.Shape...  2.28 us
    pallas_call x1, Pallas kernels, per_device(): pl.pallas_call(functools.partial(cross_kernel, side), out_shape=[jax.Shap...  1.87 us
    ppermute x3, waiting for transfers between devices, after(): return lax.ppermute(block, ('layer', 'pos'), route)  1.43 us
    pallas_call x1, Pallas kernels, per_device(): pl.pallas_call(update_kernel, out_shape=[jax.ShapeDtypeStruct((rows + 2 *...  1.28 us
  transfers between devices with their start and end apart: 20, of which 11 were waited for; matrix products, arithmetic and copies ran while one was open for 3% of the time, Pallas kernels for 1%

profile of v16, /device:TPU:0, one launch (start us, length us, event | category | flops | bytes accessed | tf_op | source)
XLA Modules:
  0.0 54.9 jit_solution(15533696306293946735)
XLA Ops:
  0.6 2.3 %shard_map.59 = (f32[2,296,128]{2,1,0:T(8,128)S(1)}, f32[1248,128]{1,0:T(8,128)S(1)}, bf16[2,9,72,128]{3,2,1,0:T(8,128)(2,1)S(1)}) custom-call(bf16[512,128]{1,0:T(8,128)(2,1)} %bitcast.90, bf16[512,128]{1,0:T(8,128)(2,1)} %bitcast.84, f32[128,128]{1,0:T(8,128)} %bitcast.94, f32[72,1152]{1,0:T(8,128)} %bitcast.93), custom_call_target="tpu_custom_call" | custom-call | tf_op jit(solution)/shard_map/pallas_call | solution.py:295
  3.5 2.6 %collective-permute-start = (bf16[2,512,128]{2,1,0:T(8,128)(2,1)S(1)}, bf16[2,512,128]{2,1,0:T(8,128)(2,1)S(1)}, u32[]{:S(2)}, u32[]{:S(2)}) collective-permute-start(bf16[2,512,128]{2,1,0:T(8,128)(2,1)S(1)} %pad_maximum_fusion), channel_id=1, source_target_pairs={{16,0},{17,1},{18,2},{19,3},{20,4},{21,5},{22,6},{23,7},{24,8},{25... | collective-permute-start | bytes 786440 | tf_op jit(solution)/shard_map/ppermute | solution.py:24
  6.4 1.6 %collective-permute-start.2 = (f16[296,128]{1,0:T(8,128)(2,1)S(1)}, f16[296,128]{1,0:T(8,128)(2,1)S(1)}, u32[]{:S(2)}, u32[]{:S(2)}) collective-permute-start(f16[296,128]{1,0:T(8,128)(2,1)S(1)} %pad_maximum_fusion.5), channel_id=1, source_target_pairs={{0,2},{1,3},{2,0},{3,1},{4,6},{5,7},{6,4},{7,5},{8,10},{9,11},{10,... | collective-permute-start | bytes 227336 | tf_op jit(solution)/shard_map/ppermute | solution.py:28
  8.1 2.8 %collective-permute-done.2 = f16[296,128]{1,0:T(8,128)(2,1)S(1)} collective-permute-done((f16[296,128]{1,0:T(8,128)(2,1)S(1)}, f16[296,128]{1,0:T(8,128)(2,1)S(1)}, u32[]{:S(2)}, u32[]{:S(2)}) %collective-permute-start.2) | collective-permute-done | bytes 75808 | tf_op jit(solution)/shard_map/ppermute | solution.py:28
  11.1 1.6 %collective-permute-start.3 = (f16[296,128]{1,0:T(8,128)(2,1)S(1)}, f16[296,128]{1,0:T(8,128)(2,1)S(1)}, u32[]{:S(2)}, u32[]{:S(2)}) collective-permute-start(f16[296,128]{1,0:T(8,128)(2,1)S(1)} %pad_maximum_fusion.6), channel_id=1, source_target_pairs={{0,4},{1,5},{2,6},{3,7},{4,0},{5,1},{6,2},{7,3},{8,12},{9,13},{10,... | collective-permute-start | bytes 227336 | tf_op jit(solution)/shard_map/ppermute | solution.py:28
  12.8 1.6 %collective-permute-start.5 = (f16[656,128]{1,0:T(8,128)(2,1)S(1)}, f16[656,128]{1,0:T(8,128)(2,1)S(1)}, u32[]{:S(2)}, u32[]{:S(2)}) collective-permute-start(f16[656,128]{1,0:T(8,128)(2,1)S(1)} %slice.238), channel_id=1, source_target_pairs={{0,2},{1,3},{2,0},{3,1},{4,6},{5,7},{6,4},{7,5},{8,10},{9,11},{10,... | collective-permute-start | bytes 503816 | tf_op jit(solution)/shard_map/ppermute | solution.py:28
  15.8 2.6 %collective-permute-start.4 = (f16[296,128]{1,0:T(8,128)(2,1)S(1)}, f16[296,128]{1,0:T(8,128)(2,1)S(1)}, u32[]{:S(2)}, u32[]{:S(2)}) collective-permute-start(f16[296,128]{1,0:T(8,128)(2,1)S(1)} %pad_maximum_fusion.7), channel_id=1, source_target_pairs={{0,8},{1,9},{2,10},{3,11},{4,12},{5,13},{6,14},{7,15},{8,0},{9,1},... | collective-permute-start | bytes 227336 | tf_op jit(solution)/shard_map/ppermute | solution.py:28
  18.5 2.7 %collective-permute-done.4 = f16[296,128]{1,0:T(8,128)(2,1)S(1)} collective-permute-done((f16[296,128]{1,0:T(8,128)(2,1)S(1)}, f16[296,128]{1,0:T(8,128)(2,1)S(1)}, u32[]{:S(2)}, u32[]{:S(2)}) %collective-permute-start.4) | collective-permute-done | bytes 75808 | tf_op jit(solution)/shard_map/ppermute | solution.py:28
  22.8 1.2 %collective-permute-start.7 = (bf16[32,288]{1,0:T(8,128)(2,1)S(1)}, bf16[32,288]{1,0:T(8,128)(2,1)S(1)}, u32[]{:S(2)}, u32[]{:S(2)}) collective-permute-start(bf16[32,288]{1,0:T(8,128)(2,1)S(1)} %get-tuple-element.38), channel_id=1, source_target_pairs={{0,4},{1,5},{2,6},{3,7},{4,0},{5,1},{6,2},{7,3},{8,12},{9,13},{10,... | collective-permute-start | bytes 55304 | tf_op jit(solution)/shard_map/ppermute | solution.py:28
  24.3 1.6 %collective-permute-start.8 = (bf16[2,512,128]{2,1,0:T(8,128)(2,1)S(1)}, bf16[2,512,128]{2,1,0:T(8,128)(2,1)S(1)}, u32[]{:S(2)}, u32[]{:S(2)}) collective-permute-start(bf16[2,512,128]{2,1,0:T(8,128)(2,1)S(1)} %pad_maximum_fusion.1.part_0), channel_id=1, source_target_pairs={{0,2},{1,3},{2,0},{3,1},{4,6},{5,7},{6,4},{7,5},{8,10},{9,11},{10,... | collective-permute-start | bytes 786440 | tf_op jit(solution)/shard_map/ppermute | solution.py:28
  25.8 0.8 %collective-permute-done.7 = bf16[32,288]{1,0:T(8,128)(2,1)S(1)} collective-permute-done((bf16[32,288]{1,0:T(8,128)(2,1)S(1)}, bf16[32,288]{1,0:T(8,128)(2,1)S(1)}, u32[]{:S(2)}, u32[]{:S(2)}) %collective-permute-start.7) | collective-permute-done | bytes 18464 | tf_op jit(solution)/shard_map/ppermute | solution.py:28
  26.7 3.4 %collective-permute-start.12 = (bf16[32,576]{1,0:T(8,128)(2,1)S(1)}, bf16[32,576]{1,0:T(8,128)(2,1)S(1)}, u32[]{:S(2)}, u32[]{:S(2)}) collective-permute-start(bf16[32,576]{1,0:T(8,128)(2,1)S(1)} %maximum_select_fusion.1), channel_id=1, source_target_pairs={{24,0},{25,1},{26,2},{27,3},{28,4},{29,5},{30,6},{31,7},{16,8},{17... | collective-permute-start | bytes 110600 | tf_op jit(solution)/shard_map/ppermute | solution.py:24
  30.9 1.6 %collective-permute-start.14 = (f32[64,128]{1,0:T(8,128)S(1)}, f32[64,128]{1,0:T(8,128)S(1)}, u32[]{:S(2)}, u32[]{:S(2)}) collective-permute-start(f32[64,128]{1,0:T(8,128)S(1)} %slice_bitcast_fusion.1), channel_id=1, source_target_pairs={{0,2},{1,3},{2,0},{3,1},{4,6},{5,7},{6,4},{7,5},{8,10},{9,11},{10,... | collective-permute-start | bytes 98312 | tf_op jit(solution)/shard_map/ppermute | solution.py:28
  32.7 1.4 %collective-permute-done.11 = bf16[32,576]{1,0:T(8,128)(2,1)S(1)} collective-permute-done((bf16[32,576]{1,0:T(8,128)(2,1)S(1)}, bf16[32,576]{1,0:T(8,128)(2,1)S(1)}, u32[]{:S(2)}, u32[]{:S(2)}) %collective-permute-start.11) | collective-permute-done | bytes 36896 | tf_op jit(solution)/shard_map/ppermute | solution.py:24
  34.9 1.9 %shard_map.62 = (f32[288,128]{1,0:T(8,128)S(1)}, f32[2,8,128]{2,1,0:T(8,128)S(1)}) custom-call(bf16[2,512,128]{2,1,0:T(8,128)(2,1)S(1)} %pad_maximum_fusion.1.part_0, bf16[2,512,128]{2,1,0:T(8,128)(2,1)S(1)} %collective-permute-done.8.part_1, bf16[2,512,128]{2,1,0:T(8,128)(2,1)S(1)} %collective-permute-done.9.part_2, ...), custom_call_target="tpu_custom_call" | custom-call | tf_op jit(solution)/shard_map/pallas_call | solution.py:404
  36.9 1.9 %collective-permute-start.15 = (f16[368,128]{1,0:T(8,128)(2,1)S(1)}, f16[368,128]{1,0:T(8,128)(2,1)S(1)}, u32[]{:S(2)}, u32[]{:S(2)}) collective-permute-start(f16[368,128]{1,0:T(8,128)(2,1)S(1)} %pad_maximum_fusion.3), channel_id=1, source_target_pairs={{0,4},{1,5},{2,6},{3,7},{4,0},{5,1},{6,2},{7,3},{8,12},{9,13},{10,... | collective-permute-start | bytes 282632 | tf_op jit(solution)/shard_map/ppermute | solution.py:28
  39.4 2.2 %collective-permute-done.15 = f16[368,128]{1,0:T(8,128)(2,1)S(1)} collective-permute-done((f16[368,128]{1,0:T(8,128)(2,1)S(1)}, f16[368,128]{1,0:T(8,128)(2,1)S(1)}, u32[]{:S(2)}, u32[]{:S(2)}) %collective-permute-start.15) | collective-permute-done | bytes 94240 | tf_op jit(solution)/shard_map/ppermute | solution.py:28
  41.8 0.9 %collective-permute-start.16 = (f16[368,128]{1,0:T(8,128)(2,1)S(1)}, f16[368,128]{1,0:T(8,128)(2,1)S(1)}, u32[]{:S(2)}, u32[]{:S(2)}) collective-permute-start(f16[368,128]{1,0:T(8,128)(2,1)S(1)} %pad_maximum_fusion.4), channel_id=1, source_target_pairs={{0,8},{1,9},{2,10},{3,11},{4,12},{5,13},{6,14},{7,15},{8,0},{9,1},... | collective-permute-start | bytes 282632 | tf_op jit(solution)/shard_map/ppermute | solution.py:28
  42.7 4.6 %collective-permute-done.16 = f16[368,128]{1,0:T(8,128)(2,1)S(1)} collective-permute-done((f16[368,128]{1,0:T(8,128)(2,1)S(1)}, f16[368,128]{1,0:T(8,128)(2,1)S(1)}, u32[]{:S(2)}, u32[]{:S(2)}) %collective-permute-start.16) | collective-permute-done | bytes 94240 | tf_op jit(solution)/shard_map/ppermute | solution.py:28
  47.4 1.3 %shard_map.63 = (f32[136,128]{1,0:T(8,128)S(1)}, f32[136,128]{1,0:T(8,128)S(1)}, f32[136,128]{1,0:T(8,128)S(1)}, f32[136,128]{1,0:T(8,128)S(1)}) custom-call(f32[288,128]{1,0:T(8,128)S(1)} %fusion.3.cross_t, f32[64,128]{1,0:T(8,128)S(1)} %fusion.14.gram, f32[128,128]{1,0:T(8,128)S(1)} %broadcast_multiply_fusion.g_inv, ...), custom_call_target="tpu_custom_call" | custom-call | tf_op jit(solution)/shard_map/pallas_call | solution.py:427
  48.7 1.6 %collective-permute-start.17 = (f32[136,128]{1,0:T(8,128)S(1)}, f32[136,128]{1,0:T(8,128)S(1)}, u32[]{:S(2)}, u32[]{:S(2)}) collective-permute-start(f32[136,128]{1,0:T(8,128)S(1)} %get-tuple-element.55), channel_id=1, source_target_pairs={{0,2},{1,3},{2,0},{3,1},{4,6},{5,7},{6,4},{7,5},{8,10},{9,11},{10,... | collective-permute-start | bytes 208904 | tf_op jit(solution)/shard_map/ppermute | solution.py:28
  50.9 2.2 %collective-permute-done.17.from_x = f32[136,128]{1,0:T(8,128)S(1)} collective-permute-done((f32[136,128]{1,0:T(8,128)S(1)}, f32[136,128]{1,0:T(8,128)S(1)}, u32[]{:S(2)}, u32[]{:S(2)}) %collective-permute-start.17) | collective-permute-done | bytes 69664 | tf_op jit(solution)/shard_map/ppermute | solution.py:28
  53.1 1.0 %collective-permute-done.19.from_diagonal = f32[136,128]{1,0:T(8,128)S(1)} collective-permute-done((f32[136,128]{1,0:T(8,128)S(1)}, f32[136,128]{1,0:T(8,128)S(1)}, u32[]{:S(2)}, u32[]{:S(2)}) %collective-permute-start.19) | collective-permute-done | bytes 69664 | tf_op jit(solution)/shard_map/ppermute | solution.py:28
  54.1 0.8 %shard_map.64 = (f32[72,128]{1,0:T(8,128)}, f32[2,128,128]{2,1,0:T(8,128)}) custom-call(f32[136,128]{1,0:T(8,128)S(1)} %get-tuple-element.54.mine, f32[136,128]{1,0:T(8,128)S(1)} %collective-permute-done.17.from_x, f32[136,128]{1,0:T(8,128)S(1)} %collective-permute-done.18.from_core, f32[136,128]{1,0:T(8,128)S(1)} %collective-permute-done.19.from_diagonal), custom_call_target="tpu_custom_call" | custom-call | tf_op jit(solution)/shard_map/pallas_call | solution.py:435
  (96 shorter events, 7.9 us)
Async XLA Ops:
  0.6 2.9 %copy-start = (bf16[1,2,16,16,128]{4,3,2,1,0:T(8,128)(2,1)S(1)}, bf16[1,2,16,16,128]{4,3,2,1,0:T(8,128)(2,1)}, u32[]{:S(2)}) copy-start(bf16[1,2,16,16,128]{4,3,2,1,0:T(8,128)(2,1)} %param.5) | copy-start | bytes 393220
  0.6 2.9 %copy-start.1 = (bf16[1,2,16,16,128]{4,3,2,1,0:T(8,128)(2,1)S(1)}, bf16[1,2,16,16,128]{4,3,2,1,0:T(8,128)(2,1)}, u32[]{:S(2)}) copy-start(bf16[1,2,16,16,128]{4,3,2,1,0:T(8,128)(2,1)} %param.4) | copy-start | bytes 393220
  3.0 3.2 %collective-permute-start.1 = (f16[1248,128]{1,0:T(8,128)(2,1)S(1)}, f16[1248,128]{1,0:T(8,128)(2,1)S(1)}, u32[]{:S(2)}, u32[]{:S(2)}) collective-permute-start(f16[1248,128]{1,0:T(8,128)(2,1)S(1)} %convert_element_type.42), channel_id=1, source_target_pairs={{0,1},{1,0},{2,3},{3,2},{4,5},{5,4},{6,7},{7,6},{8,9},{9,8},{10,11... | collective-permute-start | bytes 958472 | tf_op jit(solution)/shard_map/ppermute | solution.py:28
  3.5 12.2 %collective-permute-start = (bf16[2,512,128]{2,1,0:T(8,128)(2,1)S(1)}, bf16[2,512,128]{2,1,0:T(8,128)(2,1)S(1)}, u32[]{:S(2)}, u32[]{:S(2)}) collective-permute-start(bf16[2,512,128]{2,1,0:T(8,128)(2,1)S(1)} %pad_maximum_fusion), channel_id=1, source_target_pairs={{16,0},{17,1},{18,2},{19,3},{20,4},{21,5},{22,6},{23,7},{24,8},{25... | collective-permute-start | bytes 786440 | tf_op jit(solution)/shard_map/ppermute | solution.py:24
  6.4 4.5 %collective-permute-start.2 = (f16[296,128]{1,0:T(8,128)(2,1)S(1)}, f16[296,128]{1,0:T(8,128)(2,1)S(1)}, u32[]{:S(2)}, u32[]{:S(2)}) collective-permute-start(f16[296,128]{1,0:T(8,128)(2,1)S(1)} %pad_maximum_fusion.5), channel_id=1, source_target_pairs={{0,2},{1,3},{2,0},{3,1},{4,6},{5,7},{6,4},{7,5},{8,10},{9,11},{10,... | collective-permute-start | bytes 227336 | tf_op jit(solution)/shard_map/ppermute | solution.py:28
  11.1 4.4 %collective-permute-start.3 = (f16[296,128]{1,0:T(8,128)(2,1)S(1)}, f16[296,128]{1,0:T(8,128)(2,1)S(1)}, u32[]{:S(2)}, u32[]{:S(2)}) collective-permute-start(f16[296,128]{1,0:T(8,128)(2,1)S(1)} %pad_maximum_fusion.6), channel_id=1, source_target_pairs={{0,4},{1,5},{2,6},{3,7},{4,0},{5,1},{6,2},{7,3},{8,12},{9,13},{10,... | collective-permute-start | bytes 227336 | tf_op jit(solution)/shard_map/ppermute | solution.py:28
  12.8 8.4 %collective-permute-start.5 = (f16[656,128]{1,0:T(8,128)(2,1)S(1)}, f16[656,128]{1,0:T(8,128)(2,1)S(1)}, u32[]{:S(2)}, u32[]{:S(2)}) collective-permute-start(f16[656,128]{1,0:T(8,128)(2,1)S(1)} %slice.238), channel_id=1, source_target_pairs={{0,2},{1,3},{2,0},{3,1},{4,6},{5,7},{6,4},{7,5},{8,10},{9,11},{10,... | collective-permute-start | bytes 503816 | tf_op jit(solution)/shard_map/ppermute | solution.py:28
  14.4 7.4 %collective-permute-start.6 = (f16[656,128]{1,0:T(8,128)(2,1)S(1)}, f16[656,128]{1,0:T(8,128)(2,1)S(1)}, u32[]{:S(2)}, u32[]{:S(2)}) collective-permute-start(f16[656,128]{1,0:T(8,128)(2,1)S(1)} %get-tuple-element.37), channel_id=1, source_target_pairs={{0,2},{1,3},{2,0},{3,1},{4,6},{5,7},{6,4},{7,5},{8,10},{9,11},{10,... | collective-permute-start | bytes 503816 | tf_op jit(solution)/shard_map/ppermute | solution.py:28
  15.8 5.3 %collective-permute-start.4 = (f16[296,128]{1,0:T(8,128)(2,1)S(1)}, f16[296,128]{1,0:T(8,128)(2,1)S(1)}, u32[]{:S(2)}, u32[]{:S(2)}) collective-permute-start(f16[296,128]{1,0:T(8,128)(2,1)S(1)} %pad_maximum_fusion.7), channel_id=1, source_target_pairs={{0,8},{1,9},{2,10},{3,11},{4,12},{5,13},{6,14},{7,15},{8,0},{9,1},... | collective-permute-start | bytes 227336 | tf_op jit(solution)/shard_map/ppermute | solution.py:28
  22.8 3.8 %collective-permute-start.7 = (bf16[32,288]{1,0:T(8,128)(2,1)S(1)}, bf16[32,288]{1,0:T(8,128)(2,1)S(1)}, u32[]{:S(2)}, u32[]{:S(2)}) collective-permute-start(bf16[32,288]{1,0:T(8,128)(2,1)S(1)} %get-tuple-element.38), channel_id=1, source_target_pairs={{0,4},{1,5},{2,6},{3,7},{4,0},{5,1},{6,2},{7,3},{8,12},{9,13},{10,... | collective-permute-start | bytes 55304 | tf_op jit(solution)/shard_map/ppermute | solution.py:28
  24.3 8.2 %collective-permute-start.8 = (bf16[2,512,128]{2,1,0:T(8,128)(2,1)S(1)}, bf16[2,512,128]{2,1,0:T(8,128)(2,1)S(1)}, u32[]{:S(2)}, u32[]{:S(2)}) collective-permute-start(bf16[2,512,128]{2,1,0:T(8,128)(2,1)S(1)} %pad_maximum_fusion.1.part_0), channel_id=1, source_target_pairs={{0,2},{1,3},{2,0},{3,1},{4,6},{5,7},{6,4},{7,5},{8,10},{9,11},{10,... | collective-permute-start | bytes 786440 | tf_op jit(solution)/shard_map/ppermute | solution.py:28
  25.8 5.0 %collective-permute-start.13 = (f32[2,64,128]{2,1,0:T(8,128)S(1)}, f32[2,64,128]{2,1,0:T(8,128)S(1)}, u32[]{:S(2)}, u32[]{:S(2)}) collective-permute-start(f32[2,64,128]{2,1,0:T(8,128)S(1)} %get-tuple-element.45), channel_id=1, source_target_pairs={{0,1},{1,0},{2,3},{3,2},{4,5},{5,4},{6,7},{7,6},{8,9},{9,8},{10,11... | collective-permute-start | bytes 196616 | tf_op jit(solution)/shard_map/ppermute | solution.py:28
  26.7 5.9 %collective-permute-start.12 = (bf16[32,576]{1,0:T(8,128)(2,1)S(1)}, bf16[32,576]{1,0:T(8,128)(2,1)S(1)}, u32[]{:S(2)}, u32[]{:S(2)}) collective-permute-start(bf16[32,576]{1,0:T(8,128)(2,1)S(1)} %maximum_select_fusion.1), channel_id=1, source_target_pairs={{24,0},{25,1},{26,2},{27,3},{28,4},{29,5},{30,6},{31,7},{16,8},{17... | collective-permute-start | bytes 110600 | tf_op jit(solution)/shard_map/ppermute | solution.py:24
  30.1 4.0 %collective-permute-start.11 = (bf16[32,576]{1,0:T(8,128)(2,1)S(1)}, bf16[32,576]{1,0:T(8,128)(2,1)S(1)}, u32[]{:S(2)}, u32[]{:S(2)}) collective-permute-start(bf16[32,576]{1,0:T(8,128)(2,1)S(1)} %maximum_select_fusion.1), channel_id=1, source_target_pairs={{16,0},{17,1},{18,2},{19,3},{20,4},{21,5},{22,6},{23,7},{24,8},{25... | collective-permute-start | bytes 110600 | tf_op jit(solution)/shard_map/ppermute | solution.py:24
  30.8 4.0 %collective-permute-start.9 = (bf16[2,512,128]{2,1,0:T(8,128)(2,1)S(1)}, bf16[2,512,128]{2,1,0:T(8,128)(2,1)S(1)}, u32[]{:S(2)}, u32[]{:S(2)}) collective-permute-start(bf16[2,512,128]{2,1,0:T(8,128)(2,1)S(1)} %pad_maximum_fusion.1.part_0), channel_id=1, source_target_pairs={{0,1},{1,0},{2,3},{3,2},{4,5},{5,4},{6,7},{7,6},{8,9},{9,8},{10,11... | collective-permute-start | bytes 786440 | tf_op jit(solution)/shard_map/ppermute | solution.py:28
  30.9 4.0 %collective-permute-start.14 = (f32[64,128]{1,0:T(8,128)S(1)}, f32[64,128]{1,0:T(8,128)S(1)}, u32[]{:S(2)}, u32[]{:S(2)}) collective-permute-start(f32[64,128]{1,0:T(8,128)S(1)} %slice_bitcast_fusion.1), channel_id=1, source_target_pairs={{0,2},{1,3},{2,0},{3,1},{4,6},{5,7},{6,4},{7,5},{8,10},{9,11},{10,... | collective-permute-start | bytes 98312 | tf_op jit(solution)/shard_map/ppermute | solution.py:28
  32.4 2.4 %collective-permute-start.10 = (bf16[2,512,128]{2,1,0:T(8,128)(2,1)S(1)}, bf16[2,512,128]{2,1,0:T(8,128)(2,1)S(1)}, u32[]{:S(2)}, u32[]{:S(2)}) collective-permute-start(bf16[2,512,128]{2,1,0:T(8,128)(2,1)S(1)} %collective-permute-done.8.part_1), channel_id=1, source_target_pairs={{0,1},{1,0},{2,3},{3,2},{4,5},{5,4},{6,7},{7,6},{8,9},{9,8},{10,11... | collective-permute-start | bytes 786440 | tf_op jit(solution)/shard_map/ppermute | solution.py:28
  34.2 2.6 %copy-start.2 = (f32[1,128,128]{2,1,0:T(8,128)S(1)}, f32[1,128,128]{2,1,0:T(8,128)}, u32[]{:S(2)}) copy-start(f32[1,128,128]{2,1,0:T(8,128)} %param.7) | copy-start | bytes 196612
  36.9 4.6 %collective-permute-start.15 = (f16[368,128]{1,0:T(8,128)(2,1)S(1)}, f16[368,128]{1,0:T(8,128)(2,1)S(1)}, u32[]{:S(2)}, u32[]{:S(2)}) collective-permute-start(f16[368,128]{1,0:T(8,128)(2,1)S(1)} %pad_maximum_fusion.3), channel_id=1, source_target_pairs={{0,4},{1,5},{2,6},{3,7},{4,0},{5,1},{6,2},{7,3},{8,12},{9,13},{10,... | collective-permute-start | bytes 282632 | tf_op jit(solution)/shard_map/ppermute | solution.py:28
  41.8 5.5 %collective-permute-start.16 = (f16[368,128]{1,0:T(8,128)(2,1)S(1)}, f16[368,128]{1,0:T(8,128)(2,1)S(1)}, u32[]{:S(2)}, u32[]{:S(2)}) collective-permute-start(f16[368,128]{1,0:T(8,128)(2,1)S(1)} %pad_maximum_fusion.4), channel_id=1, source_target_pairs={{0,8},{1,9},{2,10},{3,11},{4,12},{5,13},{6,14},{7,15},{8,0},{9,1},... | collective-permute-start | bytes 282632 | tf_op jit(solution)/shard_map/ppermute | solution.py:28
  48.7 4.4 %collective-permute-start.17 = (f32[136,128]{1,0:T(8,128)S(1)}, f32[136,128]{1,0:T(8,128)S(1)}, u32[]{:S(2)}, u32[]{:S(2)}) collective-permute-start(f32[136,128]{1,0:T(8,128)S(1)} %get-tuple-element.55), channel_id=1, source_target_pairs={{0,2},{1,3},{2,0},{3,1},{4,6},{5,7},{6,4},{7,5},{8,10},{9,11},{10,... | collective-permute-start | bytes 208904 | tf_op jit(solution)/shard_map/ppermute | solution.py:28
  50.3 2.8 %collective-permute-start.18 = (f32[136,128]{1,0:T(8,128)S(1)}, f32[136,128]{1,0:T(8,128)S(1)}, u32[]{:S(2)}, u32[]{:S(2)}) collective-permute-start(f32[136,128]{1,0:T(8,128)S(1)} %get-tuple-element.56), channel_id=1, source_target_pairs={{0,1},{1,0},{2,3},{3,2},{4,5},{5,4},{6,7},{7,6},{8,9},{9,8},{10,11... | collective-permute-start | bytes 208904 | tf_op jit(solution)/shard_map/ppermute | solution.py:28
  50.3 3.8 %collective-permute-start.19 = (f32[136,128]{1,0:T(8,128)S(1)}, f32[136,128]{1,0:T(8,128)S(1)}, u32[]{:S(2)}, u32[]{:S(2)}) collective-permute-start(f32[136,128]{1,0:T(8,128)S(1)} %get-tuple-element.57), channel_id=1, source_target_pairs={{0,3},{1,2},{2,1},{3,0},{4,7},{5,6},{6,5},{7,4},{8,11},{9,10},{10,... | collective-permute-start | bytes 208904 | tf_op jit(solution)/shard_map/ppermute | solution.py:28

commit v17 on v16

--- a/solution.py
+++ b/solution.py
@@ -224,12 +224,18 @@
     rows = k_a.shape[2] // 2
     width = main.shape[2]
     mixed = jnp.dot(gram[gram.shape[0] // 2 :], g_inv[...], precision=HIGH)
-    mixed = jnp.concatenate([mixed, mixed], axis=0)
+    high = mixed.astype(BF16)
+    rest = (mixed - high.astype(F32)).astype(BF16)
+    mixed = jnp.concatenate([high] * 4 + [rest] * 2, axis=0)
     parts = two_parts(rows_to_lanes(cross_t))
     quarter = gram.shape[0] // 2
     for i, (k, targets) in enumerate(((k_a, (keep, send_x)), (k_b, (send_core, send_diagonal)))):
         product = dot_nt(taps_to_lanes(k.at[0]), parts) + dot_nt(taps_to_lanes(k.at[1]), parts)
-        result = main[i] - jnp.dot(product, mixed, precision=HIGH)
+        high = product.astype(BF16)
+        rest = (product - high.astype(F32)).astype(BF16)
+        result = main[i] - jnp.dot(
+            jnp.concatenate([high, rest, high], axis=1), mixed, preferred_element_type=F32
+        )
         targets[0][:rows] = result[:rows]
         targets[1][:rows] = result[rows:]
     for target in (keep, send_x, send_core, send_diagonal):

time: 55.1 us -> 54.6 us (level)
  no operation moved by 1% of the time
where the time goes in v17:
time: 54.6 us; the launch traced here: 54.4 us
  starting transfers between devices  24.7 us (45%)
  waiting for transfers between devices  19.4 us (36%)
  Pallas kernels  6.73 us (12%)
  other arithmetic  1.76 us (3%)
  between operations  1.14 us (2%)
  matrix products  0.56 us (1%)
    ppermute x17, waiting for transfers between devices, swap(): lax.ppermute(block, 'pos', [(i, i ^ bit) for i in range(lax.axis_size('po...  18 us
    ppermute x17, starting transfers between devices, swap(): lax.ppermute(block, 'pos', [(i, i ^ bit) for i in range(lax.axis_size('po...  18 us
    ppermute x3, starting transfers between devices, after(): return lax.ppermute(block, ('layer', 'pos'), route)  6.74 us
    pallas_call x1, Pallas kernels, per_device(): pl.pallas_call(functools.partial(grad_kernel, side), out_shape=[jax.Shape...  2.28 us
    pallas_call x1, Pallas kernels, per_device(): pl.pallas_call(functools.partial(cross_kernel, side), out_shape=[jax.Shap...  1.87 us
    ppermute x3, waiting for transfers between devices, after(): return lax.ppermute(block, ('layer', 'pos'), route)  1.43 us
  transfers between devices with their start and end apart: 20, of which 11 were waited for; matrix products, arithmetic and copies ran while one was open for 3% of the time, Pallas kernels for 1%

profile of v17, /device:TPU:0, one launch (start us, length us, event | category | flops | bytes accessed | tf_op | source)
XLA Modules:
  0.0 54.4 jit_solution(14510160732078621137)
XLA Ops:
  0.6 2.3 %shard_map.59 = (f32[2,296,128]{2,1,0:T(8,128)S(1)}, f32[1248,128]{1,0:T(8,128)S(1)}, bf16[2,9,72,128]{3,2,1,0:T(8,128)(2,1)S(1)}) custom-call(bf16[512,128]{1,0:T(8,128)(2,1)} %bitcast.90, bf16[512,128]{1,0:T(8,128)(2,1)} %bitcast.84, f32[128,128]{1,0:T(8,128)} %bitcast.94, f32[72,1152]{1,0:T(8,128)} %bitcast.93), custom_call_target="tpu_custom_call" | custom-call | tf_op jit(solution)/shard_map/pallas_call | solution.py:301
  3.5 2.6 %collective-permute-start = (bf16[2,512,128]{2,1,0:T(8,128)(2,1)S(1)}, bf16[2,512,128]{2,1,0:T(8,128)(2,1)S(1)}, u32[]{:S(2)}, u32[]{:S(2)}) collective-permute-start(bf16[2,512,128]{2,1,0:T(8,128)(2,1)S(1)} %pad_maximum_fusion), channel_id=1, source_target_pairs={{16,0},{17,1},{18,2},{19,3},{20,4},{21,5},{22,6},{23,7},{24,8},{25... | collective-permute-start | bytes 786440 | tf_op jit(solution)/shard_map/ppermute | solution.py:24
  6.4 1.6 %collective-permute-start.2 = (f16[296,128]{1,0:T(8,128)(2,1)S(1)}, f16[296,128]{1,0:T(8,128)(2,1)S(1)}, u32[]{:S(2)}, u32[]{:S(2)}) collective-permute-start(f16[296,128]{1,0:T(8,128)(2,1)S(1)} %pad_maximum_fusion.5), channel_id=1, source_target_pairs={{0,2},{1,3},{2,0},{3,1},{4,6},{5,7},{6,4},{7,5},{8,10},{9,11},{10,... | collective-permute-start | bytes 227336 | tf_op jit(solution)/shard_map/ppermute | solution.py:28
  8.1 2.8 %collective-permute-done.2 = f16[296,128]{1,0:T(8,128)(2,1)S(1)} collective-permute-done((f16[296,128]{1,0:T(8,128)(2,1)S(1)}, f16[296,128]{1,0:T(8,128)(2,1)S(1)}, u32[]{:S(2)}, u32[]{:S(2)}) %collective-permute-start.2) | collective-permute-done | bytes 75808 | tf_op jit(solution)/shard_map/ppermute | solution.py:28
  11.1 1.6 %collective-permute-start.3 = (f16[296,128]{1,0:T(8,128)(2,1)S(1)}, f16[296,128]{1,0:T(8,128)(2,1)S(1)}, u32[]{:S(2)}, u32[]{:S(2)}) collective-permute-start(f16[296,128]{1,0:T(8,128)(2,1)S(1)} %pad_maximum_fusion.6), channel_id=1, source_target_pairs={{0,4},{1,5},{2,6},{3,7},{4,0},{5,1},{6,2},{7,3},{8,12},{9,13},{10,... | collective-permute-start | bytes 227336 | tf_op jit(solution)/shard_map/ppermute | solution.py:28
  12.8 1.6 %collective-permute-start.5 = (f16[656,128]{1,0:T(8,128)(2,1)S(1)}, f16[656,128]{1,0:T(8,128)(2,1)S(1)}, u32[]{:S(2)}, u32[]{:S(2)}) collective-permute-start(f16[656,128]{1,0:T(8,128)(2,1)S(1)} %slice.238), channel_id=1, source_target_pairs={{0,2},{1,3},{2,0},{3,1},{4,6},{5,7},{6,4},{7,5},{8,10},{9,11},{10,... | collective-permute-start | bytes 503816 | tf_op jit(solution)/shard_map/ppermute | solution.py:28
  15.8 2.6 %collective-permute-start.4 = (f16[296,128]{1,0:T(8,128)(2,1)S(1)}, f16[296,128]{1,0:T(8,128)(2,1)S(1)}, u32[]{:S(2)}, u32[]{:S(2)}) collective-permute-start(f16[296,128]{1,0:T(8,128)(2,1)S(1)} %pad_maximum_fusion.7), channel_id=1, source_target_pairs={{0,8},{1,9},{2,10},{3,11},{4,12},{5,13},{6,14},{7,15},{8,0},{9,1},... | collective-permute-start | bytes 227336 | tf_op jit(solution)/shard_map/ppermute | solution.py:28
  18.5 2.7 %collective-permute-done.4 = f16[296,128]{1,0:T(8,128)(2,1)S(1)} collective-permute-done((f16[296,128]{1,0:T(8,128)(2,1)S(1)}, f16[296,128]{1,0:T(8,128)(2,1)S(1)}, u32[]{:S(2)}, u32[]{:S(2)}) %collective-permute-start.4) | collective-permute-done | bytes 75808 | tf_op jit(solution)/shard_map/ppermute | solution.py:28
  22.8 1.2 %collective-permute-start.7 = (bf16[32,288]{1,0:T(8,128)(2,1)S(1)}, bf16[32,288]{1,0:T(8,128)(2,1)S(1)}, u32[]{:S(2)}, u32[]{:S(2)}) collective-permute-start(bf16[32,288]{1,0:T(8,128)(2,1)S(1)} %get-tuple-element.38), channel_id=1, source_target_pairs={{0,4},{1,5},{2,6},{3,7},{4,0},{5,1},{6,2},{7,3},{8,12},{9,13},{10,... | collective-permute-start | bytes 55304 | tf_op jit(solution)/shard_map/ppermute | solution.py:28
  24.3 1.6 %collective-permute-start.8 = (bf16[2,512,128]{2,1,0:T(8,128)(2,1)S(1)}, bf16[2,512,128]{2,1,0:T(8,128)(2,1)S(1)}, u32[]{:S(2)}, u32[]{:S(2)}) collective-permute-start(bf16[2,512,128]{2,1,0:T(8,128)(2,1)S(1)} %pad_maximum_fusion.1.part_0), channel_id=1, source_target_pairs={{0,2},{1,3},{2,0},{3,1},{4,6},{5,7},{6,4},{7,5},{8,10},{9,11},{10,... | collective-permute-start | bytes 786440 | tf_op jit(solution)/shard_map/ppermute | solution.py:28
  25.8 0.8 %collective-permute-done.7 = bf16[32,288]{1,0:T(8,128)(2,1)S(1)} collective-permute-done((bf16[32,288]{1,0:T(8,128)(2,1)S(1)}, bf16[32,288]{1,0:T(8,128)(2,1)S(1)}, u32[]{:S(2)}, u32[]{:S(2)}) %collective-permute-start.7) | collective-permute-done | bytes 18464 | tf_op jit(solution)/shard_map/ppermute | solution.py:28
  26.7 3.4 %collective-permute-start.12 = (bf16[32,576]{1,0:T(8,128)(2,1)S(1)}, bf16[32,576]{1,0:T(8,128)(2,1)S(1)}, u32[]{:S(2)}, u32[]{:S(2)}) collective-permute-start(bf16[32,576]{1,0:T(8,128)(2,1)S(1)} %maximum_select_fusion.1), channel_id=1, source_target_pairs={{24,0},{25,1},{26,2},{27,3},{28,4},{29,5},{30,6},{31,7},{16,8},{17... | collective-permute-start | bytes 110600 | tf_op jit(solution)/shard_map/ppermute | solution.py:24
  30.9 1.6 %collective-permute-start.14 = (f32[64,128]{1,0:T(8,128)S(1)}, f32[64,128]{1,0:T(8,128)S(1)}, u32[]{:S(2)}, u32[]{:S(2)}) collective-permute-start(f32[64,128]{1,0:T(8,128)S(1)} %slice_bitcast_fusion.1), channel_id=1, source_target_pairs={{0,2},{1,3},{2,0},{3,1},{4,6},{5,7},{6,4},{7,5},{8,10},{9,11},{10,... | collective-permute-start | bytes 98312 | tf_op jit(solution)/shard_map/ppermute | solution.py:28
  32.7 1.4 %collective-permute-done.11 = bf16[32,576]{1,0:T(8,128)(2,1)S(1)} collective-permute-done((bf16[32,576]{1,0:T(8,128)(2,1)S(1)}, bf16[32,576]{1,0:T(8,128)(2,1)S(1)}, u32[]{:S(2)}, u32[]{:S(2)}) %collective-permute-start.11) | collective-permute-done | bytes 36896 | tf_op jit(solution)/shard_map/ppermute | solution.py:24
  34.9 1.9 %shard_map.62 = (f32[288,128]{1,0:T(8,128)S(1)}, f32[2,8,128]{2,1,0:T(8,128)S(1)}) custom-call(bf16[2,512,128]{2,1,0:T(8,128)(2,1)S(1)} %pad_maximum_fusion.1.part_0, bf16[2,512,128]{2,1,0:T(8,128)(2,1)S(1)} %collective-permute-done.8.part_1, bf16[2,512,128]{2,1,0:T(8,128)(2,1)S(1)} %collective-permute-done.9.part_2, ...), custom_call_target="tpu_custom_call" | custom-call | tf_op jit(solution)/shard_map/pallas_call | solution.py:410
  36.9 1.9 %collective-permute-start.15 = (f16[368,128]{1,0:T(8,128)(2,1)S(1)}, f16[368,128]{1,0:T(8,128)(2,1)S(1)}, u32[]{:S(2)}, u32[]{:S(2)}) collective-permute-start(f16[368,128]{1,0:T(8,128)(2,1)S(1)} %pad_maximum_fusion.3), channel_id=1, source_target_pairs={{0,4},{1,5},{2,6},{3,7},{4,0},{5,1},{6,2},{7,3},{8,12},{9,13},{10,... | collective-permute-start | bytes 282632 | tf_op jit(solution)/shard_map/ppermute | solution.py:28
  39.4 2.2 %collective-permute-done.15 = f16[368,128]{1,0:T(8,128)(2,1)S(1)} collective-permute-done((f16[368,128]{1,0:T(8,128)(2,1)S(1)}, f16[368,128]{1,0:T(8,128)(2,1)S(1)}, u32[]{:S(2)}, u32[]{:S(2)}) %collective-permute-start.15) | collective-permute-done | bytes 94240 | tf_op jit(solution)/shard_map/ppermute | solution.py:28
  41.8 0.9 %collective-permute-start.16 = (f16[368,128]{1,0:T(8,128)(2,1)S(1)}, f16[368,128]{1,0:T(8,128)(2,1)S(1)}, u32[]{:S(2)}, u32[]{:S(2)}) collective-permute-start(f16[368,128]{1,0:T(8,128)(2,1)S(1)} %pad_maximum_fusion.4), channel_id=1, source_target_pairs={{0,8},{1,9},{2,10},{3,11},{4,12},{5,13},{6,14},{7,15},{8,0},{9,1},... | collective-permute-start | bytes 282632 | tf_op jit(solution)/shard_map/ppermute | solution.py:28
  42.7 4.6 %collective-permute-done.16 = f16[368,128]{1,0:T(8,128)(2,1)S(1)} collective-permute-done((f16[368,128]{1,0:T(8,128)(2,1)S(1)}, f16[368,128]{1,0:T(8,128)(2,1)S(1)}, u32[]{:S(2)}, u32[]{:S(2)}) %collective-permute-start.16) | collective-permute-done | bytes 94240 | tf_op jit(solution)/shard_map/ppermute | solution.py:28
  47.4 0.8 %shard_map.63 = (f32[136,128]{1,0:T(8,128)S(1)}, f32[136,128]{1,0:T(8,128)S(1)}, f32[136,128]{1,0:T(8,128)S(1)}, f32[136,128]{1,0:T(8,128)S(1)}) custom-call(f32[288,128]{1,0:T(8,128)S(1)} %fusion.3.cross_t, f32[64,128]{1,0:T(8,128)S(1)} %fusion.14.gram, f32[128,128]{1,0:T(8,128)S(1)} %broadcast_multiply_fusion.g_inv, ...), custom_call_target="tpu_custom_call" | custom-call | tf_op jit(solution)/shard_map/pallas_call | solution.py:433
  48.2 1.6 %collective-permute-start.17 = (f32[136,128]{1,0:T(8,128)S(1)}, f32[136,128]{1,0:T(8,128)S(1)}, u32[]{:S(2)}, u32[]{:S(2)}) collective-permute-start(f32[136,128]{1,0:T(8,128)S(1)} %get-tuple-element.55), channel_id=1, source_target_pairs={{0,2},{1,3},{2,0},{3,1},{4,6},{5,7},{6,4},{7,5},{8,10},{9,11},{10,... | collective-permute-start | bytes 208904 | tf_op jit(solution)/shard_map/ppermute | solution.py:28
  50.4 2.2 %collective-permute-done.17.from_x = f32[136,128]{1,0:T(8,128)S(1)} collective-permute-done((f32[136,128]{1,0:T(8,128)S(1)}, f32[136,128]{1,0:T(8,128)S(1)}, u32[]{:S(2)}, u32[]{:S(2)}) %collective-permute-start.17) | collective-permute-done | bytes 69664 | tf_op jit(solution)/shard_map/ppermute | solution.py:28
  52.6 1.0 %collective-permute-done.19.from_diagonal = f32[136,128]{1,0:T(8,128)S(1)} collective-permute-done((f32[136,128]{1,0:T(8,128)S(1)}, f32[136,128]{1,0:T(8,128)S(1)}, u32[]{:S(2)}, u32[]{:S(2)}) %collective-permute-start.19) | collective-permute-done | bytes 69664 | tf_op jit(solution)/shard_map/ppermute | solution.py:28
  53.6 0.8 %shard_map.64 = (f32[72,128]{1,0:T(8,128)}, f32[2,128,128]{2,1,0:T(8,128)}) custom-call(f32[136,128]{1,0:T(8,128)S(1)} %get-tuple-element.54.mine, f32[136,128]{1,0:T(8,128)S(1)} %collective-permute-done.17.from_x, f32[136,128]{1,0:T(8,128)S(1)} %collective-permute-done.18.from_core, f32[136,128]{1,0:T(8,128)S(1)} %collective-permute-done.19.from_diagonal), custom_call_target="tpu_custom_call" | custom-call | tf_op jit(solution)/shard_map/pallas_call | solution.py:441
  (96 shorter events, 7.9 us)
Async XLA Ops:
  0.6 2.9 %copy-start = (bf16[1,2,16,16,128]{4,3,2,1,0:T(8,128)(2,1)S(1)}, bf16[1,2,16,16,128]{4,3,2,1,0:T(8,128)(2,1)}, u32[]{:S(2)}) copy-start(bf16[1,2,16,16,128]{4,3,2,1,0:T(8,128)(2,1)} %param.5) | copy-start | bytes 393220
  0.6 2.9 %copy-start.1 = (bf16[1,2,16,16,128]{4,3,2,1,0:T(8,128)(2,1)S(1)}, bf16[1,2,16,16,128]{4,3,2,1,0:T(8,128)(2,1)}, u32[]{:S(2)}) copy-start(bf16[1,2,16,16,128]{4,3,2,1,0:T(8,128)(2,1)} %param.4) | copy-start | bytes 393220
  3.0 3.2 %collective-permute-start.1 = (f16[1248,128]{1,0:T(8,128)(2,1)S(1)}, f16[1248,128]{1,0:T(8,128)(2,1)S(1)}, u32[]{:S(2)}, u32[]{:S(2)}) collective-permute-start(f16[1248,128]{1,0:T(8,128)(2,1)S(1)} %convert_element_type.42), channel_id=1, source_target_pairs={{0,1},{1,0},{2,3},{3,2},{4,5},{5,4},{6,7},{7,6},{8,9},{9,8},{10,11... | collective-permute-start | bytes 958472 | tf_op jit(solution)/shard_map/ppermute | solution.py:28
  3.5 12.2 %collective-permute-start = (bf16[2,512,128]{2,1,0:T(8,128)(2,1)S(1)}, bf16[2,512,128]{2,1,0:T(8,128)(2,1)S(1)}, u32[]{:S(2)}, u32[]{:S(2)}) collective-permute-start(bf16[2,512,128]{2,1,0:T(8,128)(2,1)S(1)} %pad_maximum_fusion), channel_id=1, source_target_pairs={{16,0},{17,1},{18,2},{19,3},{20,4},{21,5},{22,6},{23,7},{24,8},{25... | collective-permute-start | bytes 786440 | tf_op jit(solution)/shard_map/ppermute | solution.py:24
  6.4 4.5 %collective-permute-start.2 = (f16[296,128]{1,0:T(8,128)(2,1)S(1)}, f16[296,128]{1,0:T(8,128)(2,1)S(1)}, u32[]{:S(2)}, u32[]{:S(2)}) collective-permute-start(f16[296,128]{1,0:T(8,128)(2,1)S(1)} %pad_maximum_fusion.5), channel_id=1, source_target_pairs={{0,2},{1,3},{2,0},{3,1},{4,6},{5,7},{6,4},{7,5},{8,10},{9,11},{10,... | collective-permute-start | bytes 227336 | tf_op jit(solution)/shard_map/ppermute | solution.py:28
  11.1 4.4 %collective-permute-start.3 = (f16[296,128]{1,0:T(8,128)(2,1)S(1)}, f16[296,128]{1,0:T(8,128)(2,1)S(1)}, u32[]{:S(2)}, u32[]{:S(2)}) collective-permute-start(f16[296,128]{1,0:T(8,128)(2,1)S(1)} %pad_maximum_fusion.6), channel_id=1, source_target_pairs={{0,4},{1,5},{2,6},{3,7},{4,0},{5,1},{6,2},{7,3},{8,12},{9,13},{10,... | collective-permute-start | bytes 227336 | tf_op jit(solution)/shard_map/ppermute | solution.py:28
  12.8 8.4 %collective-permute-start.5 = (f16[656,128]{1,0:T(8,128)(2,1)S(1)}, f16[656,128]{1,0:T(8,128)(2,1)S(1)}, u32[]{:S(2)}, u32[]{:S(2)}) collective-permute-start(f16[656,128]{1,0:T(8,128)(2,1)S(1)} %slice.238), channel_id=1, source_target_pairs={{0,2},{1,3},{2,0},{3,1},{4,6},{5,7},{6,4},{7,5},{8,10},{9,11},{10,... | collective-permute-start | bytes 503816 | tf_op jit(solution)/shard_map/ppermute | solution.py:28
  14.4 7.4 %collective-permute-start.6 = (f16[656,128]{1,0:T(8,128)(2,1)S(1)}, f16[656,128]{1,0:T(8,128)(2,1)S(1)}, u32[]{:S(2)}, u32[]{:S(2)}) collective-permute-start(f16[656,128]{1,0:T(8,128)(2,1)S(1)} %get-tuple-element.37), channel_id=1, source_target_pairs={{0,2},{1,3},{2,0},{3,1},{4,6},{5,7},{6,4},{7,5},{8,10},{9,11},{10,... | collective-permute-start | bytes 503816 | tf_op jit(solution)/shard_map/ppermute | solution.py:28
  15.8 5.3 %collective-permute-start.4 = (f16[296,128]{1,0:T(8,128)(2,1)S(1)}, f16[296,128]{1,0:T(8,128)(2,1)S(1)}, u32[]{:S(2)}, u32[]{:S(2)}) collective-permute-start(f16[296,128]{1,0:T(8,128)(2,1)S(1)} %pad_maximum_fusion.7), channel_id=1, source_target_pairs={{0,8},{1,9},{2,10},{3,11},{4,12},{5,13},{6,14},{7,15},{8,0},{9,1},... | collective-permute-start | bytes 227336 | tf_op jit(solution)/shard_map/ppermute | solution.py:28
  22.8 3.8 %collective-permute-start.7 = (bf16[32,288]{1,0:T(8,128)(2,1)S(1)}, bf16[32,288]{1,0:T(8,128)(2,1)S(1)}, u32[]{:S(2)}, u32[]{:S(2)}) collective-permute-start(bf16[32,288]{1,0:T(8,128)(2,1)S(1)} %get-tuple-element.38), channel_id=1, source_target_pairs={{0,4},{1,5},{2,6},{3,7},{4,0},{5,1},{6,2},{7,3},{8,12},{9,13},{10,... | collective-permute-start | bytes 55304 | tf_op jit(solution)/shard_map/ppermute | solution.py:28
  24.3 8.2 %collective-permute-start.8 = (bf16[2,512,128]{2,1,0:T(8,128)(2,1)S(1)}, bf16[2,512,128]{2,1,0:T(8,128)(2,1)S(1)}, u32[]{:S(2)}, u32[]{:S(2)}) collective-permute-start(bf16[2,512,128]{2,1,0:T(8,128)(2,1)S(1)} %pad_maximum_fusion.1.part_0), channel_id=1, source_target_pairs={{0,2},{1,3},{2,0},{3,1},{4,6},{5,7},{6,4},{7,5},{8,10},{9,11},{10,... | collective-permute-start | bytes 786440 | tf_op jit(solution)/shard_map/ppermute | solution.py:28
  25.8 5.0 %collective-permute-start.13 = (f32[2,64,128]{2,1,0:T(8,128)S(1)}, f32[2,64,128]{2,1,0:T(8,128)S(1)}, u32[]{:S(2)}, u32[]{:S(2)}) collective-permute-start(f32[2,64,128]{2,1,0:T(8,128)S(1)} %get-tuple-element.45), channel_id=1, source_target_pairs={{0,1},{1,0},{2,3},{3,2},{4,5},{5,4},{6,7},{7,6},{8,9},{9,8},{10,11... | collective-permute-start | bytes 196616 | tf_op jit(solution)/shard_map/ppermute | solution.py:28
  26.7 5.9 %collective-permute-start.12 = (bf16[32,576]{1,0:T(8,128)(2,1)S(1)}, bf16[32,576]{1,0:T(8,128)(2,1)S(1)}, u32[]{:S(2)}, u32[]{:S(2)}) collective-permute-start(bf16[32,576]{1,0:T(8,128)(2,1)S(1)} %maximum_select_fusion.1), channel_id=1, source_target_pairs={{24,0},{25,1},{26,2},{27,3},{28,4},{29,5},{30,6},{31,7},{16,8},{17... | collective-permute-start | bytes 110600 | tf_op jit(solution)/shard_map/ppermute | solution.py:24
  30.1 4.0 %collective-permute-start.11 = (bf16[32,576]{1,0:T(8,128)(2,1)S(1)}, bf16[32,576]{1,0:T(8,128)(2,1)S(1)}, u32[]{:S(2)}, u32[]{:S(2)}) collective-permute-start(bf16[32,576]{1,0:T(8,128)(2,1)S(1)} %maximum_select_fusion.1), channel_id=1, source_target_pairs={{16,0},{17,1},{18,2},{19,3},{20,4},{21,5},{22,6},{23,7},{24,8},{25... | collective-permute-start | bytes 110600 | tf_op jit(solution)/shard_map/ppermute | solution.py:24
  30.8 4.0 %collective-permute-start.9 = (bf16[2,512,128]{2,1,0:T(8,128)(2,1)S(1)}, bf16[2,512,128]{2,1,0:T(8,128)(2,1)S(1)}, u32[]{:S(2)}, u32[]{:S(2)}) collective-permute-start(bf16[2,512,128]{2,1,0:T(8,128)(2,1)S(1)} %pad_maximum_fusion.1.part_0), channel_id=1, source_target_pairs={{0,1},{1,0},{2,3},{3,2},{4,5},{5,4},{6,7},{7,6},{8,9},{9,8},{10,11... | collective-permute-start | bytes 786440 | tf_op jit(solution)/shard_map/ppermute | solution.py:28
  30.9 4.0 %collective-permute-start.14 = (f32[64,128]{1,0:T(8,128)S(1)}, f32[64,128]{1,0:T(8,128)S(1)}, u32[]{:S(2)}, u32[]{:S(2)}) collective-permute-start(f32[64,128]{1,0:T(8,128)S(1)} %slice_bitcast_fusion.1), channel_id=1, source_target_pairs={{0,2},{1,3},{2,0},{3,1},{4,6},{5,7},{6,4},{7,5},{8,10},{9,11},{10,... | collective-permute-start | bytes 98312 | tf_op jit(solution)/shard_map/ppermute | solution.py:28
  32.4 2.4 %collective-permute-start.10 = (bf16[2,512,128]{2,1,0:T(8,128)(2,1)S(1)}, bf16[2,512,128]{2,1,0:T(8,128)(2,1)S(1)}, u32[]{:S(2)}, u32[]{:S(2)}) collective-permute-start(bf16[2,512,128]{2,1,0:T(8,128)(2,1)S(1)} %collective-permute-done.8.part_1), channel_id=1, source_target_pairs={{0,1},{1,0},{2,3},{3,2},{4,5},{5,4},{6,7},{7,6},{8,9},{9,8},{10,11... | collective-permute-start | bytes 786440 | tf_op jit(solution)/shard_map/ppermute | solution.py:28
  34.2 2.6 %copy-start.2 = (f32[1,128,128]{2,1,0:T(8,128)S(1)}, f32[1,128,128]{2,1,0:T(8,128)}, u32[]{:S(2)}) copy-start(f32[1,128,128]{2,1,0:T(8,128)} %param.7) | copy-start | bytes 196612
  36.9 4.6 %collective-permute-start.15 = (f16[368,128]{1,0:T(8,128)(2,1)S(1)}, f16[368,128]{1,0:T(8,128)(2,1)S(1)}, u32[]{:S(2)}, u32[]{:S(2)}) collective-permute-start(f16[368,128]{1,0:T(8,128)(2,1)S(1)} %pad_maximum_fusion.3), channel_id=1, source_target_pairs={{0,4},{1,5},{2,6},{3,7},{4,0},{5,1},{6,2},{7,3},{8,12},{9,13},{10,... | collective-permute-start | bytes 282632 | tf_op jit(solution)/shard_map/ppermute | solution.py:28
  41.8 5.5 %collective-permute-start.16 = (f16[368,128]{1,0:T(8,128)(2,1)S(1)}, f16[368,128]{1,0:T(8,128)(2,1)S(1)}, u32[]{:S(2)}, u32[]{:S(2)}) collective-permute-start(f16[368,128]{1,0:T(8,128)(2,1)S(1)} %pad_maximum_fusion.4), channel_id=1, source_target_pairs={{0,8},{1,9},{2,10},{3,11},{4,12},{5,13},{6,14},{7,15},{8,0},{9,1},... | collective-permute-start | bytes 282632 | tf_op jit(solution)/shard_map/ppermute | solution.py:28
  48.2 4.4 %collective-permute-start.17 = (f32[136,128]{1,0:T(8,128)S(1)}, f32[136,128]{1,0:T(8,128)S(1)}, u32[]{:S(2)}, u32[]{:S(2)}) collective-permute-start(f32[136,128]{1,0:T(8,128)S(1)} %get-tuple-element.55), channel_id=1, source_target_pairs={{0,2},{1,3},{2,0},{3,1},{4,6},{5,7},{6,4},{7,5},{8,10},{9,11},{10,... | collective-permute-start | bytes 208904 | tf_op jit(solution)/shard_map/ppermute | solution.py:28
  49.8 2.8 %collective-permute-start.18 = (f32[136,128]{1,0:T(8,128)S(1)}, f32[136,128]{1,0:T(8,128)S(1)}, u32[]{:S(2)}, u32[]{:S(2)}) collective-permute-start(f32[136,128]{1,0:T(8,128)S(1)} %get-tuple-element.56), channel_id=1, source_target_pairs={{0,1},{1,0},{2,3},{3,2},{4,5},{5,4},{6,7},{7,6},{8,9},{9,8},{10,11... | collective-permute-start | bytes 208904 | tf_op jit(solution)/shard_map/ppermute | solution.py:28
  49.8 3.8 %collective-permute-start.19 = (f32[136,128]{1,0:T(8,128)S(1)}, f32[136,128]{1,0:T(8,128)S(1)}, u32[]{:S(2)}, u32[]{:S(2)}) collective-permute-start(f32[136,128]{1,0:T(8,128)S(1)} %get-tuple-element.57), channel_id=1, source_target_pairs={{0,3},{1,2},{2,1},{3,0},{4,7},{5,6},{6,5},{7,4},{8,11},{9,10},{10,... | collective-permute-start | bytes 208904 | tf_op jit(solution)/shard_map/ppermute | solution.py:28
